TPU v7x, 32 devices: a whole 2x2x4 slice. The times are simulated.
32 devices in a mesh: gz: 4 (over y, core), gy: 8 (over z, x).
Axes of the slice: x: 2, y: 2, z: 4, core: 2. Of those that a mesh axis runs over, the one named last changes fastest.
Arguments:
- displacement: float32 [9, 128, 128, 128], P(None, 'gy', 'gz'), may hold values from -0.8 to 0.8
- density: float32 [128, 128, 128], P('gy', 'gz'), may hold values from 0.01 to 1
- passive: int32 [128, 128, 128], P('gy', 'gz'), may hold values 0 or 1
- solid: int32 [128, 128, 128], P('gy', 'gz'), may hold values 0 or 1
- stiffness: float32 [24, 24], replicated, may hold values from -0.06 to 2.5, as said below
Outputs:
- new_density: float32 [128, 128, 128], P('gy', 'gz')
- log_multiplier: float32 [], replicated
Inputs may be any that keep to these rules, and one draw needn't show every extreme that they name: `stiffness`: symmetric.
All inputs are finite; a program needn't handle non-finite values. No bound on the sum of `passive` or of `solid` on one device may be relied on, other than what follows from the above.
Results may differ from a plain program's by a relative error of at most 0.0003.
Values sent between devices are 32-bit elements; how exact they have to be, the bound alone decides.
No kernel may reach another device: no remote copies, remote signals or barrier semaphores. Data moves between devices by JAX's collectives and lax.ppermute only.
A program may use at most 64 MiB of HBM per device.

v0:
```python
import jax
import jax.numpy as jnp
from jax import lax
from jax.sharding import PartitionSpec as P

ITERS = 8


smoothing = 0.52
move_limit = 0.2
floor_density = 0.001
bracket_end = 12.0


def extended_2(cells, sides, width):
    for axis, dim in sides:
        count = lax.axis_size(axis)
        ends = count - 1
        head = lax.slice_in_dim(cells, 0, width, axis=dim)
        tail = lax.slice_in_dim(cells, cells.shape[dim] - width, cells.shape[dim], axis=dim)
        cells = jnp.concatenate(
            [
                lax.ppermute(tail, axis, [(i, (i + 1) % count) for i in range(ends)]),
                cells,
                lax.ppermute(head, axis, [((i + 1) % count, i) for i in range(ends)]),
            ],
            axis=dim,
        )
    return cells


def from_behind(value, axis, steps):
    count = lax.axis_size(axis)
    initial, last = (max(0, -steps), min(count, count - steps))
    return lax.ppermute(value, axis, [(source, source + steps) for source in range(initial, last)])


def cheb_weights():
    spectrum_top = 1.0 + 12.0 * smoothing
    centre_value = (spectrum_top + 1.0) / 2.0
    half_width = (spectrum_top - 1.0) / 2.0
    ratio_value = centre_value / half_width
    first_rho = 1.0 / ratio_value
    second_rho = 1.0 / (2.0 * ratio_value - first_rho)
    third_rho = 1.0 / (2.0 * ratio_value - second_rho)
    return (
        centre_value,
        second_rho * first_rho,
        2.0 * second_rho / half_width,
        third_rho * second_rho,
        2.0 * third_rho / half_width,
    )


def stencil(field):
    centre = field[1:-1, 1:-1]
    xpadded = jnp.pad(centre, ((0, 0), (0, 0), (1, 1)))
    beside = field[2:, 1:-1] + field[:-2, 1:-1] + field[1:-1, 2:] + field[1:-1, :-2]
    beside = beside + xpadded[:, :, 2:] + xpadded[:, :, :-2]
    return (1.0 + 6.0 * smoothing) * centre - smoothing * beside


def energy(lower, upper, stiffness):
    zcount = lower.shape[1] - 1
    xcount = lower.shape[2]
    planes = (jnp.pad(lower, ((0, 0), (0, 0), (0, 1))), jnp.pad(upper, ((0, 0), (0, 0), (0, 1))))
    corners = []
    for ylift in (0, 1):
        for zlift in (0, 1):
            for xlift in (0, 1):
                corners.append(planes[ylift][:, zlift : zlift + zcount, xlift : xlift + xcount])
    stacked = jnp.stack(corners).reshape(8, 3, 3, zcount * xcount)
    dofs = jnp.transpose(stacked, (0, 2, 1, 3)).reshape(24, 3 * zcount * xcount)
    forces = jnp.dot(
        stiffness, dofs, precision=lax.Precision.HIGHEST, preferred_element_type=jnp.float32
    )
    return jnp.sum(dofs * forces, axis=0).reshape(3, zcount, xcount).sum(axis=0)


def update(density, drive, passive, solid, loglam):
    candidate = density * jnp.sqrt(drive * jnp.exp(-loglam))
    lower = jnp.maximum(density - move_limit, floor_density)
    upper = jnp.minimum(density + move_limit, 1.0)
    candidate = jnp.clip(candidate, lower, upper)
    return jnp.where(solid == 1, 1.0, jnp.where(passive == 1, floor_density, candidate))


def volume_total(value):
    partial_y = lax.psum(value, "gy")
    return lax.psum(partial_y, "gz")


def apply_face(field):
    padded = extended_2(field, (("gz", 1), ("gy", 0)), 1)
    return stencil(padded)


def on_device(displacement, density, passive, solid, stiffness):
    rows_local = density.shape[0]
    face_y = displacement[:, 0:1]
    below_y = from_behind(face_y, "gy", -1)
    with_y = jnp.concatenate([displacement, below_y], axis=1)
    face_z = with_y[:, :, 0:1]
    below_z = from_behind(face_z, "gz", -1)
    extended = jnp.concatenate([with_y, below_z], axis=2)

    def one_row(index):
        lower = lax.dynamic_index_in_dim(extended, index, 1, keepdims=False)
        upper = lax.dynamic_index_in_dim(extended, index + 1, 1, keepdims=False)
        return energy(lower, upper, stiffness)

    work = lax.map(one_row, jnp.arange(rows_local, dtype=jnp.int32))
    source = density * (-3.0 * density * density * work)
    centre_value, weight_one, weight_two, weight_three, weight_four = cheb_weights()
    first = source / centre_value
    resid = source - apply_face(first)
    second = weight_one * first + weight_two * resid
    iterate = first + second
    resid = resid - apply_face(second)
    iterate = iterate + weight_three * second + weight_four * resid
    drive = jnp.maximum(-iterate / density, 0.0)
    masked = jnp.where(solid == 1, 1.0, jnp.where(passive == 1, floor_density, density))
    target = volume_total(jnp.sum(masked))
    start = (jnp.asarray(-bracket_end, jnp.float32), jnp.asarray(bracket_end, jnp.float32))

    def bisect(step, bounds):
        lower_log, upper_log = bounds
        middle = 0.5 * (lower_log + upper_log)
        volume = volume_total(jnp.sum(update(density, drive, passive, solid, middle)))
        above = volume > target
        return (jnp.where(above, middle, lower_log), jnp.where(above, upper_log, middle))

    lower_log, upper_log = lax.fori_loop(0, ITERS, bisect, start)
    log_multiplier = 0.5 * (lower_log + upper_log)
    return (update(density, drive, passive, solid, log_multiplier), log_multiplier)


def solution(mesh):
    placed = (
        P(None, "gy", "gz", None),
        P("gy", "gz", None),
        P("gy", "gz", None),
        P("gy", "gz", None),
        P(),
    )
    return jax.shard_map(
        on_device, mesh=mesh, in_specs=placed, out_specs=(P("gy", "gz", None), P()), check_vma=False
    )
```

profile of v0, /device:TPU:0, one launch (start us, length us, event | category | flops | bytes accessed | tf_op | source)
XLA Modules:
  0.0 445.5 jit_solution(13299543544742768845)
XLA Ops:
  4.8 5.5 %collective-permute-done = f32[9,1,32,128]{3,2,0,1:T(8,128)S(1)} collective-permute-done((f32[9,1,32,128]{3,2,0,1:T(8,128)S(1)}, f32[9,1,32,128]{3,2,0,1:T(8,128)S(1)}, u32[]{:S(2)}, u32[]{:S(2)}) %collective-permute-start) | collective-permute-done | bytes 147488 | tf_op jit(solution)/shard_map/ppermute | solution.py:35
  15.5 148.9 %while.28 = (s32[]{:T(128)}, f32[16,32,128]{2,1,0:T(8,128)}, s32[16]{0:T(128)S(1)}, f32[9,17,33,128]{3,2,0,1:T(8,128)}, f32[24,24]{1,0:T(8,128)S(1)}) while((s32[]{:T(128)}, f32[16,32,128]{2,1,0:T(8,128)}, s32[16]{0:T(128)S(1)}, f32[9,17,33,128]{3,2,0,1:T(8,128)}, f32[24,24]{1,0:T(8,128)S(1)}) %tuple.90), condition=%wide.region_3.4_spmd.clone, body=%wide.region_0.3_spmd.sunk.clone | while | flops 85520392 | bytes 14250917 | solution.py:112
  165.5 4.6 %collective-permute-start.2 = (f32[16,1,128]{2,1,0:T(1,128)S(1)}, f32[16,1,128]{2,1,0:T(1,128)S(1)}, u32[]{:S(2)}, u32[]{:S(2)}) collective-permute-start(f32[16,1,128]{2,1,0:T(1,128)S(1)} %get-tuple-element.224), channel_id=1, source_target_pairs={{0,8},{8,16},{16,24},{1,9},{9,17},{17,25},{2,10},{10,18},{18,26},{... | collective-permute-start | bytes 24584 | tf_op jit(solution)/shard_map/ppermute | solution.py:23
  174.5 5.1 %collective-permute-start.5 = (f32[1,34,128]{2,1,0:T(8,128)S(1)}, f32[1,34,128]{2,1,0:T(8,128)S(1)}, u32[]{:S(2)}, u32[]{:S(2)}) collective-permute-start(f32[1,34,128]{2,1,0:T(8,128)S(1)} %get-tuple-element.219), channel_id=1, source_target_pairs={{0,1},{1,2},{2,3},{3,4},{4,5},{5,6},{6,7},{8,9},{9,10},{10,11},{11... | collective-permute-start | bytes 52232 | tf_op jit(solution)/shard_map/ppermute | solution.py:23
  190.7 5.4 %collective-permute-start.9 = (f32[1,34,128]{2,1,0:T(8,128)S(1)}, f32[1,34,128]{2,1,0:T(8,128)S(1)}, u32[]{:S(2)}, u32[]{:S(2)}) collective-permute-start(f32[1,34,128]{2,1,0:T(8,128)S(1)} %get-tuple-element.217), channel_id=1, source_target_pairs={{0,1},{1,2},{2,3},{3,4},{4,5},{5,6},{6,7},{8,9},{9,10},{10,11},{11... | collective-permute-start | bytes 52232 | tf_op jit(solution)/shard_map/ppermute | solution.py:23
  196.2 22.3 %psum.34 = f32[]{:T(128)} all-reduce(f32[]{:T(128)} %get-tuple-element.199), channel_id=1, replica_groups=mesh['gz'=4,'gy'=8] {'gy'}, use_global_device_ids=true, to_apply=%region_5.6 | all-reduce | flops 1 | bytes 8 | tf_op jit(solution)/shard_map/psum | solution.py:89
  218.5 6.5 %psum.35 = f32[]{:T(128)} all-reduce(f32[]{:T(128)} %psum.34), channel_id=1, replica_groups=mesh['gz'=4,'gy'=8] {'gz'}, use_global_device_ids=true, to_apply=%region_6.7 | all-reduce | flops 1 | bytes 8 | tf_op jit(solution)/shard_map/psum | solution.py:90
  225.5 217.9 %while.29 = (s32[]{:T(128)}, f32[]{:T(128)}, f32[]{:T(128)}, s32[16,32,128]{2,1,0:T(8,128)S(1)}, s32[16,32,128]{2,1,0:T(8,128)S(1)}, /*index=5*/f32[16,32,128]{2,1,0:T(8,128)S(1)}, f32[16,32,128]{2,1,0:T(8,128)S(1)}, f32[]{:T(128)}) while((s32[]{:T(128)}, f32[]{:T(128)}, f32[]{:T(128)}, s32[16,32,128]{2,1,0:T(8,128)S(1)}, ...), condition=%wide.region_11.12_spmd.clone, body=%wide.region_7.11_spmd.sunk.clone | while | flops 851977 | bytes 1048760 | solution.py:133
  226.3 17.7 %psum.40 = f32[]{:T(128)} all-reduce(f32[]{:T(128)} %select_reduce_fusion.4), channel_id=1, replica_groups=mesh['gz'=4,'gy'=8] {'gy'}, use_global_device_ids=true, to_apply=%region_9.9 | all-reduce | flops 1 | bytes 8 | tf_op jit(solution)/shard_map/while/body/eval_jaxpr/psum | solution.py:89
  244.1 6.4 %psum.41 = f32[]{:T(128)} all-reduce(f32[]{:T(128)} %psum.40), channel_id=1, replica_groups=mesh['gz'=4,'gy'=8] {'gz'}, use_global_device_ids=true, to_apply=%region_10.10 | all-reduce | flops 1 | bytes 8 | tf_op jit(solution)/shard_map/while/body/eval_jaxpr/psum | solution.py:90
  252.6 19.7 %psum.40 = f32[]{:T(128)} all-reduce(f32[]{:T(128)} %select_reduce_fusion.4), channel_id=1, replica_groups=mesh['gz'=4,'gy'=8] {'gy'}, use_global_device_ids=true, to_apply=%region_9.9 | all-reduce | flops 1 | bytes 8 | tf_op jit(solution)/shard_map/while/body/eval_jaxpr/psum | solution.py:89
  272.3 6.4 %psum.41 = f32[]{:T(128)} all-reduce(f32[]{:T(128)} %psum.40), channel_id=1, replica_groups=mesh['gz'=4,'gy'=8] {'gz'}, use_global_device_ids=true, to_apply=%region_10.10 | all-reduce | flops 1 | bytes 8 | tf_op jit(solution)/shard_map/while/body/eval_jaxpr/psum | solution.py:90
  280.8 17.7 %psum.40 = f32[]{:T(128)} all-reduce(f32[]{:T(128)} %select_reduce_fusion.4), channel_id=1, replica_groups=mesh['gz'=4,'gy'=8] {'gy'}, use_global_device_ids=true, to_apply=%region_9.9 | all-reduce | flops 1 | bytes 8 | tf_op jit(solution)/shard_map/while/body/eval_jaxpr/psum | solution.py:89
  298.6 6.4 %psum.41 = f32[]{:T(128)} all-reduce(f32[]{:T(128)} %psum.40), channel_id=1, replica_groups=mesh['gz'=4,'gy'=8] {'gz'}, use_global_device_ids=true, to_apply=%region_10.10 | all-reduce | flops 1 | bytes 8 | tf_op jit(solution)/shard_map/while/body/eval_jaxpr/psum | solution.py:90
  307.0 19.7 %psum.40 = f32[]{:T(128)} all-reduce(f32[]{:T(128)} %select_reduce_fusion.4), channel_id=1, replica_groups=mesh['gz'=4,'gy'=8] {'gy'}, use_global_device_ids=true, to_apply=%region_9.9 | all-reduce | flops 1 | bytes 8 | tf_op jit(solution)/shard_map/while/body/eval_jaxpr/psum | solution.py:89
  326.8 6.4 %psum.41 = f32[]{:T(128)} all-reduce(f32[]{:T(128)} %psum.40), channel_id=1, replica_groups=mesh['gz'=4,'gy'=8] {'gz'}, use_global_device_ids=true, to_apply=%region_10.10 | all-reduce | flops 1 | bytes 8 | tf_op jit(solution)/shard_map/while/body/eval_jaxpr/psum | solution.py:90
  335.3 17.7 %psum.40 = f32[]{:T(128)} all-reduce(f32[]{:T(128)} %select_reduce_fusion.4), channel_id=1, replica_groups=mesh['gz'=4,'gy'=8] {'gy'}, use_global_device_ids=true, to_apply=%region_9.9 | all-reduce | flops 1 | bytes 8 | tf_op jit(solution)/shard_map/while/body/eval_jaxpr/psum | solution.py:89
  353.0 6.4 %psum.41 = f32[]{:T(128)} all-reduce(f32[]{:T(128)} %psum.40), channel_id=1, replica_groups=mesh['gz'=4,'gy'=8] {'gz'}, use_global_device_ids=true, to_apply=%region_10.10 | all-reduce | flops 1 | bytes 8 | tf_op jit(solution)/shard_map/while/body/eval_jaxpr/psum | solution.py:90
  361.5 19.7 %psum.40 = f32[]{:T(128)} all-reduce(f32[]{:T(128)} %select_reduce_fusion.4), channel_id=1, replica_groups=mesh['gz'=4,'gy'=8] {'gy'}, use_global_device_ids=true, to_apply=%region_9.9 | all-reduce | flops 1 | bytes 8 | tf_op jit(solution)/shard_map/while/body/eval_jaxpr/psum | solution.py:89
  381.3 6.4 %psum.41 = f32[]{:T(128)} all-reduce(f32[]{:T(128)} %psum.40), channel_id=1, replica_groups=mesh['gz'=4,'gy'=8] {'gz'}, use_global_device_ids=true, to_apply=%region_10.10 | all-reduce | flops 1 | bytes 8 | tf_op jit(solution)/shard_map/while/body/eval_jaxpr/psum | solution.py:90
  389.8 17.7 %psum.40 = f32[]{:T(128)} all-reduce(f32[]{:T(128)} %select_reduce_fusion.4), channel_id=1, replica_groups=mesh['gz'=4,'gy'=8] {'gy'}, use_global_device_ids=true, to_apply=%region_9.9 | all-reduce | flops 1 | bytes 8 | tf_op jit(solution)/shard_map/while/body/eval_jaxpr/psum | solution.py:89
  407.5 6.4 %psum.41 = f32[]{:T(128)} all-reduce(f32[]{:T(128)} %psum.40), channel_id=1, replica_groups=mesh['gz'=4,'gy'=8] {'gz'}, use_global_device_ids=true, to_apply=%region_10.10 | all-reduce | flops 1 | bytes 8 | tf_op jit(solution)/shard_map/while/body/eval_jaxpr/psum | solution.py:90
  416.0 19.7 %psum.40 = f32[]{:T(128)} all-reduce(f32[]{:T(128)} %select_reduce_fusion.4), channel_id=1, replica_groups=mesh['gz'=4,'gy'=8] {'gy'}, use_global_device_ids=true, to_apply=%region_9.9 | all-reduce | flops 1 | bytes 8 | tf_op jit(solution)/shard_map/while/body/eval_jaxpr/psum | solution.py:89
  435.8 6.4 %psum.41 = f32[]{:T(128)} all-reduce(f32[]{:T(128)} %psum.40), channel_id=1, replica_groups=mesh['gz'=4,'gy'=8] {'gz'}, use_global_device_ids=true, to_apply=%region_10.10 | all-reduce | flops 1 | bytes 8 | tf_op jit(solution)/shard_map/while/body/eval_jaxpr/psum | solution.py:90
  (434 shorter events, 130.0 us)
Async XLA Ops:
  1.6 8.7 %collective-permute-start = (f32[9,1,32,128]{3,2,0,1:T(8,128)S(1)}, f32[9,1,32,128]{3,2,0,1:T(8,128)S(1)}, u32[]{:S(2)}, u32[]{:S(2)}) collective-permute-start(f32[9,1,32,128]{3,2,0,1:T(8,128)S(1)} %copy.15), channel_id=1, source_target_pairs={{1,0},{2,1},{3,2},{4,3},{5,4},{6,5},{7,6},{9,8},{10,9},{11,10},{12... | collective-permute-start | bytes 442376 | tf_op jit(solution)/shard_map/ppermute | solution.py:35
  10.4 3.2 collective-permute-start.1
  11.7 3.8 copy-start.4
  15.5 148.9 %copy-start = (f32[16,32,128]{2,1,0:T(8,128)S(1)}, f32[16,32,128]{2,1,0:T(8,128)}, u32[]{:S(2)}) copy-start(f32[16,32,128]{2,1,0:T(8,128)} %param.10) | copy-start | bytes 786436
  15.5 165.5 %copy-start.1 = (s32[16,32,128]{2,1,0:T(8,128)S(1)}, s32[16,32,128]{2,1,0:T(8,128)}, u32[]{:S(2)}) copy-start(s32[16,32,128]{2,1,0:T(8,128)} %param.11) | copy-start | bytes 786436
  164.4 60.7 %copy-start.3 = (f32[16,32,128]{2,1,0:T(8,128)S(1)}, f32[16,32,128]{2,1,0:T(8,128)}, u32[]{:S(2)}) copy-start(f32[16,32,128]{2,1,0:T(8,128)} %get-tuple-element.170) | copy-start | bytes 786436
  165.5 5.9 %collective-permute-start.2 = (f32[16,1,128]{2,1,0:T(1,128)S(1)}, f32[16,1,128]{2,1,0:T(1,128)S(1)}, u32[]{:S(2)}, u32[]{:S(2)}) collective-permute-start(f32[16,1,128]{2,1,0:T(1,128)S(1)} %get-tuple-element.224), channel_id=1, source_target_pairs={{0,8},{8,16},{16,24},{1,9},{9,17},{17,25},{2,10},{10,18},{18,26},{... | collective-permute-start | bytes 24584 | tf_op jit(solution)/shard_map/ppermute | solution.py:23
  170.1 3.1 collective-permute-start.3
  173.2 6.4 %collective-permute-start.4 = (f32[1,34,128]{2,1,0:T(8,128)S(1)}, f32[1,34,128]{2,1,0:T(8,128)S(1)}, u32[]{:S(2)}, u32[]{:S(2)}) collective-permute-start(f32[1,34,128]{2,1,0:T(8,128)S(1)} %get-tuple-element.218), channel_id=1, source_target_pairs={{1,0},{2,1},{3,2},{4,3},{5,4},{6,5},{7,6},{9,8},{10,9},{11,10},{12... | collective-permute-start | bytes 52232 | tf_op jit(solution)/shard_map/ppermute | solution.py:25
  174.5 51.0 %copy-start.2 = (s32[16,32,128]{2,1,0:T(8,128)S(1)}, s32[16,32,128]{2,1,0:T(8,128)}, u32[]{:S(2)}) copy-start(s32[16,32,128]{2,1,0:T(8,128)} %param.12) | copy-start | bytes 786436
  174.5 6.5 %collective-permute-start.5 = (f32[1,34,128]{2,1,0:T(8,128)S(1)}, f32[1,34,128]{2,1,0:T(8,128)S(1)}, u32[]{:S(2)}, u32[]{:S(2)}) collective-permute-start(f32[1,34,128]{2,1,0:T(8,128)S(1)} %get-tuple-element.219), channel_id=1, source_target_pairs={{0,1},{1,2},{2,3},{3,4},{4,5},{5,6},{6,7},{8,9},{9,10},{10,11},{11... | collective-permute-start | bytes 52232 | tf_op jit(solution)/shard_map/ppermute | solution.py:23
  183.0 4.3 collective-permute-start.6
  186.0 3.5 collective-permute-start.7
  189.4 35.6 %collective-permute-start.8 = (f32[1,34,128]{2,1,0:T(8,128)S(1)}, f32[1,34,128]{2,1,0:T(8,128)S(1)}, u32[]{:S(2)}, u32[]{:S(2)}) collective-permute-start(f32[1,34,128]{2,1,0:T(8,128)S(1)} %get-tuple-element.216), channel_id=1, source_target_pairs={{1,0},{2,1},{3,2},{4,3},{5,4},{6,5},{7,6},{9,8},{10,9},{11,10},{12... | collective-permute-start | bytes 52232 | tf_op jit(solution)/shard_map/ppermute | solution.py:25
  190.7 34.3 %collective-permute-start.9 = (f32[1,34,128]{2,1,0:T(8,128)S(1)}, f32[1,34,128]{2,1,0:T(8,128)S(1)}, u32[]{:S(2)}, u32[]{:S(2)}) collective-permute-start(f32[1,34,128]{2,1,0:T(8,128)S(1)} %get-tuple-element.217), channel_id=1, source_target_pairs={{0,1},{1,2},{2,3},{3,4},{4,5},{5,6},{6,7},{8,9},{9,10},{10,11},{11... | collective-permute-start | bytes 52232 | tf_op jit(solution)/shard_map/ppermute | solution.py:23
where the time goes:
time: 447 us; the launch traced here: 445 us
  blocking collectives  230 us (51%)
  local copies, waits for them, and re-layouts  80.6 us (18%)
  loops' own time  63.1 us (14%)
  starting transfers between devices  25.8 us (6%)
  matrix products  18.8 us (4%)
  waiting for transfers between devices  12.7 us (3%)
  other arithmetic  12.6 us (3%)
    psum x9, blocking collectives, volume_total(): partial_y = lax.psum(value, 'gy')  172 us
    psum x9, blocking collectives, volume_total(): return lax.psum(partial_y, 'gz')  57.5 us
    another operation x1, loops' own time, on_device(): work = lax.map(one_row, jnp.arange(rows_local, dtype=jnp.int32))  52.3 us
    dot_general x16, matrix products, energy(): jnp.dot(stiffness, dofs, precision=lax.Precision.HIGHEST, preferred_eleme...  18.8 us
    ppermute x4, starting transfers between devices, extended_2(): lax.ppermute(tail, axis, [(i, (i + 1) % count) for i in range(ends)])  18.1 us
    squeeze x16, local copies, waits for them, and re-layouts, one_row(): upper = lax.dynamic_index_in_dim(extended, index + 1, 1, keepdims=False)  16.7 us
    while x128, local copies, waits for them, and re-layouts  16.3 us
    transpose x16, local copies, waits for them, and re-layouts, energy(): dofs = jnp.transpose(stacked, (0, 2, 1, 3)).reshape(24, 3 * zcount * xcount)  13 us
  transfers between devices with their start and end apart: 10, of which 5 were waited for; matrix products, arithmetic and copies ran while one was open for 0% of the time, Pallas kernels for 0%

commit v1 on v0

v1 whole, which is shorter than its diff:
```python
import functools

import jax
import jax.numpy as jnp
from jax import lax
from jax.experimental import pallas as pl
from jax.experimental.pallas import tpu as pltpu
from jax.sharding import PartitionSpec as P

ITERS = 8
POINTS = 2**ITERS

smoothing = 0.52
move_limit = 0.2
floor_density = 0.001
bracket_end = 12.0

f32 = jnp.float32
bf16 = jnp.bfloat16


def cheb_weights():
    spectrum_top = 1.0 + 12.0 * smoothing
    centre_value = (spectrum_top + 1.0) / 2.0
    half_width = (spectrum_top - 1.0) / 2.0
    ratio_value = centre_value / half_width
    first_rho = 1.0 / ratio_value
    second_rho = 1.0 / (2.0 * ratio_value - first_rho)
    third_rho = 1.0 / (2.0 * ratio_value - second_rho)
    return (
        centre_value,
        second_rho * first_rho,
        2.0 * second_rho / half_width,
        third_rho * second_rho,
        2.0 * third_rho / half_width,
    )


def filter_weights():
    t, w1, w2, w3, w4 = cheb_weights()
    diag = 1.0 + 6.0 * smoothing
    alpha = w1 / t + w2 * (1.0 - diag / t)
    beta = w2 * smoothing / t
    gamma = 1.0 / t - w4 * w1 / (t * w2)
    delta = 1.0 + w3 + w4 / w2 - w4 * diag
    eps = w4 * smoothing
    return alpha, beta, gamma, delta, eps


def lane_up(v):
    n = v.shape[-1]
    lane = lax.broadcasted_iota(jnp.int32, v.shape, v.ndim - 1)
    return jnp.where(lane < n - 1, pltpu.roll(v, n - 1, v.ndim - 1), 0.0)


def lane_down(v):
    n = v.shape[-1]
    lane = lax.broadcasted_iota(jnp.int32, v.shape, v.ndim - 1)
    return jnp.where(lane > 0, pltpu.roll(v, 1, v.ndim - 1), 0.0)


def build_matrix(stiff, mat):
    shape = (24, 112)
    col = lax.broadcasted_iota(jnp.int32, shape, 1)
    row = lax.broadcasted_iota(jnp.int32, shape, 0)
    main = col < 96
    dy = jnp.where(main, jnp.where(col >= 48, 1, 0), jnp.where(col >= 104, 1, 0))
    q = col - 48 * dy
    e = col - 96 - 8 * dy
    c = jnp.where(main, q >> 4, e >> 1)
    dx = jnp.where(main, (q >> 3) & 1, e & 1)
    valid = main | (e < 6)
    dof0 = 3 * (4 * dy + dx) + c
    pick0 = jnp.where(main & (row == dof0), 1.0, 0.0)
    pick1 = jnp.where(valid & (row == dof0 + 6), 1.0, 0.0)
    k = stiff[...]
    hp = lax.Precision.HIGHEST
    k0 = jnp.dot(k, pick0, precision=hp, preferred_element_type=f32)
    k1 = jnp.dot(k, pick1, precision=hp, preferred_element_type=f32)
    col8 = lax.broadcasted_iota(jnp.int32, (8, 112), 1)
    row8 = lax.broadcasted_iota(jnp.int32, (8, 112), 0)
    main8 = col8 < 96
    zc = col8 & 7
    m0 = main8 & (zc == row8)
    m1 = jnp.where(main8, zc, 8) == row8 + 1
    rows = []
    for dz in range(2):
        for dy_ in range(2):
            for c_ in range(3):
                for dx_ in range(2):
                    r = 3 * (4 * dy_ + 2 * dz + dx_) + c_
                    rows.append(jnp.where(m0, k0[r : r + 1], 0.0) + jnp.where(m1, k1[r : r + 1], 0.0))
    full = jnp.concatenate(rows, axis=0)
    hi = full.astype(bf16)
    lo = (full - hi.astype(f32)).astype(bf16)
    mat[:, 0:112] = hi
    mat[:, 112:224] = lo


def prepare(plane, ext, p, main_s, ext_s, mul_s):
    for l in range(3):
        for c in range(3):
            u = plane(3 * l + c)
            x = ext(3 * l + c)
            nz, nx = u.shape
            last = lax.broadcasted_iota(jnp.int32, u.shape, 0) == nz - 1
            both = (u, lane_up(u))
            bothx = (x, lane_up(x))
            for w in range(nz // 8):
                sl = slice(8 * w, 8 * w + 8)
                main_s[p, l, 16 * c : 16 * c + 16, w * nx : (w + 1) * nx] = jnp.concatenate(
                    [both[0][sl], both[1][sl]], axis=0
                ).astype(bf16)
            for dx in range(2):
                v, vx = both[dx], bothx[dx]
                k = 2 * c + dx
                for w in range(nz // 8):
                    nxt = v[8 * w + 8 : 8 * w + 9] if 8 * w + 8 < nz else vx
                    ext_s[p, l, k : k + 1, w * nx : (w + 1) * nx] = nxt
                m = 2.0 * v - v.astype(bf16).astype(f32)
                mx = 2.0 * vx - vx.astype(bf16).astype(f32)
                mul_s[p, l, k, 0] = m
                mul_s[p, l, k, 1] = jnp.where(last, jnp.broadcast_to(mx, v.shape), pltpu.roll(m, nz - 1, 0))


def energy_kernel(disp, fy, fz, fc, dens, stiff, src, zlow, zhigh, mat, main_s, ext_s, mul_s):
    _, ny, nz, nx = disp.shape
    build_matrix(stiff, mat)
    ext_s[...] = jnp.zeros_like(ext_s)

    prepare(lambda i: fy[i], lambda i: fc[i : i + 1], ny, main_s, ext_s, mul_s)

    def prep_body(y, _):
        prepare(lambda i: disp[i, y], lambda i: fz[i, pl.ds(y, 1)], y, main_s, ext_s, mul_s)
        return 0

    lax.fori_loop(0, ny, prep_body, 0)

    def body(y, _):
        acc = [None] * (nz // 8)
        for l in range(3):
            ext = jnp.concatenate([ext_s[y, l], ext_s[y + 1, l]], axis=0).astype(bf16)
            one = jnp.concatenate([main_s[y, l], main_s[y + 1, l], ext], axis=0)
            rhs = jnp.concatenate([one, one], axis=0)
            force = jnp.dot(mat[...], rhs, preferred_element_type=f32)
            i = 0
            for dz in range(2):
                for dy in range(2):
                    for k in range(6):
                        for w in range(nz // 8):
                            term = (
                                force[8 * i : 8 * i + 8, w * nx : (w + 1) * nx]
                                * mul_s[y + dy, l, k, dz, 8 * w : 8 * w + 8]
                            )
                            acc[w] = term if acc[w] is None else acc[w] + term
                        i += 1
        d = dens[y]
        s = d * (-3.0 * d * d * jnp.concatenate(acc, axis=0))
        src[y] = s
        for layer in range(2):
            zlow[layer, pl.ds(y, 1)] = s[layer : layer + 1]
            zhigh[layer, pl.ds(y, 1)] = s[nz - 2 + layer : nz - 1 + layer]
        return 0

    lax.fori_loop(0, ny, body, 0)


def energy_call(disp, fy, fz, fc, dens, stiff):
    _, ny, nz, nx = disp.shape
    return pl.pallas_call(
        energy_kernel,
        out_shape=(
            jax.ShapeDtypeStruct((ny, nz, nx), f32),
            jax.ShapeDtypeStruct((2, ny, nx), f32),
            jax.ShapeDtypeStruct((2, ny, nx), f32),
        ),
        scratch_shapes=[
            pltpu.VMEM((192, 224), bf16),
            pltpu.VMEM((ny + 1, 3, 48, nx * (nz // 8)), bf16),
            pltpu.VMEM((ny + 1, 3, 8, nx * (nz // 8)), f32),
            pltpu.VMEM((ny + 1, 3, 6, 2, nz, nx), f32),
        ],
        compiler_params=pltpu.CompilerParams(vmem_limit_bytes=48 * 2**20),
        name="energy",
    )(disp, fy, fz, fc, dens, stiff)


def filter_kernel(flags, src, yl, yh, zl, zh, dens, passive, solid, amp, low, high, vols, s_s, d_s, acc_s):
    ny, nz, nx = src.shape
    alpha, beta, gamma, delta, eps = filter_weights()
    off = 8
    s_s[2 : ny + 2, off : off + nz] = src[...]
    s_s[0:2, off : off + nz] = yl[...]
    s_s[ny + 2 : ny + 4, off : off + nz] = yh[...]
    for y in range(ny + 4):
        s_s[y, off - 2 : off] = jnp.concatenate([zl[0, y : y + 1], zl[1, y : y + 1]], axis=0)
        s_s[y, off + nz : off + nz + 2] = jnp.concatenate([zh[0, y : y + 1], zh[1, y : y + 1]], axis=0)

    rows = s_s.shape[1]

    def beside(v):
        return pltpu.roll(v, 1, 0) + pltpu.roll(v, rows - 1, 0) + lane_up(v) + lane_down(v)

    row = lax.broadcasted_iota(jnp.int32, (rows, nx), 0)
    keep = jnp.where(row < off, flags[2], jnp.where(row >= off + nz, flags[3], 1)) == 1

    def second(y, _):
        c = s_s[y + 1]
        d2 = alpha * c + beta * (beside(c) + s_s[y] + s_s[y + 2])
        inside = jnp.where(y == 0, flags[0], jnp.where(y == ny + 1, flags[1], 1)) == 1
        d_s[y] = jnp.where(keep & inside, d2, 0.0)
        return 0

    lax.fori_loop(0, ny + 2, second, 0)

    def third(y, total):
        d2 = d_s[y + 1]
        p3 = gamma * s_s[y + 2] + delta * d2 + eps * (beside(d2) + d_s[y] + d_s[y + 2])
        p3 = p3[off : off + nz]
        d = dens[y]
        amp[y] = jnp.sqrt(jnp.maximum(-p3 * d, 0.0))
        sol = solid[y] == 1
        pas = passive[y] == 1
        lower = jnp.maximum(d - move_limit, floor_density)
        upper = jnp.minimum(d + move_limit, 1.0)
        low[y] = jnp.where(sol, 1.0, jnp.where(pas, floor_density, lower))
        high[y] = jnp.where(sol, 1.0, jnp.where(pas, floor_density, upper))
        masked = jnp.where(sol, 1.0, jnp.where(pas, floor_density, d))
        return total + masked

    total = lax.fori_loop(0, ny, third, jnp.zeros((nz, nx), f32))
    target = jnp.sum(total, axis=0, keepdims=True)

    groups = POINTS // 8
    half = groups // 2
    sub = lax.broadcasted_iota(jnp.int32, (8, nx), 0)
    for part in range(2):
        scale = []
        for g in range(half):
            k = sub + 8 * (part * half + g)
            mid = -bracket_end + (2.0 * bracket_end / POINTS) * k.astype(f32)
            scale.append(jnp.exp(-0.5 * mid))

        def volume(y, acc):
            acc = list(acc)
            for z in range(nz):
                a = jnp.broadcast_to(amp[y, z : z + 1], (8, nx))
                lo = jnp.broadcast_to(low[y, z : z + 1], (8, nx))
                hi = jnp.broadcast_to(high[y, z : z + 1], (8, nx))
                for g in range(half):
                    acc[g] = acc[g] + jnp.minimum(jnp.maximum(a * scale[g], lo), hi)
            return tuple(acc)

        acc = lax.fori_loop(0, ny, volume, tuple(jnp.zeros((8, nx), f32) for _ in range(half)))
        for g in range(half):
            value = acc[g]
            if part == 0 and g == 0:
                value = jnp.where(sub == 0, jnp.broadcast_to(target, (8, nx)), value)
            acc_s[8 * (part * half + g) : 8 * (part * half + g) + 8] = value
    vols[...] = jnp.sum(jnp.transpose(acc_s[...]), axis=0, keepdims=True)


def filter_call(flags, src, yl, yh, zl, zh, dens, passive, solid):
    ny, nz, nx = src.shape
    field = jax.ShapeDtypeStruct((ny, nz, nx), f32)
    vmem = pl.BlockSpec(memory_space=pltpu.VMEM)
    return pl.pallas_call(
        filter_kernel,
        in_specs=[pl.BlockSpec(memory_space=pltpu.SMEM)] + [vmem] * 8,
        out_shape=(field, field, field, jax.ShapeDtypeStruct((1, POINTS), f32)),
        scratch_shapes=[
            pltpu.VMEM((ny + 4, nz + 16, nx), f32),
            pltpu.VMEM((ny + 2, nz + 16, nx), f32),
            pltpu.VMEM((POINTS, nx), f32),
        ],
        compiler_params=pltpu.CompilerParams(vmem_limit_bytes=32 * 2**20),
        name="filter",
    )(flags, src, yl, yh, zl, zh, dens, passive, solid)


def update_kernel(vols, amp, low, high, new, logm):
    target = vols[0, 0]
    k = jnp.int32(0)
    step = POINTS // 2
    while step >= 1:
        k = jnp.where(vols[0, k + step] > target, k + step, k)
        step //= 2
    middle = -bracket_end + (2.0 * bracket_end / POINTS) * (k.astype(f32) + 0.5)
    logm[0] = middle
    scale = jnp.exp(jnp.full((1, amp.shape[-1]), -0.5 * middle, f32))

    def body(y, _):
        new[y] = jnp.minimum(jnp.maximum(amp[y] * scale, low[y]), high[y])
        return 0

    lax.fori_loop(0, amp.shape[0], body, 0)


def update_call(vols, amp, low, high):
    vmem = pl.BlockSpec(memory_space=pltpu.VMEM)
    return pl.pallas_call(
        update_kernel,
        in_specs=[pl.BlockSpec(memory_space=pltpu.SMEM), vmem, vmem, vmem],
        out_specs=(vmem, pl.BlockSpec(memory_space=pltpu.SMEM)),
        out_shape=(jax.ShapeDtypeStruct(amp.shape, f32), jax.ShapeDtypeStruct((1,), f32)),
        name="update",
    )(vols, amp, low, high)


def to_lower(value, axis):
    count = lax.axis_size(axis)
    return lax.ppermute(value, axis, [(i + 1, i) for i in range(count - 1)])


def to_upper(value, axis):
    count = lax.axis_size(axis)
    return lax.ppermute(value, axis, [(i, i + 1) for i in range(count - 1)])


def on_device(displacement, density, passive, solid, stiffness):
    ny, nz, nx = density.shape
    gy, gz = lax.axis_size("gy"), lax.axis_size("gz")
    iy, iz = lax.axis_index("gy"), lax.axis_index("gz")

    fy = to_lower(displacement[:, 0], "gy")
    fz = to_lower(displacement[:, :, 0], "gz")
    pairs = [((z + 1) * gy + y + 1, z * gy + y) for z in range(gz - 1) for y in range(gy - 1)]
    fc = lax.ppermute(displacement[:, 0, 0], ("gz", "gy"), pairs)
    src, zlow, zhigh = energy_call(displacement, fy, fz, fc, density, stiffness)

    yl = to_upper(src[ny - 2 :], "gy")
    yh = to_lower(src[:2], "gy")
    own_low = jnp.concatenate([yl[:, 0:2].swapaxes(0, 1), zlow, yh[:, 0:2].swapaxes(0, 1)], axis=1)
    own_high = jnp.concatenate([yl[:, nz - 2 :].swapaxes(0, 1), zhigh, yh[:, nz - 2 :].swapaxes(0, 1)], axis=1)
    zl = to_upper(own_high, "gz")
    zh = to_lower(own_low, "gz")
    flags = jnp.stack([iy > 0, iy < gy - 1, iz > 0, iz < gz - 1]).astype(jnp.int32)
    amp, low, high, vols = filter_call(flags, src, yl, yh, zl, zh, density, passive, solid)

    vols = lax.psum(vols, ("gz", "gy"))
    new, logm = update_call(vols, amp, low, high)
    return new, logm.reshape(())


def solution(mesh):
    placed = (
        P(None, "gy", "gz", None),
        P("gy", "gz", None),
        P("gy", "gz", None),
        P("gy", "gz", None),
        P(),
    )
    return jax.shard_map(
        on_device, mesh=mesh, in_specs=placed, out_specs=(P("gy", "gz", None), P()), check_vma=False
    )
```

time: 447 us -> 99.7 us (0.22)
  blocking collectives: 230 us -> 43.2 us
  local copies, waits for them, and re-layouts: 80.6 us -> 8.45 us
  loops' own time: 63.1 us -> 0 us
  Pallas kernels: 0 us -> 22 us
  matrix products: 18.8 us -> 0 us
  other arithmetic: 12.6 us -> 0.1 us
  starting transfers between devices: 25.8 us -> 14 us
    psum x18 -> x1, blocking collectives: 230 us -> 43.2 us  [on_device(): vols = lax.psum(vols, ('gz', 'gy'))]
    another operation x2 -> x0, loops' own time: 63.1 us -> none  [the longest x1 52.3 us: on_device(): work = lax.map(one_row, jnp.arange(rows_local, dtype=jnp.int32))]
    pallas_call x0 -> x3, Pallas kernels: none -> 22 us  [the longest x1 12.6 us: filter_call(): pl.pallas_call(filter_kernel, in_specs=[pl.BlockSpec(memory_space=pltpu.S...]
    dot_general x16 -> x0, matrix products: 18.8 us -> none  [energy(): jnp.dot(stiffness, dofs, precision=lax.Precision.HIGHEST, preferred_eleme...]
    while x128 -> x0, local copies, waits for them, and re-layouts: 16.3 us -> none
    squeeze x16 -> x1, local copies, waits for them, and re-layouts: 16.7 us -> 0.97 us  [on_device(): fy = to_lower(displacement[:, 0], 'gy')]
    transpose x16 -> x2, local copies, waits for them, and re-layouts: 13 us -> 0.01 us  [the longest x1 0.01 us: on_device(): yh[:, 0:2].swapaxes(0, 1)]
    ppermute x10 -> x7, starting transfers between devices: 25.8 us -> 14 us  [the longest x2 7.55 us: to_upper(): return lax.ppermute(value, axis, [(i, i + 1) for i in range(count - 1)])]
  transfers between devices with their start and end apart: 10 -> 7, of which waited for: 5 -> 3; matrix products, arithmetic and copies ran while one was open for 0% -> 2% of each run, Pallas kernels for 0% -> 0%
where the time goes in v1:
time: 99.7 us; the launch traced here: 99.1 us
  blocking collectives  43.2 us (43%)
  Pallas kernels  22 us (22%)
  starting transfers between devices  14 us (14%)
  waiting for transfers between devices  10.6 us (11%)
  local copies, waits for them, and re-layouts  8.45 us (8%)
    psum x1, blocking collectives, on_device(): vols = lax.psum(vols, ('gz', 'gy'))  43.2 us
    pallas_call x1, Pallas kernels, filter_call(): pl.pallas_call(filter_kernel, in_specs=[pl.BlockSpec(memory_space=pltpu.S...  12.6 us
    ppermute x2, starting transfers between devices, to_upper(): return lax.ppermute(value, axis, [(i, i + 1) for i in range(count - 1)])  7.55 us
    pallas_call x1, Pallas kernels, energy_call(): pl.pallas_call(energy_kernel, out_shape=(jax.ShapeDtypeStruct((ny, nz, nx...  7.44 us
    ppermute x1, waiting for transfers between devices, on_device(): fc = lax.ppermute(displacement[:, 0, 0], ('gz', 'gy'), pairs)  6.23 us
    unnamed x19, local copies, waits for them, and re-layouts  5.41 us
    ppermute x4, starting transfers between devices, to_lower(): return lax.ppermute(value, axis, [(i + 1, i) for i in range(count - 1)])  5.17 us
    ppermute x4, waiting for transfers between devices, to_lower(): return lax.ppermute(value, axis, [(i + 1, i) for i in range(count - 1)])  2.63 us
  transfers between devices with their start and end apart: 7, of which 3 were waited for; matrix products, arithmetic and copies ran while one was open for 2% of the time, Pallas kernels for 0%

profile of v1, /device:TPU:0, one launch (start us, length us, event | category | flops | bytes accessed | tf_op | source)
XLA Modules:
  0.0 99.1 jit_solution(17256892222921603145)
XLA Ops:
  0.6 1.0 slice_bitcast_fusion
  1.6 1.3 %collective-permute-start = (f32[9,32,128]{2,1,0:T(8,128)S(1)}, f32[9,32,128]{2,1,0:T(8,128)S(1)}, u32[]{:S(2)}, u32[]{:S(2)}) collective-permute-start(f32[9,32,128]{2,1,0:T(8,128)S(1)} %slice_bitcast_fusion), channel_id=1, source_target_pairs={{1,0},{2,1},{3,2},{4,3},{5,4},{6,5},{7,6},{9,8},{10,9},{11,10},{12... | collective-permute-start | bytes 442376 | tf_op jit(solution)/shard_map/ppermute | solution.py:312
  2.9 1.1 %slice.28 = f32[9,16,1,128]{3,2,1,0:T(1,128)S(1)} slice(f32[9,16,32,128]{3,2,1,0:T(8,128)} %disp.1), slice={[0:9], [0:16], [0:1], [0:128]} | slice | bytes 147456 | tf_op jit(solution)/shard_map/slice | solution.py:326
  4.0 1.3 %collective-permute-start.1 = (f32[9,16,128]{2,1,0:T(8,128)S(1)}, f32[9,16,128]{2,1,0:T(8,128)S(1)}, u32[]{:S(2)}, u32[]{:S(2)}) collective-permute-start(f32[9,16,128]{2,1,0:T(8,128)S(1)} %bitcast.23), channel_id=1, source_target_pairs={{8,0},{16,8},{24,16},{9,1},{17,9},{25,17},{10,2},{18,10},{26,18},{... | collective-permute-start | bytes 221192 | tf_op jit(solution)/shard_map/ppermute | solution.py:312
  5.3 0.8 slice.29
  6.1 1.3 %collective-permute-start.2 = (f32[9,128]{1,0:T(8,128)S(1)}, f32[9,128]{1,0:T(8,128)S(1)}, u32[]{:S(2)}, u32[]{:S(2)}) collective-permute-start(f32[9,128]{1,0:T(8,128)S(1)} %bitcast.24), channel_id=1, source_target_pairs={{9,0},{10,1},{11,2},{12,3},{13,4},{14,5},{15,6},{17,8},{18,9},{19,... | collective-permute-start | bytes 13832 | tf_op jit(solution)/shard_map/ppermute | solution.py:328
  7.4 6.2 %collective-permute-done.2.fc = f32[9,128]{1,0:T(8,128)S(1)} collective-permute-done((f32[9,128]{1,0:T(8,128)S(1)}, f32[9,128]{1,0:T(8,128)S(1)}, u32[]{:S(2)}, u32[]{:S(2)}) %collective-permute-start.2) | collective-permute-done | bytes 4640 | tf_op jit(solution)/shard_map/ppermute | solution.py:328
  13.6 1.7 %copy-done = f32[9,16,32,128]{3,2,1,0:T(8,128)S(1)} copy-done((f32[9,16,32,128]{3,2,1,0:T(8,128)S(1)}, f32[9,16,32,128]{3,2,1,0:T(8,128)}, u32[]{:S(2)}) %copy-start) | copy-done | bytes 2359320
  15.3 0.9 copy-done.1
  16.2 0.7 copy-done.8
  17.0 7.4 %energy.1 = (f32[16,32,128]{2,1,0:T(8,128)S(1)}, f32[2,16,128]{2,1,0:T(8,128)S(1)}, f32[2,16,128]{2,1,0:T(8,128)S(1)}) custom-call(f32[9,16,32,128]{3,2,1,0:T(8,128)S(1)} %copy-done, f32[9,32,128]{2,1,0:T(8,128)S(1)} %collective-permute-done.fy, f32[9,16,128]{2,1,0:T(8,128)S(1)} %collective-permute-done.1.fz, f32[9,128]{1,0:T(8,128)S(1)} %collective-permute-done.2.fc, ...), custom_call_target="tpu_custom_call" | custom-call | tf_op jit(solution)/shard_map/energy/pallas_call | solution.py:170
  24.4 0.2 copy.10
  24.6 1.3 %collective-permute-start.4 = (f32[2,32,128]{2,0,1:T(2,128)S(1)}, f32[2,32,128]{2,0,1:T(2,128)S(1)}, u32[]{:S(2)}, u32[]{:S(2)}) collective-permute-start(f32[2,32,128]{2,0,1:T(2,128)S(1)} %get-tuple-element.20), channel_id=1, source_target_pairs={{1,0},{2,1},{3,2},{4,3},{5,4},{6,5},{7,6},{9,8},{10,9},{11,10},{12... | collective-permute-start | bytes 98312 | tf_op jit(solution)/shard_map/ppermute | solution.py:312
  25.9 5.4 %collective-permute-start.3 = (f32[2,32,128]{2,0,1:T(2,128)S(1)}, f32[2,32,128]{2,0,1:T(2,128)S(1)}, u32[]{:S(2)}, u32[]{:S(2)}) collective-permute-start(f32[2,32,128]{2,0,1:T(2,128)S(1)} %get-tuple-element.21), channel_id=1, source_target_pairs={{0,1},{1,2},{2,3},{3,4},{4,5},{5,6},{6,7},{8,9},{9,10},{10,11},{11... | collective-permute-start | bytes 98312 | tf_op jit(solution)/shard_map/ppermute | solution.py:317
  31.4 1.7 %collective-permute-done.3 = f32[2,32,128]{2,0,1:T(2,128)S(1)} collective-permute-done((f32[2,32,128]{2,0,1:T(2,128)S(1)}, f32[2,32,128]{2,0,1:T(2,128)S(1)}, u32[]{:S(2)}, u32[]{:S(2)}) %collective-permute-start.3) | collective-permute-done | bytes 32800 | tf_op jit(solution)/shard_map/ppermute | solution.py:317
  33.1 2.1 %collective-permute-start.5 = (f32[2,20,128]{2,1,0:T(8,128)S(1)}, f32[2,20,128]{2,1,0:T(8,128)S(1)}, u32[]{:S(2)}, u32[]{:S(2)}) collective-permute-start(f32[2,20,128]{2,1,0:T(8,128)S(1)} %pad_maximum_fusion), channel_id=1, source_target_pairs={{0,8},{8,16},{16,24},{1,9},{9,17},{17,25},{2,10},{10,18},{18,26},{... | collective-permute-start | bytes 61448 | tf_op jit(solution)/shard_map/ppermute | solution.py:317
  35.2 1.3 %collective-permute-start.6 = (f32[2,20,128]{2,1,0:T(8,128)S(1)}, f32[2,20,128]{2,1,0:T(8,128)S(1)}, u32[]{:S(2)}, u32[]{:S(2)}) collective-permute-start(f32[2,20,128]{2,1,0:T(8,128)S(1)} %pad_maximum_fusion.1), channel_id=1, source_target_pairs={{8,0},{16,8},{24,16},{9,1},{17,9},{25,17},{10,2},{18,10},{26,18},{... | collective-permute-start | bytes 61448 | tf_op jit(solution)/shard_map/ppermute | solution.py:312
  36.6 2.6 %collective-permute-done.6.zh = f32[2,20,128]{2,1,0:T(8,128)S(1)} collective-permute-done((f32[2,20,128]{2,1,0:T(8,128)S(1)}, f32[2,20,128]{2,1,0:T(8,128)S(1)}, u32[]{:S(2)}, u32[]{:S(2)}) %collective-permute-start.6) | collective-permute-done | bytes 20512 | tf_op jit(solution)/shard_map/ppermute | solution.py:312
  39.3 12.6 %filter.1 = (f32[16,32,128]{2,1,0:T(8,128)S(1)}, f32[16,32,128]{2,1,0:T(8,128)S(1)}, f32[16,32,128]{2,1,0:T(8,128)S(1)}, f32[1,256]{1,0:T(1,128)S(1)}) custom-call(s32[4]{0:T(128)S(1)} %add_convert_fusion.flags, f32[16,32,128]{2,1,0:T(8,128)S(1)} %get-tuple-element.11.src, f32[2,32,128]{2,1,0:T(8,128)S(1)} %copy.12.yl, f32[2,32,128]{2,1,0:T(8,128)S(1)} %copy.13.yh, ...), custom_call_target="tpu_custom_call" | custom-call | tf_op jit(solution)/shard_map/filter/pallas_call | solution.py:267
  51.9 0.7 copy-done.3
  52.5 0.7 copy-done.4
  53.2 0.7 copy-done.5
  53.9 43.2 %psum.7.vols = f32[1,256]{1,0:T(1,128)} all-reduce(f32[1,256]{1,0:T(1,128)S(1)} %get-tuple-element.14), channel_id=1, replica_groups=mesh['gz'=4,'gy'=8] {'gz','gy'}, use_global_device_ids=true, to_apply=%region_0.0 | all-reduce | flops 256 | bytes 2048 | tf_op jit(solution)/shard_map/psum | solution.py:340
  97.1 2.0 %update.1 = (f32[16,32,128]{2,1,0:T(8,128)}, f32[1]{0:T(128)}) custom-call(f32[1,256]{1,0:T(1,128)} %psum.7.vols, f32[16,32,128]{2,1,0:T(8,128)} %copy-done.3, f32[16,32,128]{2,1,0:T(8,128)} %copy-done.4, f32[16,32,128]{2,1,0:T(8,128)} %copy-done.5), custom_call_target="tpu_custom_call" | custom-call | tf_op jit(solution)/shard_map/update/pallas_call | solution.py:301
  (25 shorter events, 0.2 us)
Async XLA Ops:
  0.6 38.6 %copy-start.2 = (f32[16,32,128]{2,1,0:T(8,128)S(1)}, f32[16,32,128]{2,1,0:T(8,128)}, u32[]{:S(2)}) copy-start(f32[16,32,128]{2,1,0:T(8,128)} %dens.3) | copy-start | bytes 786436
  1.6 12.0 %collective-permute-start = (f32[9,32,128]{2,1,0:T(8,128)S(1)}, f32[9,32,128]{2,1,0:T(8,128)S(1)}, u32[]{:S(2)}, u32[]{:S(2)}) collective-permute-start(f32[9,32,128]{2,1,0:T(8,128)S(1)} %slice_bitcast_fusion), channel_id=1, source_target_pairs={{1,0},{2,1},{3,2},{4,3},{5,4},{6,5},{7,6},{9,8},{10,9},{11,10},{12... | collective-permute-start | bytes 442376 | tf_op jit(solution)/shard_map/ppermute | solution.py:312
  4.0 9.6 %collective-permute-start.1 = (f32[9,16,128]{2,1,0:T(8,128)S(1)}, f32[9,16,128]{2,1,0:T(8,128)S(1)}, u32[]{:S(2)}, u32[]{:S(2)}) collective-permute-start(f32[9,16,128]{2,1,0:T(8,128)S(1)} %bitcast.23), channel_id=1, source_target_pairs={{8,0},{16,8},{24,16},{9,1},{17,9},{25,17},{10,2},{18,10},{26,18},{... | collective-permute-start | bytes 221192 | tf_op jit(solution)/shard_map/ppermute | solution.py:312
  6.1 7.5 %collective-permute-start.2 = (f32[9,128]{1,0:T(8,128)S(1)}, f32[9,128]{1,0:T(8,128)S(1)}, u32[]{:S(2)}, u32[]{:S(2)}) collective-permute-start(f32[9,128]{1,0:T(8,128)S(1)} %bitcast.24), channel_id=1, source_target_pairs={{9,0},{10,1},{11,2},{12,3},{13,4},{14,5},{15,6},{17,8},{18,9},{19,... | collective-permute-start | bytes 13832 | tf_op jit(solution)/shard_map/ppermute | solution.py:328
  13.6 1.7 %copy-start = (f32[9,16,32,128]{3,2,1,0:T(8,128)S(1)}, f32[9,16,32,128]{3,2,1,0:T(8,128)}, u32[]{:S(2)}) copy-start(f32[9,16,32,128]{3,2,1,0:T(8,128)} %disp.1) | copy-start | bytes 7077892
  15.3 0.9 copy-start.1
  16.2 0.7 copy-start.8
  17.0 22.3 %copy-start.6 = (s32[16,32,128]{2,1,0:T(8,128)S(1)}, s32[16,32,128]{2,1,0:T(8,128)}, u32[]{:S(2)}) copy-start(s32[16,32,128]{2,1,0:T(8,128)} %passive.1) | copy-start | bytes 786436
  17.0 22.3 %copy-start.7 = (s32[16,32,128]{2,1,0:T(8,128)S(1)}, s32[16,32,128]{2,1,0:T(8,128)}, u32[]{:S(2)}) copy-start(s32[16,32,128]{2,1,0:T(8,128)} %solid.1) | copy-start | bytes 786436
  24.6 6.8 %collective-permute-start.4 = (f32[2,32,128]{2,0,1:T(2,128)S(1)}, f32[2,32,128]{2,0,1:T(2,128)S(1)}, u32[]{:S(2)}, u32[]{:S(2)}) collective-permute-start(f32[2,32,128]{2,0,1:T(2,128)S(1)} %get-tuple-element.20), channel_id=1, source_target_pairs={{1,0},{2,1},{3,2},{4,3},{5,4},{6,5},{7,6},{9,8},{10,9},{11,10},{12... | collective-permute-start | bytes 98312 | tf_op jit(solution)/shard_map/ppermute | solution.py:312
  25.9 7.2 %collective-permute-start.3 = (f32[2,32,128]{2,0,1:T(2,128)S(1)}, f32[2,32,128]{2,0,1:T(2,128)S(1)}, u32[]{:S(2)}, u32[]{:S(2)}) collective-permute-start(f32[2,32,128]{2,0,1:T(2,128)S(1)} %get-tuple-element.21), channel_id=1, source_target_pairs={{0,1},{1,2},{2,3},{3,4},{4,5},{5,6},{6,7},{8,9},{9,10},{10,11},{11... | collective-permute-start | bytes 98312 | tf_op jit(solution)/shard_map/ppermute | solution.py:317
  33.1 3.5 %collective-permute-start.5 = (f32[2,20,128]{2,1,0:T(8,128)S(1)}, f32[2,20,128]{2,1,0:T(8,128)S(1)}, u32[]{:S(2)}, u32[]{:S(2)}) collective-permute-start(f32[2,20,128]{2,1,0:T(8,128)S(1)} %pad_maximum_fusion), channel_id=1, source_target_pairs={{0,8},{8,16},{16,24},{1,9},{9,17},{17,25},{2,10},{10,18},{18,26},{... | collective-permute-start | bytes 61448 | tf_op jit(solution)/shard_map/ppermute | solution.py:317
  35.2 4.0 %collective-permute-start.6 = (f32[2,20,128]{2,1,0:T(8,128)S(1)}, f32[2,20,128]{2,1,0:T(8,128)S(1)}, u32[]{:S(2)}, u32[]{:S(2)}) collective-permute-start(f32[2,20,128]{2,1,0:T(8,128)S(1)} %pad_maximum_fusion.1), channel_id=1, source_target_pairs={{8,0},{16,8},{24,16},{9,1},{17,9},{25,17},{10,2},{18,10},{26,18},{... | collective-permute-start | bytes 61448 | tf_op jit(solution)/shard_map/ppermute | solution.py:312
  51.8 0.7 copy-start.3
  52.5 0.7 copy-start.4
  53.2 0.7 copy-start.5

commit v2 on v1

--- a/solution.py
+++ b/solution.py
@@ -317,6 +317,15 @@
     return lax.ppermute(value, axis, [(i, i + 1) for i in range(count - 1)])
 
 
+def total_over(value, axis):
+    count = lax.axis_size(axis)
+    bit = 1
+    while bit < count:
+        value = value + lax.ppermute(value, axis, [(i, i ^ bit) for i in range(count)])
+        bit *= 2
+    return value
+
+
 def on_device(displacement, density, passive, solid, stiffness):
     ny, nz, nx = density.shape
     gy, gz = lax.axis_size("gy"), lax.axis_size("gz")
@@ -337,7 +346,7 @@
     flags = jnp.stack([iy > 0, iy < gy - 1, iz > 0, iz < gz - 1]).astype(jnp.int32)
     amp, low, high, vols = filter_call(flags, src, yl, yh, zl, zh, density, passive, solid)
 
-    vols = lax.psum(vols, ("gz", "gy"))
+    vols = total_over(total_over(vols, "gz"), "gy")
     new, logm = update_call(vols, amp, low, high)
     return new, logm.reshape(())
 

time: 99.7 us -> 78.3 us (0.79)
  blocking collectives: 43.2 us -> 0 us
  starting transfers between devices: 14 us -> 26.5 us
  waiting for transfers between devices: 10.6 us -> 19.4 us
    psum x1 -> x0, blocking collectives: 43.2 us -> none  [on_device(): vols = lax.psum(vols, ('gz', 'gy'))]
    ppermute x0 -> x5, starting transfers between devices: none -> 12.5 us  [total_over(): lax.ppermute(value, axis, [(i, i ^ bit) for i in range(count)])]
    ppermute x0 -> x5, waiting for transfers between devices: none -> 8.81 us  [total_over(): lax.ppermute(value, axis, [(i, i ^ bit) for i in range(count)])]
  transfers between devices with their start and end apart: 7 -> 12, of which waited for: 3 -> 8; matrix products, arithmetic and copies ran while one was open for 2% -> 3% of each run, Pallas kernels for 0% -> 0%
where the time goes in v2:
time: 78.3 us; the launch traced here: 77.8 us
  starting transfers between devices  26.5 us (34%)
  Pallas kernels  22 us (28%)
  waiting for transfers between devices  19.4 us (25%)
  local copies, waits for them, and re-layouts  8.46 us (11%)
  between operations  0.81 us (1%)
    pallas_call x1, Pallas kernels, filter_call(): pl.pallas_call(filter_kernel, in_specs=[pl.BlockSpec(memory_space=pltpu.S...  12.6 us
    ppermute x5, starting transfers between devices, total_over(): lax.ppermute(value, axis, [(i, i ^ bit) for i in range(count)])  12.5 us
    ppermute x5, waiting for transfers between devices, total_over(): lax.ppermute(value, axis, [(i, i ^ bit) for i in range(count)])  8.81 us
    ppermute x2, starting transfers between devices, to_upper(): return lax.ppermute(value, axis, [(i, i + 1) for i in range(count - 1)])  7.55 us
    pallas_call x1, Pallas kernels, energy_call(): pl.pallas_call(energy_kernel, out_shape=(jax.ShapeDtypeStruct((ny, nz, nx...  7.44 us
    ppermute x1, waiting for transfers between devices, on_device(): fc = lax.ppermute(displacement[:, 0, 0], ('gz', 'gy'), pairs)  6.23 us
    unnamed x19, local copies, waits for them, and re-layouts  5.42 us
    ppermute x4, starting transfers between devices, to_lower(): return lax.ppermute(value, axis, [(i + 1, i) for i in range(count - 1)])  5.17 us
  transfers between devices with their start and end apart: 12, of which 8 were waited for; matrix products, arithmetic and copies ran while one was open for 3% of the time, Pallas kernels for 0%

profile of v2, /device:TPU:0, one launch (start us, length us, event | category | flops | bytes accessed | tf_op | source)
XLA Modules:
  0.0 77.8 jit_solution(13960325941217682285)
XLA Ops:
  0.6 1.0 %slice_bitcast_fusion = f32[9,32,128]{2,1,0:T(8,128)S(1)} fusion(f32[9,16,32,128]{3,2,1,0:T(8,128)} %disp.1), kind=kLoop, calls=%fused_computation | loop fusion | bytes 294912 | tf_op jit(solution)/shard_map/squeeze | solution.py:334
  1.6 1.3 %collective-permute-start = (f32[9,32,128]{2,1,0:T(8,128)S(1)}, f32[9,32,128]{2,1,0:T(8,128)S(1)}, u32[]{:S(2)}, u32[]{:S(2)}) collective-permute-start(f32[9,32,128]{2,1,0:T(8,128)S(1)} %slice_bitcast_fusion), channel_id=1, source_target_pairs={{1,0},{2,1},{3,2},{4,3},{5,4},{6,5},{7,6},{9,8},{10,9},{11,10},{12... | collective-permute-start | bytes 442376 | tf_op jit(solution)/shard_map/ppermute | solution.py:312
  2.9 1.1 %slice.28 = f32[9,16,1,128]{3,2,1,0:T(1,128)S(1)} slice(f32[9,16,32,128]{3,2,1,0:T(8,128)} %disp.1), slice={[0:9], [0:16], [0:1], [0:128]} | slice | bytes 147456 | tf_op jit(solution)/shard_map/slice | solution.py:335
  4.0 1.3 %collective-permute-start.1 = (f32[9,16,128]{2,1,0:T(8,128)S(1)}, f32[9,16,128]{2,1,0:T(8,128)S(1)}, u32[]{:S(2)}, u32[]{:S(2)}) collective-permute-start(f32[9,16,128]{2,1,0:T(8,128)S(1)} %bitcast.23), channel_id=1, source_target_pairs={{8,0},{16,8},{24,16},{9,1},{17,9},{25,17},{10,2},{18,10},{26,18},{... | collective-permute-start | bytes 221192 | tf_op jit(solution)/shard_map/ppermute | solution.py:312
  6.1 1.3 %collective-permute-start.2 = (f32[9,128]{1,0:T(8,128)S(1)}, f32[9,128]{1,0:T(8,128)S(1)}, u32[]{:S(2)}, u32[]{:S(2)}) collective-permute-start(f32[9,128]{1,0:T(8,128)S(1)} %bitcast.24), channel_id=1, source_target_pairs={{9,0},{10,1},{11,2},{12,3},{13,4},{14,5},{15,6},{17,8},{18,9},{19,... | collective-permute-start | bytes 13832 | tf_op jit(solution)/shard_map/ppermute | solution.py:337
  7.4 6.2 %collective-permute-done.2.fc = f32[9,128]{1,0:T(8,128)S(1)} collective-permute-done((f32[9,128]{1,0:T(8,128)S(1)}, f32[9,128]{1,0:T(8,128)S(1)}, u32[]{:S(2)}, u32[]{:S(2)}) %collective-permute-start.2) | collective-permute-done | bytes 4640 | tf_op jit(solution)/shard_map/ppermute | solution.py:337
  13.6 1.7 %copy-done = f32[9,16,32,128]{3,2,1,0:T(8,128)S(1)} copy-done((f32[9,16,32,128]{3,2,1,0:T(8,128)S(1)}, f32[9,16,32,128]{3,2,1,0:T(8,128)}, u32[]{:S(2)}) %copy-start) | copy-done | bytes 2359320
  17.0 7.4 %energy.1 = (f32[16,32,128]{2,1,0:T(8,128)S(1)}, f32[2,16,128]{2,1,0:T(8,128)S(1)}, f32[2,16,128]{2,1,0:T(8,128)S(1)}) custom-call(f32[9,16,32,128]{3,2,1,0:T(8,128)S(1)} %copy-done, f32[9,32,128]{2,1,0:T(8,128)S(1)} %collective-permute-done.fy, f32[9,16,128]{2,1,0:T(8,128)S(1)} %collective-permute-done.1.fz, f32[9,128]{1,0:T(8,128)S(1)} %collective-permute-done.2.fc, ...), custom_call_target="tpu_custom_call" | custom-call | tf_op jit(solution)/shard_map/energy/pallas_call | solution.py:170
  24.6 1.3 %collective-permute-start.4 = (f32[2,32,128]{2,0,1:T(2,128)S(1)}, f32[2,32,128]{2,0,1:T(2,128)S(1)}, u32[]{:S(2)}, u32[]{:S(2)}) collective-permute-start(f32[2,32,128]{2,0,1:T(2,128)S(1)} %get-tuple-element.20), channel_id=1, source_target_pairs={{1,0},{2,1},{3,2},{4,3},{5,4},{6,5},{7,6},{9,8},{10,9},{11,10},{12... | collective-permute-start | bytes 98312 | tf_op jit(solution)/shard_map/ppermute | solution.py:312
  25.9 5.4 %collective-permute-start.3 = (f32[2,32,128]{2,0,1:T(2,128)S(1)}, f32[2,32,128]{2,0,1:T(2,128)S(1)}, u32[]{:S(2)}, u32[]{:S(2)}) collective-permute-start(f32[2,32,128]{2,0,1:T(2,128)S(1)} %get-tuple-element.21), channel_id=1, source_target_pairs={{0,1},{1,2},{2,3},{3,4},{4,5},{5,6},{6,7},{8,9},{9,10},{10,11},{11... | collective-permute-start | bytes 98312 | tf_op jit(solution)/shard_map/ppermute | solution.py:317
  31.4 1.7 %collective-permute-done.3 = f32[2,32,128]{2,0,1:T(2,128)S(1)} collective-permute-done((f32[2,32,128]{2,0,1:T(2,128)S(1)}, f32[2,32,128]{2,0,1:T(2,128)S(1)}, u32[]{:S(2)}, u32[]{:S(2)}) %collective-permute-start.3) | collective-permute-done | bytes 32800 | tf_op jit(solution)/shard_map/ppermute | solution.py:317
  33.1 2.1 %collective-permute-start.5 = (f32[2,20,128]{2,1,0:T(8,128)S(1)}, f32[2,20,128]{2,1,0:T(8,128)S(1)}, u32[]{:S(2)}, u32[]{:S(2)}) collective-permute-start(f32[2,20,128]{2,1,0:T(8,128)S(1)} %pad_maximum_fusion), channel_id=1, source_target_pairs={{0,8},{8,16},{16,24},{1,9},{9,17},{17,25},{2,10},{10,18},{18,26},{... | collective-permute-start | bytes 61448 | tf_op jit(solution)/shard_map/ppermute | solution.py:317
  35.2 1.3 %collective-permute-start.6 = (f32[2,20,128]{2,1,0:T(8,128)S(1)}, f32[2,20,128]{2,1,0:T(8,128)S(1)}, u32[]{:S(2)}, u32[]{:S(2)}) collective-permute-start(f32[2,20,128]{2,1,0:T(8,128)S(1)} %pad_maximum_fusion.1), channel_id=1, source_target_pairs={{8,0},{16,8},{24,16},{9,1},{17,9},{25,17},{10,2},{18,10},{26,18},{... | collective-permute-start | bytes 61448 | tf_op jit(solution)/shard_map/ppermute | solution.py:312
  36.6 2.6 %collective-permute-done.6.zh = f32[2,20,128]{2,1,0:T(8,128)S(1)} collective-permute-done((f32[2,20,128]{2,1,0:T(8,128)S(1)}, f32[2,20,128]{2,1,0:T(8,128)S(1)}, u32[]{:S(2)}, u32[]{:S(2)}) %collective-permute-start.6) | collective-permute-done | bytes 20512 | tf_op jit(solution)/shard_map/ppermute | solution.py:312
  39.3 12.6 %filter.1 = (f32[16,32,128]{2,1,0:T(8,128)S(1)}, f32[16,32,128]{2,1,0:T(8,128)S(1)}, f32[16,32,128]{2,1,0:T(8,128)S(1)}, f32[1,256]{1,0:T(1,128)S(1)}) custom-call(s32[4]{0:T(128)S(1)} %add_convert_fusion.flags, f32[16,32,128]{2,1,0:T(8,128)S(1)} %get-tuple-element.11.src, f32[2,32,128]{2,1,0:T(8,128)S(1)} %copy.12.yl, f32[2,32,128]{2,1,0:T(8,128)S(1)} %copy.13.yh, ...), custom_call_target="tpu_custom_call" | custom-call | tf_op jit(solution)/shard_map/filter/pallas_call | solution.py:267
  53.9 2.6 %collective-permute-start.7 = (f32[1,256]{1,0:T(1,128)S(1)}, f32[1,256]{1,0:T(1,128)S(1)}, u32[]{:S(2)}, u32[]{:S(2)}) collective-permute-start(f32[1,256]{1,0:T(1,128)S(1)} %get-tuple-element.14), channel_id=1, source_target_pairs={{0,8},{8,0},{16,24},{24,16},{1,9},{9,1},{17,25},{25,17},{2,10},{10... | collective-permute-start | bytes 3080 | tf_op jit(solution)/shard_map/ppermute | solution.py:324
  57.5 3.4 %collective-permute-done.8 = f32[1,256]{1,0:T(1,128)S(1)} collective-permute-done((f32[1,256]{1,0:T(1,128)S(1)}, f32[1,256]{1,0:T(1,128)S(1)}, u32[]{:S(2)}, u32[]{:S(2)}) %collective-permute-start.8) | collective-permute-done | bytes 1056 | tf_op jit(solution)/shard_map/ppermute | solution.py:324
  60.9 2.9 %collective-permute-start.9 = (f32[1,256]{1,0:T(1,128)S(1)}, f32[1,256]{1,0:T(1,128)S(1)}, u32[]{:S(2)}, u32[]{:S(2)}) collective-permute-start(f32[1,256]{1,0:T(1,128)S(1)} %add.16), channel_id=1, source_target_pairs={{0,1},{1,0},{2,3},{3,2},{4,5},{5,4},{6,7},{7,6},{8,9},{9,8},{10,11... | collective-permute-start | bytes 3080 | tf_op jit(solution)/shard_map/ppermute | solution.py:324
  63.8 1.5 %collective-permute-done.9 = f32[1,256]{1,0:T(1,128)S(1)} collective-permute-done((f32[1,256]{1,0:T(1,128)S(1)}, f32[1,256]{1,0:T(1,128)S(1)}, u32[]{:S(2)}, u32[]{:S(2)}) %collective-permute-start.9) | collective-permute-done | bytes 1056 | tf_op jit(solution)/shard_map/ppermute | solution.py:324
  65.3 3.8 %collective-permute-start.10 = (f32[1,256]{1,0:T(1,128)S(1)}, f32[1,256]{1,0:T(1,128)S(1)}, u32[]{:S(2)}, u32[]{:S(2)}) collective-permute-start(f32[1,256]{1,0:T(1,128)S(1)} %add.17), channel_id=1, source_target_pairs={{0,2},{1,3},{2,0},{3,1},{4,6},{5,7},{6,4},{7,5},{8,10},{9,11},{10,... | collective-permute-start | bytes 3080 | tf_op jit(solution)/shard_map/ppermute | solution.py:324
  69.1 1.5 %collective-permute-done.10 = f32[1,256]{1,0:T(1,128)S(1)} collective-permute-done((f32[1,256]{1,0:T(1,128)S(1)}, f32[1,256]{1,0:T(1,128)S(1)}, u32[]{:S(2)}, u32[]{:S(2)}) %collective-permute-start.10) | collective-permute-done | bytes 1056 | tf_op jit(solution)/shard_map/ppermute | solution.py:324
  70.7 3.0 %collective-permute-start.11 = (f32[1,256]{1,0:T(1,128)S(1)}, f32[1,256]{1,0:T(1,128)S(1)}, u32[]{:S(2)}, u32[]{:S(2)}) collective-permute-start(f32[1,256]{1,0:T(1,128)S(1)} %add.18), channel_id=1, source_target_pairs={{0,4},{1,5},{2,6},{3,7},{4,0},{5,1},{6,2},{7,3},{8,12},{9,13},{10,... | collective-permute-start | bytes 3080 | tf_op jit(solution)/shard_map/ppermute | solution.py:324
  73.7 1.5 %collective-permute-done.11 = f32[1,256]{1,0:T(1,128)S(1)} collective-permute-done((f32[1,256]{1,0:T(1,128)S(1)}, f32[1,256]{1,0:T(1,128)S(1)}, u32[]{:S(2)}, u32[]{:S(2)}) %collective-permute-start.11) | collective-permute-done | bytes 1056 | tf_op jit(solution)/shard_map/ppermute | solution.py:324
  75.8 2.0 %update.1 = (f32[16,32,128]{2,1,0:T(8,128)}, f32[1]{0:T(128)}) custom-call(f32[1,256]{1,0:T(1,128)} %add.19.vols, f32[16,32,128]{2,1,0:T(8,128)} %copy-done.3, f32[16,32,128]{2,1,0:T(8,128)} %copy-done.4, f32[16,32,128]{2,1,0:T(8,128)} %copy-done.5), custom_call_target="tpu_custom_call" | custom-call | tf_op jit(solution)/shard_map/update/pallas_call | solution.py:301
  (39 shorter events, 6.5 us)
Async XLA Ops:
  0.6 38.6 %copy-start.2 = (f32[16,32,128]{2,1,0:T(8,128)S(1)}, f32[16,32,128]{2,1,0:T(8,128)}, u32[]{:S(2)}) copy-start(f32[16,32,128]{2,1,0:T(8,128)} %dens.3) | copy-start | bytes 786436
  1.6 12.0 %collective-permute-start = (f32[9,32,128]{2,1,0:T(8,128)S(1)}, f32[9,32,128]{2,1,0:T(8,128)S(1)}, u32[]{:S(2)}, u32[]{:S(2)}) collective-permute-start(f32[9,32,128]{2,1,0:T(8,128)S(1)} %slice_bitcast_fusion), channel_id=1, source_target_pairs={{1,0},{2,1},{3,2},{4,3},{5,4},{6,5},{7,6},{9,8},{10,9},{11,10},{12... | collective-permute-start | bytes 442376 | tf_op jit(solution)/shard_map/ppermute | solution.py:312
  4.0 9.6 %collective-permute-start.1 = (f32[9,16,128]{2,1,0:T(8,128)S(1)}, f32[9,16,128]{2,1,0:T(8,128)S(1)}, u32[]{:S(2)}, u32[]{:S(2)}) collective-permute-start(f32[9,16,128]{2,1,0:T(8,128)S(1)} %bitcast.23), channel_id=1, source_target_pairs={{8,0},{16,8},{24,16},{9,1},{17,9},{25,17},{10,2},{18,10},{26,18},{... | collective-permute-start | bytes 221192 | tf_op jit(solution)/shard_map/ppermute | solution.py:312
  6.1 7.5 %collective-permute-start.2 = (f32[9,128]{1,0:T(8,128)S(1)}, f32[9,128]{1,0:T(8,128)S(1)}, u32[]{:S(2)}, u32[]{:S(2)}) collective-permute-start(f32[9,128]{1,0:T(8,128)S(1)} %bitcast.24), channel_id=1, source_target_pairs={{9,0},{10,1},{11,2},{12,3},{13,4},{14,5},{15,6},{17,8},{18,9},{19,... | collective-permute-start | bytes 13832 | tf_op jit(solution)/shard_map/ppermute | solution.py:337
  13.6 1.7 %copy-start = (f32[9,16,32,128]{3,2,1,0:T(8,128)S(1)}, f32[9,16,32,128]{3,2,1,0:T(8,128)}, u32[]{:S(2)}) copy-start(f32[9,16,32,128]{3,2,1,0:T(8,128)} %disp.1) | copy-start | bytes 7077892
  15.3 0.9 %copy-start.1 = (f32[16,32,128]{2,1,0:T(8,128)S(1)}, f32[16,32,128]{2,1,0:T(8,128)}, u32[]{:S(2)}) copy-start(f32[16,32,128]{2,1,0:T(8,128)} %dens.3) | copy-start | bytes 786436
  16.2 0.7 copy-start.8
  17.0 22.3 %copy-start.6 = (s32[16,32,128]{2,1,0:T(8,128)S(1)}, s32[16,32,128]{2,1,0:T(8,128)}, u32[]{:S(2)}) copy-start(s32[16,32,128]{2,1,0:T(8,128)} %passive.1) | copy-start | bytes 786436
  17.0 22.3 %copy-start.7 = (s32[16,32,128]{2,1,0:T(8,128)S(1)}, s32[16,32,128]{2,1,0:T(8,128)}, u32[]{:S(2)}) copy-start(s32[16,32,128]{2,1,0:T(8,128)} %solid.1) | copy-start | bytes 786436
  24.6 6.8 %collective-permute-start.4 = (f32[2,32,128]{2,0,1:T(2,128)S(1)}, f32[2,32,128]{2,0,1:T(2,128)S(1)}, u32[]{:S(2)}, u32[]{:S(2)}) collective-permute-start(f32[2,32,128]{2,0,1:T(2,128)S(1)} %get-tuple-element.20), channel_id=1, source_target_pairs={{1,0},{2,1},{3,2},{4,3},{5,4},{6,5},{7,6},{9,8},{10,9},{11,10},{12... | collective-permute-start | bytes 98312 | tf_op jit(solution)/shard_map/ppermute | solution.py:312
  25.9 7.2 %collective-permute-start.3 = (f32[2,32,128]{2,0,1:T(2,128)S(1)}, f32[2,32,128]{2,0,1:T(2,128)S(1)}, u32[]{:S(2)}, u32[]{:S(2)}) collective-permute-start(f32[2,32,128]{2,0,1:T(2,128)S(1)} %get-tuple-element.21), channel_id=1, source_target_pairs={{0,1},{1,2},{2,3},{3,4},{4,5},{5,6},{6,7},{8,9},{9,10},{10,11},{11... | collective-permute-start | bytes 98312 | tf_op jit(solution)/shard_map/ppermute | solution.py:317
  33.1 3.5 %collective-permute-start.5 = (f32[2,20,128]{2,1,0:T(8,128)S(1)}, f32[2,20,128]{2,1,0:T(8,128)S(1)}, u32[]{:S(2)}, u32[]{:S(2)}) collective-permute-start(f32[2,20,128]{2,1,0:T(8,128)S(1)} %pad_maximum_fusion), channel_id=1, source_target_pairs={{0,8},{8,16},{16,24},{1,9},{9,17},{17,25},{2,10},{10,18},{18,26},{... | collective-permute-start | bytes 61448 | tf_op jit(solution)/shard_map/ppermute | solution.py:317
  35.2 4.0 %collective-permute-start.6 = (f32[2,20,128]{2,1,0:T(8,128)S(1)}, f32[2,20,128]{2,1,0:T(8,128)S(1)}, u32[]{:S(2)}, u32[]{:S(2)}) collective-permute-start(f32[2,20,128]{2,1,0:T(8,128)S(1)} %pad_maximum_fusion.1), channel_id=1, source_target_pairs={{8,0},{16,8},{24,16},{9,1},{17,9},{25,17},{10,2},{18,10},{26,18},{... | collective-permute-start | bytes 61448 | tf_op jit(solution)/shard_map/ppermute | solution.py:312
  51.8 0.7 copy-start.3
  52.5 0.7 copy-start.4
  53.2 0.7 copy-start.5
  53.9 3.4 %collective-permute-start.7 = (f32[1,256]{1,0:T(1,128)S(1)}, f32[1,256]{1,0:T(1,128)S(1)}, u32[]{:S(2)}, u32[]{:S(2)}) collective-permute-start(f32[1,256]{1,0:T(1,128)S(1)} %get-tuple-element.14), channel_id=1, source_target_pairs={{0,8},{8,0},{16,24},{24,16},{1,9},{9,1},{17,25},{25,17},{2,10},{10... | collective-permute-start | bytes 3080 | tf_op jit(solution)/shard_map/ppermute | solution.py:324
  57.3 3.6 %collective-permute-start.8 = (f32[1,256]{1,0:T(1,128)S(1)}, f32[1,256]{1,0:T(1,128)S(1)}, u32[]{:S(2)}, u32[]{:S(2)}) collective-permute-start(f32[1,256]{1,0:T(1,128)S(1)} %add.15), channel_id=1, source_target_pairs={{0,16},{8,24},{16,0},{24,8},{1,17},{9,25},{17,1},{25,9},{2,18},{10... | collective-permute-start | bytes 3080 | tf_op jit(solution)/shard_map/ppermute | solution.py:324
  60.9 4.5 %collective-permute-start.9 = (f32[1,256]{1,0:T(1,128)S(1)}, f32[1,256]{1,0:T(1,128)S(1)}, u32[]{:S(2)}, u32[]{:S(2)}) collective-permute-start(f32[1,256]{1,0:T(1,128)S(1)} %add.16), channel_id=1, source_target_pairs={{0,1},{1,0},{2,3},{3,2},{4,5},{5,4},{6,7},{7,6},{8,9},{9,8},{10,11... | collective-permute-start | bytes 3080 | tf_op jit(solution)/shard_map/ppermute | solution.py:324
  65.3 5.3 %collective-permute-start.10 = (f32[1,256]{1,0:T(1,128)S(1)}, f32[1,256]{1,0:T(1,128)S(1)}, u32[]{:S(2)}, u32[]{:S(2)}) collective-permute-start(f32[1,256]{1,0:T(1,128)S(1)} %add.17), channel_id=1, source_target_pairs={{0,2},{1,3},{2,0},{3,1},{4,6},{5,7},{6,4},{7,5},{8,10},{9,11},{10,... | collective-permute-start | bytes 3080 | tf_op jit(solution)/shard_map/ppermute | solution.py:324
  70.7 4.6 %collective-permute-start.11 = (f32[1,256]{1,0:T(1,128)S(1)}, f32[1,256]{1,0:T(1,128)S(1)}, u32[]{:S(2)}, u32[]{:S(2)}) collective-permute-start(f32[1,256]{1,0:T(1,128)S(1)} %add.18), channel_id=1, source_target_pairs={{0,4},{1,5},{2,6},{3,7},{4,0},{5,1},{6,2},{7,3},{8,12},{9,13},{10,... | collective-permute-start | bytes 3080 | tf_op jit(solution)/shard_map/ppermute | solution.py:324

commit v3 on v1

--- a/solution.py
+++ b/solution.py
@@ -337,7 +337,7 @@
     flags = jnp.stack([iy > 0, iy < gy - 1, iz > 0, iz < gz - 1]).astype(jnp.int32)
     amp, low, high, vols = filter_call(flags, src, yl, yh, zl, zh, density, passive, solid)
 
-    vols = lax.psum(vols, ("gz", "gy"))
+    vols = lax.all_gather(vols.reshape(2, POINTS // 2), ("gz", "gy")).sum(axis=0).reshape(1, POINTS)
     new, logm = update_call(vols, amp, low, high)
     return new, logm.reshape(())
 

time: 99.7 us -> 127 us (1.27)
  blocking collectives: 43.2 us -> 68.8 us
    all_gather x0 -> x1, blocking collectives: none -> 68.8 us  [on_device(): lax.all_gather(vols.reshape(2, POINTS // 2), ('gz', 'gy')).sum(axis=0)]
    psum x1 -> x0, blocking collectives: 43.2 us -> none  [on_device(): vols = lax.psum(vols, ('gz', 'gy'))]
where the time goes in v3:
time: 127 us; the launch traced here: 125 us
  blocking collectives  68.8 us (54%)
  Pallas kernels  22 us (17%)
  starting transfers between devices  14 us (11%)
  waiting for transfers between devices  10.6 us (8%)
  local copies, waits for them, and re-layouts  8.45 us (7%)
    all_gather x1, blocking collectives, on_device(): lax.all_gather(vols.reshape(2, POINTS // 2), ('gz', 'gy')).sum(axis=0)  68.8 us
    pallas_call x1, Pallas kernels, filter_call(): pl.pallas_call(filter_kernel, in_specs=[pl.BlockSpec(memory_space=pltpu.S...  12.6 us
    ppermute x2, starting transfers between devices, to_upper(): return lax.ppermute(value, axis, [(i, i + 1) for i in range(count - 1)])  7.55 us
    pallas_call x1, Pallas kernels, energy_call(): pl.pallas_call(energy_kernel, out_shape=(jax.ShapeDtypeStruct((ny, nz, nx...  7.44 us
    ppermute x1, waiting for transfers between devices, on_device(): fc = lax.ppermute(displacement[:, 0, 0], ('gz', 'gy'), pairs)  6.23 us
    unnamed x19, local copies, waits for them, and re-layouts  5.41 us
    ppermute x4, starting transfers between devices, to_lower(): return lax.ppermute(value, axis, [(i + 1, i) for i in range(count - 1)])  5.17 us
    ppermute x4, waiting for transfers between devices, to_lower(): return lax.ppermute(value, axis, [(i + 1, i) for i in range(count - 1)])  2.63 us
  transfers between devices with their start and end apart: 7, of which 3 were waited for; matrix products, arithmetic and copies ran while one was open for 2% of the time, Pallas kernels for 0%

profile of v3, /device:TPU:0, one launch (start us, length us, event | category | flops | bytes accessed | tf_op | source)
XLA Modules:
  0.0 125.3 jit_solution(7816590164345218694)
XLA Ops:
  0.6 1.0 slice_bitcast_fusion
  1.6 1.3 %collective-permute-start = (f32[9,32,128]{2,1,0:T(8,128)S(1)}, f32[9,32,128]{2,1,0:T(8,128)S(1)}, u32[]{:S(2)}, u32[]{:S(2)}) collective-permute-start(f32[9,32,128]{2,1,0:T(8,128)S(1)} %slice_bitcast_fusion), channel_id=1, source_target_pairs={{1,0},{2,1},{3,2},{4,3},{5,4},{6,5},{7,6},{9,8},{10,9},{11,10},{12... | collective-permute-start | bytes 442376 | tf_op jit(solution)/shard_map/ppermute | solution.py:312
  2.9 1.1 slice.28
  4.0 1.3 %collective-permute-start.1 = (f32[9,16,128]{2,1,0:T(8,128)S(1)}, f32[9,16,128]{2,1,0:T(8,128)S(1)}, u32[]{:S(2)}, u32[]{:S(2)}) collective-permute-start(f32[9,16,128]{2,1,0:T(8,128)S(1)} %bitcast.26), channel_id=1, source_target_pairs={{8,0},{16,8},{24,16},{9,1},{17,9},{25,17},{10,2},{18,10},{26,18},{... | collective-permute-start | bytes 221192 | tf_op jit(solution)/shard_map/ppermute | solution.py:312
  5.3 0.8 slice.29
  6.1 1.3 %collective-permute-start.2 = (f32[9,128]{1,0:T(8,128)S(1)}, f32[9,128]{1,0:T(8,128)S(1)}, u32[]{:S(2)}, u32[]{:S(2)}) collective-permute-start(f32[9,128]{1,0:T(8,128)S(1)} %bitcast.27), channel_id=1, source_target_pairs={{9,0},{10,1},{11,2},{12,3},{13,4},{14,5},{15,6},{17,8},{18,9},{19,... | collective-permute-start | bytes 13832 | tf_op jit(solution)/shard_map/ppermute | solution.py:328
  7.4 6.2 %collective-permute-done.2.fc = f32[9,128]{1,0:T(8,128)S(1)} collective-permute-done((f32[9,128]{1,0:T(8,128)S(1)}, f32[9,128]{1,0:T(8,128)S(1)}, u32[]{:S(2)}, u32[]{:S(2)}) %collective-permute-start.2) | collective-permute-done | bytes 4640 | tf_op jit(solution)/shard_map/ppermute | solution.py:328
  13.6 1.7 %copy-done = f32[9,16,32,128]{3,2,1,0:T(8,128)S(1)} copy-done((f32[9,16,32,128]{3,2,1,0:T(8,128)S(1)}, f32[9,16,32,128]{3,2,1,0:T(8,128)}, u32[]{:S(2)}) %copy-start) | copy-done | bytes 2359320
  15.3 0.9 copy-done.1
  16.2 0.7 copy-done.8
  17.0 7.4 %energy.1 = (f32[16,32,128]{2,1,0:T(8,128)S(1)}, f32[2,16,128]{2,1,0:T(8,128)S(1)}, f32[2,16,128]{2,1,0:T(8,128)S(1)}) custom-call(f32[9,16,32,128]{3,2,1,0:T(8,128)S(1)} %copy-done, f32[9,32,128]{2,1,0:T(8,128)S(1)} %collective-permute-done.fy, f32[9,16,128]{2,1,0:T(8,128)S(1)} %collective-permute-done.1.fz, f32[9,128]{1,0:T(8,128)S(1)} %collective-permute-done.2.fc, ...), custom_call_target="tpu_custom_call" | custom-call | tf_op jit(solution)/shard_map/energy/pallas_call | solution.py:170
  24.6 1.3 %collective-permute-start.4 = (f32[2,32,128]{2,0,1:T(2,128)S(1)}, f32[2,32,128]{2,0,1:T(2,128)S(1)}, u32[]{:S(2)}, u32[]{:S(2)}) collective-permute-start(f32[2,32,128]{2,0,1:T(2,128)S(1)} %get-tuple-element.20), channel_id=1, source_target_pairs={{1,0},{2,1},{3,2},{4,3},{5,4},{6,5},{7,6},{9,8},{10,9},{11,10},{12... | collective-permute-start | bytes 98312 | tf_op jit(solution)/shard_map/ppermute | solution.py:312
  25.9 5.4 %collective-permute-start.3 = (f32[2,32,128]{2,0,1:T(2,128)S(1)}, f32[2,32,128]{2,0,1:T(2,128)S(1)}, u32[]{:S(2)}, u32[]{:S(2)}) collective-permute-start(f32[2,32,128]{2,0,1:T(2,128)S(1)} %get-tuple-element.21), channel_id=1, source_target_pairs={{0,1},{1,2},{2,3},{3,4},{4,5},{5,6},{6,7},{8,9},{9,10},{10,11},{11... | collective-permute-start | bytes 98312 | tf_op jit(solution)/shard_map/ppermute | solution.py:317
  31.4 1.7 %collective-permute-done.3 = f32[2,32,128]{2,0,1:T(2,128)S(1)} collective-permute-done((f32[2,32,128]{2,0,1:T(2,128)S(1)}, f32[2,32,128]{2,0,1:T(2,128)S(1)}, u32[]{:S(2)}, u32[]{:S(2)}) %collective-permute-start.3) | collective-permute-done | bytes 32800 | tf_op jit(solution)/shard_map/ppermute | solution.py:317
  33.1 2.1 %collective-permute-start.5 = (f32[2,20,128]{2,1,0:T(8,128)S(1)}, f32[2,20,128]{2,1,0:T(8,128)S(1)}, u32[]{:S(2)}, u32[]{:S(2)}) collective-permute-start(f32[2,20,128]{2,1,0:T(8,128)S(1)} %pad_maximum_fusion), channel_id=1, source_target_pairs={{0,8},{8,16},{16,24},{1,9},{9,17},{17,25},{2,10},{10,18},{18,26},{... | collective-permute-start | bytes 61448 | tf_op jit(solution)/shard_map/ppermute | solution.py:317
  35.2 1.3 %collective-permute-start.6 = (f32[2,20,128]{2,1,0:T(8,128)S(1)}, f32[2,20,128]{2,1,0:T(8,128)S(1)}, u32[]{:S(2)}, u32[]{:S(2)}) collective-permute-start(f32[2,20,128]{2,1,0:T(8,128)S(1)} %pad_maximum_fusion.1), channel_id=1, source_target_pairs={{8,0},{16,8},{24,16},{9,1},{17,9},{25,17},{10,2},{18,10},{26,18},{... | collective-permute-start | bytes 61448 | tf_op jit(solution)/shard_map/ppermute | solution.py:312
  36.6 2.6 %collective-permute-done.6.zh = f32[2,20,128]{2,1,0:T(8,128)S(1)} collective-permute-done((f32[2,20,128]{2,1,0:T(8,128)S(1)}, f32[2,20,128]{2,1,0:T(8,128)S(1)}, u32[]{:S(2)}, u32[]{:S(2)}) %collective-permute-start.6) | collective-permute-done | bytes 20512 | tf_op jit(solution)/shard_map/ppermute | solution.py:312
  39.3 12.6 %filter.1 = (f32[16,32,128]{2,1,0:T(8,128)S(1)}, f32[16,32,128]{2,1,0:T(8,128)S(1)}, f32[16,32,128]{2,1,0:T(8,128)S(1)}, f32[1,256]{1,0:T(1,128)S(1)}) custom-call(s32[4]{0:T(128)S(1)} %add_convert_fusion.flags, f32[16,32,128]{2,1,0:T(8,128)S(1)} %get-tuple-element.11.src, f32[2,32,128]{2,1,0:T(8,128)S(1)} %copy.19.yl, f32[2,32,128]{2,1,0:T(8,128)S(1)} %copy.20.yh, ...), custom_call_target="tpu_custom_call" | custom-call | tf_op jit(solution)/shard_map/filter/pallas_call | solution.py:267
  51.9 0.7 copy-done.3
  52.5 0.7 copy-done.4
  53.2 0.7 copy-done.5
  53.9 68.8 %all_gather.3 = f32[32,2,128]{2,1,0:T(2,128)S(1)} all-gather(f32[1,2,128]{2,1,0:T(2,128)S(1)} %bitcast.25), channel_id=1, replica_groups=mesh['gz'=4,'gy'=8] {'gz','gy'}, dimensions={0}, use_global_device_ids=true | all-gather | bytes 33792 | tf_op jit(solution)/shard_map/all_gather | solution.py:340
  122.7 0.6 reduce_sum.9
  123.3 2.0 %update.1 = (f32[16,32,128]{2,1,0:T(8,128)}, f32[1]{0:T(128)}) custom-call(f32[1,256]{1,0:T(1,128)} %bitcast.28, f32[16,32,128]{2,1,0:T(8,128)} %copy-done.3, f32[16,32,128]{2,1,0:T(8,128)} %copy-done.4, f32[16,32,128]{2,1,0:T(8,128)} %copy-done.5), custom_call_target="tpu_custom_call" | custom-call | tf_op jit(solution)/shard_map/update/pallas_call | solution.py:301
  (26 shorter events, 0.3 us)
Async XLA Ops:
  0.6 38.6 %copy-start.2 = (f32[16,32,128]{2,1,0:T(8,128)S(1)}, f32[16,32,128]{2,1,0:T(8,128)}, u32[]{:S(2)}) copy-start(f32[16,32,128]{2,1,0:T(8,128)} %dens.3) | copy-start | bytes 786436
  1.6 12.0 %collective-permute-start = (f32[9,32,128]{2,1,0:T(8,128)S(1)}, f32[9,32,128]{2,1,0:T(8,128)S(1)}, u32[]{:S(2)}, u32[]{:S(2)}) collective-permute-start(f32[9,32,128]{2,1,0:T(8,128)S(1)} %slice_bitcast_fusion), channel_id=1, source_target_pairs={{1,0},{2,1},{3,2},{4,3},{5,4},{6,5},{7,6},{9,8},{10,9},{11,10},{12... | collective-permute-start | bytes 442376 | tf_op jit(solution)/shard_map/ppermute | solution.py:312
  4.0 9.6 %collective-permute-start.1 = (f32[9,16,128]{2,1,0:T(8,128)S(1)}, f32[9,16,128]{2,1,0:T(8,128)S(1)}, u32[]{:S(2)}, u32[]{:S(2)}) collective-permute-start(f32[9,16,128]{2,1,0:T(8,128)S(1)} %bitcast.26), channel_id=1, source_target_pairs={{8,0},{16,8},{24,16},{9,1},{17,9},{25,17},{10,2},{18,10},{26,18},{... | collective-permute-start | bytes 221192 | tf_op jit(solution)/shard_map/ppermute | solution.py:312
  6.1 7.5 %collective-permute-start.2 = (f32[9,128]{1,0:T(8,128)S(1)}, f32[9,128]{1,0:T(8,128)S(1)}, u32[]{:S(2)}, u32[]{:S(2)}) collective-permute-start(f32[9,128]{1,0:T(8,128)S(1)} %bitcast.27), channel_id=1, source_target_pairs={{9,0},{10,1},{11,2},{12,3},{13,4},{14,5},{15,6},{17,8},{18,9},{19,... | collective-permute-start | bytes 13832 | tf_op jit(solution)/shard_map/ppermute | solution.py:328
  13.6 1.7 %copy-start = (f32[9,16,32,128]{3,2,1,0:T(8,128)S(1)}, f32[9,16,32,128]{3,2,1,0:T(8,128)}, u32[]{:S(2)}) copy-start(f32[9,16,32,128]{3,2,1,0:T(8,128)} %disp.1) | copy-start | bytes 7077892
  15.3 0.9 copy-start.1
  16.2 0.7 copy-start.8
  17.0 22.3 %copy-start.6 = (s32[16,32,128]{2,1,0:T(8,128)S(1)}, s32[16,32,128]{2,1,0:T(8,128)}, u32[]{:S(2)}) copy-start(s32[16,32,128]{2,1,0:T(8,128)} %passive.1) | copy-start | bytes 786436
  17.0 22.3 %copy-start.7 = (s32[16,32,128]{2,1,0:T(8,128)S(1)}, s32[16,32,128]{2,1,0:T(8,128)}, u32[]{:S(2)}) copy-start(s32[16,32,128]{2,1,0:T(8,128)} %solid.1) | copy-start | bytes 786436
  24.6 6.8 %collective-permute-start.4 = (f32[2,32,128]{2,0,1:T(2,128)S(1)}, f32[2,32,128]{2,0,1:T(2,128)S(1)}, u32[]{:S(2)}, u32[]{:S(2)}) collective-permute-start(f32[2,32,128]{2,0,1:T(2,128)S(1)} %get-tuple-element.20), channel_id=1, source_target_pairs={{1,0},{2,1},{3,2},{4,3},{5,4},{6,5},{7,6},{9,8},{10,9},{11,10},{12... | collective-permute-start | bytes 98312 | tf_op jit(solution)/shard_map/ppermute | solution.py:312
  25.9 7.2 %collective-permute-start.3 = (f32[2,32,128]{2,0,1:T(2,128)S(1)}, f32[2,32,128]{2,0,1:T(2,128)S(1)}, u32[]{:S(2)}, u32[]{:S(2)}) collective-permute-start(f32[2,32,128]{2,0,1:T(2,128)S(1)} %get-tuple-element.21), channel_id=1, source_target_pairs={{0,1},{1,2},{2,3},{3,4},{4,5},{5,6},{6,7},{8,9},{9,10},{10,11},{11... | collective-permute-start | bytes 98312 | tf_op jit(solution)/shard_map/ppermute | solution.py:317
  33.1 3.5 %collective-permute-start.5 = (f32[2,20,128]{2,1,0:T(8,128)S(1)}, f32[2,20,128]{2,1,0:T(8,128)S(1)}, u32[]{:S(2)}, u32[]{:S(2)}) collective-permute-start(f32[2,20,128]{2,1,0:T(8,128)S(1)} %pad_maximum_fusion), channel_id=1, source_target_pairs={{0,8},{8,16},{16,24},{1,9},{9,17},{17,25},{2,10},{10,18},{18,26},{... | collective-permute-start | bytes 61448 | tf_op jit(solution)/shard_map/ppermute | solution.py:317
  35.2 4.0 %collective-permute-start.6 = (f32[2,20,128]{2,1,0:T(8,128)S(1)}, f32[2,20,128]{2,1,0:T(8,128)S(1)}, u32[]{:S(2)}, u32[]{:S(2)}) collective-permute-start(f32[2,20,128]{2,1,0:T(8,128)S(1)} %pad_maximum_fusion.1), channel_id=1, source_target_pairs={{8,0},{16,8},{24,16},{9,1},{17,9},{25,17},{10,2},{18,10},{26,18},{... | collective-permute-start | bytes 61448 | tf_op jit(solution)/shard_map/ppermute | solution.py:312
  51.8 0.7 copy-start.3
  52.5 0.7 copy-start.4
  53.2 0.7 copy-start.5

commit v4 on v3

--- a/solution.py
+++ b/solution.py
@@ -337,7 +337,8 @@
     flags = jnp.stack([iy > 0, iy < gy - 1, iz > 0, iz < gz - 1]).astype(jnp.int32)
     amp, low, high, vols = filter_call(flags, src, yl, yh, zl, zh, density, passive, solid)
 
-    vols = lax.all_gather(vols.reshape(2, POINTS // 2), ("gz", "gy")).sum(axis=0).reshape(1, POINTS)
+    everyone = jnp.broadcast_to(vols, (gz * gy, POINTS))
+    vols = lax.all_to_all(everyone, ("gz", "gy"), 0, 0, tiled=True).sum(axis=0).reshape(1, POINTS)
     new, logm = update_call(vols, amp, low, high)
     return new, logm.reshape(())
 

time: 127 us -> 73.3 us (0.58)
  blocking collectives: 68.8 us -> 16.2 us
    all_gather x1 -> x0, blocking collectives: 68.8 us -> none  [on_device(): lax.all_gather(vols.reshape(2, POINTS // 2), ('gz', 'gy')).sum(axis=0)]
    all_to_all x0 -> x1, blocking collectives: none -> 16.2 us  [on_device(): lax.all_to_all(everyone, ('gz', 'gy'), 0, 0, tiled=True).sum(axis=0)]
  transfers between devices with their start and end apart: 7 -> 7, of which waited for: 3 -> 3; matrix products, arithmetic and copies ran while one was open for 2% -> 3% of each run, Pallas kernels for 0% -> 0%
where the time goes in v4:
time: 73.3 us; the launch traced here: 72.8 us
  Pallas kernels  22 us (30%)
  blocking collectives  16.2 us (22%)
  starting transfers between devices  14 us (19%)
  waiting for transfers between devices  10.6 us (14%)
  local copies, waits for them, and re-layouts  8.46 us (12%)
  between operations  0.8 us (1%)
    all_to_all x1, blocking collectives, on_device(): lax.all_to_all(everyone, ('gz', 'gy'), 0, 0, tiled=True).sum(axis=0)  16.2 us
    pallas_call x1, Pallas kernels, filter_call(): pl.pallas_call(filter_kernel, in_specs=[pl.BlockSpec(memory_space=pltpu.S...  12.6 us
    ppermute x2, starting transfers between devices, to_upper(): return lax.ppermute(value, axis, [(i, i + 1) for i in range(count - 1)])  7.55 us
    pallas_call x1, Pallas kernels, energy_call(): pl.pallas_call(energy_kernel, out_shape=(jax.ShapeDtypeStruct((ny, nz, nx...  7.44 us
    ppermute x1, waiting for transfers between devices, on_device(): fc = lax.ppermute(displacement[:, 0, 0], ('gz', 'gy'), pairs)  6.23 us
    unnamed x19, local copies, waits for them, and re-layouts  5.41 us
    ppermute x4, starting transfers between devices, to_lower(): return lax.ppermute(value, axis, [(i + 1, i) for i in range(count - 1)])  5.17 us
    ppermute x4, waiting for transfers between devices, to_lower(): return lax.ppermute(value, axis, [(i + 1, i) for i in range(count - 1)])  2.63 us
  transfers between devices with their start and end apart: 7, of which 3 were waited for; matrix products, arithmetic and copies ran while one was open for 3% of the time, Pallas kernels for 0%

profile of v4, /device:TPU:0, one launch (start us, length us, event | category | flops | bytes accessed | tf_op | source)
XLA Modules:
  0.0 72.8 jit_solution(3993489814196146921)
XLA Ops:
  0.6 1.0 %slice_bitcast_fusion = f32[9,32,128]{2,1,0:T(8,128)S(1)} fusion(f32[9,16,32,128]{3,2,1,0:T(8,128)} %disp.1), kind=kLoop, calls=%fused_computation | loop fusion | bytes 294912 | tf_op jit(solution)/shard_map/squeeze | solution.py:325
  1.6 1.3 %collective-permute-start = (f32[9,32,128]{2,1,0:T(8,128)S(1)}, f32[9,32,128]{2,1,0:T(8,128)S(1)}, u32[]{:S(2)}, u32[]{:S(2)}) collective-permute-start(f32[9,32,128]{2,1,0:T(8,128)S(1)} %slice_bitcast_fusion), channel_id=1, source_target_pairs={{1,0},{2,1},{3,2},{4,3},{5,4},{6,5},{7,6},{9,8},{10,9},{11,10},{12... | collective-permute-start | bytes 442376 | tf_op jit(solution)/shard_map/ppermute | solution.py:312
  2.9 1.1 %slice.28 = f32[9,16,1,128]{3,2,1,0:T(1,128)S(1)} slice(f32[9,16,32,128]{3,2,1,0:T(8,128)} %disp.1), slice={[0:9], [0:16], [0:1], [0:128]} | slice | bytes 147456 | tf_op jit(solution)/shard_map/slice | solution.py:326
  4.0 1.3 %collective-permute-start.1 = (f32[9,16,128]{2,1,0:T(8,128)S(1)}, f32[9,16,128]{2,1,0:T(8,128)S(1)}, u32[]{:S(2)}, u32[]{:S(2)}) collective-permute-start(f32[9,16,128]{2,1,0:T(8,128)S(1)} %bitcast.26), channel_id=1, source_target_pairs={{8,0},{16,8},{24,16},{9,1},{17,9},{25,17},{10,2},{18,10},{26,18},{... | collective-permute-start | bytes 221192 | tf_op jit(solution)/shard_map/ppermute | solution.py:312
  5.3 0.8 %slice.29 = f32[9,1,1,128]{3,2,1,0:T(1,128)S(1)} slice(f32[9,16,32,128]{3,2,1,0:T(8,128)} %disp.1), slice={[0:9], [0:1], [0:1], [0:128]} | slice | bytes 9216 | tf_op jit(solution)/shard_map/slice | solution.py:328
  6.1 1.3 %collective-permute-start.2 = (f32[9,128]{1,0:T(8,128)S(1)}, f32[9,128]{1,0:T(8,128)S(1)}, u32[]{:S(2)}, u32[]{:S(2)}) collective-permute-start(f32[9,128]{1,0:T(8,128)S(1)} %bitcast.27), channel_id=1, source_target_pairs={{9,0},{10,1},{11,2},{12,3},{13,4},{14,5},{15,6},{17,8},{18,9},{19,... | collective-permute-start | bytes 13832 | tf_op jit(solution)/shard_map/ppermute | solution.py:328
  7.4 6.2 %collective-permute-done.2.fc = f32[9,128]{1,0:T(8,128)S(1)} collective-permute-done((f32[9,128]{1,0:T(8,128)S(1)}, f32[9,128]{1,0:T(8,128)S(1)}, u32[]{:S(2)}, u32[]{:S(2)}) %collective-permute-start.2) | collective-permute-done | bytes 4640 | tf_op jit(solution)/shard_map/ppermute | solution.py:328
  13.6 1.7 %copy-done = f32[9,16,32,128]{3,2,1,0:T(8,128)S(1)} copy-done((f32[9,16,32,128]{3,2,1,0:T(8,128)S(1)}, f32[9,16,32,128]{3,2,1,0:T(8,128)}, u32[]{:S(2)}) %copy-start) | copy-done | bytes 2359320
  15.3 0.9 %copy-done.1 = f32[16,32,128]{2,1,0:T(8,128)S(1)} copy-done((f32[16,32,128]{2,1,0:T(8,128)S(1)}, f32[16,32,128]{2,1,0:T(8,128)}, u32[]{:S(2)}) %copy-start.1) | copy-done | bytes 262168
  16.2 0.7 copy-done.8
  17.0 7.4 %energy.1 = (f32[16,32,128]{2,1,0:T(8,128)S(1)}, f32[2,16,128]{2,1,0:T(8,128)S(1)}, f32[2,16,128]{2,1,0:T(8,128)S(1)}) custom-call(f32[9,16,32,128]{3,2,1,0:T(8,128)S(1)} %copy-done, f32[9,32,128]{2,1,0:T(8,128)S(1)} %collective-permute-done.fy, f32[9,16,128]{2,1,0:T(8,128)S(1)} %collective-permute-done.1.fz, f32[9,128]{1,0:T(8,128)S(1)} %collective-permute-done.2.fc, ...), custom_call_target="tpu_custom_call" | custom-call | tf_op jit(solution)/shard_map/energy/pallas_call | solution.py:170
  24.6 1.3 %collective-permute-start.4 = (f32[2,32,128]{2,0,1:T(2,128)S(1)}, f32[2,32,128]{2,0,1:T(2,128)S(1)}, u32[]{:S(2)}, u32[]{:S(2)}) collective-permute-start(f32[2,32,128]{2,0,1:T(2,128)S(1)} %get-tuple-element.20), channel_id=1, source_target_pairs={{1,0},{2,1},{3,2},{4,3},{5,4},{6,5},{7,6},{9,8},{10,9},{11,10},{12... | collective-permute-start | bytes 98312 | tf_op jit(solution)/shard_map/ppermute | solution.py:312
  25.9 5.4 %collective-permute-start.3 = (f32[2,32,128]{2,0,1:T(2,128)S(1)}, f32[2,32,128]{2,0,1:T(2,128)S(1)}, u32[]{:S(2)}, u32[]{:S(2)}) collective-permute-start(f32[2,32,128]{2,0,1:T(2,128)S(1)} %get-tuple-element.21), channel_id=1, source_target_pairs={{0,1},{1,2},{2,3},{3,4},{4,5},{5,6},{6,7},{8,9},{9,10},{10,11},{11... | collective-permute-start | bytes 98312 | tf_op jit(solution)/shard_map/ppermute | solution.py:317
  31.4 1.7 %collective-permute-done.3 = f32[2,32,128]{2,0,1:T(2,128)S(1)} collective-permute-done((f32[2,32,128]{2,0,1:T(2,128)S(1)}, f32[2,32,128]{2,0,1:T(2,128)S(1)}, u32[]{:S(2)}, u32[]{:S(2)}) %collective-permute-start.3) | collective-permute-done | bytes 32800 | tf_op jit(solution)/shard_map/ppermute | solution.py:317
  33.1 2.1 %collective-permute-start.5 = (f32[2,20,128]{2,1,0:T(8,128)S(1)}, f32[2,20,128]{2,1,0:T(8,128)S(1)}, u32[]{:S(2)}, u32[]{:S(2)}) collective-permute-start(f32[2,20,128]{2,1,0:T(8,128)S(1)} %pad_maximum_fusion), channel_id=1, source_target_pairs={{0,8},{8,16},{16,24},{1,9},{9,17},{17,25},{2,10},{10,18},{18,26},{... | collective-permute-start | bytes 61448 | tf_op jit(solution)/shard_map/ppermute | solution.py:317
  35.2 1.3 %collective-permute-start.6 = (f32[2,20,128]{2,1,0:T(8,128)S(1)}, f32[2,20,128]{2,1,0:T(8,128)S(1)}, u32[]{:S(2)}, u32[]{:S(2)}) collective-permute-start(f32[2,20,128]{2,1,0:T(8,128)S(1)} %pad_maximum_fusion.1), channel_id=1, source_target_pairs={{8,0},{16,8},{24,16},{9,1},{17,9},{25,17},{10,2},{18,10},{26,18},{... | collective-permute-start | bytes 61448 | tf_op jit(solution)/shard_map/ppermute | solution.py:312
  36.6 2.6 %collective-permute-done.6.zh = f32[2,20,128]{2,1,0:T(8,128)S(1)} collective-permute-done((f32[2,20,128]{2,1,0:T(8,128)S(1)}, f32[2,20,128]{2,1,0:T(8,128)S(1)}, u32[]{:S(2)}, u32[]{:S(2)}) %collective-permute-start.6) | collective-permute-done | bytes 20512 | tf_op jit(solution)/shard_map/ppermute | solution.py:312
  39.3 12.6 %filter.1 = (f32[16,32,128]{2,1,0:T(8,128)S(1)}, f32[16,32,128]{2,1,0:T(8,128)S(1)}, f32[16,32,128]{2,1,0:T(8,128)S(1)}, f32[1,256]{1,0:T(1,128)S(1)}) custom-call(s32[4]{0:T(128)S(1)} %add_convert_fusion.flags, f32[16,32,128]{2,1,0:T(8,128)S(1)} %get-tuple-element.11.src, f32[2,32,128]{2,1,0:T(8,128)S(1)} %copy.26.yl, f32[2,32,128]{2,1,0:T(8,128)S(1)} %copy.27.yh, ...), custom_call_target="tpu_custom_call" | custom-call | tf_op jit(solution)/shard_map/filter/pallas_call | solution.py:267
  51.9 0.7 copy-done.3
  52.5 0.7 copy-done.4
  53.2 0.7 copy-done.5
  53.9 16.2 %all_to_all.6 = f32[32,1,256]{2,1,0:T(1,128)S(1)} all-to-all(f32[32,1,256]{2,1,0:T(1,128)S(1)} %broadcast_in_dim.2), channel_id=1, replica_groups=mesh['gz'=4,'gy'=8] {'gz','gy'}, dimensions={0} | all-to-all | bytes 65536 | tf_op jit(solution)/shard_map/all_to_all | solution.py:341
  70.1 0.6 reduce_sum.9
  70.8 2.0 %update.1 = (f32[16,32,128]{2,1,0:T(8,128)}, f32[1]{0:T(128)}) custom-call(f32[1,256]{1,0:T(1,128)} %bitcast.28, f32[16,32,128]{2,1,0:T(8,128)} %copy-done.3, f32[16,32,128]{2,1,0:T(8,128)} %copy-done.4, f32[16,32,128]{2,1,0:T(8,128)} %copy-done.5), custom_call_target="tpu_custom_call" | custom-call | tf_op jit(solution)/shard_map/update/pallas_call | solution.py:301
  (27 shorter events, 0.4 us)
Async XLA Ops:
  0.6 38.6 %copy-start.2 = (f32[16,32,128]{2,1,0:T(8,128)S(1)}, f32[16,32,128]{2,1,0:T(8,128)}, u32[]{:S(2)}) copy-start(f32[16,32,128]{2,1,0:T(8,128)} %dens.3) | copy-start | bytes 786436
  1.6 12.0 %collective-permute-start = (f32[9,32,128]{2,1,0:T(8,128)S(1)}, f32[9,32,128]{2,1,0:T(8,128)S(1)}, u32[]{:S(2)}, u32[]{:S(2)}) collective-permute-start(f32[9,32,128]{2,1,0:T(8,128)S(1)} %slice_bitcast_fusion), channel_id=1, source_target_pairs={{1,0},{2,1},{3,2},{4,3},{5,4},{6,5},{7,6},{9,8},{10,9},{11,10},{12... | collective-permute-start | bytes 442376 | tf_op jit(solution)/shard_map/ppermute | solution.py:312
  4.0 9.6 %collective-permute-start.1 = (f32[9,16,128]{2,1,0:T(8,128)S(1)}, f32[9,16,128]{2,1,0:T(8,128)S(1)}, u32[]{:S(2)}, u32[]{:S(2)}) collective-permute-start(f32[9,16,128]{2,1,0:T(8,128)S(1)} %bitcast.26), channel_id=1, source_target_pairs={{8,0},{16,8},{24,16},{9,1},{17,9},{25,17},{10,2},{18,10},{26,18},{... | collective-permute-start | bytes 221192 | tf_op jit(solution)/shard_map/ppermute | solution.py:312
  6.1 7.5 %collective-permute-start.2 = (f32[9,128]{1,0:T(8,128)S(1)}, f32[9,128]{1,0:T(8,128)S(1)}, u32[]{:S(2)}, u32[]{:S(2)}) collective-permute-start(f32[9,128]{1,0:T(8,128)S(1)} %bitcast.27), channel_id=1, source_target_pairs={{9,0},{10,1},{11,2},{12,3},{13,4},{14,5},{15,6},{17,8},{18,9},{19,... | collective-permute-start | bytes 13832 | tf_op jit(solution)/shard_map/ppermute | solution.py:328
  13.6 1.7 %copy-start = (f32[9,16,32,128]{3,2,1,0:T(8,128)S(1)}, f32[9,16,32,128]{3,2,1,0:T(8,128)}, u32[]{:S(2)}) copy-start(f32[9,16,32,128]{3,2,1,0:T(8,128)} %disp.1) | copy-start | bytes 7077892
  15.3 0.9 %copy-start.1 = (f32[16,32,128]{2,1,0:T(8,128)S(1)}, f32[16,32,128]{2,1,0:T(8,128)}, u32[]{:S(2)}) copy-start(f32[16,32,128]{2,1,0:T(8,128)} %dens.3) | copy-start | bytes 786436
  16.2 0.7 copy-start.8
  17.0 22.3 %copy-start.6 = (s32[16,32,128]{2,1,0:T(8,128)S(1)}, s32[16,32,128]{2,1,0:T(8,128)}, u32[]{:S(2)}) copy-start(s32[16,32,128]{2,1,0:T(8,128)} %passive.1) | copy-start | bytes 786436
  17.0 22.3 %copy-start.7 = (s32[16,32,128]{2,1,0:T(8,128)S(1)}, s32[16,32,128]{2,1,0:T(8,128)}, u32[]{:S(2)}) copy-start(s32[16,32,128]{2,1,0:T(8,128)} %solid.1) | copy-start | bytes 786436
  24.6 6.8 %collective-permute-start.4 = (f32[2,32,128]{2,0,1:T(2,128)S(1)}, f32[2,32,128]{2,0,1:T(2,128)S(1)}, u32[]{:S(2)}, u32[]{:S(2)}) collective-permute-start(f32[2,32,128]{2,0,1:T(2,128)S(1)} %get-tuple-element.20), channel_id=1, source_target_pairs={{1,0},{2,1},{3,2},{4,3},{5,4},{6,5},{7,6},{9,8},{10,9},{11,10},{12... | collective-permute-start | bytes 98312 | tf_op jit(solution)/shard_map/ppermute | solution.py:312
  25.9 7.2 %collective-permute-start.3 = (f32[2,32,128]{2,0,1:T(2,128)S(1)}, f32[2,32,128]{2,0,1:T(2,128)S(1)}, u32[]{:S(2)}, u32[]{:S(2)}) collective-permute-start(f32[2,32,128]{2,0,1:T(2,128)S(1)} %get-tuple-element.21), channel_id=1, source_target_pairs={{0,1},{1,2},{2,3},{3,4},{4,5},{5,6},{6,7},{8,9},{9,10},{10,11},{11... | collective-permute-start | bytes 98312 | tf_op jit(solution)/shard_map/ppermute | solution.py:317
  33.1 3.5 %collective-permute-start.5 = (f32[2,20,128]{2,1,0:T(8,128)S(1)}, f32[2,20,128]{2,1,0:T(8,128)S(1)}, u32[]{:S(2)}, u32[]{:S(2)}) collective-permute-start(f32[2,20,128]{2,1,0:T(8,128)S(1)} %pad_maximum_fusion), channel_id=1, source_target_pairs={{0,8},{8,16},{16,24},{1,9},{9,17},{17,25},{2,10},{10,18},{18,26},{... | collective-permute-start | bytes 61448 | tf_op jit(solution)/shard_map/ppermute | solution.py:317
  35.2 4.0 %collective-permute-start.6 = (f32[2,20,128]{2,1,0:T(8,128)S(1)}, f32[2,20,128]{2,1,0:T(8,128)S(1)}, u32[]{:S(2)}, u32[]{:S(2)}) collective-permute-start(f32[2,20,128]{2,1,0:T(8,128)S(1)} %pad_maximum_fusion.1), channel_id=1, source_target_pairs={{8,0},{16,8},{24,16},{9,1},{17,9},{25,17},{10,2},{18,10},{26,18},{... | collective-permute-start | bytes 61448 | tf_op jit(solution)/shard_map/ppermute | solution.py:312
  51.8 0.7 copy-start.3
  52.5 0.7 copy-start.4
  53.2 0.7 copy-start.5

commit v5 on v4

v5 whole, which is shorter than its diff:
```python
import functools

import jax
import jax.numpy as jnp
from jax import lax
from jax.experimental import pallas as pl
from jax.experimental.pallas import tpu as pltpu
from jax.sharding import PartitionSpec as P

ITERS = 8
POINTS = 2**ITERS
OFF = 8

smoothing = 0.52
move_limit = 0.2
floor_density = 0.001
bracket_end = 12.0

f32 = jnp.float32
bf16 = jnp.bfloat16
VMEM = pl.BlockSpec(memory_space=pltpu.VMEM)
SMEM = pl.BlockSpec(memory_space=pltpu.SMEM)
HBM = pl.BlockSpec(memory_space=pltpu.HBM)


def cheb_weights():
    spectrum_top = 1.0 + 12.0 * smoothing
    centre_value = (spectrum_top + 1.0) / 2.0
    half_width = (spectrum_top - 1.0) / 2.0
    ratio_value = centre_value / half_width
    first_rho = 1.0 / ratio_value
    second_rho = 1.0 / (2.0 * ratio_value - first_rho)
    third_rho = 1.0 / (2.0 * ratio_value - second_rho)
    return (
        centre_value,
        second_rho * first_rho,
        2.0 * second_rho / half_width,
        third_rho * second_rho,
        2.0 * third_rho / half_width,
    )


def filter_weights():
    t, w1, w2, w3, w4 = cheb_weights()
    diag = 1.0 + 6.0 * smoothing
    alpha = w1 / t + w2 * (1.0 - diag / t)
    beta = w2 * smoothing / t
    gamma = 1.0 / t - w4 * w1 / (t * w2)
    delta = 1.0 + w3 + w4 / w2 - w4 * diag
    eps = w4 * smoothing
    return alpha, beta, gamma, delta, eps


def lane_up(v):
    n = v.shape[-1]
    lane = lax.broadcasted_iota(jnp.int32, v.shape, v.ndim - 1)
    return jnp.where(lane < n - 1, pltpu.roll(v, n - 1, v.ndim - 1), 0.0)


def lane_down(v):
    n = v.shape[-1]
    lane = lax.broadcasted_iota(jnp.int32, v.shape, v.ndim - 1)
    return jnp.where(lane > 0, pltpu.roll(v, 1, v.ndim - 1), 0.0)


def estimate(us):
    return pl.CostEstimate(flops=int(us * 1e9), bytes_accessed=1 << 20, transcendentals=0)


def build_matrix(k, mat):
    shape = (24, 112)
    col = lax.broadcasted_iota(jnp.int32, shape, 1)
    row = lax.broadcasted_iota(jnp.int32, shape, 0)
    main = col < 96
    dy = jnp.where(main, jnp.where(col >= 48, 1, 0), jnp.where(col >= 104, 1, 0))
    q = col - 48 * dy
    e = col - 96 - 8 * dy
    c = jnp.where(main, q >> 4, e >> 1)
    dx = jnp.where(main, (q >> 3) & 1, e & 1)
    valid = main | (e < 6)
    dof0 = 3 * (4 * dy + dx) + c
    pick0 = jnp.where(main & (row == dof0), 1.0, 0.0)
    pick1 = jnp.where(valid & (row == dof0 + 6), 1.0, 0.0)
    hp = lax.Precision.HIGHEST
    k0 = jnp.dot(k, pick0, precision=hp, preferred_element_type=f32)
    k1 = jnp.dot(k, pick1, precision=hp, preferred_element_type=f32)
    col8 = lax.broadcasted_iota(jnp.int32, (8, 112), 1)
    row8 = lax.broadcasted_iota(jnp.int32, (8, 112), 0)
    main8 = col8 < 96
    zc = col8 & 7
    m0 = main8 & (zc == row8)
    m1 = jnp.where(main8, zc, 8) == row8 + 1
    rows = []
    for dz in range(2):
        for dy_ in range(2):
            for c_ in range(3):
                for dx_ in range(2):
                    r = 3 * (4 * dy_ + 2 * dz + dx_) + c_
                    rows.append(jnp.where(m0, k0[r : r + 1], 0.0) + jnp.where(m1, k1[r : r + 1], 0.0))
    full = jnp.concatenate(rows, axis=0)
    hi = full.astype(bf16)
    lo = (full - hi.astype(f32)).astype(bf16)
    mat[:, 0:112] = hi
    mat[:, 112:224] = lo


def prepare(plane, p, main_s, ext_s, mul_s):
    for l in range(3):
        for c in range(3):
            u = plane(3 * l + c)
            nz, nx = u.shape
            last = lax.broadcasted_iota(jnp.int32, u.shape, 0) == nz - 1
            both = (u, lane_up(u))
            for w in range(nz // 8):
                sl = slice(8 * w, 8 * w + 8)
                main_s[p, l, 16 * c : 16 * c + 16, w * nx : (w + 1) * nx] = jnp.concatenate(
                    [both[0][sl], both[1][sl]], axis=0
                ).astype(bf16)
            for dx in range(2):
                v = both[dx]
                k = 2 * c + dx
                if ext_s is not None:
                    for w in range(nz // 8 - 1):
                        ext_s[p, l, k : k + 1, w * nx : (w + 1) * nx] = v[8 * w + 8 : 8 * w + 9]
                m = 2.0 * v - v.astype(bf16).astype(f32)
                mul_s[p, l, k, 0] = m
                mul_s[p, l, k, 1] = jnp.where(last, 0.0, pltpu.roll(m, nz - 1, 0))


def quadratic(force, mul, count, nx, acc):
    i = 0
    for dz in range(2):
        for dy in range(2):
            for k in range(6):
                for w in range(count):
                    term = force[8 * i : 8 * i + 8, w * nx : (w + 1) * nx] * mul(dy, k, dz, w)
                    acc[w] = term if acc[w] is None else acc[w] + term
                i += 1


def energy_row(p, mat, main_s, ext_s, mul_s, density):
    nz, nx = density.shape
    count = nz // 8
    acc = [None] * count
    for l in range(3):
        ext = jnp.concatenate([ext_s[p, l], ext_s[p + 1, l]], axis=0).astype(bf16)
        one = jnp.concatenate([main_s[p, l], main_s[p + 1, l], ext], axis=0)
        force = jnp.dot(mat[...], jnp.concatenate([one, one], axis=0), preferred_element_type=f32)
        quadratic(force, lambda dy, k, dz, w: mul_s[p + dy, l, k, dz, 8 * w : 8 * w + 8], count, nx, acc)
    return density * (-3.0 * density * density * jnp.concatenate(acc, axis=0))


def put_row(out, y, s):
    nz, nx = s.shape
    out[y, 0:OFF] = jnp.zeros((OFF, nx), f32)
    out[y, OFF : OFF + nz] = s
    out[y, OFF + nz :] = jnp.zeros((out.shape[1] - OFF - nz, nx), f32)


def first_kernel(disp, dens, stiff, src, mat, own_low, own_high, disp_s, dens_s, stiff_s, main_s, ext_s, mul_s, sems):
    _, ny, nz, nx = disp_s.shape
    half = ny // 2
    copy_k = pltpu.make_async_copy(stiff, stiff_s, sems.at[ny + 1])
    copy_k.start()
    copies = [pltpu.make_async_copy(disp.at[:, p], disp_s.at[:, p], sems.at[p]) for p in range(ny)]
    for p in range(2):
        copies[p].start()
    copy_d = pltpu.make_async_copy(dens, dens_s, sems.at[ny])
    copy_d.start()
    for p in range(2, ny):
        copies[p].start()
    ext_s[...] = jnp.zeros_like(ext_s)
    copy_k.wait()
    build_matrix(stiff_s[...], mat)
    for p in range(2):
        copies[p].wait()
        prepare(lambda i: disp_s[i, p], p, main_s, ext_s, mul_s)
    copy_d.wait()
    for p in range(2, half + 1):
        copies[p].wait()

    def body(y, _):
        put_row(src, y, energy_row(y, mat, main_s, ext_s, mul_s, dens_s[y]))
        prepare(lambda i: disp_s[i, y + 2], y + 2, main_s, ext_s, mul_s)
        return 0

    lax.fori_loop(0, half - 1, body, 0)
    put_row(src, half - 1, energy_row(half - 1, mat, main_s, ext_s, mul_s, dens_s[half - 1]))
    for p in range(half + 1, ny):
        copies[p].wait()

    def pack(y, _):
        for i in range(9):
            own_low[y, 2 * i : 2 * i + 2] = disp_s[i, y, nz - 2 : nz]
            own_high[y, 3 * i : 3 * i + 3] = disp_s[i, y, 0:3]
        own_low[y, 18:20] = dens_s[y, nz - 2 : nz]
        own_high[y, 27:29] = dens_s[y, 0:2]
        own_high[y, 29:30] = jnp.zeros((1, nx), f32)
        return 0

    lax.fori_loop(0, ny, pack, 0)


def energy_scratch(planes, nz, nx):
    lanes = nx * (nz // 8)
    return [
        pltpu.VMEM((planes, 3, 48, lanes), bf16),
        pltpu.VMEM((planes, 3, 8, lanes), f32),
        pltpu.VMEM((planes, 3, 6, 2, nz, nx), f32),
    ]


def first_call(disp, dens, stiff):
    _, ny, nz, nx = disp.shape
    half = ny // 2
    return pl.pallas_call(
        first_kernel,
        in_specs=[HBM, HBM, HBM],
        out_shape=(
            jax.ShapeDtypeStruct((half, nz + 2 * OFF, nx), f32),
            jax.ShapeDtypeStruct((192, 224), bf16),
            jax.ShapeDtypeStruct((ny, 20, nx), f32),
            jax.ShapeDtypeStruct((ny, 30, nx), f32),
        ),
        scratch_shapes=[pltpu.VMEM((9, ny, nz, nx), f32), pltpu.VMEM((ny, nz, nx), f32), pltpu.VMEM((24, 24), f32)]
        + energy_scratch(half + 1, nz, nx)
        + [pltpu.SemaphoreType.DMA((ny + 2,))],
        compiler_params=pltpu.CompilerParams(vmem_limit_bytes=24 * 2**20),
        cost_estimate=estimate(5),
        name="energy_first",
    )(disp, dens, stiff)


def last_kernel(disp, dens, fy, mat, src, disp_s, dens_s, main_s, ext_s, mul_s, sems):
    _, half, nz, nx = disp_s.shape
    copies = [pltpu.make_async_copy(disp.at[:, half + p], disp_s.at[:, p], sems.at[p]) for p in range(half)]
    for p in range(2):
        copies[p].start()
    copy_d = pltpu.make_async_copy(dens.at[pl.ds(half, half)], dens_s, sems.at[half])
    copy_d.start()
    for p in range(2, half):
        copies[p].start()
    ext_s[...] = jnp.zeros_like(ext_s)
    for p in range(2):
        copies[p].wait()
        prepare(lambda i: disp_s[i, p], p, main_s, ext_s, mul_s)
    copy_d.wait()
    for p in range(2, half):
        copies[p].wait()

    def row(y):
        put_row(src, y, energy_row(y, mat, main_s, ext_s, mul_s, dens_s[y]))

    def body(y, _):
        row(y)
        prepare(lambda i: disp_s[i, y + 2], y + 2, main_s, ext_s, mul_s)
        return 0

    lax.fori_loop(0, half - 2, body, 0)
    row(half - 2)
    prepare(lambda i: fy[i], half, main_s, ext_s, mul_s)
    row(half - 1)


def last_call(disp, dens, fy, mat):
    _, ny, nz, nx = disp.shape
    half = ny // 2
    return pl.pallas_call(
        last_kernel,
        in_specs=[HBM, HBM, VMEM, VMEM],
        out_shape=jax.ShapeDtypeStruct((half, nz + 2 * OFF, nx), f32),
        scratch_shapes=[pltpu.VMEM((9, half, nz, nx), f32), pltpu.VMEM((half, nz, nx), f32)]
        + energy_scratch(half + 1, nz, nx)
        + [pltpu.SemaphoreType.DMA((half + 1,))],
        compiler_params=pltpu.CompilerParams(vmem_limit_bytes=24 * 2**20),
        cost_estimate=estimate(5),
        name="energy_last",
    )(disp, dens, fy, mat)


def rim_kernel(flags, got_low, got_high, own_low, own_high, fy, mat, src_a, src_b, rim, msg_even, msg_odd, w_s, d_s, main_s, mul_s, t_s):
    ny, _, nx = own_low.shape
    nz = src_a.shape[1] - 2 * OFF
    half = ny // 2

    def window(p, low, high, first, last):
        for i in range(9):
            w_s[p, i, 0:2] = low(2 * i, 2)
            w_s[p, i, 2:3] = first(i)
            w_s[p, i, 3:4] = last(i)
            w_s[p, i, 4:7] = high(3 * i, 3)
            w_s[p, i, 7:8] = jnp.zeros((1, nx), f32)
        prepare(lambda i: w_s[p, i], p, main_s, None, mul_s)

    def own(p, _):
        window(
            p,
            lambda a, n: got_low[p, a : a + n],
            lambda a, n: got_high[p, a : a + n],
            lambda i: own_high[p, 3 * i : 3 * i + 1],
            lambda i: own_low[p, 2 * i + 1 : 2 * i + 2],
        )
        d_s[p] = jnp.zeros((8, nx), f32)
        d_s[p, 0:2] = got_low[p, 18:20]
        d_s[p, 3:4] = own_low[p, 19:20]
        d_s[p, 4:6] = got_high[p, 27:29]
        return 0

    lax.fori_loop(0, ny, own, 0)
    window(
        ny,
        lambda a, n: got_low[ny, a : a + n],
        lambda a, n: got_high[ny, a : a + n],
        lambda i: fy[i, 0:1],
        lambda i: fy[i, nz - 1 : nz],
    )

    group = 4

    def rows(g, _):
        acc = [None] * group
        for l in range(3):
            parts = [
                jnp.concatenate([main_s[g * group + j + dy, l] for j in range(group)], axis=1) for dy in range(2)
            ]
            one = jnp.concatenate(parts + [jnp.zeros((16, group * nx), bf16)], axis=0)
            force = jnp.dot(mat[...], jnp.concatenate([one, one], axis=0), preferred_element_type=f32)
            quadratic(force, lambda dy, k, dz, w: mul_s[g * group + w + dy, l, k, dz], group, nx, acc)
        for j in range(group):
            d = d_s[g * group + j]
            rim[g * group + j] = d * (-3.0 * d * d * acc[j])
        return 0

    lax.fori_loop(0, ny // group, rows, 0)

    for j in range(4):
        y = j if j < 2 else ny - 4 + j
        t_s[j] = src_a[y] if j < 2 else src_b[y - half]
        put_rim(t_s, j, rim[y], nz)
    odd = flags[4] == 1
    msg_even[...] = jnp.where(odd, t_s[0:2], t_s[2:4])
    msg_odd[...] = jnp.where(odd, t_s[2:4], t_s[0:2])


def put_rim(s, y, rim, nz):
    s[y, OFF - 2 : OFF] = rim[0:2]
    s[y, OFF + nz - 1 : OFF + nz + 2] = rim[3:6]


def rim_call(flags, got_low, got_high, own_low, own_high, fy, mat, src_a, src_b):
    ny, _, nx = own_low.shape
    rows = src_a.shape[1]
    return pl.pallas_call(
        rim_kernel,
        in_specs=[SMEM] + [VMEM] * 8,
        out_shape=(
            jax.ShapeDtypeStruct((ny, 8, nx), f32),
            jax.ShapeDtypeStruct((2, rows, nx), f32),
            jax.ShapeDtypeStruct((2, rows, nx), f32),
        ),
        scratch_shapes=[
            pltpu.VMEM((ny + 1, 9, 8, nx), f32),
            pltpu.VMEM((ny, 8, nx), f32),
            pltpu.VMEM((ny + 1, 3, 48, nx), bf16),
            pltpu.VMEM((ny + 1, 3, 6, 2, 8, nx), f32),
            pltpu.VMEM((4, rows, nx), f32),
        ],
        compiler_params=pltpu.CompilerParams(vmem_limit_bytes=16 * 2**20),
        cost_estimate=estimate(2),
        name="energy_rim",
    )(flags, got_low, got_high, own_low, own_high, fy, mat, src_a, src_b)


def filter_block(s_s, d_s, n, z_edges, y_edges, finish):
    rows, nx = s_s.shape[1:]
    nz = rows - 2 * OFF
    alpha, beta, gamma, delta, eps = filter_weights()
    row = lax.broadcasted_iota(jnp.int32, (rows, nx), 0)
    keep = jnp.where(row < OFF, z_edges[0], jnp.where(row >= OFF + nz, z_edges[1], 1)) == 1

    def beside(v):
        return pltpu.roll(v, 1, 0) + pltpu.roll(v, rows - 1, 0) + lane_up(v) + lane_down(v)

    def second(j, _):
        c = s_s[j + 1]
        d2 = alpha * c + beta * (beside(c) + s_s[j] + s_s[j + 2])
        ok = keep
        if y_edges is not None:
            ok = keep & (jnp.where(j == 0, y_edges[0], jnp.where(j == n - 3, y_edges[1], 1)) == 1)
        d_s[j] = jnp.where(ok, d2, 0.0)
        return 0

    def third(j, _):
        d2 = d_s[j + 1]
        p3 = gamma * s_s[j + 2] + delta * d2 + eps * (beside(d2) + d_s[j] + d_s[j + 2])
        finish(j, p3[OFF : OFF + nz])
        return 0

    lax.fori_loop(0, n - 2, second, 0)
    lax.fori_loop(0, n - 4, third, 0)


def limits(p3, d, pas, sol):
    amp = jnp.sqrt(jnp.maximum(-p3 * d, 0.0))
    lower = jnp.maximum(d - move_limit, floor_density)
    upper = jnp.minimum(d + move_limit, 1.0)
    low = jnp.where(sol, 1.0, jnp.where(pas, floor_density, lower))
    high = jnp.where(sol, 1.0, jnp.where(pas, floor_density, upper))
    return amp, low, high


def table(n, nz, nx, amp, low, high, dens, start, acc_s):
    groups = POINTS // 8
    half = groups // 2
    sub = lax.broadcasted_iota(jnp.int32, (8, nx), 0)
    for part in range(2):
        scale = []
        for g in range(half):
            k = sub + 8 * (part * half + g)
            mid = -bracket_end + (2.0 * bracket_end / POINTS) * k.astype(f32)
            scale.append(jnp.exp(-0.5 * mid))

        def volume(j, acc):
            acc = list(acc)
            for z in range(nz):
                a = jnp.broadcast_to(amp[j, z : z + 1], (8, nx))
                lo = jnp.broadcast_to(low[j, z : z + 1], (8, nx))
                hi = jnp.broadcast_to(high[j, z : z + 1], (8, nx))
                for g in range(half):
                    t = a * scale[g]
                    if part == 0 and g == 0:
                        t = jnp.where(sub == 0, jnp.broadcast_to(dens(j, z), (8, nx)), t)
                    acc[g] = acc[g] + jnp.minimum(jnp.maximum(t, lo), hi)
            return tuple(acc)

        at = [slice(8 * (part * half + g), 8 * (part * half + g) + 8) for g in range(half)]
        acc = lax.fori_loop(0, n, volume, tuple(start(at[g]) for g in range(half)))
        for g in range(half):
            acc_s[at[g]] = acc[g]


def inner_kernel(flags, src_a, src_b, rim, dens, passive, solid, amp, low, high, acc, s_s, d_s):
    ny, nz, nx = dens.shape
    half = ny // 2
    s_s[0:half] = src_a[...]
    s_s[half:ny] = src_b[...]

    def fix(y, _):
        put_rim(s_s, y, rim[y], nz)
        return 0

    lax.fori_loop(0, ny, fix, 0)

    def finish(j, p3):
        y = j + 2
        amp[j], low[j], high[j] = limits(p3, dens[y], passive[y] == 1, solid[y] == 1)

    filter_block(s_s, d_s, ny, (flags[2], flags[3]), None, finish)
    table(
        ny - 4, nz, nx, amp, low, high, lambda j, z: dens[j + 2, z : z + 1], lambda at: jnp.zeros((8, nx), f32), acc
    )


def inner_call(flags, src_a, src_b, rim, dens, passive, solid):
    ny, nz, nx = dens.shape
    field = jax.ShapeDtypeStruct((ny - 4, nz, nx), f32)
    return pl.pallas_call(
        inner_kernel,
        in_specs=[SMEM] + [VMEM] * 6,
        out_shape=(field, field, field, jax.ShapeDtypeStruct((POINTS, nx), f32)),
        scratch_shapes=[pltpu.VMEM((ny, nz + 2 * OFF, nx), f32), pltpu.VMEM((ny - 2, nz + 2 * OFF, nx), f32)],
        compiler_params=pltpu.CompilerParams(vmem_limit_bytes=16 * 2**20),
        cost_estimate=estimate(9),
        name="filter_inner",
    )(flags, src_a, src_b, rim, dens, passive, solid)


def outer_kernel(
    flags, src_a, src_b, rim, got_even, got_odd, dens, passive, solid, acc, amp, low, high, vols, s_s, d_s, dens_s, acc_s
):
    ny, nz, nx = dens.shape
    half = ny // 2
    odd = flags[4] == 1
    s_s[0, 0:2] = jnp.where(odd, got_even[...], got_odd[...])
    s_s[1, 4:6] = jnp.where(odd, got_odd[...], got_even[...])
    for j in range(4):
        s_s[0, 2 + j] = src_a[j]
        put_rim(s_s.at[0], 2 + j, rim[j], nz)
        s_s[1, j] = src_b[half - 4 + j]
        put_rim(s_s.at[1], j, rim[ny - 4 + j], nz)
    for b in range(2):
        y0 = 0 if b == 0 else ny - 2

        def finish(j, p3):
            y = y0 + j
            at = 2 * b + j
            amp[at], low[at], high[at] = limits(p3, dens[y], passive[y] == 1, solid[y] == 1)
            dens_s[at] = dens[y]

        edges = (flags[0], 1) if b == 0 else (1, flags[1])
        filter_block(s_s.at[b], d_s, 6, (flags[2], flags[3]), edges, finish)
    table(4, nz, nx, amp, low, high, lambda j, z: dens_s[j, z : z + 1], lambda at: acc[at], acc_s)
    vols[...] = jnp.sum(jnp.transpose(acc_s[...]), axis=0, keepdims=True)


def outer_call(flags, src_a, src_b, rim, got_even, got_odd, dens, passive, solid, acc):
    ny, nz, nx = dens.shape
    rows = nz + 2 * OFF
    field = jax.ShapeDtypeStruct((4, nz, nx), f32)
    return pl.pallas_call(
        outer_kernel,
        in_specs=[SMEM] + [VMEM] * 9,
        out_shape=(field, field, field, jax.ShapeDtypeStruct((1, POINTS), f32)),
        scratch_shapes=[
            pltpu.VMEM((2, 6, rows, nx), f32),
            pltpu.VMEM((4, rows, nx), f32),
            pltpu.VMEM((4, nz, nx), f32),
            pltpu.VMEM((POINTS, nx), f32),
        ],
        compiler_params=pltpu.CompilerParams(vmem_limit_bytes=16 * 2**20),
        cost_estimate=estimate(3),
        name="filter_outer",
    )(flags, src_a, src_b, rim, got_even, got_odd, dens, passive, solid, acc)


def update_kernel(tables, amp_i, low_i, high_i, amp_o, low_o, high_o, new, logm):
    inner = amp_i.shape[0]
    nx = amp_i.shape[-1]
    total = jnp.sum(tables[...], axis=0, keepdims=True)
    above = jnp.where(total > total[:, 0:1], 1.0, 0.0)
    middle = -bracket_end + (2.0 * bracket_end / POINTS) * (jnp.sum(above) + 0.5)
    logm[0] = middle
    scale = jnp.exp(jnp.full((1, nx), -0.5 * middle, f32))

    def new_row(amp, low, high):
        return jnp.minimum(jnp.maximum(amp * scale, low), high)

    def body(j, _):
        new[j + 2] = new_row(amp_i[j], low_i[j], high_i[j])
        return 0

    lax.fori_loop(0, inner, body, 0)
    for j in range(4):
        new[j if j < 2 else inner + j] = new_row(amp_o[j], low_o[j], high_o[j])


def update_call(tables, inner, outer):
    n, nz, nx = inner[0].shape
    return pl.pallas_call(
        update_kernel,
        in_specs=[VMEM] * 7,
        out_specs=(VMEM, SMEM),
        out_shape=(jax.ShapeDtypeStruct((n + 4, nz, nx), f32), jax.ShapeDtypeStruct((1,), f32)),
        compiler_params=pltpu.CompilerParams(vmem_limit_bytes=8 * 2**20),
        cost_estimate=estimate(1),
        name="update",
    )(tables, *inner, *outer)


def to_lower(value, axis):
    count = lax.axis_size(axis)
    return lax.ppermute(value, axis, [(i + 1, i) for i in range(count - 1)])


def to_upper(value, axis):
    count = lax.axis_size(axis)
    return lax.ppermute(value, axis, [(i, i + 1) for i in range(count - 1)])


def swap(value, axis, start):
    pairs = []
    for i in range(start, lax.axis_size(axis) - 1, 2):
        pairs += [(i, i + 1), (i + 1, i)]
    return lax.ppermute(value, axis, pairs)


def on_device(displacement, density, passive, solid, stiffness):
    ny, nz, nx = density.shape
    gy, gz = lax.axis_size("gy"), lax.axis_size("gz")
    iy, iz = lax.axis_index("gy"), lax.axis_index("gz")
    flags = jnp.stack([iy > 0, iy < gy - 1, iz > 0, iz < gz - 1, iy % 2 == 1]).astype(jnp.int32)

    fy = to_lower(displacement[:, 0], "gy")
    src_a, mat, own_low, own_high = first_call(displacement, density, stiffness)

    rim_low = jnp.pad(fy[:, nz - 2 :].reshape(1, 18, nx), ((0, 0), (0, 2), (0, 0)))
    rim_high = jnp.pad(fy[:, :3].reshape(1, 27, nx), ((0, 0), (0, 3), (0, 0)))
    got_low = to_upper(jnp.concatenate([own_low, rim_low]), "gz")
    got_high = to_lower(jnp.concatenate([own_high, rim_high]), "gz")
    src_b = last_call(displacement, density, fy, mat)
    rim, msg_even, msg_odd = rim_call(flags, got_low, got_high, own_low, own_high, fy, mat, src_a, src_b)

    got_odd = swap(msg_odd, "gy", 1)
    got_even = swap(msg_even, "gy", 0)
    *inner, acc = inner_call(flags, src_a, src_b, rim, density, passive, solid)
    *outer, vols = outer_call(flags, src_a, src_b, rim, got_even, got_odd, density, passive, solid, acc)

    everyone = jnp.broadcast_to(vols, (gz * gy, POINTS))
    tables = lax.all_to_all(everyone, ("gz", "gy"), 0, 0, tiled=True)
    new, logm = update_call(tables, inner, outer)
    return new, logm.reshape(())


def solution(mesh):
    placed = (
        P(None, "gy", "gz", None),
        P("gy", "gz", None),
        P("gy", "gz", None),
        P("gy", "gz", None),
        P(),
    )
    return jax.shard_map(
        on_device, mesh=mesh, in_specs=placed, out_specs=(P("gy", "gz", None), P()), check_vma=False
    )
```

time: 73.3 us -> 59.2 us (0.81)
  waiting for transfers between devices: 10.6 us -> 0.01 us
  starting transfers between devices: 14 us -> 9.9 us
  Pallas kernels: 22 us -> 25 us
  local copies, waits for them, and re-layouts: 8.46 us -> 6.47 us
    ppermute x1 -> x2, waiting for transfers between devices: 6.23 us -> 0.01 us  [swap(): return lax.ppermute(value, axis, pairs)]
    ppermute x2 -> x1, starting transfers between devices: 7.55 us -> 3.04 us  [to_upper(): return lax.ppermute(value, axis, [(i, i + 1) for i in range(count - 1)])]
    pallas_call x3 -> x6, Pallas kernels: 22 us -> 25 us  [the longest x1 9.66 us: inner_call(): pl.pallas_call(inner_kernel, in_specs=[SMEM] + [VMEM] * 6, out_shape=(fie...]
    ppermute x1 -> x2, starting transfers between devices: 1.28 us -> 4.29 us  [swap(): return lax.ppermute(value, axis, pairs)]
    ppermute x4 -> x2, waiting for transfers between devices: 2.63 us -> 0.01 us  [to_lower(): return lax.ppermute(value, axis, [(i + 1, i) for i in range(count - 1)])]
    ppermute x4 -> x2, starting transfers between devices: 5.17 us -> 2.57 us  [to_lower(): return lax.ppermute(value, axis, [(i + 1, i) for i in range(count - 1)])]
    slice x3 -> x2, local copies, waits for them, and re-layouts: 1.9 us -> 0.01 us  [the longest x1 0.01 us: on_device(): fy[:, nz - 2:].reshape(1, 18, nx)]
    ppermute x2 -> x1, waiting for transfers between devices: 1.7 us -> 0.01 us  [to_upper(): return lax.ppermute(value, axis, [(i, i + 1) for i in range(count - 1)])]
  transfers between devices with their start and end apart: 7 -> 5, of which waited for: 3 -> 0; matrix products, arithmetic and copies ran while one was open for 3% -> 0% of each run, Pallas kernels for 0% -> 28%
where the time goes in v5:
time: 59.2 us; the launch traced here: 58.8 us
  Pallas kernels  25 us (42%)
  blocking collectives  15.8 us (27%)
  starting transfers between devices  9.9 us (17%)
  local copies, waits for them, and re-layouts  6.47 us (11%)
  between operations  0.86 us (1%)
  other arithmetic  0.74 us (1%)
    all_to_all x1, blocking collectives, on_device(): tables = lax.all_to_all(everyone, ('gz', 'gy'), 0, 0, tiled=True)  15.8 us
    pallas_call x1, Pallas kernels, inner_call(): pl.pallas_call(inner_kernel, in_specs=[SMEM] + [VMEM] * 6, out_shape=(fie...  9.66 us
    unnamed x23, local copies, waits for them, and re-layouts  5.39 us
    ppermute x2, starting transfers between devices, swap(): return lax.ppermute(value, axis, pairs)  4.29 us
    pallas_call x1, Pallas kernels, outer_call(): pl.pallas_call(outer_kernel, in_specs=[SMEM] + [VMEM] * 9, out_shape=(fie...  3.98 us
    pallas_call x1, Pallas kernels, first_call(): pl.pallas_call(first_kernel, in_specs=[HBM, HBM, HBM], out_shape=(jax.Sha...  3.84 us
    pallas_call x1, Pallas kernels, rim_call(): pl.pallas_call(rim_kernel, in_specs=[SMEM] + [VMEM] * 8, out_shape=(jax.S...  3.47 us
    pallas_call x1, Pallas kernels, last_call(): pl.pallas_call(last_kernel, in_specs=[HBM, HBM, VMEM, VMEM], out_shape=ja...  3.08 us
  transfers between devices with their start and end apart: 5, of which 0 were waited for; matrix products, arithmetic and copies ran while one was open for 0% of the time, Pallas kernels for 28%

profile of v5, /device:TPU:0, one launch (start us, length us, event | category | flops | bytes accessed | tf_op | source)
XLA Modules:
  0.0 58.8 jit_solution(12279199054555833891)
XLA Ops:
  0.6 0.9 %slice_bitcast_fusion = f32[9,32,128]{2,1,0:T(8,128)S(1)} fusion(f32[9,16,32,128]{3,2,1,0:T(8,128)} %disp.3), kind=kLoop, calls=%fused_computation.4 | loop fusion | bytes 294912 | tf_op jit(solution)/shard_map/squeeze | solution.py:583
  1.6 1.3 %collective-permute-start = (f32[9,32,128]{2,1,0:T(8,128)S(1)}, f32[9,32,128]{2,1,0:T(8,128)S(1)}, u32[]{:S(2)}, u32[]{:S(2)}) collective-permute-start(f32[9,32,128]{2,1,0:T(8,128)S(1)} %slice_bitcast_fusion), channel_id=1, source_target_pairs={{1,0},{2,1},{3,2},{4,3},{5,4},{6,5},{7,6},{9,8},{10,9},{11,10},{12... | collective-permute-start | bytes 442376 | tf_op jit(solution)/shard_map/ppermute | solution.py:562
  2.9 0.0 copy-start
  2.9 1.7 %copy-done = f32[9,16,32,128]{3,2,1,0:T(8,128)S(1)} copy-done((f32[9,16,32,128]{3,2,1,0:T(8,128)S(1)}, f32[9,16,32,128]{3,2,1,0:T(8,128)}, u32[]{:S(2)}) %copy-start) | copy-done | bytes 2359320
  4.5 0.9 %copy-done.2 = f32[16,32,128]{2,1,0:T(8,128)S(1)} copy-done((f32[16,32,128]{2,1,0:T(8,128)S(1)}, f32[16,32,128]{2,1,0:T(8,128)}, u32[]{:S(2)}) %copy-start.2) | copy-done | bytes 262168
  5.5 0.7 %copy-done.6 = f32[24,24]{1,0:T(8,128)S(1)} copy-done((f32[24,24]{1,0:T(8,128)S(1)}, f32[24,24]{1,0:T(8,128)}, u32[]{:S(2)}) %copy-start.6) | copy-done | bytes 2328
  6.2 3.8 %energy_first.1 = (f32[8,48,128]{2,1,0:T(8,128)S(1)}, bf16[192,224]{1,0:T(8,128)(2,1)S(1)}, f32[16,20,128]{2,1,0:T(8,128)S(1)}, f32[16,30,128]{2,1,0:T(8,128)S(1)}) custom-call(f32[9,16,32,128]{3,2,1,0:T(8,128)S(1)} %copy-done, f32[16,32,128]{2,1,0:T(8,128)S(1)} %copy-done.2, f32[24,24]{1,0:T(8,128)S(1)} %copy-done.6), custom_call_target="tpu_custom_call" | custom-call | flops 5000000000 | bytes 1048576 | tf_op jit(solution)/shard_map/energy_first/pallas_call | solution.py:216
  10.0 0.0 copy-start.7
  10.1 0.7 %copy-done.7 = f32[8,48,128]{2,1,0:T(8,128)} copy-done((f32[8,48,128]{2,1,0:T(8,128)}, f32[8,48,128]{2,1,0:T(8,128)S(1)}, u32[]{:S(2)}) %copy-start.7) | copy-done | bytes 196632
  10.7 0.1 stack.23
  10.9 0.5 copy-done.9
  11.4 0.7 %select_maximum_fusion = f32[17,30,128]{2,1,0:T(8,128)} fusion(f32[1,27,128]{2,1,0:T(8,128)S(1)} %reshape.20, f32[16,30,128]{2,1,0:T(8,128)S(1)} %get-tuple-element.22.own_high), kind=kLoop, calls=%fused_computation | loop fusion | flops 195840 | bytes 520704 | tf_op jit(solution)/shard_map/concatenate | solution.py:589
  12.1 1.3 %collective-permute-start.2 = (f32[17,30,128]{2,1,0:T(8,128)}, f32[17,30,128]{2,1,0:T(8,128)S(1)}, u32[]{:S(2)}, u32[]{:S(2)}) collective-permute-start(f32[17,30,128]{2,1,0:T(8,128)} %select_maximum_fusion), channel_id=1, source_target_pairs={{8,0},{16,8},{24,16},{9,1},{17,9},{25,17},{10,2},{18,10},{26,18},{... | collective-permute-start | bytes 783368 | tf_op jit(solution)/shard_map/ppermute | solution.py:562
  13.4 3.0 %collective-permute-start.1 = (f32[17,20,128]{2,1,0:T(8,128)S(1)}, f32[17,20,128]{2,1,0:T(8,128)S(1)}, u32[]{:S(2)}, u32[]{:S(2)}) collective-permute-start(f32[17,20,128]{2,1,0:T(8,128)S(1)} %select_maximum_fusion.1), channel_id=1, source_target_pairs={{0,8},{8,16},{16,24},{1,9},{9,17},{17,25},{2,10},{10,18},{18,26},{... | collective-permute-start | bytes 522248 | tf_op jit(solution)/shard_map/ppermute | solution.py:567
  16.5 0.9 %copy-done.10 = bf16[192,224]{1,0:T(8,128)(2,1)S(1)} copy-done((bf16[192,224]{1,0:T(8,128)(2,1)S(1)}, bf16[192,224]{1,0:T(8,128)(2,1)}, u32[]{:S(2)}) %copy-start.10) | copy-done | bytes 86040
  17.4 3.1 %energy_last.1.src_b = f32[8,48,128]{2,1,0:T(8,128)S(1)} custom-call(f32[9,16,32,128]{3,2,1,0:T(8,128)S(1)} %copy-done.1, f32[16,32,128]{2,1,0:T(8,128)S(1)} %copy-done.3, f32[9,32,128]{2,1,0:T(8,128)S(1)} %collective-permute-done.fy, bf16[192,224]{1,0:T(8,128)(2,1)S(1)} %copy-done.10), custom_call_target="tpu_custom_call" | custom-call | flops 5000000000 | bytes 1048576 | tf_op jit(solution)/shard_map/energy_last/pallas_call | solution.py:268
  20.5 0.0 copy-start.4
  20.5 3.5 %energy_rim.1 = (f32[16,8,128]{2,1,0:T(8,128)S(1)}, f32[2,48,128]{2,1,0:T(8,128)S(1)}, f32[2,48,128]{2,1,0:T(8,128)S(1)}) custom-call(s32[5]{0:T(128)S(1)} %convert_element_type.7.flags, f32[17,20,128]{2,1,0:T(8,128)S(1)} %collective-permute-done.1.got_low, f32[17,30,128]{2,1,0:T(8,128)S(1)} %collective-permute-done.2.got_high, ...), custom_call_target="tpu_custom_call" | custom-call | flops 2000000000 | bytes 1048576 | tf_op jit(solution)/shard_map/energy_rim/pallas_call | solution.py:353
  24.0 3.6 %collective-permute-start.3 = (f32[2,48,128]{2,1,0:T(8,128)S(1)}, f32[2,48,128]{2,1,0:T(8,128)S(1)}, u32[]{:S(2)}, u32[]{:S(2)}) collective-permute-start(f32[2,48,128]{2,1,0:T(8,128)S(1)} %get-tuple-element.24), channel_id=1, source_target_pairs={{0,1},{1,0},{2,3},{3,2},{4,5},{5,4},{6,7},{7,6},{8,9},{9,8},{10,11... | collective-permute-start | bytes 147464 | tf_op jit(solution)/shard_map/ppermute | solution.py:574
  27.6 0.7 %collective-permute-start.4 = (f32[2,48,128]{2,1,0:T(8,128)S(1)}, f32[2,48,128]{2,1,0:T(8,128)S(1)}, u32[]{:S(2)}, u32[]{:S(2)}) collective-permute-start(f32[2,48,128]{2,1,0:T(8,128)S(1)} %get-tuple-element.25), channel_id=1, source_target_pairs={{1,2},{2,1},{3,4},{4,3},{5,6},{6,5},{9,10},{10,9},{11,12},{12,11},... | collective-permute-start | bytes 147464 | tf_op jit(solution)/shard_map/ppermute | solution.py:574
  28.3 9.7 %filter_inner.1 = (f32[12,32,128]{2,1,0:T(8,128)S(1)}, f32[12,32,128]{2,1,0:T(8,128)S(1)}, f32[12,32,128]{2,1,0:T(8,128)S(1)}, f32[256,128]{1,0:T(8,128)S(1)}) custom-call(s32[5]{0:T(128)S(1)} %convert_element_type.7.flags, f32[8,48,128]{2,1,0:T(8,128)S(1)} %copy-done.8, f32[8,48,128]{2,1,0:T(8,128)S(1)} %energy_last.1.src_b, ...), custom_call_target="tpu_custom_call" | custom-call | flops 8999999488 | bytes 1048576 | tf_op jit(solution)/shard_map/filter_inner/pallas_call | solution.py:467
  38.0 4.0 %filter_outer.1 = (f32[4,32,128]{2,1,0:T(8,128)S(1)}, f32[4,32,128]{2,1,0:T(8,128)S(1)}, f32[4,32,128]{2,1,0:T(8,128)S(1)}, f32[1,256]{1,0:T(1,128)S(1)}) custom-call(s32[5]{0:T(128)S(1)} %convert_element_type.7.flags, f32[8,48,128]{2,1,0:T(8,128)S(1)} %copy-done.8, f32[8,48,128]{2,1,0:T(8,128)S(1)} %energy_last.1.src_b, ...), custom_call_target="tpu_custom_call" | custom-call | flops 3000000000 | bytes 1048576 | tf_op jit(solution)/shard_map/filter_outer/pallas_call | solution.py:510
  42.0 15.8 %all_to_all.8 = f32[32,1,256]{2,1,0:T(1,128)S(1)} all-to-all(f32[32,1,256]{2,1,0:T(1,128)S(1)} %broadcast_in_dim.2), channel_id=1, replica_groups=mesh['gz'=4,'gy'=8] {'gz','gy'}, dimensions={0} | all-to-all | bytes 65536 | tf_op jit(solution)/shard_map/all_to_all | solution.py:599
  57.8 1.0 %update.1 = (f32[16,32,128]{2,1,0:T(8,128)}, f32[1]{0:T(128)}) custom-call(f32[32,256]{1,0:T(8,128)S(1)} %bitcast.14, f32[12,32,128]{2,1,0:T(8,128)S(1)} %get-tuple-element.28.amp_i, f32[12,32,128]{2,1,0:T(8,128)S(1)} %get-tuple-element.29.low_i, f32[12,32,128]{2,1,0:T(8,128)S(1)} %get-tuple-element.30.high_i, f32[4,32,128]{2,1,0:T(8,128)S(1)} %get-tuple-element.31.amp_o, ...), custom_call_target="tpu_custom_call" | custom-call | flops 1000000000 | bytes 1048576 | tf_op jit(solution)/shard_map/update/pallas_call | solution.py:549
  (26 shorter events, 0.1 us)
Async XLA Ops:
  1.6 9.3 %collective-permute-start = (f32[9,32,128]{2,1,0:T(8,128)S(1)}, f32[9,32,128]{2,1,0:T(8,128)S(1)}, u32[]{:S(2)}, u32[]{:S(2)}) collective-permute-start(f32[9,32,128]{2,1,0:T(8,128)S(1)} %slice_bitcast_fusion), channel_id=1, source_target_pairs={{1,0},{2,1},{3,2},{4,3},{5,4},{6,5},{7,6},{9,8},{10,9},{11,10},{12... | collective-permute-start | bytes 442376 | tf_op jit(solution)/shard_map/ppermute | solution.py:562
  2.9 1.7 %copy-start = (f32[9,16,32,128]{3,2,1,0:T(8,128)S(1)}, f32[9,16,32,128]{3,2,1,0:T(8,128)}, u32[]{:S(2)}) copy-start(f32[9,16,32,128]{3,2,1,0:T(8,128)} %disp.3) | copy-start | bytes 7077892
  4.5 0.9 %copy-start.2 = (f32[16,32,128]{2,1,0:T(8,128)S(1)}, f32[16,32,128]{2,1,0:T(8,128)}, u32[]{:S(2)}) copy-start(f32[16,32,128]{2,1,0:T(8,128)} %dens.7) | copy-start | bytes 786436
  5.5 0.7 %copy-start.6 = (f32[24,24]{1,0:T(8,128)S(1)}, f32[24,24]{1,0:T(8,128)}, u32[]{:S(2)}) copy-start(f32[24,24]{1,0:T(8,128)} %stiff.1) | copy-start | bytes 6916
  6.2 10.3 %copy-start.1 = (f32[9,16,32,128]{3,2,1,0:T(8,128)S(1)}, f32[9,16,32,128]{3,2,1,0:T(8,128)}, u32[]{:S(2)}) copy-start(f32[9,16,32,128]{3,2,1,0:T(8,128)} %disp.3) | copy-start | bytes 7077892
  6.2 10.3 %copy-start.3 = (f32[16,32,128]{2,1,0:T(8,128)S(1)}, f32[16,32,128]{2,1,0:T(8,128)}, u32[]{:S(2)}) copy-start(f32[16,32,128]{2,1,0:T(8,128)} %dens.7) | copy-start | bytes 786436
  10.0 0.7 %copy-start.7 = (f32[8,48,128]{2,1,0:T(8,128)}, f32[8,48,128]{2,1,0:T(8,128)S(1)}, u32[]{:S(2)}) copy-start(f32[8,48,128]{2,1,0:T(8,128)S(1)} %get-tuple-element.19.src_a) | copy-start | bytes 589828
  10.7 0.6 %copy-start.9 = (bf16[192,224]{1,0:T(8,128)(2,1)}, bf16[192,224]{1,0:T(8,128)(2,1)S(1)}, u32[]{:S(2)}) copy-start(bf16[192,224]{1,0:T(8,128)(2,1)S(1)} %get-tuple-element.20.mat) | copy-start | bytes 258052
  12.1 8.4 %collective-permute-start.2 = (f32[17,30,128]{2,1,0:T(8,128)}, f32[17,30,128]{2,1,0:T(8,128)S(1)}, u32[]{:S(2)}, u32[]{:S(2)}) collective-permute-start(f32[17,30,128]{2,1,0:T(8,128)} %select_maximum_fusion), channel_id=1, source_target_pairs={{8,0},{16,8},{24,16},{9,1},{17,9},{25,17},{10,2},{18,10},{26,18},{... | collective-permute-start | bytes 783368 | tf_op jit(solution)/shard_map/ppermute | solution.py:562
  13.4 7.1 %collective-permute-start.1 = (f32[17,20,128]{2,1,0:T(8,128)S(1)}, f32[17,20,128]{2,1,0:T(8,128)S(1)}, u32[]{:S(2)}, u32[]{:S(2)}) collective-permute-start(f32[17,20,128]{2,1,0:T(8,128)S(1)} %select_maximum_fusion.1), channel_id=1, source_target_pairs={{0,8},{8,16},{16,24},{1,9},{9,17},{17,25},{2,10},{10,18},{18,26},{... | collective-permute-start | bytes 522248 | tf_op jit(solution)/shard_map/ppermute | solution.py:567
  16.5 0.9 %copy-start.10 = (bf16[192,224]{1,0:T(8,128)(2,1)S(1)}, bf16[192,224]{1,0:T(8,128)(2,1)}, u32[]{:S(2)}) copy-start(bf16[192,224]{1,0:T(8,128)(2,1)} %copy-done.9) | copy-start | bytes 258052
  17.4 3.1 %copy-start.8 = (f32[8,48,128]{2,1,0:T(8,128)S(1)}, f32[8,48,128]{2,1,0:T(8,128)}, u32[]{:S(2)}) copy-start(f32[8,48,128]{2,1,0:T(8,128)} %copy-done.7) | copy-start | bytes 589828
  20.5 7.8 %copy-start.4 = (s32[16,32,128]{2,1,0:T(8,128)S(1)}, s32[16,32,128]{2,1,0:T(8,128)}, u32[]{:S(2)}) copy-start(s32[16,32,128]{2,1,0:T(8,128)} %passive.3) | copy-start | bytes 786436
  20.5 7.8 %copy-start.5 = (s32[16,32,128]{2,1,0:T(8,128)S(1)}, s32[16,32,128]{2,1,0:T(8,128)}, u32[]{:S(2)}) copy-start(s32[16,32,128]{2,1,0:T(8,128)} %solid.3) | copy-start | bytes 786436
  24.0 14.0 %collective-permute-start.3 = (f32[2,48,128]{2,1,0:T(8,128)S(1)}, f32[2,48,128]{2,1,0:T(8,128)S(1)}, u32[]{:S(2)}, u32[]{:S(2)}) collective-permute-start(f32[2,48,128]{2,1,0:T(8,128)S(1)} %get-tuple-element.24), channel_id=1, source_target_pairs={{0,1},{1,0},{2,3},{3,2},{4,5},{5,4},{6,7},{7,6},{8,9},{9,8},{10,11... | collective-permute-start | bytes 147464 | tf_op jit(solution)/shard_map/ppermute | solution.py:574
  27.6 10.4 %collective-permute-start.4 = (f32[2,48,128]{2,1,0:T(8,128)S(1)}, f32[2,48,128]{2,1,0:T(8,128)S(1)}, u32[]{:S(2)}, u32[]{:S(2)}) collective-permute-start(f32[2,48,128]{2,1,0:T(8,128)S(1)} %get-tuple-element.25), channel_id=1, source_target_pairs={{1,2},{2,1},{3,4},{4,3},{5,6},{6,5},{9,10},{10,9},{11,12},{12,11},... | collective-permute-start | bytes 147464 | tf_op jit(solution)/shard_map/ppermute | solution.py:574

commit v6 on v5

--- a/solution.py
+++ b/solution.py
@@ -195,6 +195,7 @@
             own_high[y, 3 * i : 3 * i + 3] = disp_s[i, y, 0:3]
         own_low[y, 18:20] = dens_s[y, nz - 2 : nz]
         own_high[y, 27:29] = dens_s[y, 0:2]
+        own_low[y, 20:30] = jnp.zeros((10, nx), f32)
         own_high[y, 29:30] = jnp.zeros((1, nx), f32)
         return 0
 
@@ -219,7 +220,7 @@
         out_shape=(
             jax.ShapeDtypeStruct((half, nz + 2 * OFF, nx), f32),
             jax.ShapeDtypeStruct((192, 224), bf16),
-            jax.ShapeDtypeStruct((ny, 20, nx), f32),
+            jax.ShapeDtypeStruct((ny, 30, nx), f32),
             jax.ShapeDtypeStruct((ny, 30, nx), f32),
         ),
         scratch_shapes=[pltpu.VMEM((9, ny, nz, nx), f32), pltpu.VMEM((ny, nz, nx), f32), pltpu.VMEM((24, 24), f32)]
@@ -278,42 +279,35 @@
     )(disp, dens, fy, mat)
 
 
-def rim_kernel(flags, got_low, got_high, own_low, own_high, fy, mat, src_a, src_b, rim, msg_even, msg_odd, w_s, d_s, main_s, mul_s, t_s):
+def rim_kernel(
+    flags, got_even, got_odd, own_low, own_high, fy, mat, src_a, src_b, rim, msg_even, msg_odd, d_s, main_s, mul_s, t_s
+):
     ny, _, nx = own_low.shape
     nz = src_a.shape[1] - 2 * OFF
     half = ny // 2
-
-    def window(p, low, high, first, last):
-        for i in range(9):
-            w_s[p, i, 0:2] = low(2 * i, 2)
-            w_s[p, i, 2:3] = first(i)
-            w_s[p, i, 3:4] = last(i)
-            w_s[p, i, 4:7] = high(3 * i, 3)
-            w_s[p, i, 7:8] = jnp.zeros((1, nx), f32)
-        prepare(lambda i: w_s[p, i], p, main_s, None, mul_s)
+    z_odd = flags[5] == 1
+
+    def below(p, a, n):
+        return jnp.where(z_odd, got_even[p, a : a + n], got_odd[p, a : a + n])
+
+    def above(p, a, n):
+        return jnp.where(z_odd, got_odd[p, a : a + n], got_even[p, a : a + n])
+
+    def window(p, first, last):
+        def rows(i):
+            zero = jnp.zeros((1, nx), f32)
+            return jnp.concatenate([below(p, 2 * i, 2), first(i), last(i), above(p, 3 * i, 3), zero], axis=0)
+
+        prepare(rows, p, main_s, None, mul_s)
 
     def own(p, _):
-        window(
-            p,
-            lambda a, n: got_low[p, a : a + n],
-            lambda a, n: got_high[p, a : a + n],
-            lambda i: own_high[p, 3 * i : 3 * i + 1],
-            lambda i: own_low[p, 2 * i + 1 : 2 * i + 2],
-        )
-        d_s[p] = jnp.zeros((8, nx), f32)
-        d_s[p, 0:2] = got_low[p, 18:20]
-        d_s[p, 3:4] = own_low[p, 19:20]
-        d_s[p, 4:6] = got_high[p, 27:29]
-        return 0
-
-    lax.fori_loop(0, ny, own, 0)
-    window(
-        ny,
-        lambda a, n: got_low[ny, a : a + n],
-        lambda a, n: got_high[ny, a : a + n],
-        lambda i: fy[i, 0:1],
-        lambda i: fy[i, nz - 1 : nz],
-    )
+        window(p, lambda i: own_high[p, 3 * i : 3 * i + 1], lambda i: own_low[p, 2 * i + 1 : 2 * i + 2])
+        zero = jnp.zeros((1, nx), f32)
+        d_s[p] = jnp.concatenate([below(p, 18, 2), zero, own_low[p, 19:20], above(p, 27, 2), zero, zero], axis=0)
+        return 0
+
+    lax.fori_loop(0, ny, own, 0, unroll=4)
+    window(ny, lambda i: fy[i, 0:1], lambda i: fy[i, nz - 1 : nz])
 
     group = 4
 
@@ -347,7 +341,7 @@
     s[y, OFF + nz - 1 : OFF + nz + 2] = rim[3:6]
 
 
-def rim_call(flags, got_low, got_high, own_low, own_high, fy, mat, src_a, src_b):
+def rim_call(flags, got_even, got_odd, own_low, own_high, fy, mat, src_a, src_b):
     ny, _, nx = own_low.shape
     rows = src_a.shape[1]
     return pl.pallas_call(
@@ -359,7 +353,6 @@
             jax.ShapeDtypeStruct((2, rows, nx), f32),
         ),
         scratch_shapes=[
-            pltpu.VMEM((ny + 1, 9, 8, nx), f32),
             pltpu.VMEM((ny, 8, nx), f32),
             pltpu.VMEM((ny + 1, 3, 48, nx), bf16),
             pltpu.VMEM((ny + 1, 3, 6, 2, 8, nx), f32),
@@ -368,7 +361,7 @@
         compiler_params=pltpu.CompilerParams(vmem_limit_bytes=16 * 2**20),
         cost_estimate=estimate(2),
         name="energy_rim",
-    )(flags, got_low, got_high, own_low, own_high, fy, mat, src_a, src_b)
+    )(flags, got_even, got_odd, own_low, own_high, fy, mat, src_a, src_b)
 
 
 def filter_block(s_s, d_s, n, z_edges, y_edges, finish):
@@ -562,11 +555,6 @@
     return lax.ppermute(value, axis, [(i + 1, i) for i in range(count - 1)])
 
 
-def to_upper(value, axis):
-    count = lax.axis_size(axis)
-    return lax.ppermute(value, axis, [(i, i + 1) for i in range(count - 1)])
-
-
 def swap(value, axis, start):
     pairs = []
     for i in range(start, lax.axis_size(axis) - 1, 2):
@@ -574,29 +562,41 @@
     return lax.ppermute(value, axis, pairs)
 
 
+def to_all(row, axis):
+    everyone = jnp.broadcast_to(row, (lax.axis_size(axis), row.shape[1]))
+    return lax.all_to_all(everyone, axis, 0, 0, tiled=True)
+
+
 def on_device(displacement, density, passive, solid, stiffness):
     ny, nz, nx = density.shape
     gy, gz = lax.axis_size("gy"), lax.axis_size("gz")
     iy, iz = lax.axis_index("gy"), lax.axis_index("gz")
-    flags = jnp.stack([iy > 0, iy < gy - 1, iz > 0, iz < gz - 1, iy % 2 == 1]).astype(jnp.int32)
+    flags = jnp.stack([iy > 0, iy < gy - 1, iz > 0, iz < gz - 1, iy % 2 == 1, iz % 2 == 1]).astype(jnp.int32)
+
+    disp_hbm = pltpu.with_memory_space_constraint(displacement, pltpu.HBM)
+    dens_hbm = pltpu.with_memory_space_constraint(density, pltpu.HBM)
+    stiff_hbm = pltpu.with_memory_space_constraint(stiffness, pltpu.HBM)
 
     fy = to_lower(displacement[:, 0], "gy")
-    src_a, mat, own_low, own_high = first_call(displacement, density, stiffness)
-
-    rim_low = jnp.pad(fy[:, nz - 2 :].reshape(1, 18, nx), ((0, 0), (0, 2), (0, 0)))
+    src_a, mat, own_low, own_high = first_call(disp_hbm, dens_hbm, stiff_hbm)
+
+    rim_low = jnp.pad(fy[:, nz - 2 :].reshape(1, 18, nx), ((0, 0), (0, 12), (0, 0)))
     rim_high = jnp.pad(fy[:, :3].reshape(1, 27, nx), ((0, 0), (0, 3), (0, 0)))
-    got_low = to_upper(jnp.concatenate([own_low, rim_low]), "gz")
-    got_high = to_lower(jnp.concatenate([own_high, rim_high]), "gz")
-    src_b = last_call(displacement, density, fy, mat)
-    rim, msg_even, msg_odd = rim_call(flags, got_low, got_high, own_low, own_high, fy, mat, src_a, src_b)
+    to_above = jnp.concatenate([own_low, rim_low])
+    to_below = jnp.concatenate([own_high, rim_high])
+    z_odd = iz % 2 == 1
+    z_got_odd = swap(jnp.where(z_odd, to_above, to_below), "gz", 1)
+    z_got_even = swap(jnp.where(z_odd, to_below, to_above), "gz", 0)
+    src_b = last_call(disp_hbm, dens_hbm, fy, mat)
+    rim, msg_even, msg_odd = rim_call(flags, z_got_even, z_got_odd, own_low, own_high, fy, mat, src_a, src_b)
 
     got_odd = swap(msg_odd, "gy", 1)
     got_even = swap(msg_even, "gy", 0)
     *inner, acc = inner_call(flags, src_a, src_b, rim, density, passive, solid)
     *outer, vols = outer_call(flags, src_a, src_b, rim, got_even, got_odd, density, passive, solid, acc)
 
-    everyone = jnp.broadcast_to(vols, (gz * gy, POINTS))
-    tables = lax.all_to_all(everyone, ("gz", "gy"), 0, 0, tiled=True)
+    vols = to_all(vols, "gz").sum(axis=0, keepdims=True)
+    tables = to_all(vols, "gy")
     new, logm = update_call(tables, inner, outer)
     return new, logm.reshape(())
 

time: 59.2 us -> 58.5 us (0.988)
  blocking collectives: 15.8 us -> 22.6 us
  local copies, waits for them, and re-layouts: 6.47 us -> 1.1 us
  starting transfers between devices: 9.9 us -> 5.39 us
  waiting for transfers between devices: 0.01 us -> 2.85 us
  other arithmetic: 0.74 us -> 0.08 us
    all_to_all x1 -> x2, blocking collectives: 15.8 us -> 22.6 us  [to_all(): return lax.all_to_all(everyone, axis, 0, 0, tiled=True)]
    unnamed x23 -> x7, local copies, waits for them, and re-layouts: 5.39 us -> 0.02 us
    ppermute x1 -> x0, starting transfers between devices: 3.04 us -> none  [to_upper(): return lax.ppermute(value, axis, [(i, i + 1) for i in range(count - 1)])]
    ppermute x2 -> x1, waiting for transfers between devices: 0.01 us -> 2.84 us  [to_lower(): return lax.ppermute(value, axis, [(i + 1, i) for i in range(count - 1)])]
    ppermute x2 -> x1, starting transfers between devices: 2.57 us -> 1.29 us  [to_lower(): return lax.ppermute(value, axis, [(i + 1, i) for i in range(count - 1)])]
    pallas_call x1, Pallas kernels: 3.47 us -> 2.48 us  [rim_call(): pl.pallas_call(rim_kernel, in_specs=[SMEM] + [VMEM] * 8, out_shape=(jax.S...]
    pallas_call x1, Pallas kernels: 3.08 us -> 3.85 us  [last_call(): pl.pallas_call(last_kernel, in_specs=[HBM, HBM, VMEM, VMEM], out_shape=ja...]
    concatenate x2 -> x0, other arithmetic: 0.74 us -> none  [the longest x1 0.72 us: on_device(): got_high = to_lower(jnp.concatenate([own_high, rim_high]), 'gz')]
  transfers between devices with their start and end apart: 5 -> 5, of which waited for: 0 -> 1; matrix products, arithmetic and copies ran while one was open for 0% -> 0% of each run, Pallas kernels for 28% -> 31%
where the time goes in v6:
time: 58.5 us; the launch traced here: 58.2 us
  Pallas kernels  25.4 us (43%)
  blocking collectives  22.6 us (39%)
  starting transfers between devices  5.39 us (9%)
  waiting for transfers between devices  2.85 us (5%)
  local copies, waits for them, and re-layouts  1.1 us (2%)
  between operations  0.84 us (1%)
    all_to_all x2, blocking collectives, to_all(): return lax.all_to_all(everyone, axis, 0, 0, tiled=True)  22.6 us
    pallas_call x1, Pallas kernels, inner_call(): pl.pallas_call(inner_kernel, in_specs=[SMEM] + [VMEM] * 6, out_shape=(fie...  9.65 us
    pallas_call x1, Pallas kernels, first_call(): pl.pallas_call(first_kernel, in_specs=[HBM, HBM, HBM], out_shape=(jax.Sha...  4.4 us
    ppermute x4, starting transfers between devices, swap(): return lax.ppermute(value, axis, pairs)  4.1 us
    pallas_call x1, Pallas kernels, outer_call(): pl.pallas_call(outer_kernel, in_specs=[SMEM] + [VMEM] * 9, out_shape=(fie...  3.98 us
    pallas_call x1, Pallas kernels, last_call(): pl.pallas_call(last_kernel, in_specs=[HBM, HBM, VMEM, VMEM], out_shape=ja...  3.85 us
    ppermute x1, waiting for transfers between devices, to_lower(): return lax.ppermute(value, axis, [(i + 1, i) for i in range(count - 1)])  2.84 us
    pallas_call x1, Pallas kernels, rim_call(): pl.pallas_call(rim_kernel, in_specs=[SMEM] + [VMEM] * 8, out_shape=(jax.S...  2.48 us
  transfers between devices with their start and end apart: 5, of which 1 were waited for; matrix products, arithmetic and copies ran while one was open for 0% of the time, Pallas kernels for 31%

profile of v6, /device:TPU:0, one launch (start us, length us, event | category | flops | bytes accessed | tf_op | source)
XLA Modules:
  0.0 58.2 jit_solution(11254835290898310452)
XLA Ops:
  0.6 0.9 %slice_bitcast_fusion = f32[9,32,128]{2,1,0:T(8,128)S(1)} fusion(f32[9,16,32,128]{3,2,1,0:T(8,128)} %disp.3), kind=kLoop, calls=%fused_computation.5 | loop fusion | bytes 294912 | tf_op jit(solution)/shard_map/squeeze | solution.py:580
  1.6 1.3 %collective-permute-start = (f32[9,32,128]{2,1,0:T(8,128)S(1)}, f32[9,32,128]{2,1,0:T(8,128)S(1)}, u32[]{:S(2)}, u32[]{:S(2)}) collective-permute-start(f32[9,32,128]{2,1,0:T(8,128)S(1)} %slice_bitcast_fusion), channel_id=1, source_target_pairs={{1,0},{2,1},{3,2},{4,3},{5,4},{6,5},{7,6},{9,8},{10,9},{11,10},{12... | collective-permute-start | bytes 442376 | tf_op jit(solution)/shard_map/ppermute | solution.py:555
  2.9 4.4 %energy_first.1 = (f32[8,48,128]{2,1,0:T(8,128)S(1)}, bf16[192,224]{1,0:T(8,128)(2,1)S(1)}, f32[16,30,128]{2,1,0:T(8,128)S(1)}, f32[16,30,128]{2,1,0:T(8,128)S(1)}) custom-call(f32[9,16,32,128]{3,2,1,0:T(8,128)} %disp.3, f32[16,32,128]{2,1,0:T(8,128)} %dens.7, f32[24,24]{1,0:T(8,128)} %stiff.1), custom_call_target="tpu_custom_call" | custom-call | flops 5000000000 | bytes 1048576 | tf_op jit(solution)/shard_map/energy_first/pallas_call | solution.py:217
  7.3 0.1 stack.27
  7.4 2.8 %collective-permute-done.fy = f32[9,32,128]{2,1,0:T(8,128)S(1)} collective-permute-done((f32[9,32,128]{2,1,0:T(8,128)S(1)}, f32[9,32,128]{2,1,0:T(8,128)S(1)}, u32[]{:S(2)}, u32[]{:S(2)}) %collective-permute-start) | collective-permute-done | bytes 147488 | tf_op jit(solution)/shard_map/ppermute | solution.py:555
  10.4 0.1 collective-permute-start.1
  10.4 0.7 %collective-permute-start.2 = (f32[17,30,128]{2,1,0:T(8,128)S(1)}, f32[17,30,128]{2,1,0:T(8,128)S(1)}, u32[]{:S(2)}, u32[]{:S(2)}) collective-permute-start(f32[17,30,128]{2,1,0:T(8,128)S(1)} %get-tuple-element.36), channel_id=1, source_target_pairs={{8,16},{16,8},{9,17},{17,9},{10,18},{18,10},{11,19},{19,11},{12,20... | collective-permute-start | bytes 783368 | tf_op jit(solution)/shard_map/ppermute | solution.py:562
  11.1 3.9 %energy_last.1.src_b = f32[8,48,128]{2,1,0:T(8,128)S(1)} custom-call(f32[9,16,32,128]{3,2,1,0:T(8,128)} %disp.3, f32[16,32,128]{2,1,0:T(8,128)} %dens.7, f32[9,32,128]{2,1,0:T(8,128)S(1)} %collective-permute-done.fy, bf16[192,224]{1,0:T(8,128)(2,1)S(1)} %get-tuple-element.20.mat), custom_call_target="tpu_custom_call" | custom-call | flops 5000000000 | bytes 1048576 | tf_op jit(solution)/shard_map/energy_last/pallas_call | solution.py:269
  15.0 0.0 collective-permute-done.1.got_even
  15.0 0.0 collective-permute-done.2.got_odd
  15.0 0.0 copy-start
  15.0 0.0 copy-start.1
  15.0 0.0 copy-start.2
  15.0 2.5 %energy_rim.1 = (f32[16,8,128]{2,1,0:T(8,128)S(1)}, f32[2,48,128]{2,1,0:T(8,128)S(1)}, f32[2,48,128]{2,1,0:T(8,128)S(1)}) custom-call(s32[6]{0:T(128)S(1)} %convert_element_type.7.flags, f32[17,30,128]{2,1,0:T(8,128)S(1)} %collective-permute-done.1.got_even, f32[17,30,128]{2,1,0:T(8,128)S(1)} %collective-permute-done.2.got_odd, ...), custom_call_target="tpu_custom_call" | custom-call | flops 2000000000 | bytes 1048576 | tf_op jit(solution)/shard_map/energy_rim/pallas_call | solution.py:347
  17.5 2.7 %collective-permute-start.3 = (f32[2,48,128]{2,1,0:T(8,128)S(1)}, f32[2,48,128]{2,1,0:T(8,128)S(1)}, u32[]{:S(2)}, u32[]{:S(2)}) collective-permute-start(f32[2,48,128]{2,1,0:T(8,128)S(1)} %get-tuple-element.24), channel_id=1, source_target_pairs={{0,1},{1,0},{2,3},{3,2},{4,5},{5,4},{6,7},{7,6},{8,9},{9,8},{10,11... | collective-permute-start | bytes 147464 | tf_op jit(solution)/shard_map/ppermute | solution.py:562
  20.2 0.7 %collective-permute-start.4 = (f32[2,48,128]{2,1,0:T(8,128)S(1)}, f32[2,48,128]{2,1,0:T(8,128)S(1)}, u32[]{:S(2)}, u32[]{:S(2)}) collective-permute-start(f32[2,48,128]{2,1,0:T(8,128)S(1)} %get-tuple-element.25), channel_id=1, source_target_pairs={{1,2},{2,1},{3,4},{4,3},{5,6},{6,5},{9,10},{10,9},{11,12},{12,11},... | collective-permute-start | bytes 147464 | tf_op jit(solution)/shard_map/ppermute | solution.py:562
  20.9 0.0 copy-done
  20.9 9.7 %filter_inner.1 = (f32[12,32,128]{2,1,0:T(8,128)S(1)}, f32[12,32,128]{2,1,0:T(8,128)S(1)}, f32[12,32,128]{2,1,0:T(8,128)S(1)}, f32[256,128]{1,0:T(8,128)S(1)}) custom-call(s32[6]{0:T(128)S(1)} %convert_element_type.7.flags, f32[8,48,128]{2,1,0:T(8,128)S(1)} %get-tuple-element.19.src_a, f32[8,48,128]{2,1,0:T(8,128)S(1)} %energy_last.1.src_b, ...), custom_call_target="tpu_custom_call" | custom-call | flops 8999999488 | bytes 1048576 | tf_op jit(solution)/shard_map/filter_inner/pallas_call | solution.py:460
  30.6 0.0 collective-permute-done.3.got_even
  30.6 0.0 collective-permute-done.4.got_odd
  30.6 4.0 %filter_outer.1 = (f32[4,32,128]{2,1,0:T(8,128)S(1)}, f32[4,32,128]{2,1,0:T(8,128)S(1)}, f32[4,32,128]{2,1,0:T(8,128)S(1)}, f32[1,256]{1,0:T(1,128)S(1)}) custom-call(s32[6]{0:T(128)S(1)} %convert_element_type.7.flags, f32[8,48,128]{2,1,0:T(8,128)S(1)} %get-tuple-element.19.src_a, f32[8,48,128]{2,1,0:T(8,128)S(1)} %energy_last.1.src_b, ...), custom_call_target="tpu_custom_call" | custom-call | flops 3000000000 | bytes 1048576 | tf_op jit(solution)/shard_map/filter_outer/pallas_call | solution.py:503
  34.6 9.6 %all_to_all.14 = f32[4,1,256]{2,1,0:T(1,128)S(1)} all-to-all(f32[4,1,256]{2,1,0:T(1,128)S(1)} %broadcast_in_dim.4), channel_id=1, replica_groups=mesh['gz'=4,'gy'=8] {'gz'}, dimensions={0} | all-to-all | bytes 8192 | tf_op jit(solution)/shard_map/all_to_all | solution.py:567
  44.3 12.9 %all_to_all.15 = f32[8,1,256]{2,1,0:T(1,128)S(1)} all-to-all(f32[8,1,256]{2,1,0:T(1,128)S(1)} %broadcast_in_dim.5), channel_id=1, replica_groups=mesh['gz'=4,'gy'=8] {'gy'}, dimensions={0} | all-to-all | bytes 16384 | tf_op jit(solution)/shard_map/all_to_all | solution.py:567
  57.2 1.0 %update.1 = (f32[16,32,128]{2,1,0:T(8,128)}, f32[1]{0:T(128)}) custom-call(f32[8,256]{1,0:T(8,128)S(1)} %bitcast.15, f32[12,32,128]{2,1,0:T(8,128)S(1)} %get-tuple-element.28.amp_i, f32[12,32,128]{2,1,0:T(8,128)S(1)} %get-tuple-element.29.low_i, f32[12,32,128]{2,1,0:T(8,128)S(1)} %get-tuple-element.30.high_i, f32[4,32,128]{2,1,0:T(8,128)S(1)} %get-tuple-element.31.amp_o, ...), custom_call_target="tpu_custom_call" | custom-call | flops 1000000000 | bytes 1048576 | tf_op jit(solution)/shard_map/update/pallas_call | solution.py:542
  (12 shorter events, 0.1 us)
Async XLA Ops:
  1.6 8.7 %collective-permute-start = (f32[9,32,128]{2,1,0:T(8,128)S(1)}, f32[9,32,128]{2,1,0:T(8,128)S(1)}, u32[]{:S(2)}, u32[]{:S(2)}) collective-permute-start(f32[9,32,128]{2,1,0:T(8,128)S(1)} %slice_bitcast_fusion), channel_id=1, source_target_pairs={{1,0},{2,1},{3,2},{4,3},{5,4},{6,5},{7,6},{9,8},{10,9},{11,10},{12... | collective-permute-start | bytes 442376 | tf_op jit(solution)/shard_map/ppermute | solution.py:555
  10.4 4.6 %collective-permute-start.1 = (f32[17,30,128]{2,1,0:T(8,128)S(1)}, f32[17,30,128]{2,1,0:T(8,128)S(1)}, u32[]{:S(2)}, u32[]{:S(2)}) collective-permute-start(f32[17,30,128]{2,1,0:T(8,128)S(1)} %get-tuple-element.37), channel_id=1, source_target_pairs={{0,8},{8,0},{16,24},{24,16},{1,9},{9,1},{17,25},{25,17},{2,10},{10... | collective-permute-start | bytes 783368 | tf_op jit(solution)/shard_map/ppermute | solution.py:562
  10.4 4.6 %collective-permute-start.2 = (f32[17,30,128]{2,1,0:T(8,128)S(1)}, f32[17,30,128]{2,1,0:T(8,128)S(1)}, u32[]{:S(2)}, u32[]{:S(2)}) collective-permute-start(f32[17,30,128]{2,1,0:T(8,128)S(1)} %get-tuple-element.36), channel_id=1, source_target_pairs={{8,16},{16,8},{9,17},{17,9},{10,18},{18,10},{11,19},{19,11},{12,20... | collective-permute-start | bytes 783368 | tf_op jit(solution)/shard_map/ppermute | solution.py:562
  15.0 5.9 %copy-start = (f32[16,32,128]{2,1,0:T(8,128)S(1)}, f32[16,32,128]{2,1,0:T(8,128)}, u32[]{:S(2)}) copy-start(f32[16,32,128]{2,1,0:T(8,128)} %dens.7) | copy-start | bytes 786436
  15.0 5.9 %copy-start.1 = (s32[16,32,128]{2,1,0:T(8,128)S(1)}, s32[16,32,128]{2,1,0:T(8,128)}, u32[]{:S(2)}) copy-start(s32[16,32,128]{2,1,0:T(8,128)} %passive.3) | copy-start | bytes 786436
  15.0 5.9 %copy-start.2 = (s32[16,32,128]{2,1,0:T(8,128)S(1)}, s32[16,32,128]{2,1,0:T(8,128)}, u32[]{:S(2)}) copy-start(s32[16,32,128]{2,1,0:T(8,128)} %solid.3) | copy-start | bytes 786436
  17.5 13.1 %collective-permute-start.3 = (f32[2,48,128]{2,1,0:T(8,128)S(1)}, f32[2,48,128]{2,1,0:T(8,128)S(1)}, u32[]{:S(2)}, u32[]{:S(2)}) collective-permute-start(f32[2,48,128]{2,1,0:T(8,128)S(1)} %get-tuple-element.24), channel_id=1, source_target_pairs={{0,1},{1,0},{2,3},{3,2},{4,5},{5,4},{6,7},{7,6},{8,9},{9,8},{10,11... | collective-permute-start | bytes 147464 | tf_op jit(solution)/shard_map/ppermute | solution.py:562
  20.2 10.4 %collective-permute-start.4 = (f32[2,48,128]{2,1,0:T(8,128)S(1)}, f32[2,48,128]{2,1,0:T(8,128)S(1)}, u32[]{:S(2)}, u32[]{:S(2)}) collective-permute-start(f32[2,48,128]{2,1,0:T(8,128)S(1)} %get-tuple-element.25), channel_id=1, source_target_pairs={{1,2},{2,1},{3,4},{4,3},{5,6},{6,5},{9,10},{10,9},{11,12},{12,11},... | collective-permute-start | bytes 147464 | tf_op jit(solution)/shard_map/ppermute | solution.py:562

commit v7 on v6

--- a/solution.py
+++ b/solution.py
@@ -1,4 +1,4 @@
-import functools
+import math
 
 import jax
 import jax.numpy as jnp
@@ -157,49 +157,36 @@
     out[y, OFF + nz :] = jnp.zeros((out.shape[1] - OFF - nz, nx), f32)
 
 
-def first_kernel(disp, dens, stiff, src, mat, own_low, own_high, disp_s, dens_s, stiff_s, main_s, ext_s, mul_s, sems):
-    _, ny, nz, nx = disp_s.shape
-    half = ny // 2
-    copy_k = pltpu.make_async_copy(stiff, stiff_s, sems.at[ny + 1])
-    copy_k.start()
-    copies = [pltpu.make_async_copy(disp.at[:, p], disp_s.at[:, p], sems.at[p]) for p in range(ny)]
-    for p in range(2):
-        copies[p].start()
-    copy_d = pltpu.make_async_copy(dens, dens_s, sems.at[ny])
-    copy_d.start()
-    for p in range(2, ny):
-        copies[p].start()
-    ext_s[...] = jnp.zeros_like(ext_s)
-    copy_k.wait()
+def load_kernel(disp, dens, stiff, face, disp_v, dens_v, mat, stiff_s, sems):
+    copies = [
+        pltpu.make_async_copy(stiff, stiff_s, sems.at[0]),
+        pltpu.make_async_copy(disp.at[:, 0], face, sems.at[1]),
+        pltpu.make_async_copy(disp, disp_v, sems.at[2]),
+        pltpu.make_async_copy(dens, dens_v, sems.at[3]),
+    ]
+    for copy in copies:
+        copy.start()
+    copies[0].wait()
     build_matrix(stiff_s[...], mat)
-    for p in range(2):
-        copies[p].wait()
-        prepare(lambda i: disp_s[i, p], p, main_s, ext_s, mul_s)
-    copy_d.wait()
-    for p in range(2, half + 1):
-        copies[p].wait()
-
-    def body(y, _):
-        put_row(src, y, energy_row(y, mat, main_s, ext_s, mul_s, dens_s[y]))
-        prepare(lambda i: disp_s[i, y + 2], y + 2, main_s, ext_s, mul_s)
-        return 0
-
-    lax.fori_loop(0, half - 1, body, 0)
-    put_row(src, half - 1, energy_row(half - 1, mat, main_s, ext_s, mul_s, dens_s[half - 1]))
-    for p in range(half + 1, ny):
-        copies[p].wait()
-
-    def pack(y, _):
-        for i in range(9):
-            own_low[y, 2 * i : 2 * i + 2] = disp_s[i, y, nz - 2 : nz]
-            own_high[y, 3 * i : 3 * i + 3] = disp_s[i, y, 0:3]
-        own_low[y, 18:20] = dens_s[y, nz - 2 : nz]
-        own_high[y, 27:29] = dens_s[y, 0:2]
-        own_low[y, 20:30] = jnp.zeros((10, nx), f32)
-        own_high[y, 29:30] = jnp.zeros((1, nx), f32)
-        return 0
-
-    lax.fori_loop(0, ny, pack, 0)
+    for copy in copies[1:]:
+        copy.wait()
+
+
+def load_call(disp, dens, stiff):
+    _, ny, nz, nx = disp.shape
+    return pl.pallas_call(
+        load_kernel,
+        in_specs=[HBM, HBM, HBM],
+        out_shape=(
+            jax.ShapeDtypeStruct((9, nz, nx), f32),
+            jax.ShapeDtypeStruct((9, ny, nz, nx), f32),
+            jax.ShapeDtypeStruct((ny, nz, nx), f32),
+            jax.ShapeDtypeStruct((192, 224), bf16),
+        ),
+        scratch_shapes=[pltpu.VMEM((24, 24), f32), pltpu.SemaphoreType.DMA((4,))],
+        compiler_params=pltpu.CompilerParams(vmem_limit_bytes=16 * 2**20),
+        name="load",
+    )(disp, dens, stiff)
 
 
 def energy_scratch(planes, nz, nx):
@@ -211,50 +198,68 @@
     ]
 
 
-def first_call(disp, dens, stiff):
+def first_kernel(disp, dens, mat, src, own_low, own_high, main_s, ext_s, mul_s):
+    _, ny, nz, nx = disp.shape
+    half = ny // 2
+    ext_s[...] = jnp.zeros_like(ext_s)
+    for p in range(2):
+        prepare(lambda i: disp[i, p], p, main_s, ext_s, mul_s)
+
+    def row(y):
+        put_row(src, y, energy_row(y, mat, main_s, ext_s, mul_s, dens[y]))
+
+    def body(y, _):
+        row(y)
+        prepare(lambda i: disp[i, y + 2], y + 2, main_s, ext_s, mul_s)
+        return 0
+
+    lax.fori_loop(0, half - 1, body, 0)
+    row(half - 1)
+
+    def pack(y, _):
+        for i in range(9):
+            own_low[y, 2 * i : 2 * i + 2] = disp[i, y, nz - 2 : nz]
+            own_high[y, 3 * i : 3 * i + 3] = disp[i, y, 0:3]
+        own_low[y, 18:20] = dens[y, nz - 2 : nz]
+        own_high[y, 27:29] = dens[y, 0:2]
+        own_low[y, 20:30] = jnp.zeros((10, nx), f32)
+        own_high[y, 29:30] = jnp.zeros((1, nx), f32)
+        return 0
+
+    lax.fori_loop(0, ny, pack, 0, unroll=2)
+
+
+def first_call(disp, dens, mat):
     _, ny, nz, nx = disp.shape
     half = ny // 2
     return pl.pallas_call(
         first_kernel,
-        in_specs=[HBM, HBM, HBM],
+        in_specs=[VMEM] * 3,
         out_shape=(
             jax.ShapeDtypeStruct((half, nz + 2 * OFF, nx), f32),
-            jax.ShapeDtypeStruct((192, 224), bf16),
             jax.ShapeDtypeStruct((ny, 30, nx), f32),
             jax.ShapeDtypeStruct((ny, 30, nx), f32),
         ),
-        scratch_shapes=[pltpu.VMEM((9, ny, nz, nx), f32), pltpu.VMEM((ny, nz, nx), f32), pltpu.VMEM((24, 24), f32)]
-        + energy_scratch(half + 1, nz, nx)
-        + [pltpu.SemaphoreType.DMA((ny + 2,))],
+        scratch_shapes=energy_scratch(half + 1, nz, nx),
         compiler_params=pltpu.CompilerParams(vmem_limit_bytes=24 * 2**20),
         cost_estimate=estimate(5),
         name="energy_first",
-    )(disp, dens, stiff)
-
-
-def last_kernel(disp, dens, fy, mat, src, disp_s, dens_s, main_s, ext_s, mul_s, sems):
-    _, half, nz, nx = disp_s.shape
-    copies = [pltpu.make_async_copy(disp.at[:, half + p], disp_s.at[:, p], sems.at[p]) for p in range(half)]
-    for p in range(2):
-        copies[p].start()
-    copy_d = pltpu.make_async_copy(dens.at[pl.ds(half, half)], dens_s, sems.at[half])
-    copy_d.start()
-    for p in range(2, half):
-        copies[p].start()
+    )(disp, dens, mat)
+
+
+def last_kernel(disp, dens, fy, mat, src, main_s, ext_s, mul_s):
+    _, ny, nz, nx = disp.shape
+    half = ny // 2
     ext_s[...] = jnp.zeros_like(ext_s)
     for p in range(2):
-        copies[p].wait()
-        prepare(lambda i: disp_s[i, p], p, main_s, ext_s, mul_s)
-    copy_d.wait()
-    for p in range(2, half):
-        copies[p].wait()
+        prepare(lambda i: disp[i, half + p], p, main_s, ext_s, mul_s)
 
     def row(y):
-        put_row(src, y, energy_row(y, mat, main_s, ext_s, mul_s, dens_s[y]))
+        put_row(src, y, energy_row(y, mat, main_s, ext_s, mul_s, dens[half + y]))
 
     def body(y, _):
         row(y)
-        prepare(lambda i: disp_s[i, y + 2], y + 2, main_s, ext_s, mul_s)
+        prepare(lambda i: disp[i, half + y + 2], y + 2, main_s, ext_s, mul_s)
         return 0
 
     lax.fori_loop(0, half - 2, body, 0)
@@ -268,11 +273,9 @@
     half = ny // 2
     return pl.pallas_call(
         last_kernel,
-        in_specs=[HBM, HBM, VMEM, VMEM],
+        in_specs=[VMEM] * 4,
         out_shape=jax.ShapeDtypeStruct((half, nz + 2 * OFF, nx), f32),
-        scratch_shapes=[pltpu.VMEM((9, half, nz, nx), f32), pltpu.VMEM((half, nz, nx), f32)]
-        + energy_scratch(half + 1, nz, nx)
-        + [pltpu.SemaphoreType.DMA((half + 1,))],
+        scratch_shapes=energy_scratch(half + 1, nz, nx),
         compiler_params=pltpu.CompilerParams(vmem_limit_bytes=24 * 2**20),
         cost_estimate=estimate(5),
         name="energy_last",
@@ -364,7 +367,7 @@
     )(flags, got_even, got_odd, own_low, own_high, fy, mat, src_a, src_b)
 
 
-def filter_block(s_s, d_s, n, z_edges, y_edges, finish):
+def filter_block(s_s, d_s, n, z_edges, y_edges, finish, unroll):
     rows, nx = s_s.shape[1:]
     nz = rows - 2 * OFF
     alpha, beta, gamma, delta, eps = filter_weights()
@@ -389,50 +392,62 @@
         finish(j, p3[OFF : OFF + nz])
         return 0
 
-    lax.fori_loop(0, n - 2, second, 0)
-    lax.fori_loop(0, n - 4, third, 0)
+    lax.fori_loop(0, n - 2, second, 0, unroll=unroll)
+    lax.fori_loop(0, n - 4, third, 0, unroll=unroll)
 
 
 def limits(p3, d, pas, sol):
     amp = jnp.sqrt(jnp.maximum(-p3 * d, 0.0))
     lower = jnp.maximum(d - move_limit, floor_density)
     upper = jnp.minimum(d + move_limit, 1.0)
-    low = jnp.where(sol, 1.0, jnp.where(pas, floor_density, lower))
-    high = jnp.where(sol, 1.0, jnp.where(pas, floor_density, upper))
-    return amp, low, high
-
-
-def table(n, nz, nx, amp, low, high, dens, start, acc_s):
-    groups = POINTS // 8
-    half = groups // 2
-    sub = lax.broadcasted_iota(jnp.int32, (8, nx), 0)
-    for part in range(2):
-        scale = []
-        for g in range(half):
-            k = sub + 8 * (part * half + g)
-            mid = -bracket_end + (2.0 * bracket_end / POINTS) * k.astype(f32)
-            scale.append(jnp.exp(-0.5 * mid))
+    low, high, now = (jnp.where(sol, 1.0, jnp.where(pas, floor_density, v)) for v in (lower, upper, d))
+    return amp, low, high, now
+
+
+FINE = 16
+COARSE = POINTS // FINE
+
+
+def table(n, nz, nx, amp, low, high, now, fine_s, vol, tgt, start):
+    spacing = 2.0 * bracket_end / POINTS
+
+    def fine(j, _):
+        a = amp[j]
+        for f in range(FINE):
+            fine_s[f, j] = a * math.exp(-0.5 * spacing * f)
+        return 0
+
+    lax.fori_loop(0, n, fine, 0)
+    pair = 2
+    for first in range(0, COARSE, pair):
+        inverse = [math.exp(0.5 * (-bracket_end + spacing * FINE * i)) for i in range(first, first + pair)]
 
         def volume(j, acc):
             acc = list(acc)
-            for z in range(nz):
-                a = jnp.broadcast_to(amp[j, z : z + 1], (8, nx))
-                lo = jnp.broadcast_to(low[j, z : z + 1], (8, nx))
-                hi = jnp.broadcast_to(high[j, z : z + 1], (8, nx))
-                for g in range(half):
-                    t = a * scale[g]
-                    if part == 0 and g == 0:
-                        t = jnp.where(sub == 0, jnp.broadcast_to(dens(j, z), (8, nx)), t)
-                    acc[g] = acc[g] + jnp.minimum(jnp.maximum(t, lo), hi)
+            for w in range(nz // 8):
+                at = slice(8 * w, 8 * w + 8)
+                lo, hi, d = low[j, at], high[j, at], now[j, at]
+                los, his = [lo * c for c in inverse], [hi * c for c in inverse]
+                for i, c in enumerate(inverse):
+                    acc[pair * FINE + i] = acc[pair * FINE + i] + d * c
+                for f in range(FINE):
+                    t = fine_s[f, j, at]
+                    for i in range(pair):
+                        acc[i * FINE + f] = acc[i * FINE + f] + jnp.minimum(jnp.maximum(t, los[i]), his[i])
             return tuple(acc)
 
-        at = [slice(8 * (part * half + g), 8 * (part * half + g) + 8) for g in range(half)]
-        acc = lax.fori_loop(0, n, volume, tuple(start(at[g]) for g in range(half)))
-        for g in range(half):
-            acc_s[at[g]] = acc[g]
-
-
-def inner_kernel(flags, src_a, src_b, rim, dens, passive, solid, amp, low, high, acc, s_s, d_s):
+        places = [(vol, 8 * (first * FINE + e)) for e in range(pair * FINE)]
+        places += [(tgt, 8 * (first + i)) for i in range(pair)]
+        if start is None:
+            begin = tuple(jnp.zeros((8, nx), f32) for _ in places)
+        else:
+            begin = tuple((start[0] if ref is vol else start[1])[at : at + 8] for ref, at in places)
+        acc = lax.fori_loop(0, n, volume, begin)
+        for (ref, at), value in zip(places, acc):
+            ref[at : at + 8] = value
+
+
+def inner_kernel(flags, src_a, src_b, rim, dens, passive, solid, amp, low, high, vol, tgt, s_s, d_s, now_s, fine_s):
     ny, nz, nx = dens.shape
     half = ny // 2
     s_s[0:half] = src_a[...]
@@ -442,16 +457,14 @@
         put_rim(s_s, y, rim[y], nz)
         return 0
 
-    lax.fori_loop(0, ny, fix, 0)
+    lax.fori_loop(0, ny, fix, 0, unroll=4)
 
     def finish(j, p3):
         y = j + 2
-        amp[j], low[j], high[j] = limits(p3, dens[y], passive[y] == 1, solid[y] == 1)
-
-    filter_block(s_s, d_s, ny, (flags[2], flags[3]), None, finish)
-    table(
-        ny - 4, nz, nx, amp, low, high, lambda j, z: dens[j + 2, z : z + 1], lambda at: jnp.zeros((8, nx), f32), acc
-    )
+        amp[j], low[j], high[j], now_s[j] = limits(p3, dens[y], passive[y] == 1, solid[y] == 1)
+
+    filter_block(s_s, d_s, ny, (flags[2], flags[3]), None, finish, 2)
+    table(ny - 4, nz, nx, amp, low, high, now_s, fine_s, vol, tgt, None)
 
 
 def inner_call(flags, src_a, src_b, rim, dens, passive, solid):
@@ -460,16 +473,28 @@
     return pl.pallas_call(
         inner_kernel,
         in_specs=[SMEM] + [VMEM] * 6,
-        out_shape=(field, field, field, jax.ShapeDtypeStruct((POINTS, nx), f32)),
-        scratch_shapes=[pltpu.VMEM((ny, nz + 2 * OFF, nx), f32), pltpu.VMEM((ny - 2, nz + 2 * OFF, nx), f32)],
-        compiler_params=pltpu.CompilerParams(vmem_limit_bytes=16 * 2**20),
+        out_shape=(
+            field,
+            field,
+            field,
+            jax.ShapeDtypeStruct((8 * POINTS, nx), f32),
+            jax.ShapeDtypeStruct((8 * COARSE, nx), f32),
+        ),
+        scratch_shapes=[
+            pltpu.VMEM((ny, nz + 2 * OFF, nx), f32),
+            pltpu.VMEM((ny - 2, nz + 2 * OFF, nx), f32),
+            pltpu.VMEM((ny - 4, nz, nx), f32),
+            pltpu.VMEM((FINE, ny - 4, nz, nx), f32),
+        ],
+        compiler_params=pltpu.CompilerParams(vmem_limit_bytes=24 * 2**20),
         cost_estimate=estimate(9),
         name="filter_inner",
     )(flags, src_a, src_b, rim, dens, passive, solid)
 
 
 def outer_kernel(
-    flags, src_a, src_b, rim, got_even, got_odd, dens, passive, solid, acc, amp, low, high, vols, s_s, d_s, dens_s, acc_s
+    flags, src_a, src_b, rim, got_even, got_odd, dens, passive, solid, vol_i, tgt_i,
+    amp, low, high, excess, s_s, d_s, now_s, fine_s, vol, tgt,
 ):
     ny, nz, nx = dens.shape
     half = ny // 2
@@ -487,40 +512,51 @@
         def finish(j, p3):
             y = y0 + j
             at = 2 * b + j
-            amp[at], low[at], high[at] = limits(p3, dens[y], passive[y] == 1, solid[y] == 1)
-            dens_s[at] = dens[y]
+            amp[at], low[at], high[at], now_s[at] = limits(p3, dens[y], passive[y] == 1, solid[y] == 1)
 
         edges = (flags[0], 1) if b == 0 else (1, flags[1])
-        filter_block(s_s.at[b], d_s, 6, (flags[2], flags[3]), edges, finish)
-    table(4, nz, nx, amp, low, high, lambda j, z: dens_s[j, z : z + 1], lambda at: acc[at], acc_s)
-    vols[...] = jnp.sum(jnp.transpose(acc_s[...]), axis=0, keepdims=True)
-
-
-def outer_call(flags, src_a, src_b, rim, got_even, got_odd, dens, passive, solid, acc):
+        filter_block(s_s.at[b], d_s.at[b], 6, (flags[2], flags[3]), edges, finish, True)
+    table(4, nz, nx, amp, low, high, now_s, fine_s, vol, tgt, (vol_i, tgt_i))
+
+    def lanes(ref, count):
+        total = ref[pl.ds(0, count, stride=8), :]
+        for s in range(1, 8):
+            total = total + ref[pl.ds(s, count, stride=8), :]
+        return total
+
+    volumes, targets = lanes(vol, POINTS), lanes(tgt, COARSE)
+    over = [volumes[FINE * i : FINE * i + FINE] - targets[i : i + 1] for i in range(COARSE)]
+    excess[...] = jnp.sum(jnp.transpose(jnp.concatenate(over, axis=0)), axis=0, keepdims=True)
+
+
+def outer_call(flags, src_a, src_b, rim, got_even, got_odd, dens, passive, solid, vol_i, tgt_i):
     ny, nz, nx = dens.shape
     rows = nz + 2 * OFF
     field = jax.ShapeDtypeStruct((4, nz, nx), f32)
     return pl.pallas_call(
         outer_kernel,
-        in_specs=[SMEM] + [VMEM] * 9,
+        in_specs=[SMEM] + [VMEM] * 10,
         out_shape=(field, field, field, jax.ShapeDtypeStruct((1, POINTS), f32)),
         scratch_shapes=[
             pltpu.VMEM((2, 6, rows, nx), f32),
-            pltpu.VMEM((4, rows, nx), f32),
+            pltpu.VMEM((2, 4, rows, nx), f32),
             pltpu.VMEM((4, nz, nx), f32),
-            pltpu.VMEM((POINTS, nx), f32),
+            pltpu.VMEM((FINE, 4, nz, nx), f32),
+            pltpu.VMEM((8 * POINTS, nx), f32),
+            pltpu.VMEM((8 * COARSE, nx), f32),
         ],
         compiler_params=pltpu.CompilerParams(vmem_limit_bytes=16 * 2**20),
         cost_estimate=estimate(3),
         name="filter_outer",
-    )(flags, src_a, src_b, rim, got_even, got_odd, dens, passive, solid, acc)
+    )(flags, src_a, src_b, rim, got_even, got_odd, dens, passive, solid, vol_i, tgt_i)
 
 
 def update_kernel(tables, amp_i, low_i, high_i, amp_o, low_o, high_o, new, logm):
     inner = amp_i.shape[0]
     nx = amp_i.shape[-1]
     total = jnp.sum(tables[...], axis=0, keepdims=True)
-    above = jnp.where(total > total[:, 0:1], 1.0, 0.0)
+    lane = lax.broadcasted_iota(jnp.int32, total.shape, 1)
+    above = jnp.where((total > 0.0) & (lane > 0), 1.0, 0.0)
     middle = -bracket_end + (2.0 * bracket_end / POINTS) * (jnp.sum(above) + 0.5)
     logm[0] = middle
     scale = jnp.exp(jnp.full((1, nx), -0.5 * middle, f32))
@@ -562,11 +598,6 @@
     return lax.ppermute(value, axis, pairs)
 
 
-def to_all(row, axis):
-    everyone = jnp.broadcast_to(row, (lax.axis_size(axis), row.shape[1]))
-    return lax.all_to_all(everyone, axis, 0, 0, tiled=True)
-
-
 def on_device(displacement, density, passive, solid, stiffness):
     ny, nz, nx = density.shape
     gy, gz = lax.axis_size("gy"), lax.axis_size("gz")
@@ -577,8 +608,9 @@
     dens_hbm = pltpu.with_memory_space_constraint(density, pltpu.HBM)
     stiff_hbm = pltpu.with_memory_space_constraint(stiffness, pltpu.HBM)
 
-    fy = to_lower(displacement[:, 0], "gy")
-    src_a, mat, own_low, own_high = first_call(disp_hbm, dens_hbm, stiff_hbm)
+    face, disp, dens, mat = load_call(disp_hbm, dens_hbm, stiff_hbm)
+    fy = to_lower(face, "gy")
+    src_a, own_low, own_high = first_call(disp, dens, mat)
 
     rim_low = jnp.pad(fy[:, nz - 2 :].reshape(1, 18, nx), ((0, 0), (0, 12), (0, 0)))
     rim_high = jnp.pad(fy[:, :3].reshape(1, 27, nx), ((0, 0), (0, 3), (0, 0)))
@@ -587,16 +619,16 @@
     z_odd = iz % 2 == 1
     z_got_odd = swap(jnp.where(z_odd, to_above, to_below), "gz", 1)
     z_got_even = swap(jnp.where(z_odd, to_below, to_above), "gz", 0)
-    src_b = last_call(disp_hbm, dens_hbm, fy, mat)
+    src_b = last_call(disp, dens, fy, mat)
     rim, msg_even, msg_odd = rim_call(flags, z_got_even, z_got_odd, own_low, own_high, fy, mat, src_a, src_b)
 
     got_odd = swap(msg_odd, "gy", 1)
     got_even = swap(msg_even, "gy", 0)
-    *inner, acc = inner_call(flags, src_a, src_b, rim, density, passive, solid)
-    *outer, vols = outer_call(flags, src_a, src_b, rim, got_even, got_odd, density, passive, solid, acc)
-
-    vols = to_all(vols, "gz").sum(axis=0, keepdims=True)
-    tables = to_all(vols, "gy")
+    *inner, vol, tgt = inner_call(flags, src_a, src_b, rim, dens, passive, solid)
+    *outer, excess = outer_call(flags, src_a, src_b, rim, got_even, got_odd, dens, passive, solid, vol, tgt)
+
+    everyone = jnp.broadcast_to(excess, (gz * gy, POINTS))
+    tables = lax.all_to_all(everyone, ("gz", "gy"), 0, 0, tiled=True)
     new, logm = update_call(tables, inner, outer)
     return new, logm.reshape(())
 

time: 58.5 us -> 52.1 us (0.89)
  blocking collectives: 22.6 us -> 18.2 us
  Pallas kernels: 25.4 us -> 22.7 us
  waiting for transfers between devices: 2.85 us -> 3.72 us
    all_to_all x2 -> x1, blocking collectives: 22.6 us -> 18.2 us  [on_device(): tables = lax.all_to_all(everyone, ('gz', 'gy'), 0, 0, tiled=True)]
    pallas_call x3 -> x4, Pallas kernels: 12.2 us -> 10.6 us  [the longest x1 3.32 us: outer_call(): pl.pallas_call(outer_kernel, in_specs=[SMEM] + [VMEM] * 10, out_shape=(fi...]
    squeeze x1 -> x0, local copies, waits for them, and re-layouts: 0.93 us -> none  [on_device(): fy = to_lower(displacement[:, 0], 'gy')]
    pallas_call x1, Pallas kernels: 9.65 us -> 8.73 us  [inner_call(): pl.pallas_call(inner_kernel, in_specs=[SMEM] + [VMEM] * 6, out_shape=(fie...]
    ppermute x1, waiting for transfers between devices: 2.84 us -> 3.71 us  [to_lower(): return lax.ppermute(value, axis, [(i + 1, i) for i in range(count - 1)])]
    unnamed x7 -> x9, local copies, waits for them, and re-layouts: 0.02 us -> 0.69 us
  transfers between devices with their start and end apart: 5 -> 5, of which waited for: 1 -> 1; matrix products, arithmetic and copies ran while one was open for 0% -> 0% of each run, Pallas kernels for 31% -> 27%
where the time goes in v7:
time: 52.1 us; the launch traced here: 51.9 us
  Pallas kernels  22.7 us (44%)
  blocking collectives  18.2 us (35%)
  starting transfers between devices  5.52 us (11%)
  waiting for transfers between devices  3.72 us (7%)
  local copies, waits for them, and re-layouts  0.86 us (2%)
  between operations  0.83 us (2%)
    all_to_all x1, blocking collectives, on_device(): tables = lax.all_to_all(everyone, ('gz', 'gy'), 0, 0, tiled=True)  18.2 us
    pallas_call x1, Pallas kernels, inner_call(): pl.pallas_call(inner_kernel, in_specs=[SMEM] + [VMEM] * 6, out_shape=(fie...  8.73 us
    ppermute x4, starting transfers between devices, swap(): return lax.ppermute(value, axis, pairs)  4.22 us
    ppermute x1, waiting for transfers between devices, to_lower(): return lax.ppermute(value, axis, [(i + 1, i) for i in range(count - 1)])  3.71 us
    pallas_call x1, Pallas kernels, outer_call(): pl.pallas_call(outer_kernel, in_specs=[SMEM] + [VMEM] * 10, out_shape=(fi...  3.32 us
    pallas_call x1, Pallas kernels, first_call(): pl.pallas_call(first_kernel, in_specs=[VMEM] * 3, out_shape=(jax.ShapeDty...  2.87 us
    pallas_call x1, Pallas kernels, last_call(): pl.pallas_call(last_kernel, in_specs=[VMEM] * 4, out_shape=jax.ShapeDtype...  2.55 us
    pallas_call x1, Pallas kernels, rim_call(): pl.pallas_call(rim_kernel, in_specs=[SMEM] + [VMEM] * 8, out_shape=(jax.S...  2.48 us
  transfers between devices with their start and end apart: 5, of which 1 were waited for; matrix products, arithmetic and copies ran while one was open for 0% of the time, Pallas kernels for 27%

profile of v7, /device:TPU:0, one launch (start us, length us, event | category | flops | bytes accessed | tf_op | source)
XLA Modules:
  0.0 51.9 jit_solution(16430026124381512156)
XLA Ops:
  0.6 1.8 %load.1 = (f32[9,32,128]{2,1,0:T(8,128)S(1)}, f32[9,16,32,128]{3,2,1,0:T(8,128)S(1)}, f32[16,32,128]{2,1,0:T(8,128)S(1)}, bf16[192,224]{1,0:T(8,128)(2,1)S(1)}) custom-call(f32[9,16,32,128]{3,2,1,0:T(8,128)} %disp.1, f32[16,32,128]{2,1,0:T(8,128)} %dens.1, f32[24,24]{1,0:T(8,128)} %stiff.1), custom_call_target="tpu_custom_call" | custom-call | tf_op jit(solution)/shard_map/load/pallas_call | solution.py:177
  2.4 1.3 %collective-permute-start = (f32[9,32,128]{2,1,0:T(8,128)S(1)}, f32[9,32,128]{2,1,0:T(8,128)S(1)}, u32[]{:S(2)}, u32[]{:S(2)}) collective-permute-start(f32[9,32,128]{2,1,0:T(8,128)S(1)} %get-tuple-element.27), channel_id=1, source_target_pairs={{1,0},{2,1},{3,2},{4,3},{5,4},{6,5},{7,6},{9,8},{10,9},{11,10},{12... | collective-permute-start | bytes 442376 | tf_op jit(solution)/shard_map/ppermute | solution.py:591
  3.7 2.9 %energy_first.1 = (f32[8,48,128]{2,1,0:T(8,128)S(1)}, f32[16,30,128]{2,1,0:T(8,128)S(1)}, f32[16,30,128]{2,1,0:T(8,128)S(1)}) custom-call(f32[9,16,32,128]{3,2,1,0:T(8,128)S(1)} %get-tuple-element.23.disp, f32[16,32,128]{2,1,0:T(8,128)S(1)} %get-tuple-element.24.dens, bf16[192,224]{1,0:T(8,128)(2,1)S(1)} %get-tuple-element.25.mat), custom_call_target="tpu_custom_call" | custom-call | flops 5000000000 | bytes 1048576 | tf_op jit(solution)/shard_map/energy_first/pallas_call | solution.py:235
  6.6 0.0 copy-start.2
  6.6 0.7 %copy-done.2 = f32[8,48,128]{2,1,0:T(8,128)} copy-done((f32[8,48,128]{2,1,0:T(8,128)}, f32[8,48,128]{2,1,0:T(8,128)S(1)}, u32[]{:S(2)}) %copy-start.2) | copy-done | bytes 196632
  7.3 0.1 stack.27
  7.4 3.7 %collective-permute-done.fy = f32[9,32,128]{2,1,0:T(8,128)S(1)} collective-permute-done((f32[9,32,128]{2,1,0:T(8,128)S(1)}, f32[9,32,128]{2,1,0:T(8,128)S(1)}, u32[]{:S(2)}, u32[]{:S(2)}) %collective-permute-start) | collective-permute-done | bytes 147488 | tf_op jit(solution)/shard_map/ppermute | solution.py:591
  11.2 0.1 collective-permute-start.1
  11.3 0.0 copy-start.3
  11.3 0.8 %collective-permute-start.2 = (f32[17,30,128]{2,1,0:T(8,128)S(1)}, f32[17,30,128]{2,1,0:T(8,128)S(1)}, u32[]{:S(2)}, u32[]{:S(2)}) collective-permute-start(f32[17,30,128]{2,1,0:T(8,128)S(1)} %get-tuple-element.44), channel_id=1, source_target_pairs={{8,16},{16,8},{9,17},{17,9},{10,18},{18,10},{11,19},{19,11},{12,20... | collective-permute-start | bytes 783368 | tf_op jit(solution)/shard_map/ppermute | solution.py:598
  12.2 2.6 %energy_last.1.src_b = f32[8,48,128]{2,1,0:T(8,128)S(1)} custom-call(f32[9,16,32,128]{3,2,1,0:T(8,128)S(1)} %get-tuple-element.23.disp, f32[16,32,128]{2,1,0:T(8,128)S(1)} %get-tuple-element.24.dens, f32[9,32,128]{2,1,0:T(8,128)S(1)} %collective-permute-done.fy, bf16[192,224]{1,0:T(8,128)(2,1)S(1)} %get-tuple-element.25.mat), custom_call_target="tpu_custom_call" | custom-call | flops 5000000000 | bytes 1048576 | tf_op jit(solution)/shard_map/energy_last/pallas_call | solution.py:274
  14.7 0.0 collective-permute-done.1.got_even
  14.7 0.0 collective-permute-done.2.got_odd
  14.7 0.0 copy-start
  14.8 0.0 copy-start.1
  14.8 2.5 %energy_rim.1 = (f32[16,8,128]{2,1,0:T(8,128)S(1)}, f32[2,48,128]{2,1,0:T(8,128)S(1)}, f32[2,48,128]{2,1,0:T(8,128)S(1)}) custom-call(s32[6]{0:T(128)S(1)} %convert_element_type.7.flags, f32[17,30,128]{2,1,0:T(8,128)S(1)} %collective-permute-done.1.got_even, f32[17,30,128]{2,1,0:T(8,128)S(1)} %collective-permute-done.2.got_odd, ...), custom_call_target="tpu_custom_call" | custom-call | flops 2000000000 | bytes 1048576 | tf_op jit(solution)/shard_map/energy_rim/pallas_call | solution.py:350
  17.3 2.7 %collective-permute-start.3 = (f32[2,48,128]{2,1,0:T(8,128)S(1)}, f32[2,48,128]{2,1,0:T(8,128)S(1)}, u32[]{:S(2)}, u32[]{:S(2)}) collective-permute-start(f32[2,48,128]{2,1,0:T(8,128)S(1)} %get-tuple-element.31), channel_id=1, source_target_pairs={{0,1},{1,0},{2,3},{3,2},{4,5},{5,4},{6,7},{7,6},{8,9},{9,8},{10,11... | collective-permute-start | bytes 147464 | tf_op jit(solution)/shard_map/ppermute | solution.py:598
  19.9 0.7 %collective-permute-start.4 = (f32[2,48,128]{2,1,0:T(8,128)S(1)}, f32[2,48,128]{2,1,0:T(8,128)S(1)}, u32[]{:S(2)}, u32[]{:S(2)}) collective-permute-start(f32[2,48,128]{2,1,0:T(8,128)S(1)} %get-tuple-element.32), channel_id=1, source_target_pairs={{1,2},{2,1},{3,4},{4,3},{5,6},{6,5},{9,10},{10,9},{11,12},{12,11},... | collective-permute-start | bytes 147464 | tf_op jit(solution)/shard_map/ppermute | solution.py:598
  20.6 8.7 %filter_inner.1 = (f32[12,32,128]{2,1,0:T(8,128)S(1)}, f32[12,32,128]{2,1,0:T(8,128)S(1)}, f32[12,32,128]{2,1,0:T(8,128)S(1)}, f32[2048,128]{1,0:T(8,128)S(1)}, f32[128,128]{1,0:T(8,128)S(1)}) custom-call(s32[6]{0:T(128)S(1)} %convert_element_type.7.flags, f32[8,48,128]{2,1,0:T(8,128)S(1)} %copy-done.3, f32[8,48,128]{2,1,0:T(8,128)S(1)} %energy_last.1.src_b, ...), custom_call_target="tpu_custom_call" | custom-call | flops 8999999488 | bytes 1048576 | tf_op jit(solution)/shard_map/filter_inner/pallas_call | solution.py:473
  29.4 0.0 collective-permute-done.3.got_even
  29.4 0.0 collective-permute-done.4.got_odd
  29.4 3.3 %filter_outer.1 = (f32[4,32,128]{2,1,0:T(8,128)S(1)}, f32[4,32,128]{2,1,0:T(8,128)S(1)}, f32[4,32,128]{2,1,0:T(8,128)S(1)}, f32[1,256]{1,0:T(1,128)S(1)}) custom-call(s32[6]{0:T(128)S(1)} %convert_element_type.7.flags, f32[8,48,128]{2,1,0:T(8,128)S(1)} %copy-done.3, f32[8,48,128]{2,1,0:T(8,128)S(1)} %energy_last.1.src_b, ...), custom_call_target="tpu_custom_call" | custom-call | flops 3000000000 | bytes 1048576 | tf_op jit(solution)/shard_map/filter_outer/pallas_call | solution.py:536
  32.7 18.2 %all_to_all.8 = f32[32,1,256]{2,1,0:T(1,128)S(1)} all-to-all(f32[32,1,256]{2,1,0:T(1,128)S(1)} %broadcast_in_dim.2), channel_id=1, replica_groups=mesh['gz'=4,'gy'=8] {'gz','gy'}, dimensions={0} | all-to-all | bytes 65536 | tf_op jit(solution)/shard_map/all_to_all | solution.py:631
  50.9 0.9 %update.1 = (f32[16,32,128]{2,1,0:T(8,128)}, f32[1]{0:T(128)}) custom-call(f32[32,256]{1,0:T(8,128)S(1)} %bitcast.11, f32[12,32,128]{2,1,0:T(8,128)S(1)} %get-tuple-element.36.amp_i, f32[12,32,128]{2,1,0:T(8,128)S(1)} %get-tuple-element.37.low_i, f32[12,32,128]{2,1,0:T(8,128)S(1)} %get-tuple-element.38.high_i, f32[4,32,128]{2,1,0:T(8,128)S(1)} %get-tuple-element.39.amp_o, ...), custom_call_target="tpu_custom_call" | custom-call | flops 1000000000 | bytes 1048576 | tf_op jit(solution)/shard_map/update/pallas_call | solution.py:578
  (11 shorter events, 0.1 us)
Async XLA Ops:
  2.4 8.7 %collective-permute-start = (f32[9,32,128]{2,1,0:T(8,128)S(1)}, f32[9,32,128]{2,1,0:T(8,128)S(1)}, u32[]{:S(2)}, u32[]{:S(2)}) collective-permute-start(f32[9,32,128]{2,1,0:T(8,128)S(1)} %get-tuple-element.27), channel_id=1, source_target_pairs={{1,0},{2,1},{3,2},{4,3},{5,4},{6,5},{7,6},{9,8},{10,9},{11,10},{12... | collective-permute-start | bytes 442376 | tf_op jit(solution)/shard_map/ppermute | solution.py:591
  6.6 0.7 %copy-start.2 = (f32[8,48,128]{2,1,0:T(8,128)}, f32[8,48,128]{2,1,0:T(8,128)S(1)}, u32[]{:S(2)}) copy-start(f32[8,48,128]{2,1,0:T(8,128)S(1)} %get-tuple-element.26.src_a) | copy-start | bytes 589828
  11.2 3.5 %collective-permute-start.1 = (f32[17,30,128]{2,1,0:T(8,128)S(1)}, f32[17,30,128]{2,1,0:T(8,128)S(1)}, u32[]{:S(2)}, u32[]{:S(2)}) collective-permute-start(f32[17,30,128]{2,1,0:T(8,128)S(1)} %get-tuple-element.45), channel_id=1, source_target_pairs={{0,8},{8,0},{16,24},{24,16},{1,9},{9,1},{17,25},{25,17},{2,10},{10... | collective-permute-start | bytes 783368 | tf_op jit(solution)/shard_map/ppermute | solution.py:598
  11.3 3.4 %copy-start.3 = (f32[8,48,128]{2,1,0:T(8,128)S(1)}, f32[8,48,128]{2,1,0:T(8,128)}, u32[]{:S(2)}) copy-start(f32[8,48,128]{2,1,0:T(8,128)} %copy-done.2) | copy-start | bytes 589828
  11.3 3.4 %collective-permute-start.2 = (f32[17,30,128]{2,1,0:T(8,128)S(1)}, f32[17,30,128]{2,1,0:T(8,128)S(1)}, u32[]{:S(2)}, u32[]{:S(2)}) collective-permute-start(f32[17,30,128]{2,1,0:T(8,128)S(1)} %get-tuple-element.44), channel_id=1, source_target_pairs={{8,16},{16,8},{9,17},{17,9},{10,18},{18,10},{11,19},{19,11},{12,20... | collective-permute-start | bytes 783368 | tf_op jit(solution)/shard_map/ppermute | solution.py:598
  14.7 5.9 %copy-start = (s32[16,32,128]{2,1,0:T(8,128)S(1)}, s32[16,32,128]{2,1,0:T(8,128)}, u32[]{:S(2)}) copy-start(s32[16,32,128]{2,1,0:T(8,128)} %passive.3) | copy-start | bytes 786436
  14.8 5.9 %copy-start.1 = (s32[16,32,128]{2,1,0:T(8,128)S(1)}, s32[16,32,128]{2,1,0:T(8,128)}, u32[]{:S(2)}) copy-start(s32[16,32,128]{2,1,0:T(8,128)} %solid.3) | copy-start | bytes 786436
  17.3 12.1 %collective-permute-start.3 = (f32[2,48,128]{2,1,0:T(8,128)S(1)}, f32[2,48,128]{2,1,0:T(8,128)S(1)}, u32[]{:S(2)}, u32[]{:S(2)}) collective-permute-start(f32[2,48,128]{2,1,0:T(8,128)S(1)} %get-tuple-element.31), channel_id=1, source_target_pairs={{0,1},{1,0},{2,3},{3,2},{4,5},{5,4},{6,7},{7,6},{8,9},{9,8},{10,11... | collective-permute-start | bytes 147464 | tf_op jit(solution)/shard_map/ppermute | solution.py:598
  19.9 9.4 %collective-permute-start.4 = (f32[2,48,128]{2,1,0:T(8,128)S(1)}, f32[2,48,128]{2,1,0:T(8,128)S(1)}, u32[]{:S(2)}, u32[]{:S(2)}) collective-permute-start(f32[2,48,128]{2,1,0:T(8,128)S(1)} %get-tuple-element.32), channel_id=1, source_target_pairs={{1,2},{2,1},{3,4},{4,3},{5,6},{6,5},{9,10},{10,9},{11,12},{12,11},... | collective-permute-start | bytes 147464 | tf_op jit(solution)/shard_map/ppermute | solution.py:598

commit v8 on v7

v8 whole, which is shorter than its diff:
```python
import math

import jax
import jax.numpy as jnp
from jax import lax
from jax.experimental import pallas as pl
from jax.experimental.pallas import tpu as pltpu
from jax.sharding import PartitionSpec as P

ITERS = 8
POINTS = 2**ITERS
OFF = 8

smoothing = 0.52
move_limit = 0.2
floor_density = 0.001
bracket_end = 12.0

f32 = jnp.float32
bf16 = jnp.bfloat16
VMEM = pl.BlockSpec(memory_space=pltpu.VMEM)
SMEM = pl.BlockSpec(memory_space=pltpu.SMEM)
HBM = pl.BlockSpec(memory_space=pltpu.HBM)


def cheb_weights():
    spectrum_top = 1.0 + 12.0 * smoothing
    centre_value = (spectrum_top + 1.0) / 2.0
    half_width = (spectrum_top - 1.0) / 2.0
    ratio_value = centre_value / half_width
    first_rho = 1.0 / ratio_value
    second_rho = 1.0 / (2.0 * ratio_value - first_rho)
    third_rho = 1.0 / (2.0 * ratio_value - second_rho)
    return (
        centre_value,
        second_rho * first_rho,
        2.0 * second_rho / half_width,
        third_rho * second_rho,
        2.0 * third_rho / half_width,
    )


def filter_weights():
    t, w1, w2, w3, w4 = cheb_weights()
    diag = 1.0 + 6.0 * smoothing
    alpha = w1 / t + w2 * (1.0 - diag / t)
    beta = w2 * smoothing / t
    gamma = 1.0 / t - w4 * w1 / (t * w2)
    delta = 1.0 + w3 + w4 / w2 - w4 * diag
    eps = w4 * smoothing
    return alpha, beta, gamma, delta, eps


def lane_up(v):
    n = v.shape[-1]
    lane = lax.broadcasted_iota(jnp.int32, v.shape, v.ndim - 1)
    return jnp.where(lane < n - 1, pltpu.roll(v, n - 1, v.ndim - 1), 0.0)


def lane_down(v):
    n = v.shape[-1]
    lane = lax.broadcasted_iota(jnp.int32, v.shape, v.ndim - 1)
    return jnp.where(lane > 0, pltpu.roll(v, 1, v.ndim - 1), 0.0)


def estimate(us):
    return pl.CostEstimate(flops=int(us * 1e9), bytes_accessed=1 << 20, transcendentals=0)


def build_matrix(k, mat, plane, band):
    shape = (24, 112)
    col = lax.broadcasted_iota(jnp.int32, shape, 1)
    row = lax.broadcasted_iota(jnp.int32, shape, 0)
    main = col < 96
    q = jnp.where(main, jnp.where(col >= 48, 1, 0), jnp.where(col >= 104, 1, 0))
    m = col - 48 * q
    e = col - 96 - 8 * q
    c = jnp.where(main, m >> 4, e >> 1)
    dx = jnp.where(main, (m >> 3) & 1, e & 1)
    valid = main | (e < 6)
    dof0 = 3 * (plane * q + dx) + c
    pick0 = jnp.where(main & (row == dof0), 1.0, 0.0)
    pick1 = jnp.where(valid & (row == dof0 + 3 * band), 1.0, 0.0)
    hp = lax.Precision.HIGHEST
    k0 = jnp.dot(k, pick0, precision=hp, preferred_element_type=f32)
    k1 = jnp.dot(k, pick1, precision=hp, preferred_element_type=f32)
    col8 = lax.broadcasted_iota(jnp.int32, (8, 112), 1)
    row8 = lax.broadcasted_iota(jnp.int32, (8, 112), 0)
    main8 = col8 < 96
    rc = col8 & 7
    m0 = main8 & (rc == row8)
    m1 = jnp.where(main8, rc, 8) == row8 + 1
    rows = []
    for b in range(2):
        for q_ in range(2):
            for c_ in range(3):
                for dx_ in range(2):
                    r = 3 * (plane * q_ + band * b + dx_) + c_
                    rows.append(jnp.where(m0, k0[r : r + 1], 0.0) + jnp.where(m1, k1[r : r + 1], 0.0))
    full = jnp.concatenate(rows, axis=0)
    hi = full.astype(bf16)
    lo = (full - hi.astype(f32)).astype(bf16)
    mat[:, 0:112] = hi
    mat[:, 112:224] = lo


def prepare(segments, p, work):
    main_s, ext_s, mul_s = work
    for l in range(3):
        for c in range(3):
            w0 = 0
            for u, x in segments(3 * l + c):
                size, nx = u.shape
                n = size // 8
                last = lax.broadcasted_iota(jnp.int32, u.shape, 0) == size - 1
                both = (u, lane_up(u))
                after = (None, None) if x is None else (x, lane_up(x))
                for w in range(n):
                    sl = slice(8 * w, 8 * w + 8)
                    main_s[p, l, 16 * c : 16 * c + 16, (w0 + w) * nx : (w0 + w + 1) * nx] = jnp.concatenate(
                        [both[0][sl], both[1][sl]], axis=0
                    ).astype(bf16)
                for dx in range(2):
                    v, vx = both[dx], after[dx]
                    k = 2 * c + dx
                    for w in range(n):
                        nxt = v[8 * w + 8 : 8 * w + 9] if w < n - 1 else vx
                        if nxt is not None:
                            ext_s[p, l, k : k + 1, (w0 + w) * nx : (w0 + w + 1) * nx] = nxt
                    m = 2.0 * v - v.astype(bf16).astype(f32)
                    mx = 0.0 if vx is None else jnp.broadcast_to(2.0 * vx - vx.astype(bf16).astype(f32), v.shape)
                    at = slice(8 * w0, 8 * (w0 + n))
                    mul_s[p, l, k, 0, at] = m
                    mul_s[p, l, k, 1, at] = jnp.where(last, mx, pltpu.roll(m, size - 1, 0))
                w0 += n


def energy_rows(p, mat, work, density):
    main_s, ext_s, mul_s = work
    rows, nx = density.shape
    count = rows // 8
    acc = [None] * count
    for l in range(3):
        ext = jnp.concatenate([ext_s[p, l], ext_s[p + 1, l]], axis=0).astype(bf16)
        one = jnp.concatenate([main_s[p, l], main_s[p + 1, l], ext], axis=0)
        force = jnp.dot(mat[...], jnp.concatenate([one, one], axis=0), preferred_element_type=f32)
        i = 0
        for b in range(2):
            for q in range(2):
                for k in range(6):
                    for w in range(count):
                        at = slice(8 * w, 8 * w + 8)
                        term = force[8 * i : 8 * i + 8, w * nx : (w + 1) * nx] * mul_s[p + q, l, k, b, at]
                        acc[w] = term if acc[w] is None else acc[w] + term
                    i += 1
    return density * (-3.0 * density * density * jnp.concatenate(acc, axis=0))


def workspace(planes, windows, nx):
    return [
        pltpu.VMEM((planes, 3, 48, windows * nx), bf16),
        pltpu.VMEM((planes, 3, 8, windows * nx), f32),
        pltpu.VMEM((planes, 3, 6, 2, 8 * windows, nx), f32),
    ]


def sweep(rows, segments, put, work):
    work[1][...] = jnp.zeros_like(work[1])
    for p in range(2):
        prepare(segments(p), p, work)

    def body(y, _):
        put(y)
        prepare(segments(y + 2), y + 2, work)
        return 0

    lax.fori_loop(0, rows - 1, body, 0, unroll=2)
    put(rows - 1)


def load_kernel(disp, dens, stiff, disp_v, dens_v, mat, mat_y, stiff_s, sems):
    copies = [
        pltpu.make_async_copy(stiff, stiff_s, sems.at[0]),
        pltpu.make_async_copy(disp, disp_v, sems.at[1]),
        pltpu.make_async_copy(dens, dens_v, sems.at[2]),
    ]
    for copy in copies:
        copy.start()
    copies[0].wait()
    build_matrix(stiff_s[...], mat, 4, 2)
    build_matrix(stiff_s[...], mat_y, 2, 4)
    for copy in copies[1:]:
        copy.wait()


def load_call(disp, dens, stiff):
    matrix = jax.ShapeDtypeStruct((192, 224), bf16)
    return pl.pallas_call(
        load_kernel,
        in_specs=[HBM, HBM, HBM],
        out_shape=(
            jax.ShapeDtypeStruct(disp.shape, f32),
            jax.ShapeDtypeStruct(dens.shape, f32),
            matrix,
            matrix,
        ),
        scratch_shapes=[pltpu.VMEM((24, 24), f32), pltpu.SemaphoreType.DMA((3,))],
        compiler_params=pltpu.CompilerParams(vmem_limit_bytes=16 * 2**20),
        cost_estimate=estimate(2),
        name="load",
    )(disp, dens, stiff)


def ends_kernel(disp, dens, mat, ends, up, down, *work):
    _, ny, nz, nx = disp.shape

    def segments(p):
        return lambda i: [(disp[i, p, 0:8], disp[i, p, 8:9]), (disp[i, p, nz - 8 : nz], None)]

    def put(y):
        d = jnp.concatenate([dens[y, 0:8], dens[y, nz - 8 : nz]], axis=0)
        ends[y] = energy_rows(y, mat, work, d)

    sweep(ny - 1, segments, put, work)
    for y in range(ny):
        row = slice(y, y + 1)
        for i in range(9):
            up[i, row] = disp[i, y, nz - 1 : nz]
            down[i, row] = disp[i, y, 0:1]
        up[9, row] = dens[y, nz - 1 : nz]
        if y < ny - 1:
            up[10, row] = ends[y, 14:15]
            down[9, row] = ends[y, 0:1]
            down[10, row] = ends[y, 1:2]
    up[11] = jnp.zeros((ny, nx), f32)
    down[11] = jnp.zeros((ny, nx), f32)


def ends_call(disp, dens, mat):
    _, ny, nz, nx = disp.shape
    message = jax.ShapeDtypeStruct((12, ny, nx), f32)
    return pl.pallas_call(
        ends_kernel,
        in_specs=[VMEM] * 3,
        out_shape=(jax.ShapeDtypeStruct((ny, 16, nx), f32), message, message),
        scratch_shapes=workspace(ny, 2, nx),
        compiler_params=pltpu.CompilerParams(vmem_limit_bytes=16 * 2**20),
        cost_estimate=estimate(4),
        name="energy_ends",
    )(disp, dens, mat)


def top_kernel(flags, disp, dens, fy, mat, ends, up, down, top, up_full, down_full, msg_even, msg_odd, *work):
    _, ny, nz, nx = disp.shape
    work[1][...] = jnp.zeros_like(work[1])
    prepare(lambda i: [(disp[i, ny - 1], None)], 0, work)
    prepare(lambda i: [(fy[i], None)], 1, work)
    up_full[...] = up[...]
    down_full[...] = down[...]
    for i in range(9):
        up_full[11, i : i + 1] = fy[i, nz - 1 : nz]
        down_full[11, i : i + 1] = fy[i, 0:1]
    s = energy_rows(0, mat, work, dens[ny - 1])
    top[...] = s
    up_full[10, ny - 1 : ny] = s[nz - 2 : nz - 1]
    down_full[9, ny - 1 : ny] = s[0:1]
    down_full[10, ny - 1 : ny] = s[1:2]
    odd = flags[5] == 1
    msg_even[...] = jnp.where(odd, down_full[...], up_full[...])
    msg_odd[...] = jnp.where(odd, up_full[...], down_full[...])


def top_call(flags, disp, dens, fy, mat, ends, up, down):
    _, ny, nz, nx = disp.shape
    message = jax.ShapeDtypeStruct((12, ny, nx), f32)
    return pl.pallas_call(
        top_kernel,
        in_specs=[SMEM] + [VMEM] * 7,
        out_shape=(jax.ShapeDtypeStruct((nz, nx), f32),) + (message,) * 4,
        scratch_shapes=workspace(2, nz // 8, nx),
        compiler_params=pltpu.CompilerParams(vmem_limit_bytes=16 * 2**20),
        cost_estimate=estimate(1),
        name="energy_top",
    )(flags, disp, dens, fy, mat, ends, up, down)


def middle_kernel(disp, dens, mat, ends, top, src, *work):
    _, ny, nz, nx = disp.shape

    def segments(p):
        return lambda i: [(disp[i, p, 8 : nz - 8], disp[i, p, nz - 8 : nz - 7])]

    def frame(y):
        src[y, 0:OFF] = jnp.zeros((OFF, nx), f32)
        src[y, OFF + nz :] = jnp.zeros((src.shape[1] - OFF - nz, nx), f32)

    def put(y):
        frame(y)
        src[y, OFF : OFF + 8] = ends[y, 0:8]
        src[y, OFF + 8 : OFF + nz - 8] = energy_rows(y, mat, work, dens[y, 8 : nz - 8])
        src[y, OFF + nz - 8 : OFF + nz] = ends[y, 8:16]

    sweep(ny - 1, segments, put, work)
    frame(ny - 1)
    src[ny - 1, OFF : OFF + nz] = top[...]


def middle_call(disp, dens, mat, ends, top):
    _, ny, nz, nx = disp.shape
    return pl.pallas_call(
        middle_kernel,
        in_specs=[VMEM] * 5,
        out_shape=jax.ShapeDtypeStruct((ny, nz + 2 * OFF, nx), f32),
        scratch_shapes=workspace(ny, nz // 8 - 2, nx),
        compiler_params=pltpu.CompilerParams(vmem_limit_bytes=24 * 2**20),
        cost_estimate=estimate(4),
        name="energy_middle",
    )(disp, dens, mat, ends, top)


def rim_kernel(flags, got_even, got_odd, up, down, mat_y, src, rim, msg_even, msg_odd, low_s, high_s, t_s, *work):
    ny, rows, nx = src.shape
    nz = rows - 2 * OFF
    odd = flags[5] == 1
    low_s[...] = jnp.where(odd, got_even[...], got_odd[...])
    high_s[...] = jnp.where(odd, got_odd[...], got_even[...])
    work[1][...] = jnp.zeros_like(work[1])
    prepare(lambda i: [(low_s[i], low_s[11, i : i + 1]), (up[i], up[11, i : i + 1])], 0, work)
    prepare(lambda i: [(down[i], down[11, i : i + 1]), (high_s[i], high_s[11, i : i + 1])], 1, work)
    s = energy_rows(0, mat_y, work, jnp.concatenate([low_s[9], up[9]], axis=0))
    columns = (low_s[10], s[0:ny], s[ny : 2 * ny], high_s[9], high_s[10])
    for y in range(ny):
        for r, column in enumerate(columns):
            rim[y, r : r + 1] = column[y : y + 1]
        rim[y, 5:8] = jnp.zeros((3, nx), f32)
    for j in range(4):
        y = j if j < 2 else ny - 4 + j
        t_s[j] = src[y]
        put_rim(t_s, j, rim[y], nz)
    odd = flags[4] == 1
    msg_even[...] = jnp.where(odd, t_s[0:2], t_s[2:4])
    msg_odd[...] = jnp.where(odd, t_s[2:4], t_s[0:2])


def put_rim(s, y, rim, nz):
    s[y, OFF - 2 : OFF] = rim[0:2]
    s[y, OFF + nz - 1 : OFF + nz + 2] = rim[2:5]


def rim_call(flags, got_even, got_odd, up, down, mat_y, src):
    ny, rows, nx = src.shape
    return pl.pallas_call(
        rim_kernel,
        in_specs=[SMEM] + [VMEM] * 6,
        out_shape=(
            jax.ShapeDtypeStruct((ny, 8, nx), f32),
            jax.ShapeDtypeStruct((2, rows, nx), f32),
            jax.ShapeDtypeStruct((2, rows, nx), f32),
        ),
        scratch_shapes=[
            pltpu.VMEM((12, ny, nx), f32),
            pltpu.VMEM((12, ny, nx), f32),
            pltpu.VMEM((4, rows, nx), f32),
        ]
        + workspace(2, 2 * (ny // 8), nx),
        compiler_params=pltpu.CompilerParams(vmem_limit_bytes=16 * 2**20),
        cost_estimate=estimate(2),
        name="energy_rim",
    )(flags, got_even, got_odd, up, down, mat_y, src)


def filter_block(s_s, d_s, n, z_edges, y_edges, finish, unroll):
    rows, nx = s_s.shape[1:]
    nz = rows - 2 * OFF
    alpha, beta, gamma, delta, eps = filter_weights()
    row = lax.broadcasted_iota(jnp.int32, (rows, nx), 0)
    keep = jnp.where(row < OFF, z_edges[0], jnp.where(row >= OFF + nz, z_edges[1], 1)) == 1

    def beside(v):
        return pltpu.roll(v, 1, 0) + pltpu.roll(v, rows - 1, 0) + lane_up(v) + lane_down(v)

    def second(j, _):
        c = s_s[j + 1]
        d2 = alpha * c + beta * (beside(c) + s_s[j] + s_s[j + 2])
        ok = keep
        if y_edges is not None:
            ok = keep & (jnp.where(j == 0, y_edges[0], jnp.where(j == n - 3, y_edges[1], 1)) == 1)
        d_s[j] = jnp.where(ok, d2, 0.0)
        return 0

    def third(j, _):
        d2 = d_s[j + 1]
        p3 = gamma * s_s[j + 2] + delta * d2 + eps * (beside(d2) + d_s[j] + d_s[j + 2])
        finish(j, p3[OFF : OFF + nz])
        return 0

    lax.fori_loop(0, n - 2, second, 0, unroll=unroll)
    lax.fori_loop(0, n - 4, third, 0, unroll=unroll)


def limits(p3, d, pas, sol):
    amp = jnp.sqrt(jnp.maximum(-p3 * d, 0.0))
    lower = jnp.maximum(d - move_limit, floor_density)
    upper = jnp.minimum(d + move_limit, 1.0)
    low, high, now = (jnp.where(sol, 1.0, jnp.where(pas, floor_density, v)) for v in (lower, upper, d))
    return amp, low, high, now


FINE = 16
COARSE = POINTS // FINE


def table(n, nz, nx, amp, low, high, now, fine_s, vol, tgt, start):
    spacing = 2.0 * bracket_end / POINTS

    def fine(j, _):
        a = amp[j]
        for f in range(FINE):
            fine_s[f, j] = a * math.exp(-0.5 * spacing * f)
        return 0

    lax.fori_loop(0, n, fine, 0)
    pair = 2
    for first in range(0, COARSE, pair):
        inverse = [math.exp(0.5 * (-bracket_end + spacing * FINE * i)) for i in range(first, first + pair)]

        def volume(j, acc):
            acc = list(acc)
            for w in range(nz // 8):
                at = slice(8 * w, 8 * w + 8)
                lo, hi, d = low[j, at], high[j, at], now[j, at]
                los, his = [lo * c for c in inverse], [hi * c for c in inverse]
                for i, c in enumerate(inverse):
                    acc[pair * FINE + i] = acc[pair * FINE + i] + d * c
                for f in range(FINE):
                    t = fine_s[f, j, at]
                    for i in range(pair):
                        acc[i * FINE + f] = acc[i * FINE + f] + jnp.minimum(jnp.maximum(t, los[i]), his[i])
            return tuple(acc)

        places = [(vol, 8 * (first * FINE + e)) for e in range(pair * FINE)]
        places += [(tgt, 8 * (first + i)) for i in range(pair)]
        if start is None:
            begin = tuple(jnp.zeros((8, nx), f32) for _ in places)
        else:
            begin = tuple((start[0] if ref is vol else start[1])[at : at + 8] for ref, at in places)
        acc = lax.fori_loop(0, n, volume, begin, unroll=2)
        for (ref, at), value in zip(places, acc):
            ref[at : at + 8] = value


def inner_kernel(flags, src, rim, dens, passive, solid, amp, low, high, vol, tgt, s_s, d_s, now_s, fine_s):
    ny, nz, nx = dens.shape
    s_s[...] = src[...]

    def fix(y, _):
        put_rim(s_s, y, rim[y], nz)
        return 0

    lax.fori_loop(0, ny, fix, 0, unroll=4)

    def finish(j, p3):
        y = j + 2
        amp[j], low[j], high[j], now_s[j] = limits(p3, dens[y], passive[y] == 1, solid[y] == 1)

    filter_block(s_s, d_s, ny, (flags[2], flags[3]), None, finish, 4)
    table(ny - 4, nz, nx, amp, low, high, now_s, fine_s, vol, tgt, None)


def inner_call(flags, src, rim, dens, passive, solid):
    ny, nz, nx = dens.shape
    field = jax.ShapeDtypeStruct((ny - 4, nz, nx), f32)
    return pl.pallas_call(
        inner_kernel,
        in_specs=[SMEM] + [VMEM] * 5,
        out_shape=(
            field,
            field,
            field,
            jax.ShapeDtypeStruct((8 * POINTS, nx), f32),
            jax.ShapeDtypeStruct((8 * COARSE, nx), f32),
        ),
        scratch_shapes=[
            pltpu.VMEM((ny, nz + 2 * OFF, nx), f32),
            pltpu.VMEM((ny - 2, nz + 2 * OFF, nx), f32),
            pltpu.VMEM((ny - 4, nz, nx), f32),
            pltpu.VMEM((FINE, ny - 4, nz, nx), f32),
        ],
        compiler_params=pltpu.CompilerParams(vmem_limit_bytes=24 * 2**20),
        cost_estimate=estimate(9),
        name="filter_inner",
    )(flags, src, rim, dens, passive, solid)


def outer_kernel(
    flags, src, rim, got_even, got_odd, dens, passive, solid, vol_i, tgt_i,
    amp, low, high, excess, s_s, d_s, now_s, fine_s, vol, tgt,
):
    ny, nz, nx = dens.shape
    odd = flags[4] == 1
    s_s[0, 0:2] = jnp.where(odd, got_even[...], got_odd[...])
    s_s[1, 4:6] = jnp.where(odd, got_odd[...], got_even[...])
    for j in range(4):
        s_s[0, 2 + j] = src[j]
        put_rim(s_s.at[0], 2 + j, rim[j], nz)
        s_s[1, j] = src[ny - 4 + j]
        put_rim(s_s.at[1], j, rim[ny - 4 + j], nz)
    for b in range(2):
        y0 = 0 if b == 0 else ny - 2

        def finish(j, p3):
            y = y0 + j
            at = 2 * b + j
            amp[at], low[at], high[at], now_s[at] = limits(p3, dens[y], passive[y] == 1, solid[y] == 1)

        edges = (flags[0], 1) if b == 0 else (1, flags[1])
        filter_block(s_s.at[b], d_s.at[b], 6, (flags[2], flags[3]), edges, finish, True)
    table(4, nz, nx, amp, low, high, now_s, fine_s, vol, tgt, (vol_i, tgt_i))

    def lanes(ref, count):
        total = ref[pl.ds(0, count, stride=8), :]
        for s in range(1, 8):
            total = total + ref[pl.ds(s, count, stride=8), :]
        return total

    volumes, targets = lanes(vol, POINTS), lanes(tgt, COARSE)
    over = [volumes[FINE * i : FINE * i + FINE] - targets[i : i + 1] for i in range(COARSE)]
    excess[...] = jnp.sum(jnp.transpose(jnp.concatenate(over, axis=0)), axis=0, keepdims=True)


def outer_call(flags, src, rim, got_even, got_odd, dens, passive, solid, vol_i, tgt_i):
    ny, nz, nx = dens.shape
    rows = nz + 2 * OFF
    field = jax.ShapeDtypeStruct((4, nz, nx), f32)
    return pl.pallas_call(
        outer_kernel,
        in_specs=[SMEM] + [VMEM] * 9,
        out_shape=(field, field, field, jax.ShapeDtypeStruct((1, POINTS), f32)),
        scratch_shapes=[
            pltpu.VMEM((2, 6, rows, nx), f32),
            pltpu.VMEM((2, 4, rows, nx), f32),
            pltpu.VMEM((4, nz, nx), f32),
            pltpu.VMEM((FINE, 4, nz, nx), f32),
            pltpu.VMEM((8 * POINTS, nx), f32),
            pltpu.VMEM((8 * COARSE, nx), f32),
        ],
        compiler_params=pltpu.CompilerParams(vmem_limit_bytes=16 * 2**20),
        cost_estimate=estimate(3),
        name="filter_outer",
    )(flags, src, rim, got_even, got_odd, dens, passive, solid, vol_i, tgt_i)


def update_kernel(tables, amp_i, low_i, high_i, amp_o, low_o, high_o, new, logm):
    inner = amp_i.shape[0]
    nx = amp_i.shape[-1]
    total = jnp.sum(tables[...], axis=0, keepdims=True)
    lane = lax.broadcasted_iota(jnp.int32, total.shape, 1)
    above = jnp.where((total > 0.0) & (lane > 0), 1.0, 0.0)
    middle = -bracket_end + (2.0 * bracket_end / POINTS) * (jnp.sum(above) + 0.5)
    logm[0] = middle
    scale = jnp.exp(jnp.full((1, nx), -0.5 * middle, f32))

    def new_row(amp, low, high):
        return jnp.minimum(jnp.maximum(amp * scale, low), high)

    def body(j, _):
        new[j + 2] = new_row(amp_i[j], low_i[j], high_i[j])
        return 0

    lax.fori_loop(0, inner, body, 0)
    for j in range(4):
        new[j if j < 2 else inner + j] = new_row(amp_o[j], low_o[j], high_o[j])


def update_call(tables, inner, outer):
    n, nz, nx = inner[0].shape
    return pl.pallas_call(
        update_kernel,
        in_specs=[VMEM] * 7,
        out_specs=(VMEM, SMEM),
        out_shape=(jax.ShapeDtypeStruct((n + 4, nz, nx), f32), jax.ShapeDtypeStruct((1,), f32)),
        compiler_params=pltpu.CompilerParams(vmem_limit_bytes=8 * 2**20),
        cost_estimate=estimate(1),
        name="update",
    )(tables, *inner, *outer)


def to_lower(value, axis):
    count = lax.axis_size(axis)
    return lax.ppermute(value, axis, [(i + 1, i) for i in range(count - 1)])


def swap(value, axis, start):
    pairs = []
    for i in range(start, lax.axis_size(axis) - 1, 2):
        pairs += [(i, i + 1), (i + 1, i)]
    return lax.ppermute(value, axis, pairs)


def on_device(displacement, density, passive, solid, stiffness):
    ny, nz, nx = density.shape
    gy, gz = lax.axis_size("gy"), lax.axis_size("gz")
    iy, iz = lax.axis_index("gy"), lax.axis_index("gz")
    flags = jnp.stack([iy > 0, iy < gy - 1, iz > 0, iz < gz - 1, iy % 2 == 1, iz % 2 == 1]).astype(jnp.int32)

    disp_hbm = pltpu.with_memory_space_constraint(displacement, pltpu.HBM)
    dens_hbm = pltpu.with_memory_space_constraint(density, pltpu.HBM)
    stiff_hbm = pltpu.with_memory_space_constraint(stiffness, pltpu.HBM)

    fy = to_lower(displacement[:, 0], "gy")
    disp, dens, mat, mat_y = load_call(disp_hbm, dens_hbm, stiff_hbm)
    ends, up, down = ends_call(disp, dens, mat)
    top, up, down, z_even, z_odd = top_call(flags, disp, dens, fy, mat, ends, up, down)

    z_got_odd = swap(z_odd, "gz", 1)
    z_got_even = swap(z_even, "gz", 0)
    src = middle_call(disp, dens, mat, ends, top)
    rim, msg_even, msg_odd = rim_call(flags, z_got_even, z_got_odd, up, down, mat_y, src)

    got_odd = swap(msg_odd, "gy", 1)
    got_even = swap(msg_even, "gy", 0)
    *inner, vol, tgt = inner_call(flags, src, rim, dens, passive, solid)
    *outer, excess = outer_call(flags, src, rim, got_even, got_odd, dens, passive, solid, vol, tgt)

    everyone = jnp.broadcast_to(excess, (gz * gy, POINTS))
    tables = lax.all_to_all(everyone, ("gz", "gy"), 0, 0, tiled=True)
    new, logm = update_call(tables, inner, outer)
    return new, logm.reshape(())


def solution(mesh):
    placed = (
        P(None, "gy", "gz", None),
        P("gy", "gz", None),
        P("gy", "gz", None),
        P("gy", "gz", None),
        P(),
    )
    return jax.shard_map(
        on_device, mesh=mesh, in_specs=placed, out_specs=(P("gy", "gz", None), P()), check_vma=False
    )
```

time: 52.1 us -> 47.4 us (0.910)
  blocking collectives: 18.2 us -> 15.9 us
  Pallas kernels: 22.7 us -> 21.3 us
  waiting for transfers between devices: 3.72 us -> 2.61 us
    all_to_all x1, blocking collectives: 18.2 us -> 15.9 us  [on_device(): tables = lax.all_to_all(everyone, ('gz', 'gy'), 0, 0, tiled=True)]
    pallas_call x5 -> x6, Pallas kernels: 20 us -> 18.7 us  [the longest x1 7.78 us: inner_call(): pl.pallas_call(inner_kernel, in_specs=[SMEM] + [VMEM] * 5, out_shape=(fie...]
    ppermute x1, waiting for transfers between devices: 3.71 us -> 2.6 us  [to_lower(): return lax.ppermute(value, axis, [(i + 1, i) for i in range(count - 1)])]
    squeeze x0 -> x1, local copies, waits for them, and re-layouts: none -> 0.93 us  [on_device(): fy = to_lower(displacement[:, 0], 'gy')]
    unnamed x9 -> x5, local copies, waits for them, and re-layouts: 0.69 us -> 0.02 us
  transfers between devices with their start and end apart: 5 -> 5, of which waited for: 1 -> 1; matrix products, arithmetic and copies ran while one was open for 0% -> 0% of each run, Pallas kernels for 27% -> 32%
where the time goes in v8:
time: 47.4 us; the launch traced here: 47.1 us
  Pallas kernels  21.3 us (45%)
  blocking collectives  15.9 us (34%)
  starting transfers between devices  5.38 us (11%)
  waiting for transfers between devices  2.61 us (6%)
  local copies, waits for them, and re-layouts  1.07 us (2%)
  between operations  0.8 us (2%)
    all_to_all x1, blocking collectives, on_device(): tables = lax.all_to_all(everyone, ('gz', 'gy'), 0, 0, tiled=True)  15.9 us
    pallas_call x1, Pallas kernels, inner_call(): pl.pallas_call(inner_kernel, in_specs=[SMEM] + [VMEM] * 5, out_shape=(fie...  7.78 us
    ppermute x4, starting transfers between devices, swap(): return lax.ppermute(value, axis, pairs)  4.09 us
    pallas_call x1, Pallas kernels, outer_call(): pl.pallas_call(outer_kernel, in_specs=[SMEM] + [VMEM] * 9, out_shape=(fie...  3.14 us
    pallas_call x1, Pallas kernels, ends_call(): pl.pallas_call(ends_kernel, in_specs=[VMEM] * 3, out_shape=(jax.ShapeDtyp...  2.92 us
    pallas_call x1, Pallas kernels, middle_call(): pl.pallas_call(middle_kernel, in_specs=[VMEM] * 5, out_shape=jax.ShapeDty...  2.88 us
    ppermute x1, waiting for transfers between devices, to_lower(): return lax.ppermute(value, axis, [(i + 1, i) for i in range(count - 1)])  2.6 us
    pallas_call x1, Pallas kernels, load_call(): pl.pallas_call(load_kernel, in_specs=[HBM, HBM, HBM], out_shape=(jax.Shap...  1.71 us
  transfers between devices with their start and end apart: 5, of which 1 were waited for; matrix products, arithmetic and copies ran while one was open for 0% of the time, Pallas kernels for 32%

profile of v8, /device:TPU:0, one launch (start us, length us, event | category | flops | bytes accessed | tf_op | source)
XLA Modules:
  0.0 47.1 jit_solution(2809189626656931780)
XLA Ops:
  0.6 0.9 %slice_bitcast_fusion = f32[9,32,128]{2,1,0:T(8,128)S(1)} fusion(f32[9,16,32,128]{3,2,1,0:T(8,128)} %disp.1), kind=kLoop, calls=%fused_computation | loop fusion | bytes 294912 | tf_op jit(solution)/shard_map/squeeze | solution.py:610
  1.6 1.3 %collective-permute-start = (f32[9,32,128]{2,1,0:T(8,128)S(1)}, f32[9,32,128]{2,1,0:T(8,128)S(1)}, u32[]{:S(2)}, u32[]{:S(2)}) collective-permute-start(f32[9,32,128]{2,1,0:T(8,128)S(1)} %slice_bitcast_fusion), channel_id=1, source_target_pairs={{1,0},{2,1},{3,2},{4,3},{5,4},{6,5},{7,6},{9,8},{10,9},{11,10},{12... | collective-permute-start | bytes 442376 | tf_op jit(solution)/shard_map/ppermute | solution.py:590
  2.9 1.7 %load.1 = (f32[9,16,32,128]{3,2,1,0:T(8,128)S(1)}, f32[16,32,128]{2,1,0:T(8,128)S(1)}, bf16[192,224]{1,0:T(8,128)(2,1)S(1)}, bf16[192,224]{1,0:T(8,128)(2,1)S(1)}) custom-call(f32[9,16,32,128]{3,2,1,0:T(8,128)} %disp.1, f32[16,32,128]{2,1,0:T(8,128)} %dens.1, f32[24,24]{1,0:T(8,128)} %stiff.1), custom_call_target="tpu_custom_call" | custom-call | flops 2000000000 | bytes 1048576 | tf_op jit(solution)/shard_map/load/pallas_call | solution.py:198
  4.6 2.9 %energy_ends.1 = (f32[16,16,128]{2,1,0:T(8,128)S(1)}, f32[12,16,128]{2,1,0:T(8,128)S(1)}, f32[12,16,128]{2,1,0:T(8,128)S(1)}) custom-call(f32[9,16,32,128]{3,2,1,0:T(8,128)S(1)} %get-tuple-element.28.disp, f32[16,32,128]{2,1,0:T(8,128)S(1)} %get-tuple-element.29.dens, bf16[192,224]{1,0:T(8,128)(2,1)S(1)} %get-tuple-element.30.mat), custom_call_target="tpu_custom_call" | custom-call | flops 4000000000 | bytes 1048576 | tf_op jit(solution)/shard_map/energy_ends/pallas_call | solution.py:242
  7.5 0.1 stack.27
  7.6 2.6 %collective-permute-done.fy = f32[9,32,128]{2,1,0:T(8,128)S(1)} collective-permute-done((f32[9,32,128]{2,1,0:T(8,128)S(1)}, f32[9,32,128]{2,1,0:T(8,128)S(1)}, u32[]{:S(2)}, u32[]{:S(2)}) %collective-permute-start) | collective-permute-done | bytes 147488 | tf_op jit(solution)/shard_map/ppermute | solution.py:590
  10.2 1.0 %energy_top.1 = (f32[32,128]{1,0:T(8,128)S(1)}, f32[12,16,128]{2,1,0:T(8,128)S(1)}, f32[12,16,128]{2,1,0:T(8,128)S(1)}, f32[12,16,128]{2,1,0:T(8,128)S(1)}, f32[12,16,128]{2,1,0:T(8,128)S(1)}) custom-call(s32[6]{0:T(128)S(1)} %convert_element_type.3.flags, f32[9,16,32,128]{3,2,1,0:T(8,128)S(1)} %get-tuple-element.28.disp, ...), custom_call_target="tpu_custom_call" | custom-call | flops 1000000000 | bytes 1048576 | tf_op jit(solution)/shard_map/energy_top/pallas_call | solution.py:276
  11.2 0.1 collective-permute-start.1
  11.3 0.7 %collective-permute-start.2 = (f32[12,16,128]{2,1,0:T(8,128)S(1)}, f32[12,16,128]{2,1,0:T(8,128)S(1)}, u32[]{:S(2)}, u32[]{:S(2)}) collective-permute-start(f32[12,16,128]{2,1,0:T(8,128)S(1)} %get-tuple-element.36), channel_id=1, source_target_pairs={{8,16},{16,8},{9,17},{17,9},{10,18},{18,10},{11,19},{19,11},{12,20... | collective-permute-start | bytes 294920 | tf_op jit(solution)/shard_map/ppermute | solution.py:597
  12.0 2.9 %energy_middle.1.src = f32[16,48,128]{2,1,0:T(8,128)S(1)} custom-call(f32[9,16,32,128]{3,2,1,0:T(8,128)S(1)} %get-tuple-element.28.disp, f32[16,32,128]{2,1,0:T(8,128)S(1)} %get-tuple-element.29.dens, bf16[192,224]{1,0:T(8,128)(2,1)S(1)} %get-tuple-element.30.mat, f32[16,16,128]{2,1,0:T(8,128)S(1)} %get-tuple-element.31.ends, ...), custom_call_target="tpu_custom_call" | custom-call | flops 4000000000 | bytes 1048576 | tf_op jit(solution)/shard_map/energy_middle/pallas_call | solution.py:310
  14.8 0.0 collective-permute-done.1.got_even
  14.9 0.0 collective-permute-done.2.got_odd
  14.9 0.0 copy-start
  14.9 0.0 copy-start.1
  14.9 1.0 %energy_rim.1 = (f32[16,8,128]{2,1,0:T(8,128)S(1)}, f32[2,48,128]{2,1,0:T(8,128)S(1)}, f32[2,48,128]{2,1,0:T(8,128)S(1)}) custom-call(s32[6]{0:T(128)S(1)} %convert_element_type.3.flags, f32[12,16,128]{2,1,0:T(8,128)S(1)} %collective-permute-done.1.got_even, f32[12,16,128]{2,1,0:T(8,128)S(1)} %collective-permute-done.2.got_odd, ...), custom_call_target="tpu_custom_call" | custom-call | flops 2000000000 | bytes 1048576 | tf_op jit(solution)/shard_map/energy_rim/pallas_call | solution.py:352
  15.9 2.7 %collective-permute-start.3 = (f32[2,48,128]{2,1,0:T(8,128)S(1)}, f32[2,48,128]{2,1,0:T(8,128)S(1)}, u32[]{:S(2)}, u32[]{:S(2)}) collective-permute-start(f32[2,48,128]{2,1,0:T(8,128)S(1)} %get-tuple-element.41), channel_id=1, source_target_pairs={{0,1},{1,0},{2,3},{3,2},{4,5},{5,4},{6,7},{7,6},{8,9},{9,8},{10,11... | collective-permute-start | bytes 147464 | tf_op jit(solution)/shard_map/ppermute | solution.py:597
  18.6 0.7 %collective-permute-start.4 = (f32[2,48,128]{2,1,0:T(8,128)S(1)}, f32[2,48,128]{2,1,0:T(8,128)S(1)}, u32[]{:S(2)}, u32[]{:S(2)}) collective-permute-start(f32[2,48,128]{2,1,0:T(8,128)S(1)} %get-tuple-element.42), channel_id=1, source_target_pairs={{1,2},{2,1},{3,4},{4,3},{5,6},{6,5},{9,10},{10,9},{11,12},{12,11},... | collective-permute-start | bytes 147464 | tf_op jit(solution)/shard_map/ppermute | solution.py:597
  19.3 0.0 copy-done
  19.3 7.8 %filter_inner.1 = (f32[12,32,128]{2,1,0:T(8,128)S(1)}, f32[12,32,128]{2,1,0:T(8,128)S(1)}, f32[12,32,128]{2,1,0:T(8,128)S(1)}, f32[2048,128]{1,0:T(8,128)S(1)}, f32[128,128]{1,0:T(8,128)S(1)}) custom-call(s32[6]{0:T(128)S(1)} %convert_element_type.3.flags, f32[16,48,128]{2,1,0:T(8,128)S(1)} %energy_middle.1.src, f32[16,8,128]{2,1,0:T(8,128)S(1)} %get-tuple-element.40.rim, ...), custom_call_target="tpu_custom_call" | custom-call | flops 8999999488 | bytes 1048576 | tf_op jit(solution)/shard_map/filter_inner/pallas_call | solution.py:473
  27.1 0.0 collective-permute-done.3.got_even
  27.1 0.0 collective-permute-done.4.got_odd
  27.1 3.1 %filter_outer.1 = (f32[4,32,128]{2,1,0:T(8,128)S(1)}, f32[4,32,128]{2,1,0:T(8,128)S(1)}, f32[4,32,128]{2,1,0:T(8,128)S(1)}, f32[1,256]{1,0:T(1,128)S(1)}) custom-call(s32[6]{0:T(128)S(1)} %convert_element_type.3.flags, f32[16,48,128]{2,1,0:T(8,128)S(1)} %energy_middle.1.src, f32[16,8,128]{2,1,0:T(8,128)S(1)} %get-tuple-element.40.rim, ...), custom_call_target="tpu_custom_call" | custom-call | flops 3000000000 | bytes 1048576 | tf_op jit(solution)/shard_map/filter_outer/pallas_call | solution.py:535
  30.2 15.9 %all_to_all.8 = f32[32,1,256]{2,1,0:T(1,128)S(1)} all-to-all(f32[32,1,256]{2,1,0:T(1,128)S(1)} %broadcast_in_dim.2), channel_id=1, replica_groups=mesh['gz'=4,'gy'=8] {'gz','gy'}, dimensions={0} | all-to-all | bytes 65536 | tf_op jit(solution)/shard_map/all_to_all | solution.py:626
  46.2 0.9 %update.1 = (f32[16,32,128]{2,1,0:T(8,128)}, f32[1]{0:T(128)}) custom-call(f32[32,256]{1,0:T(8,128)S(1)} %bitcast.15, f32[12,32,128]{2,1,0:T(8,128)S(1)} %get-tuple-element.46.amp_i, f32[12,32,128]{2,1,0:T(8,128)S(1)} %get-tuple-element.47.low_i, f32[12,32,128]{2,1,0:T(8,128)S(1)} %get-tuple-element.48.high_i, f32[4,32,128]{2,1,0:T(8,128)S(1)} %get-tuple-element.49.amp_o, ...), custom_call_target="tpu_custom_call" | custom-call | flops 1000000000 | bytes 1048576 | tf_op jit(solution)/shard_map/update/pallas_call | solution.py:577
  (4 shorter events, 0.0 us)
Async XLA Ops:
  1.6 8.7 %collective-permute-start = (f32[9,32,128]{2,1,0:T(8,128)S(1)}, f32[9,32,128]{2,1,0:T(8,128)S(1)}, u32[]{:S(2)}, u32[]{:S(2)}) collective-permute-start(f32[9,32,128]{2,1,0:T(8,128)S(1)} %slice_bitcast_fusion), channel_id=1, source_target_pairs={{1,0},{2,1},{3,2},{4,3},{5,4},{6,5},{7,6},{9,8},{10,9},{11,10},{12... | collective-permute-start | bytes 442376 | tf_op jit(solution)/shard_map/ppermute | solution.py:590
  11.2 3.6 %collective-permute-start.1 = (f32[12,16,128]{2,1,0:T(8,128)S(1)}, f32[12,16,128]{2,1,0:T(8,128)S(1)}, u32[]{:S(2)}, u32[]{:S(2)}) collective-permute-start(f32[12,16,128]{2,1,0:T(8,128)S(1)} %get-tuple-element.35), channel_id=1, source_target_pairs={{0,8},{8,0},{16,24},{24,16},{1,9},{9,1},{17,25},{25,17},{2,10},{10... | collective-permute-start | bytes 294920 | tf_op jit(solution)/shard_map/ppermute | solution.py:597
  11.3 3.6 %collective-permute-start.2 = (f32[12,16,128]{2,1,0:T(8,128)S(1)}, f32[12,16,128]{2,1,0:T(8,128)S(1)}, u32[]{:S(2)}, u32[]{:S(2)}) collective-permute-start(f32[12,16,128]{2,1,0:T(8,128)S(1)} %get-tuple-element.36), channel_id=1, source_target_pairs={{8,16},{16,8},{9,17},{17,9},{10,18},{18,10},{11,19},{19,11},{12,20... | collective-permute-start | bytes 294920 | tf_op jit(solution)/shard_map/ppermute | solution.py:597
  14.9 4.4 %copy-start = (s32[16,32,128]{2,1,0:T(8,128)S(1)}, s32[16,32,128]{2,1,0:T(8,128)}, u32[]{:S(2)}) copy-start(s32[16,32,128]{2,1,0:T(8,128)} %passive.3) | copy-start | bytes 786436
  14.9 4.4 %copy-start.1 = (s32[16,32,128]{2,1,0:T(8,128)S(1)}, s32[16,32,128]{2,1,0:T(8,128)}, u32[]{:S(2)}) copy-start(s32[16,32,128]{2,1,0:T(8,128)} %solid.3) | copy-start | bytes 786436
  15.9 11.2 %collective-permute-start.3 = (f32[2,48,128]{2,1,0:T(8,128)S(1)}, f32[2,48,128]{2,1,0:T(8,128)S(1)}, u32[]{:S(2)}, u32[]{:S(2)}) collective-permute-start(f32[2,48,128]{2,1,0:T(8,128)S(1)} %get-tuple-element.41), channel_id=1, source_target_pairs={{0,1},{1,0},{2,3},{3,2},{4,5},{5,4},{6,7},{7,6},{8,9},{9,8},{10,11... | collective-permute-start | bytes 147464 | tf_op jit(solution)/shard_map/ppermute | solution.py:597
  18.6 8.5 %collective-permute-start.4 = (f32[2,48,128]{2,1,0:T(8,128)S(1)}, f32[2,48,128]{2,1,0:T(8,128)S(1)}, u32[]{:S(2)}, u32[]{:S(2)}) collective-permute-start(f32[2,48,128]{2,1,0:T(8,128)S(1)} %get-tuple-element.42), channel_id=1, source_target_pairs={{1,2},{2,1},{3,4},{4,3},{5,6},{6,5},{9,10},{10,9},{11,12},{12,11},... | collective-permute-start | bytes 147464 | tf_op jit(solution)/shard_map/ppermute | solution.py:597

commit v9 on v8

--- a/solution.py
+++ b/solution.py
@@ -67,8 +67,8 @@
     return pl.CostEstimate(flops=int(us * 1e9), bytes_accessed=1 << 20, transcendentals=0)
 
 
-def build_matrix(k, mat, plane, band):
-    shape = (24, 112)
+def build_matrices(k, mats):
+    shape = (24, 128)
     col = lax.broadcasted_iota(jnp.int32, shape, 1)
     row = lax.broadcasted_iota(jnp.int32, shape, 0)
     main = col < 96
@@ -78,30 +78,35 @@
     c = jnp.where(main, m >> 4, e >> 1)
     dx = jnp.where(main, (m >> 3) & 1, e & 1)
     valid = main | (e < 6)
-    dof0 = 3 * (plane * q + dx) + c
-    pick0 = jnp.where(main & (row == dof0), 1.0, 0.0)
-    pick1 = jnp.where(valid & (row == dof0 + 3 * band), 1.0, 0.0)
-    hp = lax.Precision.HIGHEST
-    k0 = jnp.dot(k, pick0, precision=hp, preferred_element_type=f32)
-    k1 = jnp.dot(k, pick1, precision=hp, preferred_element_type=f32)
-    col8 = lax.broadcasted_iota(jnp.int32, (8, 112), 1)
-    row8 = lax.broadcasted_iota(jnp.int32, (8, 112), 0)
+    picks = []
+    for _, plane, band in mats:
+        dof0 = 3 * (plane * q + dx) + c
+        picks.append(jnp.where(main & (row == dof0), 1.0, 0.0))
+        picks.append(jnp.where(valid & (row == dof0 + 3 * band), 1.0, 0.0))
+    picked = jnp.dot(
+        k, jnp.concatenate(picks, axis=1), precision=lax.Precision.HIGHEST, preferred_element_type=f32
+    )
+    col8 = lax.broadcasted_iota(jnp.int32, (8, 128), 1)
+    row8 = lax.broadcasted_iota(jnp.int32, (8, 128), 0)
     main8 = col8 < 96
     rc = col8 & 7
     m0 = main8 & (rc == row8)
     m1 = jnp.where(main8, rc, 8) == row8 + 1
-    rows = []
-    for b in range(2):
-        for q_ in range(2):
-            for c_ in range(3):
-                for dx_ in range(2):
-                    r = 3 * (plane * q_ + band * b + dx_) + c_
-                    rows.append(jnp.where(m0, k0[r : r + 1], 0.0) + jnp.where(m1, k1[r : r + 1], 0.0))
-    full = jnp.concatenate(rows, axis=0)
-    hi = full.astype(bf16)
-    lo = (full - hi.astype(f32)).astype(bf16)
-    mat[:, 0:112] = hi
-    mat[:, 112:224] = lo
+    for n, (mat, plane, band) in enumerate(mats):
+        k0 = picked[:, 256 * n : 256 * n + 128]
+        k1 = picked[:, 256 * n + 128 : 256 * n + 256]
+        rows = []
+        for b in range(2):
+            for q_ in range(2):
+                for c_ in range(3):
+                    for dx_ in range(2):
+                        r = 3 * (plane * q_ + band * b + dx_) + c_
+                        rows.append(jnp.where(m0, k0[r : r + 1], 0.0) + jnp.where(m1, k1[r : r + 1], 0.0))
+        full = jnp.concatenate(rows, axis=0)
+        hi = full.astype(bf16)
+        lo = (full - hi.astype(f32)).astype(bf16)
+        mat[:, 0:112] = hi[:, 0:112]
+        mat[:, 112:224] = lo[:, 0:112]
 
 
 def prepare(segments, p, work):
@@ -187,8 +192,7 @@
     for copy in copies:
         copy.start()
     copies[0].wait()
-    build_matrix(stiff_s[...], mat, 4, 2)
-    build_matrix(stiff_s[...], mat_y, 2, 4)
+    build_matrices(stiff_s[...], ((mat, 4, 2), (mat_y, 2, 4)))
     for copy in copies[1:]:
         copy.wait()
 
@@ -318,7 +322,7 @@
     )(disp, dens, mat, ends, top)
 
 
-def rim_kernel(flags, got_even, got_odd, up, down, mat_y, src, rim, msg_even, msg_odd, low_s, high_s, t_s, *work):
+def rim_kernel(flags, got_odd, got_even, up, down, mat_y, src, rim, msg_even, msg_odd, low_s, high_s, t_s, *work):
     ny, rows, nx = src.shape
     nz = rows - 2 * OFF
     odd = flags[5] == 1
@@ -335,8 +339,8 @@
         rim[y, 5:8] = jnp.zeros((3, nx), f32)
     for j in range(4):
         y = j if j < 2 else ny - 4 + j
-        t_s[j] = src[y]
-        put_rim(t_s, j, rim[y], nz)
+        t_s[j, 0:nz] = src[y, OFF : OFF + nz]
+        t_s[j, nz : nz + 8] = rim[y]
     odd = flags[4] == 1
     msg_even[...] = jnp.where(odd, t_s[0:2], t_s[2:4])
     msg_odd[...] = jnp.where(odd, t_s[2:4], t_s[0:2])
@@ -347,26 +351,26 @@
     s[y, OFF + nz - 1 : OFF + nz + 2] = rim[2:5]
 
 
-def rim_call(flags, got_even, got_odd, up, down, mat_y, src):
+def rim_call(flags, got_odd, got_even, up, down, mat_y, src):
     ny, rows, nx = src.shape
     return pl.pallas_call(
         rim_kernel,
         in_specs=[SMEM] + [VMEM] * 6,
         out_shape=(
             jax.ShapeDtypeStruct((ny, 8, nx), f32),
-            jax.ShapeDtypeStruct((2, rows, nx), f32),
-            jax.ShapeDtypeStruct((2, rows, nx), f32),
+            jax.ShapeDtypeStruct((2, rows - OFF, nx), f32),
+            jax.ShapeDtypeStruct((2, rows - OFF, nx), f32),
         ),
         scratch_shapes=[
             pltpu.VMEM((12, ny, nx), f32),
             pltpu.VMEM((12, ny, nx), f32),
-            pltpu.VMEM((4, rows, nx), f32),
+            pltpu.VMEM((4, rows - OFF, nx), f32),
         ]
         + workspace(2, 2 * (ny // 8), nx),
         compiler_params=pltpu.CompilerParams(vmem_limit_bytes=16 * 2**20),
         cost_estimate=estimate(2),
         name="energy_rim",
-    )(flags, got_even, got_odd, up, down, mat_y, src)
+    )(flags, got_odd, got_even, up, down, mat_y, src)
 
 
 def filter_block(s_s, d_s, n, z_edges, y_edges, finish, unroll):
@@ -413,13 +417,6 @@
 def table(n, nz, nx, amp, low, high, now, fine_s, vol, tgt, start):
     spacing = 2.0 * bracket_end / POINTS
 
-    def fine(j, _):
-        a = amp[j]
-        for f in range(FINE):
-            fine_s[f, j] = a * math.exp(-0.5 * spacing * f)
-        return 0
-
-    lax.fori_loop(0, n, fine, 0)
     pair = 2
     for first in range(0, COARSE, pair):
         inverse = [math.exp(0.5 * (-bracket_end + spacing * FINE * i)) for i in range(first, first + pair)]
@@ -433,7 +430,11 @@
                 for i, c in enumerate(inverse):
                     acc[pair * FINE + i] = acc[pair * FINE + i] + d * c
                 for f in range(FINE):
-                    t = fine_s[f, j, at]
+                    if first == 0:
+                        t = amp[j, at] * math.exp(-0.5 * spacing * f)
+                        fine_s[f, j, at] = t
+                    else:
+                        t = fine_s[f, j, at]
                     for i in range(pair):
                         acc[i * FINE + f] = acc[i * FINE + f] + jnp.minimum(jnp.maximum(t, los[i]), his[i])
             return tuple(acc)
@@ -493,13 +494,19 @@
 
 
 def outer_kernel(
-    flags, src, rim, got_even, got_odd, dens, passive, solid, vol_i, tgt_i,
+    flags, src, rim, got_odd, got_even, dens, passive, solid, vol_i, tgt_i,
     amp, low, high, excess, s_s, d_s, now_s, fine_s, vol, tgt,
 ):
     ny, nz, nx = dens.shape
     odd = flags[4] == 1
-    s_s[0, 0:2] = jnp.where(odd, got_even[...], got_odd[...])
-    s_s[1, 4:6] = jnp.where(odd, got_odd[...], got_even[...])
+    got = (jnp.where(odd, got_even[...], got_odd[...]), jnp.where(odd, got_odd[...], got_even[...]))
+    for b in range(2):
+        for j in range(2):
+            at = j if b == 0 else 4 + j
+            s_s[b, at, 0:OFF] = jnp.zeros((OFF, nx), f32)
+            s_s[b, at, OFF : OFF + nz] = got[b][j, 0:nz]
+            s_s[b, at, OFF + nz :] = jnp.zeros((OFF, nx), f32)
+            put_rim(s_s.at[b], at, got[b][j, nz : nz + 8], nz)
     for j in range(4):
         s_s[0, 2 + j] = src[j]
         put_rim(s_s.at[0], 2 + j, rim[j], nz)
@@ -528,7 +535,7 @@
     excess[...] = jnp.sum(jnp.transpose(jnp.concatenate(over, axis=0)), axis=0, keepdims=True)
 
 
-def outer_call(flags, src, rim, got_even, got_odd, dens, passive, solid, vol_i, tgt_i):
+def outer_call(flags, src, rim, got_odd, got_even, dens, passive, solid, vol_i, tgt_i):
     ny, nz, nx = dens.shape
     rows = nz + 2 * OFF
     field = jax.ShapeDtypeStruct((4, nz, nx), f32)
@@ -547,7 +554,7 @@
         compiler_params=pltpu.CompilerParams(vmem_limit_bytes=16 * 2**20),
         cost_estimate=estimate(3),
         name="filter_outer",
-    )(flags, src, rim, got_even, got_odd, dens, passive, solid, vol_i, tgt_i)
+    )(flags, src, rim, got_odd, got_even, dens, passive, solid, vol_i, tgt_i)
 
 
 def update_kernel(tables, amp_i, low_i, high_i, amp_o, low_o, high_o, new, logm):
@@ -612,15 +619,15 @@
     ends, up, down = ends_call(disp, dens, mat)
     top, up, down, z_even, z_odd = top_call(flags, disp, dens, fy, mat, ends, up, down)
 
+    z_got_even = swap(z_even, "gz", 0)
     z_got_odd = swap(z_odd, "gz", 1)
-    z_got_even = swap(z_even, "gz", 0)
     src = middle_call(disp, dens, mat, ends, top)
-    rim, msg_even, msg_odd = rim_call(flags, z_got_even, z_got_odd, up, down, mat_y, src)
-
+    rim, msg_even, msg_odd = rim_call(flags, z_got_odd, z_got_even, up, down, mat_y, src)
+
+    got_even = swap(msg_even, "gy", 0)
     got_odd = swap(msg_odd, "gy", 1)
-    got_even = swap(msg_even, "gy", 0)
     *inner, vol, tgt = inner_call(flags, src, rim, dens, passive, solid)
-    *outer, excess = outer_call(flags, src, rim, got_even, got_odd, dens, passive, solid, vol, tgt)
+    *outer, excess = outer_call(flags, src, rim, got_odd, got_even, dens, passive, solid, vol, tgt)
 
     everyone = jnp.broadcast_to(excess, (gz * gy, POINTS))
     tables = lax.all_to_all(everyone, ("gz", "gy"), 0, 0, tiled=True)

time: 47.4 us -> 48 us (1.013)
  starting transfers between devices: 5.38 us -> 10.8 us
  blocking collectives: 15.9 us -> 11.4 us
    ppermute x4, starting transfers between devices: 4.09 us -> 9.46 us  [swap(): return lax.ppermute(value, axis, pairs)]
    all_to_all x1, blocking collectives: 15.9 us -> 11.4 us  [on_device(): tables = lax.all_to_all(everyone, ('gz', 'gy'), 0, 0, tiled=True)]
where the time goes in v9:
time: 48 us; the launch traced here: 47.8 us
  Pallas kernels  21.1 us (44%)
  blocking collectives  11.4 us (24%)
  starting transfers between devices  10.8 us (22%)
  waiting for transfers between devices  2.61 us (5%)
  local copies, waits for them, and re-layouts  1.07 us (2%)
  between operations  0.78 us (2%)
    all_to_all x1, blocking collectives, on_device(): tables = lax.all_to_all(everyone, ('gz', 'gy'), 0, 0, tiled=True)  11.4 us
    ppermute x4, starting transfers between devices, swap(): return lax.ppermute(value, axis, pairs)  9.46 us
    pallas_call x1, Pallas kernels, inner_call(): pl.pallas_call(inner_kernel, in_specs=[SMEM] + [VMEM] * 5, out_shape=(fie...  7.63 us
    pallas_call x1, Pallas kernels, outer_call(): pl.pallas_call(outer_kernel, in_specs=[SMEM] + [VMEM] * 9, out_shape=(fie...  3.1 us
    pallas_call x1, Pallas kernels, ends_call(): pl.pallas_call(ends_kernel, in_specs=[VMEM] * 3, out_shape=(jax.ShapeDtyp...  2.92 us
    pallas_call x1, Pallas kernels, middle_call(): pl.pallas_call(middle_kernel, in_specs=[VMEM] * 5, out_shape=jax.ShapeDty...  2.88 us
    ppermute x1, waiting for transfers between devices, to_lower(): return lax.ppermute(value, axis, [(i + 1, i) for i in range(count - 1)])  2.6 us
    pallas_call x1, Pallas kernels, load_call(): pl.pallas_call(load_kernel, in_specs=[HBM, HBM, HBM], out_shape=(jax.Shap...  1.71 us
  transfers between devices with their start and end apart: 5, of which 1 were waited for; matrix products, arithmetic and copies ran while one was open for 0% of the time, Pallas kernels for 32%

profile of v9, /device:TPU:0, one launch (start us, length us, event | category | flops | bytes accessed | tf_op | source)
XLA Modules:
  0.0 47.8 jit_solution(7247813312306924967)
XLA Ops:
  0.6 0.9 %slice_bitcast_fusion = f32[9,32,128]{2,1,0:T(8,128)S(1)} fusion(f32[9,16,32,128]{3,2,1,0:T(8,128)} %disp.1), kind=kLoop, calls=%fused_computation | loop fusion | bytes 294912 | tf_op jit(solution)/shard_map/squeeze | solution.py:617
  1.6 1.3 %collective-permute-start = (f32[9,32,128]{2,1,0:T(8,128)S(1)}, f32[9,32,128]{2,1,0:T(8,128)S(1)}, u32[]{:S(2)}, u32[]{:S(2)}) collective-permute-start(f32[9,32,128]{2,1,0:T(8,128)S(1)} %slice_bitcast_fusion), channel_id=1, source_target_pairs={{1,0},{2,1},{3,2},{4,3},{5,4},{6,5},{7,6},{9,8},{10,9},{11,10},{12... | collective-permute-start | bytes 442376 | tf_op jit(solution)/shard_map/ppermute | solution.py:597
  2.9 1.7 %load.1 = (f32[9,16,32,128]{3,2,1,0:T(8,128)S(1)}, f32[16,32,128]{2,1,0:T(8,128)S(1)}, bf16[192,224]{1,0:T(8,128)(2,1)S(1)}, bf16[192,224]{1,0:T(8,128)(2,1)S(1)}) custom-call(f32[9,16,32,128]{3,2,1,0:T(8,128)} %disp.1, f32[16,32,128]{2,1,0:T(8,128)} %dens.1, f32[24,24]{1,0:T(8,128)} %stiff.1), custom_call_target="tpu_custom_call" | custom-call | flops 2000000000 | bytes 1048576 | tf_op jit(solution)/shard_map/load/pallas_call | solution.py:202
  4.6 2.9 %energy_ends.1 = (f32[16,16,128]{2,1,0:T(8,128)S(1)}, f32[12,16,128]{2,1,0:T(8,128)S(1)}, f32[12,16,128]{2,1,0:T(8,128)S(1)}) custom-call(f32[9,16,32,128]{3,2,1,0:T(8,128)S(1)} %get-tuple-element.28.disp, f32[16,32,128]{2,1,0:T(8,128)S(1)} %get-tuple-element.29.dens, bf16[192,224]{1,0:T(8,128)(2,1)S(1)} %get-tuple-element.30.mat), custom_call_target="tpu_custom_call" | custom-call | flops 4000000000 | bytes 1048576 | tf_op jit(solution)/shard_map/energy_ends/pallas_call | solution.py:246
  7.5 0.1 stack.27
  7.6 2.6 %collective-permute-done.fy = f32[9,32,128]{2,1,0:T(8,128)S(1)} collective-permute-done((f32[9,32,128]{2,1,0:T(8,128)S(1)}, f32[9,32,128]{2,1,0:T(8,128)S(1)}, u32[]{:S(2)}, u32[]{:S(2)}) %collective-permute-start) | collective-permute-done | bytes 147488 | tf_op jit(solution)/shard_map/ppermute | solution.py:597
  10.2 1.0 %energy_top.1 = (f32[32,128]{1,0:T(8,128)S(1)}, f32[12,16,128]{2,1,0:T(8,128)S(1)}, f32[12,16,128]{2,1,0:T(8,128)S(1)}, f32[12,16,128]{2,1,0:T(8,128)S(1)}, f32[12,16,128]{2,1,0:T(8,128)S(1)}) custom-call(s32[6]{0:T(128)S(1)} %convert_element_type.3.flags, f32[9,16,32,128]{3,2,1,0:T(8,128)S(1)} %get-tuple-element.28.disp, ...), custom_call_target="tpu_custom_call" | custom-call | flops 1000000000 | bytes 1048576 | tf_op jit(solution)/shard_map/energy_top/pallas_call | solution.py:280
  11.2 0.7 %collective-permute-start.1 = (f32[12,16,128]{2,1,0:T(8,128)S(1)}, f32[12,16,128]{2,1,0:T(8,128)S(1)}, u32[]{:S(2)}, u32[]{:S(2)}) collective-permute-start(f32[12,16,128]{2,1,0:T(8,128)S(1)} %get-tuple-element.35), channel_id=1, source_target_pairs={{8,16},{16,8},{9,17},{17,9},{10,18},{18,10},{11,19},{19,11},{12,20... | collective-permute-start | bytes 294920 | tf_op jit(solution)/shard_map/ppermute | solution.py:604
  11.9 3.2 %collective-permute-start.2 = (f32[12,16,128]{2,1,0:T(8,128)S(1)}, f32[12,16,128]{2,1,0:T(8,128)S(1)}, u32[]{:S(2)}, u32[]{:S(2)}) collective-permute-start(f32[12,16,128]{2,1,0:T(8,128)S(1)} %get-tuple-element.36), channel_id=1, source_target_pairs={{0,8},{8,0},{16,24},{24,16},{1,9},{9,1},{17,25},{25,17},{2,10},{10... | collective-permute-start | bytes 294920 | tf_op jit(solution)/shard_map/ppermute | solution.py:604
  15.1 2.9 %energy_middle.1.src = f32[16,48,128]{2,1,0:T(8,128)S(1)} custom-call(f32[9,16,32,128]{3,2,1,0:T(8,128)S(1)} %get-tuple-element.28.disp, f32[16,32,128]{2,1,0:T(8,128)S(1)} %get-tuple-element.29.dens, bf16[192,224]{1,0:T(8,128)(2,1)S(1)} %get-tuple-element.30.mat, f32[16,16,128]{2,1,0:T(8,128)S(1)} %get-tuple-element.31.ends, ...), custom_call_target="tpu_custom_call" | custom-call | flops 4000000000 | bytes 1048576 | tf_op jit(solution)/shard_map/energy_middle/pallas_call | solution.py:314
  18.0 0.0 collective-permute-done.1.got_odd
  18.0 0.0 collective-permute-done.2.got_even
  18.0 0.0 copy-start
  18.0 0.0 copy-start.1
  18.0 1.0 %energy_rim.1 = (f32[16,8,128]{2,1,0:T(8,128)S(1)}, f32[2,40,128]{2,1,0:T(8,128)S(1)}, f32[2,40,128]{2,1,0:T(8,128)S(1)}) custom-call(s32[6]{0:T(128)S(1)} %convert_element_type.3.flags, f32[12,16,128]{2,1,0:T(8,128)S(1)} %collective-permute-done.1.got_odd, f32[12,16,128]{2,1,0:T(8,128)S(1)} %collective-permute-done.2.got_even, ...), custom_call_target="tpu_custom_call" | custom-call | flops 2000000000 | bytes 1048576 | tf_op jit(solution)/shard_map/energy_rim/pallas_call | solution.py:356
  19.0 0.7 %collective-permute-start.3 = (f32[2,40,128]{2,1,0:T(8,128)S(1)}, f32[2,40,128]{2,1,0:T(8,128)S(1)}, u32[]{:S(2)}, u32[]{:S(2)}) collective-permute-start(f32[2,40,128]{2,1,0:T(8,128)S(1)} %get-tuple-element.41), channel_id=1, source_target_pairs={{1,2},{2,1},{3,4},{4,3},{5,6},{6,5},{9,10},{10,9},{11,12},{12,11},... | collective-permute-start | bytes 122888 | tf_op jit(solution)/shard_map/ppermute | solution.py:604
  19.7 4.9 %collective-permute-start.4 = (f32[2,40,128]{2,1,0:T(8,128)S(1)}, f32[2,40,128]{2,1,0:T(8,128)S(1)}, u32[]{:S(2)}, u32[]{:S(2)}) collective-permute-start(f32[2,40,128]{2,1,0:T(8,128)S(1)} %get-tuple-element.42), channel_id=1, source_target_pairs={{0,1},{1,0},{2,3},{3,2},{4,5},{5,4},{6,7},{7,6},{8,9},{9,8},{10,11... | collective-permute-start | bytes 122888 | tf_op jit(solution)/shard_map/ppermute | solution.py:604
  24.6 0.0 copy-done
  24.6 7.6 %filter_inner.1 = (f32[12,32,128]{2,1,0:T(8,128)S(1)}, f32[12,32,128]{2,1,0:T(8,128)S(1)}, f32[12,32,128]{2,1,0:T(8,128)S(1)}, f32[2048,128]{1,0:T(8,128)S(1)}, f32[128,128]{1,0:T(8,128)S(1)}) custom-call(s32[6]{0:T(128)S(1)} %convert_element_type.3.flags, f32[16,48,128]{2,1,0:T(8,128)S(1)} %energy_middle.1.src, f32[16,8,128]{2,1,0:T(8,128)S(1)} %get-tuple-element.40.rim, ...), custom_call_target="tpu_custom_call" | custom-call | flops 8999999488 | bytes 1048576 | tf_op jit(solution)/shard_map/filter_inner/pallas_call | solution.py:474
  32.3 0.0 collective-permute-done.3.got_odd
  32.3 0.0 collective-permute-done.4.got_even
  32.3 3.1 %filter_outer.1 = (f32[4,32,128]{2,1,0:T(8,128)S(1)}, f32[4,32,128]{2,1,0:T(8,128)S(1)}, f32[4,32,128]{2,1,0:T(8,128)S(1)}, f32[1,256]{1,0:T(1,128)S(1)}) custom-call(s32[6]{0:T(128)S(1)} %convert_element_type.3.flags, f32[16,48,128]{2,1,0:T(8,128)S(1)} %energy_middle.1.src, f32[16,8,128]{2,1,0:T(8,128)S(1)} %get-tuple-element.40.rim, ...), custom_call_target="tpu_custom_call" | custom-call | flops 3000000000 | bytes 1048576 | tf_op jit(solution)/shard_map/filter_outer/pallas_call | solution.py:542
  35.4 11.4 %all_to_all.8 = f32[32,1,256]{2,1,0:T(1,128)S(1)} all-to-all(f32[32,1,256]{2,1,0:T(1,128)S(1)} %broadcast_in_dim.2), channel_id=1, replica_groups=mesh['gz'=4,'gy'=8] {'gz','gy'}, dimensions={0} | all-to-all | bytes 65536 | tf_op jit(solution)/shard_map/all_to_all | solution.py:633
  46.8 0.9 %update.1 = (f32[16,32,128]{2,1,0:T(8,128)}, f32[1]{0:T(128)}) custom-call(f32[32,256]{1,0:T(8,128)S(1)} %bitcast.15, f32[12,32,128]{2,1,0:T(8,128)S(1)} %get-tuple-element.46.amp_i, f32[12,32,128]{2,1,0:T(8,128)S(1)} %get-tuple-element.47.low_i, f32[12,32,128]{2,1,0:T(8,128)S(1)} %get-tuple-element.48.high_i, f32[4,32,128]{2,1,0:T(8,128)S(1)} %get-tuple-element.49.amp_o, ...), custom_call_target="tpu_custom_call" | custom-call | flops 1000000000 | bytes 1048576 | tf_op jit(solution)/shard_map/update/pallas_call | solution.py:584
  (4 shorter events, 0.0 us)
Async XLA Ops:
  1.6 8.7 %collective-permute-start = (f32[9,32,128]{2,1,0:T(8,128)S(1)}, f32[9,32,128]{2,1,0:T(8,128)S(1)}, u32[]{:S(2)}, u32[]{:S(2)}) collective-permute-start(f32[9,32,128]{2,1,0:T(8,128)S(1)} %slice_bitcast_fusion), channel_id=1, source_target_pairs={{1,0},{2,1},{3,2},{4,3},{5,4},{6,5},{7,6},{9,8},{10,9},{11,10},{12... | collective-permute-start | bytes 442376 | tf_op jit(solution)/shard_map/ppermute | solution.py:597
  11.2 6.7 %collective-permute-start.1 = (f32[12,16,128]{2,1,0:T(8,128)S(1)}, f32[12,16,128]{2,1,0:T(8,128)S(1)}, u32[]{:S(2)}, u32[]{:S(2)}) collective-permute-start(f32[12,16,128]{2,1,0:T(8,128)S(1)} %get-tuple-element.35), channel_id=1, source_target_pairs={{8,16},{16,8},{9,17},{17,9},{10,18},{18,10},{11,19},{19,11},{12,20... | collective-permute-start | bytes 294920 | tf_op jit(solution)/shard_map/ppermute | solution.py:604
  11.9 6.1 %collective-permute-start.2 = (f32[12,16,128]{2,1,0:T(8,128)S(1)}, f32[12,16,128]{2,1,0:T(8,128)S(1)}, u32[]{:S(2)}, u32[]{:S(2)}) collective-permute-start(f32[12,16,128]{2,1,0:T(8,128)S(1)} %get-tuple-element.36), channel_id=1, source_target_pairs={{0,8},{8,0},{16,24},{24,16},{1,9},{9,1},{17,25},{25,17},{2,10},{10... | collective-permute-start | bytes 294920 | tf_op jit(solution)/shard_map/ppermute | solution.py:604
  18.0 6.6 %copy-start = (s32[16,32,128]{2,1,0:T(8,128)S(1)}, s32[16,32,128]{2,1,0:T(8,128)}, u32[]{:S(2)}) copy-start(s32[16,32,128]{2,1,0:T(8,128)} %passive.3) | copy-start | bytes 786436
  18.0 6.6 %copy-start.1 = (s32[16,32,128]{2,1,0:T(8,128)S(1)}, s32[16,32,128]{2,1,0:T(8,128)}, u32[]{:S(2)}) copy-start(s32[16,32,128]{2,1,0:T(8,128)} %solid.3) | copy-start | bytes 786436
  19.0 13.3 %collective-permute-start.3 = (f32[2,40,128]{2,1,0:T(8,128)S(1)}, f32[2,40,128]{2,1,0:T(8,128)S(1)}, u32[]{:S(2)}, u32[]{:S(2)}) collective-permute-start(f32[2,40,128]{2,1,0:T(8,128)S(1)} %get-tuple-element.41), channel_id=1, source_target_pairs={{1,2},{2,1},{3,4},{4,3},{5,6},{6,5},{9,10},{10,9},{11,12},{12,11},... | collective-permute-start | bytes 122888 | tf_op jit(solution)/shard_map/ppermute | solution.py:604
  19.7 12.6 %collective-permute-start.4 = (f32[2,40,128]{2,1,0:T(8,128)S(1)}, f32[2,40,128]{2,1,0:T(8,128)S(1)}, u32[]{:S(2)}, u32[]{:S(2)}) collective-permute-start(f32[2,40,128]{2,1,0:T(8,128)S(1)} %get-tuple-element.42), channel_id=1, source_target_pairs={{0,1},{1,0},{2,3},{3,2},{4,5},{5,4},{6,7},{7,6},{8,9},{9,8},{10,11... | collective-permute-start | bytes 122888 | tf_op jit(solution)/shard_map/ppermute | solution.py:604

commit v10 on v9

--- a/solution.py
+++ b/solution.py
@@ -169,54 +169,66 @@
     ]
 
 
-def sweep(rows, segments, put, work):
+def sweep(rows, segments, put, work, ready=None):
     work[1][...] = jnp.zeros_like(work[1])
+
+    def plane(p):
+        if ready is not None:
+            ready(p)
+        prepare(segments(p), p, work)
+
     for p in range(2):
-        prepare(segments(p), p, work)
+        plane(p)
 
     def body(y, _):
         put(y)
-        prepare(segments(y + 2), y + 2, work)
+        plane(y + 2)
         return 0
 
     lax.fori_loop(0, rows - 1, body, 0, unroll=2)
     put(rows - 1)
 
 
-def load_kernel(disp, dens, stiff, disp_v, dens_v, mat, mat_y, stiff_s, sems):
-    copies = [
-        pltpu.make_async_copy(stiff, stiff_s, sems.at[0]),
-        pltpu.make_async_copy(disp, disp_v, sems.at[1]),
-        pltpu.make_async_copy(dens, dens_v, sems.at[2]),
-    ]
-    for copy in copies:
-        copy.start()
-    copies[0].wait()
+def face_kernel(disp, face, sem):
+    copy = pltpu.make_async_copy(disp.at[:, 0], face, sem)
+    copy.start()
+    copy.wait()
+
+
+def face_call(disp):
+    _, _, nz, nx = disp.shape
+    return pl.pallas_call(
+        face_kernel,
+        in_specs=[HBM],
+        out_shape=jax.ShapeDtypeStruct((9, nz, nx), f32),
+        scratch_shapes=[pltpu.SemaphoreType.DMA],
+        compiler_params=pltpu.CompilerParams(vmem_limit_bytes=2**20),
+        name="face",
+    )(disp)
+
+
+def extra(ref, row):
+    ny = ref.shape[1]
+    return 11 + row // ny, slice(row % ny, row % ny + 1)
+
+
+def ends_kernel(flags, disp_h, dens_h, stiff, disp, dens, mat, mat_y, ends, up, down, msg_even, msg_odd, stiff_s, sems, *work):
+    _, ny, nz, nx = disp.shape
+
+    def copy(p):
+        return pltpu.make_async_copy(disp_h.at[:, p], disp.at[:, p], sems.at[p])
+
+    copy_k = pltpu.make_async_copy(stiff, stiff_s, sems.at[ny])
+    copy_d = pltpu.make_async_copy(dens_h, dens, sems.at[ny + 1])
+    copy_k.start()
+    for p in range(2):
+        copy(p).start()
+    copy_d.start()
+    for p in range(2, ny):
+        copy(p).start()
+    copy_k.wait()
     build_matrices(stiff_s[...], ((mat, 4, 2), (mat_y, 2, 4)))
-    for copy in copies[1:]:
-        copy.wait()
-
-
-def load_call(disp, dens, stiff):
-    matrix = jax.ShapeDtypeStruct((192, 224), bf16)
-    return pl.pallas_call(
-        load_kernel,
-        in_specs=[HBM, HBM, HBM],
-        out_shape=(
-            jax.ShapeDtypeStruct(disp.shape, f32),
-            jax.ShapeDtypeStruct(dens.shape, f32),
-            matrix,
-            matrix,
-        ),
-        scratch_shapes=[pltpu.VMEM((24, 24), f32), pltpu.SemaphoreType.DMA((3,))],
-        compiler_params=pltpu.CompilerParams(vmem_limit_bytes=16 * 2**20),
-        cost_estimate=estimate(2),
-        name="load",
-    )(disp, dens, stiff)
-
-
-def ends_kernel(disp, dens, mat, ends, up, down, *work):
-    _, ny, nz, nx = disp.shape
+    copy_d.wait()
 
     def segments(p):
         return lambda i: [(disp[i, p, 0:8], disp[i, p, 8:9]), (disp[i, p, nz - 8 : nz], None)]
@@ -225,7 +237,9 @@
         d = jnp.concatenate([dens[y, 0:8], dens[y, nz - 8 : nz]], axis=0)
         ends[y] = energy_rows(y, mat, work, d)
 
-    sweep(ny - 1, segments, put, work)
+    sweep(ny - 1, segments, put, work, lambda p: copy(p).wait())
+    for ref in (up, down):
+        ref[9:] = jnp.zeros((ref.shape[0] - 9, ny, nx), f32)
     for y in range(ny):
         row = slice(y, y + 1)
         for i in range(9):
@@ -236,60 +250,44 @@
             up[10, row] = ends[y, 14:15]
             down[9, row] = ends[y, 0:1]
             down[10, row] = ends[y, 1:2]
-    up[11] = jnp.zeros((ny, nx), f32)
-    down[11] = jnp.zeros((ny, nx), f32)
-
-
-def ends_call(disp, dens, mat):
+    for n, y in enumerate((0, ny - 1)):
+        for i in range(9):
+            up[extra(up, 9 * n + i)] = disp[i, y, nz - 2 : nz - 1]
+            down[extra(down, 9 * n + i)] = disp[i, y, 1:2]
+            down[extra(down, 18 + 9 * n + i)] = disp[i, y, 2:3]
+    up[extra(up, 36)] = dens[ny - 1, nz - 2 : nz - 1]
+    down[extra(down, 36)] = dens[ny - 1, 0:1]
+    down[extra(down, 37)] = dens[ny - 1, 1:2]
+    odd = flags[5] == 1
+    msg_even[...] = jnp.where(odd, down[...], up[...])
+    msg_odd[...] = jnp.where(odd, up[...], down[...])
+
+
+def ends_call(flags, disp, dens, stiff):
     _, ny, nz, nx = disp.shape
-    message = jax.ShapeDtypeStruct((12, ny, nx), f32)
+    message = jax.ShapeDtypeStruct((11 + -(-38 // ny), ny, nx), f32)
+    matrix = jax.ShapeDtypeStruct((192, 224), bf16)
     return pl.pallas_call(
         ends_kernel,
-        in_specs=[VMEM] * 3,
-        out_shape=(jax.ShapeDtypeStruct((ny, 16, nx), f32), message, message),
-        scratch_shapes=workspace(ny, 2, nx),
-        compiler_params=pltpu.CompilerParams(vmem_limit_bytes=16 * 2**20),
+        in_specs=[SMEM] + [HBM] * 3,
+        out_shape=(
+            jax.ShapeDtypeStruct(disp.shape, f32),
+            jax.ShapeDtypeStruct(dens.shape, f32),
+            matrix,
+            matrix,
+            jax.ShapeDtypeStruct((ny, 16, nx), f32),
+        )
+        + (message,) * 4,
+        scratch_shapes=[pltpu.VMEM((24, 24), f32), pltpu.SemaphoreType.DMA((ny + 2,))] + workspace(ny, 2, nx),
+        compiler_params=pltpu.CompilerParams(vmem_limit_bytes=20 * 2**20),
         cost_estimate=estimate(4),
         name="energy_ends",
-    )(disp, dens, mat)
-
-
-def top_kernel(flags, disp, dens, fy, mat, ends, up, down, top, up_full, down_full, msg_even, msg_odd, *work):
+    )(flags, disp, dens, stiff)
+
+
+def middle_kernel(disp, dens, fy, mat, ends, src, *work):
     _, ny, nz, nx = disp.shape
-    work[1][...] = jnp.zeros_like(work[1])
-    prepare(lambda i: [(disp[i, ny - 1], None)], 0, work)
-    prepare(lambda i: [(fy[i], None)], 1, work)
-    up_full[...] = up[...]
-    down_full[...] = down[...]
-    for i in range(9):
-        up_full[11, i : i + 1] = fy[i, nz - 1 : nz]
-        down_full[11, i : i + 1] = fy[i, 0:1]
-    s = energy_rows(0, mat, work, dens[ny - 1])
-    top[...] = s
-    up_full[10, ny - 1 : ny] = s[nz - 2 : nz - 1]
-    down_full[9, ny - 1 : ny] = s[0:1]
-    down_full[10, ny - 1 : ny] = s[1:2]
-    odd = flags[5] == 1
-    msg_even[...] = jnp.where(odd, down_full[...], up_full[...])
-    msg_odd[...] = jnp.where(odd, up_full[...], down_full[...])
-
-
-def top_call(flags, disp, dens, fy, mat, ends, up, down):
-    _, ny, nz, nx = disp.shape
-    message = jax.ShapeDtypeStruct((12, ny, nx), f32)
-    return pl.pallas_call(
-        top_kernel,
-        in_specs=[SMEM] + [VMEM] * 7,
-        out_shape=(jax.ShapeDtypeStruct((nz, nx), f32),) + (message,) * 4,
-        scratch_shapes=workspace(2, nz // 8, nx),
-        compiler_params=pltpu.CompilerParams(vmem_limit_bytes=16 * 2**20),
-        cost_estimate=estimate(1),
-        name="energy_top",
-    )(flags, disp, dens, fy, mat, ends, up, down)
-
-
-def middle_kernel(disp, dens, mat, ends, top, src, *work):
-    _, ny, nz, nx = disp.shape
+    work, last = work[:3], work[3:]
 
     def segments(p):
         return lambda i: [(disp[i, p, 8 : nz - 8], disp[i, p, nz - 8 : nz - 7])]
@@ -305,72 +303,116 @@
         src[y, OFF + nz - 8 : OFF + nz] = ends[y, 8:16]
 
     sweep(ny - 1, segments, put, work)
+    last[1][...] = jnp.zeros_like(last[1])
+    prepare(lambda i: [(disp[i, ny - 1], None)], 0, last)
+    prepare(lambda i: [(fy[i], None)], 1, last)
     frame(ny - 1)
-    src[ny - 1, OFF : OFF + nz] = top[...]
-
-
-def middle_call(disp, dens, mat, ends, top):
+    src[ny - 1, OFF : OFF + nz] = energy_rows(0, mat, last, dens[ny - 1])
+
+
+def middle_call(disp, dens, fy, mat, ends):
     _, ny, nz, nx = disp.shape
     return pl.pallas_call(
         middle_kernel,
         in_specs=[VMEM] * 5,
         out_shape=jax.ShapeDtypeStruct((ny, nz + 2 * OFF, nx), f32),
-        scratch_shapes=workspace(ny, nz // 8 - 2, nx),
+        scratch_shapes=workspace(ny, nz // 8 - 2, nx) + workspace(2, nz // 8, nx),
         compiler_params=pltpu.CompilerParams(vmem_limit_bytes=24 * 2**20),
         cost_estimate=estimate(4),
         name="energy_middle",
-    )(disp, dens, mat, ends, top)
-
-
-def rim_kernel(flags, got_odd, got_even, up, down, mat_y, src, rim, msg_even, msg_odd, low_s, high_s, t_s, *work):
+    )(disp, dens, fy, mat, ends)
+
+
+def rim_kernel(
+    flags, got_even, got_odd, up, down, disp, dens, mat_y, src,
+    rim, nodes, msg_even, msg_odd, low_s, high_s, t_s, *work,
+):
     ny, rows, nx = src.shape
     nz = rows - 2 * OFF
     odd = flags[5] == 1
     low_s[...] = jnp.where(odd, got_even[...], got_odd[...])
     high_s[...] = jnp.where(odd, got_odd[...], got_even[...])
     work[1][...] = jnp.zeros_like(work[1])
-    prepare(lambda i: [(low_s[i], low_s[11, i : i + 1]), (up[i], up[11, i : i + 1])], 0, work)
-    prepare(lambda i: [(down[i], down[11, i : i + 1]), (high_s[i], high_s[11, i : i + 1])], 1, work)
+    prepare(lambda i: [(low_s[i], None), (up[i], None)], 0, work)
+    prepare(lambda i: [(down[i], None), (high_s[i], None)], 1, work)
     s = energy_rows(0, mat_y, work, jnp.concatenate([low_s[9], up[9]], axis=0))
-    columns = (low_s[10], s[0:ny], s[ny : 2 * ny], high_s[9], high_s[10])
+    columns = ((0, low_s[10]), (1, s[0:ny]), (3, s[ny : 2 * ny]), (4, high_s[9]), (5, high_s[10]))
     for y in range(ny):
-        for r, column in enumerate(columns):
+        rim[y] = jnp.zeros((8, nx), f32)
+        for r, column in columns:
             rim[y, r : r + 1] = column[y : y + 1]
-        rim[y, 5:8] = jnp.zeros((3, nx), f32)
-    for j in range(4):
-        y = j if j < 2 else ny - 4 + j
-        t_s[j, 0:nz] = src[y, OFF : OFF + nz]
-        t_s[j, nz : nz + 8] = rim[y]
+    half = 2 * (nz + 8)
+    zero = jnp.zeros((1, nx), f32)
+    for n, y in enumerate((0, ny - 1)):
+        row = slice(y, y + 1)
+        for i in range(9):
+            window = jnp.concatenate(
+                [
+                    low_s[extra(low_s, 9 * n + i)],
+                    low_s[i, row],
+                    disp[i, y, 0:1],
+                    disp[i, y, nz - 1 : nz],
+                    high_s[i, row],
+                    high_s[extra(high_s, 9 * n + i)],
+                    high_s[extra(high_s, 18 + 9 * n + i)],
+                    zero,
+                ],
+                axis=0,
+            )
+            nodes[n, i] = window
+            t_s[n, half + 8 * i : half + 8 * i + 8] = window
+        nodes[n, 9] = jnp.concatenate(
+            [
+                low_s[extra(low_s, 36)],
+                low_s[9, ny - 1 : ny],
+                zero,
+                dens[ny - 1, nz - 1 : nz],
+                high_s[extra(high_s, 36)],
+                high_s[extra(high_s, 37)],
+                zero,
+                zero,
+            ],
+            axis=0,
+        )
+        t_s[n, half + 72 : half + 80] = nodes[n, 9]
+        for j in range(2):
+            at = j * (nz + 8)
+            yy = j if n == 0 else ny - 2 + j
+            t_s[n, at : at + nz] = src[yy, OFF : OFF + nz]
+            t_s[n, at + nz : at + nz + 8] = rim[yy]
     odd = flags[4] == 1
-    msg_even[...] = jnp.where(odd, t_s[0:2], t_s[2:4])
-    msg_odd[...] = jnp.where(odd, t_s[2:4], t_s[0:2])
+    msg_even[...] = jnp.where(odd, t_s[0], t_s[1])
+    msg_odd[...] = jnp.where(odd, t_s[1], t_s[0])
 
 
 def put_rim(s, y, rim, nz):
     s[y, OFF - 2 : OFF] = rim[0:2]
-    s[y, OFF + nz - 1 : OFF + nz + 2] = rim[2:5]
-
-
-def rim_call(flags, got_odd, got_even, up, down, mat_y, src):
+    s[y, OFF + nz - 1 : OFF + nz + 2] = rim[3:6]
+
+
+def rim_call(flags, got_even, got_odd, up, down, disp, dens, mat_y, src):
     ny, rows, nx = src.shape
+    nz = rows - 2 * OFF
+    size = 2 * (nz + 8) + 80
     return pl.pallas_call(
         rim_kernel,
-        in_specs=[SMEM] + [VMEM] * 6,
+        in_specs=[SMEM] + [VMEM] * 8,
         out_shape=(
             jax.ShapeDtypeStruct((ny, 8, nx), f32),
-            jax.ShapeDtypeStruct((2, rows - OFF, nx), f32),
-            jax.ShapeDtypeStruct((2, rows - OFF, nx), f32),
+            jax.ShapeDtypeStruct((2, 10, 8, nx), f32),
+            jax.ShapeDtypeStruct((size, nx), f32),
+            jax.ShapeDtypeStruct((size, nx), f32),
         ),
         scratch_shapes=[
-            pltpu.VMEM((12, ny, nx), f32),
-            pltpu.VMEM((12, ny, nx), f32),
-            pltpu.VMEM((4, rows - OFF, nx), f32),
+            pltpu.VMEM(up.shape, f32),
+            pltpu.VMEM(up.shape, f32),
+            pltpu.VMEM((2, size, nx), f32),
         ]
         + workspace(2, 2 * (ny // 8), nx),
         compiler_params=pltpu.CompilerParams(vmem_limit_bytes=16 * 2**20),
         cost_estimate=estimate(2),
         name="energy_rim",
-    )(flags, got_odd, got_even, up, down, mat_y, src)
+    )(flags, got_even, got_odd, up, down, disp, dens, mat_y, src)
 
 
 def filter_block(s_s, d_s, n, z_edges, y_edges, finish, unroll):
@@ -452,25 +494,25 @@
 
 def inner_kernel(flags, src, rim, dens, passive, solid, amp, low, high, vol, tgt, s_s, d_s, now_s, fine_s):
     ny, nz, nx = dens.shape
-    s_s[...] = src[...]
+    s_s[...] = src[0 : ny - 1]
 
     def fix(y, _):
         put_rim(s_s, y, rim[y], nz)
         return 0
 
-    lax.fori_loop(0, ny, fix, 0, unroll=4)
+    lax.fori_loop(0, ny - 1, fix, 0, unroll=5)
 
     def finish(j, p3):
         y = j + 2
         amp[j], low[j], high[j], now_s[j] = limits(p3, dens[y], passive[y] == 1, solid[y] == 1)
 
-    filter_block(s_s, d_s, ny, (flags[2], flags[3]), None, finish, 4)
-    table(ny - 4, nz, nx, amp, low, high, now_s, fine_s, vol, tgt, None)
+    filter_block(s_s, d_s, ny - 1, (flags[2], flags[3]), None, finish, 4)
+    table(ny - 5, nz, nx, amp, low, high, now_s, fine_s, vol, tgt, None)
 
 
 def inner_call(flags, src, rim, dens, passive, solid):
     ny, nz, nx = dens.shape
-    field = jax.ShapeDtypeStruct((ny - 4, nz, nx), f32)
+    field = jax.ShapeDtypeStruct((ny - 5, nz, nx), f32)
     return pl.pallas_call(
         inner_kernel,
         in_specs=[SMEM] + [VMEM] * 5,
@@ -482,10 +524,10 @@
             jax.ShapeDtypeStruct((8 * COARSE, nx), f32),
         ),
         scratch_shapes=[
-            pltpu.VMEM((ny, nz + 2 * OFF, nx), f32),
-            pltpu.VMEM((ny - 2, nz + 2 * OFF, nx), f32),
-            pltpu.VMEM((ny - 4, nz, nx), f32),
-            pltpu.VMEM((FINE, ny - 4, nz, nx), f32),
+            pltpu.VMEM((ny - 1, nz + 2 * OFF, nx), f32),
+            pltpu.VMEM((ny - 3, nz + 2 * OFF, nx), f32),
+            pltpu.VMEM((ny - 5, nz, nx), f32),
+            pltpu.VMEM((FINE, ny - 5, nz, nx), f32),
         ],
         compiler_params=pltpu.CompilerParams(vmem_limit_bytes=24 * 2**20),
         cost_estimate=estimate(9),
@@ -494,26 +536,40 @@
 
 
 def outer_kernel(
-    flags, src, rim, got_odd, got_even, dens, passive, solid, vol_i, tgt_i,
-    amp, low, high, excess, s_s, d_s, now_s, fine_s, vol, tgt,
+    flags, src, rim, nodes, got_even, got_odd, mat, dens, passive, solid, vol_i, tgt_i,
+    amp, low, high, excess, s_s, d_s, now_s, fine_s, vol, tgt, below, above, *work,
 ):
     ny, nz, nx = dens.shape
     odd = flags[4] == 1
-    got = (jnp.where(odd, got_even[...], got_odd[...]), jnp.where(odd, got_odd[...], got_even[...]))
-    for b in range(2):
+    below[...] = jnp.where(odd, got_even[...], got_odd[...])
+    above[...] = jnp.where(odd, got_odd[...], got_even[...])
+    half = 2 * (nz + 8)
+
+    def window(ref, i):
+        return ref[half + 8 * i : half + 8 * i + 8]
+
+    work[1][...] = jnp.zeros_like(work[1])
+    prepare(lambda i: [(window(below, i), None), (nodes[1, i], None)], 0, work)
+    prepare(lambda i: [(nodes[0, i], None), (window(above, i), None)], 1, work)
+    corner = energy_rows(0, mat, work, jnp.concatenate([window(below, 9), nodes[1, 9]], axis=0))
+    for b, ref in enumerate((below, above)):
         for j in range(2):
-            at = j if b == 0 else 4 + j
+            at = j if b == 0 else 5 + j
+            start = j * (nz + 8)
             s_s[b, at, 0:OFF] = jnp.zeros((OFF, nx), f32)
-            s_s[b, at, OFF : OFF + nz] = got[b][j, 0:nz]
+            s_s[b, at, OFF : OFF + nz] = ref[start : start + nz]
             s_s[b, at, OFF + nz :] = jnp.zeros((OFF, nx), f32)
-            put_rim(s_s.at[b], at, got[b][j, nz : nz + 8], nz)
+            put_rim(s_s.at[b], at, ref[start + nz : start + nz + 8], nz)
     for j in range(4):
         s_s[0, 2 + j] = src[j]
         put_rim(s_s.at[0], 2 + j, rim[j], nz)
-        s_s[1, j] = src[ny - 4 + j]
-        put_rim(s_s.at[1], j, rim[ny - 4 + j], nz)
+    for j in range(5):
+        s_s[1, j] = src[ny - 5 + j]
+        put_rim(s_s.at[1], j, rim[ny - 5 + j], nz)
+    put_rim(s_s.at[0], 1, corner[0:8], nz)
+    put_rim(s_s.at[1], 4, corner[8:16], nz)
     for b in range(2):
-        y0 = 0 if b == 0 else ny - 2
+        y0 = 0 if b == 0 else ny - 3
 
         def finish(j, p3):
             y = y0 + j
@@ -521,8 +577,8 @@
             amp[at], low[at], high[at], now_s[at] = limits(p3, dens[y], passive[y] == 1, solid[y] == 1)
 
         edges = (flags[0], 1) if b == 0 else (1, flags[1])
-        filter_block(s_s.at[b], d_s.at[b], 6, (flags[2], flags[3]), edges, finish, True)
-    table(4, nz, nx, amp, low, high, now_s, fine_s, vol, tgt, (vol_i, tgt_i))
+        filter_block(s_s.at[b], d_s.at[b], 6 + b, (flags[2], flags[3]), edges, finish, True)
+    table(5, nz, nx, amp, low, high, now_s, fine_s, vol, tgt, (vol_i, tgt_i))
 
     def lanes(ref, count):
         total = ref[pl.ds(0, count, stride=8), :]
@@ -535,26 +591,29 @@
     excess[...] = jnp.sum(jnp.transpose(jnp.concatenate(over, axis=0)), axis=0, keepdims=True)
 
 
-def outer_call(flags, src, rim, got_odd, got_even, dens, passive, solid, vol_i, tgt_i):
+def outer_call(flags, src, rim, nodes, got_even, got_odd, mat, dens, passive, solid, vol_i, tgt_i):
     ny, nz, nx = dens.shape
     rows = nz + 2 * OFF
-    field = jax.ShapeDtypeStruct((4, nz, nx), f32)
+    field = jax.ShapeDtypeStruct((5, nz, nx), f32)
     return pl.pallas_call(
         outer_kernel,
-        in_specs=[SMEM] + [VMEM] * 9,
+        in_specs=[SMEM] + [VMEM] * 11,
         out_shape=(field, field, field, jax.ShapeDtypeStruct((1, POINTS), f32)),
         scratch_shapes=[
-            pltpu.VMEM((2, 6, rows, nx), f32),
-            pltpu.VMEM((2, 4, rows, nx), f32),
-            pltpu.VMEM((4, nz, nx), f32),
-            pltpu.VMEM((FINE, 4, nz, nx), f32),
+            pltpu.VMEM((2, 7, rows, nx), f32),
+            pltpu.VMEM((2, 5, rows, nx), f32),
+            pltpu.VMEM((5, nz, nx), f32),
+            pltpu.VMEM((FINE, 5, nz, nx), f32),
             pltpu.VMEM((8 * POINTS, nx), f32),
             pltpu.VMEM((8 * COARSE, nx), f32),
-        ],
-        compiler_params=pltpu.CompilerParams(vmem_limit_bytes=16 * 2**20),
+            pltpu.VMEM(got_odd.shape, f32),
+            pltpu.VMEM(got_odd.shape, f32),
+        ]
+        + workspace(2, 2, nx),
+        compiler_params=pltpu.CompilerParams(vmem_limit_bytes=20 * 2**20),
         cost_estimate=estimate(3),
         name="filter_outer",
-    )(flags, src, rim, got_odd, got_even, dens, passive, solid, vol_i, tgt_i)
+    )(flags, src, rim, nodes, got_even, got_odd, mat, dens, passive, solid, vol_i, tgt_i)
 
 
 def update_kernel(tables, amp_i, low_i, high_i, amp_o, low_o, high_o, new, logm):
@@ -575,7 +634,7 @@
         return 0
 
     lax.fori_loop(0, inner, body, 0)
-    for j in range(4):
+    for j in range(5):
         new[j if j < 2 else inner + j] = new_row(amp_o[j], low_o[j], high_o[j])
 
 
@@ -585,7 +644,7 @@
         update_kernel,
         in_specs=[VMEM] * 7,
         out_specs=(VMEM, SMEM),
-        out_shape=(jax.ShapeDtypeStruct((n + 4, nz, nx), f32), jax.ShapeDtypeStruct((1,), f32)),
+        out_shape=(jax.ShapeDtypeStruct((n + 5, nz, nx), f32), jax.ShapeDtypeStruct((1,), f32)),
         compiler_params=pltpu.CompilerParams(vmem_limit_bytes=8 * 2**20),
         cost_estimate=estimate(1),
         name="update",
@@ -614,20 +673,18 @@
     dens_hbm = pltpu.with_memory_space_constraint(density, pltpu.HBM)
     stiff_hbm = pltpu.with_memory_space_constraint(stiffness, pltpu.HBM)
 
-    fy = to_lower(displacement[:, 0], "gy")
-    disp, dens, mat, mat_y = load_call(disp_hbm, dens_hbm, stiff_hbm)
-    ends, up, down = ends_call(disp, dens, mat)
-    top, up, down, z_even, z_odd = top_call(flags, disp, dens, fy, mat, ends, up, down)
+    fy = to_lower(face_call(disp_hbm), "gy")
+    disp, dens, mat, mat_y, ends, up, down, z_even, z_odd = ends_call(flags, disp_hbm, dens_hbm, stiff_hbm)
 
     z_got_even = swap(z_even, "gz", 0)
     z_got_odd = swap(z_odd, "gz", 1)
-    src = middle_call(disp, dens, mat, ends, top)
-    rim, msg_even, msg_odd = rim_call(flags, z_got_odd, z_got_even, up, down, mat_y, src)
+    src = middle_call(disp, dens, fy, mat, ends)
+    rim, nodes, msg_even, msg_odd = rim_call(flags, z_got_even, z_got_odd, up, down, disp, dens, mat_y, src)
 
     got_even = swap(msg_even, "gy", 0)
     got_odd = swap(msg_odd, "gy", 1)
     *inner, vol, tgt = inner_call(flags, src, rim, dens, passive, solid)
-    *outer, excess = outer_call(flags, src, rim, got_odd, got_even, dens, passive, solid, vol, tgt)
+    *outer, excess = outer_call(flags, src, rim, nodes, got_even, got_odd, mat, dens, passive, solid, vol, tgt)
 
     everyone = jnp.broadcast_to(excess, (gz * gy, POINTS))
     tables = lax.all_to_all(everyone, ("gz", "gy"), 0, 0, tiled=True)

time: 48 us -> 49.6 us (1.033)
  blocking collectives: 11.4 us -> 17.5 us
  starting transfers between devices: 10.8 us -> 6.31 us
  Pallas kernels: 21.1 us -> 24.6 us
  waiting for transfers between devices: 2.61 us -> 0.01 us
  local copies, waits for them, and re-layouts: 1.07 us -> 0.14 us
    all_to_all x1, blocking collectives: 11.4 us -> 17.5 us  [on_device(): tables = lax.all_to_all(everyone, ('gz', 'gy'), 0, 0, tiled=True)]
    ppermute x4, starting transfers between devices: 9.46 us -> 5.02 us  [swap(): return lax.ppermute(value, axis, pairs)]
    pallas_call x5 -> x4, Pallas kernels: 9.69 us -> 13.3 us  [the longest x1 7.44 us: ends_call(): pl.pallas_call(ends_kernel, in_specs=[SMEM] + [HBM] * 3, out_shape=(jax.S...]
    ppermute x1, waiting for transfers between devices: 2.6 us -> 0.01 us  [to_lower(): return lax.ppermute(value, axis, [(i + 1, i) for i in range(count - 1)])]
    squeeze x1 -> x0, local copies, waits for them, and re-layouts: 0.93 us -> none  [on_device(): fy = to_lower(displacement[:, 0], 'gy')]
  transfers between devices with their start and end apart: 5 -> 5, of which waited for: 1 -> 0; matrix products, arithmetic and copies ran while one was open for 0% -> 0% of each run, Pallas kernels for 32% -> 36%
where the time goes in v10:
time: 49.6 us; the launch traced here: 49.3 us
  Pallas kernels  24.6 us (50%)
  blocking collectives  17.5 us (35%)
  starting transfers between devices  6.31 us (13%)
  between operations  0.79 us (2%)
    all_to_all x1, blocking collectives, on_device(): tables = lax.all_to_all(everyone, ('gz', 'gy'), 0, 0, tiled=True)  17.5 us
    pallas_call x1, Pallas kernels, ends_call(): pl.pallas_call(ends_kernel, in_specs=[SMEM] + [HBM] * 3, out_shape=(jax.S...  7.44 us
    pallas_call x1, Pallas kernels, inner_call(): pl.pallas_call(inner_kernel, in_specs=[SMEM] + [VMEM] * 5, out_shape=(fie...  7.3 us
    ppermute x4, starting transfers between devices, swap(): return lax.ppermute(value, axis, pairs)  5.02 us
    pallas_call x1, Pallas kernels, outer_call(): pl.pallas_call(outer_kernel, in_specs=[SMEM] + [VMEM] * 11, out_shape=(fi...  3.97 us
    pallas_call x1, Pallas kernels, middle_call(): pl.pallas_call(middle_kernel, in_specs=[VMEM] * 5, out_shape=jax.ShapeDty...  3.06 us
    ppermute x1, starting transfers between devices, to_lower(): return lax.ppermute(value, axis, [(i + 1, i) for i in range(count - 1)])  1.29 us
  transfers between devices with their start and end apart: 5, of which 0 were waited for; matrix products, arithmetic and copies ran while one was open for 0% of the time, Pallas kernels for 36%

profile of v10, /device:TPU:0, one launch (start us, length us, event | category | flops | bytes accessed | tf_op | source)
XLA Modules:
  0.0 49.3 jit_solution(11533865631152058148)
XLA Ops:
  0.6 0.9 %face.1 = f32[9,32,128]{2,1,0:T(8,128)S(1)} custom-call(f32[9,16,32,128]{3,2,1,0:T(8,128)} %disp.1), custom_call_target="tpu_custom_call" | custom-call | tf_op jit(solution)/shard_map/face/pallas_call | solution.py:200
  1.6 1.3 %collective-permute-start = (f32[9,32,128]{2,1,0:T(8,128)S(1)}, f32[9,32,128]{2,1,0:T(8,128)S(1)}, u32[]{:S(2)}, u32[]{:S(2)}) collective-permute-start(f32[9,32,128]{2,1,0:T(8,128)S(1)} %face.1), channel_id=1, source_target_pairs={{1,0},{2,1},{3,2},{4,3},{5,4},{6,5},{7,6},{9,8},{10,9},{11,10},{12... | collective-permute-start | bytes 442376 | tf_op jit(solution)/shard_map/ppermute | solution.py:656
  2.9 0.1 stack.27
  3.0 7.4 %energy_ends.1 = (f32[9,16,32,128]{3,2,1,0:T(8,128)S(1)}, f32[16,32,128]{2,1,0:T(8,128)S(1)}, bf16[192,224]{1,0:T(8,128)(2,1)S(1)}, bf16[192,224]{1,0:T(8,128)(2...) custom-call(s32[6]{0:T(128)S(1)} %convert_element_type.3.flags, ...), custom_call_target="tpu_custom_call" | custom-call | flops 4000000000 | bytes 1048576 | tf_op jit(solution)/shard_map/energy_ends/pallas_call | solution.py:270
  10.4 0.5 %collective-permute-start.1 = (f32[14,16,128]{2,1,0:T(8,128)S(1)}, f32[14,16,128]{2,1,0:T(8,128)S(1)}, u32[]{:S(2)}, u32[]{:S(2)}) collective-permute-start(f32[14,16,128]{2,1,0:T(8,128)S(1)} %get-tuple-element.30), channel_id=1, source_target_pairs={{0,8},{8,0},{16,24},{24,16},{1,9},{9,1},{17,25},{25,17},{2,10},{10... | collective-permute-start | bytes 344072 | tf_op jit(solution)/shard_map/ppermute | solution.py:663
  11.0 0.7 %collective-permute-start.2 = (f32[14,16,128]{2,1,0:T(8,128)S(1)}, f32[14,16,128]{2,1,0:T(8,128)S(1)}, u32[]{:S(2)}, u32[]{:S(2)}) collective-permute-start(f32[14,16,128]{2,1,0:T(8,128)S(1)} %get-tuple-element.31), channel_id=1, source_target_pairs={{8,16},{16,8},{9,17},{17,9},{10,18},{18,10},{11,19},{19,11},{12,20... | collective-permute-start | bytes 344072 | tf_op jit(solution)/shard_map/ppermute | solution.py:663
  11.6 0.0 collective-permute-done.fy
  11.6 3.1 %energy_middle.1.src = f32[16,48,128]{2,1,0:T(8,128)S(1)} custom-call(f32[9,16,32,128]{3,2,1,0:T(8,128)S(1)} %get-tuple-element.26.disp, f32[16,32,128]{2,1,0:T(8,128)S(1)} %get-tuple-element.27.dens, f32[9,32,128]{2,1,0:T(8,128)S(1)} %collective-permute-done.fy, bf16[192,224]{1,0:T(8,128)(2,1)S(1)} %get-tuple-element.28.mat, ...), custom_call_target="tpu_custom_call" | custom-call | flops 4000000000 | bytes 1048576 | tf_op jit(solution)/shard_map/energy_middle/pallas_call | solution.py:315
  14.7 0.0 collective-permute-done.1.got_even
  14.7 0.0 collective-permute-done.2.got_odd
  14.7 0.0 copy-start
  14.7 0.0 copy-start.1
  14.7 1.0 %energy_rim.1 = (f32[16,8,128]{2,1,0:T(8,128)S(1)}, f32[2,10,8,128]{3,2,1,0:T(8,128)S(1)}, f32[160,128]{1,0:T(8,128)S(1)}, f32[160,128]{1,0:T(8,128)S(1)}) custom-call(s32[6]{0:T(128)S(1)} %convert_element_type.3.flags, f32[14,16,128]{2,1,0:T(8,128)S(1)} %collective-permute-done.1.got_even, f32[14,16,128]{2,1,0:T(8,128)S(1)} %collective-permute-done.2.got_odd, ...), custom_call_target="tpu_custom_call" | custom-call | flops 2000000000 | bytes 1048576 | tf_op jit(solution)/shard_map/energy_rim/pallas_call | solution.py:397
  15.7 3.2 %collective-permute-start.3 = (f32[160,128]{1,0:T(8,128)S(1)}, f32[160,128]{1,0:T(8,128)S(1)}, u32[]{:S(2)}, u32[]{:S(2)}) collective-permute-start(f32[160,128]{1,0:T(8,128)S(1)} %get-tuple-element.37), channel_id=1, source_target_pairs={{0,1},{1,0},{2,3},{3,2},{4,5},{5,4},{6,7},{7,6},{8,9},{9,8},{10,11... | collective-permute-start | bytes 245768 | tf_op jit(solution)/shard_map/ppermute | solution.py:663
  18.9 0.7 %collective-permute-start.4 = (f32[160,128]{1,0:T(8,128)S(1)}, f32[160,128]{1,0:T(8,128)S(1)}, u32[]{:S(2)}, u32[]{:S(2)}) collective-permute-start(f32[160,128]{1,0:T(8,128)S(1)} %get-tuple-element.38), channel_id=1, source_target_pairs={{1,2},{2,1},{3,4},{4,3},{5,6},{6,5},{9,10},{10,9},{11,12},{12,11},... | collective-permute-start | bytes 245768 | tf_op jit(solution)/shard_map/ppermute | solution.py:663
  19.6 0.0 copy-done
  19.6 0.0 copy-done.1
  19.6 7.3 %filter_inner.1 = (f32[11,32,128]{2,1,0:T(8,128)S(1)}, f32[11,32,128]{2,1,0:T(8,128)S(1)}, f32[11,32,128]{2,1,0:T(8,128)S(1)}, f32[2048,128]{1,0:T(8,128)S(1)}, f32[128,128]{1,0:T(8,128)S(1)}) custom-call(s32[6]{0:T(128)S(1)} %convert_element_type.3.flags, f32[16,48,128]{2,1,0:T(8,128)S(1)} %energy_middle.1.src, f32[16,8,128]{2,1,0:T(8,128)S(1)} %get-tuple-element.35.rim, ...), custom_call_target="tpu_custom_call" | custom-call | flops 8999999488 | bytes 1048576 | tf_op jit(solution)/shard_map/filter_inner/pallas_call | solution.py:516
  26.9 0.0 collective-permute-done.3.got_even
  26.9 0.0 collective-permute-done.4.got_odd
  26.9 4.0 %filter_outer.1 = (f32[5,32,128]{2,1,0:T(8,128)S(1)}, f32[5,32,128]{2,1,0:T(8,128)S(1)}, f32[5,32,128]{2,1,0:T(8,128)S(1)}, f32[1,256]{1,0:T(1,128)S(1)}) custom-call(s32[6]{0:T(128)S(1)} %convert_element_type.3.flags, f32[16,48,128]{2,1,0:T(8,128)S(1)} %energy_middle.1.src, f32[16,8,128]{2,1,0:T(8,128)S(1)} %get-tuple-element.35.rim, ...), custom_call_target="tpu_custom_call" | custom-call | flops 3000000000 | bytes 1048576 | tf_op jit(solution)/shard_map/filter_outer/pallas_call | solution.py:598
  30.9 17.5 %all_to_all.8 = f32[32,1,256]{2,1,0:T(1,128)S(1)} all-to-all(f32[32,1,256]{2,1,0:T(1,128)S(1)} %broadcast_in_dim.2), channel_id=1, replica_groups=mesh['gz'=4,'gy'=8] {'gz','gy'}, dimensions={0} | all-to-all | bytes 65536 | tf_op jit(solution)/shard_map/all_to_all | solution.py:690
  48.4 0.9 %update.1 = (f32[16,32,128]{2,1,0:T(8,128)}, f32[1]{0:T(128)}) custom-call(f32[32,256]{1,0:T(8,128)S(1)} %bitcast.11, f32[11,32,128]{2,1,0:T(8,128)S(1)} %get-tuple-element.42.amp_i, f32[11,32,128]{2,1,0:T(8,128)S(1)} %get-tuple-element.43.low_i, f32[11,32,128]{2,1,0:T(8,128)S(1)} %get-tuple-element.44.high_i, f32[5,32,128]{2,1,0:T(8,128)S(1)} %get-tuple-element.45.amp_o, ...), custom_call_target="tpu_custom_call" | custom-call | flops 1000000000 | bytes 1048576 | tf_op jit(solution)/shard_map/update/pallas_call | solution.py:643
  (3 shorter events, 0.0 us)
Async XLA Ops:
  1.6 10.1 %collective-permute-start = (f32[9,32,128]{2,1,0:T(8,128)S(1)}, f32[9,32,128]{2,1,0:T(8,128)S(1)}, u32[]{:S(2)}, u32[]{:S(2)}) collective-permute-start(f32[9,32,128]{2,1,0:T(8,128)S(1)} %face.1), channel_id=1, source_target_pairs={{1,0},{2,1},{3,2},{4,3},{5,4},{6,5},{7,6},{9,8},{10,9},{11,10},{12... | collective-permute-start | bytes 442376 | tf_op jit(solution)/shard_map/ppermute | solution.py:656
  10.4 4.3 %collective-permute-start.1 = (f32[14,16,128]{2,1,0:T(8,128)S(1)}, f32[14,16,128]{2,1,0:T(8,128)S(1)}, u32[]{:S(2)}, u32[]{:S(2)}) collective-permute-start(f32[14,16,128]{2,1,0:T(8,128)S(1)} %get-tuple-element.30), channel_id=1, source_target_pairs={{0,8},{8,0},{16,24},{24,16},{1,9},{9,1},{17,25},{25,17},{2,10},{10... | collective-permute-start | bytes 344072 | tf_op jit(solution)/shard_map/ppermute | solution.py:663
  11.0 3.8 %collective-permute-start.2 = (f32[14,16,128]{2,1,0:T(8,128)S(1)}, f32[14,16,128]{2,1,0:T(8,128)S(1)}, u32[]{:S(2)}, u32[]{:S(2)}) collective-permute-start(f32[14,16,128]{2,1,0:T(8,128)S(1)} %get-tuple-element.31), channel_id=1, source_target_pairs={{8,16},{16,8},{9,17},{17,9},{10,18},{18,10},{11,19},{19,11},{12,20... | collective-permute-start | bytes 344072 | tf_op jit(solution)/shard_map/ppermute | solution.py:663
  14.7 4.9 %copy-start = (s32[16,32,128]{2,1,0:T(8,128)S(1)}, s32[16,32,128]{2,1,0:T(8,128)}, u32[]{:S(2)}) copy-start(s32[16,32,128]{2,1,0:T(8,128)} %passive.3) | copy-start | bytes 786436
  14.7 4.9 %copy-start.1 = (s32[16,32,128]{2,1,0:T(8,128)S(1)}, s32[16,32,128]{2,1,0:T(8,128)}, u32[]{:S(2)}) copy-start(s32[16,32,128]{2,1,0:T(8,128)} %solid.3) | copy-start | bytes 786436
  15.7 11.2 %collective-permute-start.3 = (f32[160,128]{1,0:T(8,128)S(1)}, f32[160,128]{1,0:T(8,128)S(1)}, u32[]{:S(2)}, u32[]{:S(2)}) collective-permute-start(f32[160,128]{1,0:T(8,128)S(1)} %get-tuple-element.37), channel_id=1, source_target_pairs={{0,1},{1,0},{2,3},{3,2},{4,5},{5,4},{6,7},{7,6},{8,9},{9,8},{10,11... | collective-permute-start | bytes 245768 | tf_op jit(solution)/shard_map/ppermute | solution.py:663
  18.9 8.0 %collective-permute-start.4 = (f32[160,128]{1,0:T(8,128)S(1)}, f32[160,128]{1,0:T(8,128)S(1)}, u32[]{:S(2)}, u32[]{:S(2)}) collective-permute-start(f32[160,128]{1,0:T(8,128)S(1)} %get-tuple-element.38), channel_id=1, source_target_pairs={{1,2},{2,1},{3,4},{4,3},{5,6},{6,5},{9,10},{10,9},{11,12},{12,11},... | collective-permute-start | bytes 245768 | tf_op jit(solution)/shard_map/ppermute | solution.py:663

commit v11 on v10

--- a/solution.py
+++ b/solution.py
@@ -169,20 +169,14 @@
     ]
 
 
-def sweep(rows, segments, put, work, ready=None):
+def sweep(rows, segments, put, work):
     work[1][...] = jnp.zeros_like(work[1])
-
-    def plane(p):
-        if ready is not None:
-            ready(p)
+    for p in range(2):
         prepare(segments(p), p, work)
-
-    for p in range(2):
-        plane(p)
 
     def body(y, _):
         put(y)
-        plane(y + 2)
+        prepare(segments(y + 2), y + 2, work)
         return 0
 
     lax.fori_loop(0, rows - 1, body, 0, unroll=2)
@@ -212,23 +206,40 @@
     return 11 + row // ny, slice(row % ny, row % ny + 1)
 
 
-def ends_kernel(flags, disp_h, dens_h, stiff, disp, dens, mat, mat_y, ends, up, down, msg_even, msg_odd, stiff_s, sems, *work):
+def load_kernel(disp_h, dens_h, stiff, disp, dens, mat, mat_y, stiff_s, sems):
+    copies = [pltpu.make_async_copy(stiff, stiff_s, sems.at[0])]
+    for l in range(3):
+        part = pl.ds(3 * l, 3)
+        copies.append(pltpu.make_async_copy(disp_h.at[part], disp.at[part], sems.at[1 + l]))
+    copies.append(pltpu.make_async_copy(dens_h, dens, sems.at[4]))
+    for copy in copies:
+        copy.start()
+    copies[0].wait()
+    build_matrices(stiff_s[...], ((mat, 4, 2), (mat_y, 2, 4)))
+    for copy in copies[1:]:
+        copy.wait()
+
+
+def load_call(disp, dens, stiff):
+    matrix = jax.ShapeDtypeStruct((192, 224), bf16)
+    return pl.pallas_call(
+        load_kernel,
+        in_specs=[HBM, HBM, HBM],
+        out_shape=(
+            jax.ShapeDtypeStruct(disp.shape, f32),
+            jax.ShapeDtypeStruct(dens.shape, f32),
+            matrix,
+            matrix,
+        ),
+        scratch_shapes=[pltpu.VMEM((24, 24), f32), pltpu.SemaphoreType.DMA((5,))],
+        compiler_params=pltpu.CompilerParams(vmem_limit_bytes=16 * 2**20),
+        cost_estimate=estimate(2),
+        name="load",
+    )(disp, dens, stiff)
+
+
+def ends_kernel(flags, disp, dens, mat, ends, up, down, msg_even, msg_odd, *work):
     _, ny, nz, nx = disp.shape
-
-    def copy(p):
-        return pltpu.make_async_copy(disp_h.at[:, p], disp.at[:, p], sems.at[p])
-
-    copy_k = pltpu.make_async_copy(stiff, stiff_s, sems.at[ny])
-    copy_d = pltpu.make_async_copy(dens_h, dens, sems.at[ny + 1])
-    copy_k.start()
-    for p in range(2):
-        copy(p).start()
-    copy_d.start()
-    for p in range(2, ny):
-        copy(p).start()
-    copy_k.wait()
-    build_matrices(stiff_s[...], ((mat, 4, 2), (mat_y, 2, 4)))
-    copy_d.wait()
 
     def segments(p):
         return lambda i: [(disp[i, p, 0:8], disp[i, p, 8:9]), (disp[i, p, nz - 8 : nz], None)]
@@ -237,7 +248,7 @@
         d = jnp.concatenate([dens[y, 0:8], dens[y, nz - 8 : nz]], axis=0)
         ends[y] = energy_rows(y, mat, work, d)
 
-    sweep(ny - 1, segments, put, work, lambda p: copy(p).wait())
+    sweep(ny - 1, segments, put, work)
     for ref in (up, down):
         ref[9:] = jnp.zeros((ref.shape[0] - 9, ny, nx), f32)
     for y in range(ny):
@@ -263,26 +274,18 @@
     msg_odd[...] = jnp.where(odd, up[...], down[...])
 
 
-def ends_call(flags, disp, dens, stiff):
+def ends_call(flags, disp, dens, mat):
     _, ny, nz, nx = disp.shape
     message = jax.ShapeDtypeStruct((11 + -(-38 // ny), ny, nx), f32)
-    matrix = jax.ShapeDtypeStruct((192, 224), bf16)
     return pl.pallas_call(
         ends_kernel,
-        in_specs=[SMEM] + [HBM] * 3,
-        out_shape=(
-            jax.ShapeDtypeStruct(disp.shape, f32),
-            jax.ShapeDtypeStruct(dens.shape, f32),
-            matrix,
-            matrix,
-            jax.ShapeDtypeStruct((ny, 16, nx), f32),
-        )
-        + (message,) * 4,
-        scratch_shapes=[pltpu.VMEM((24, 24), f32), pltpu.SemaphoreType.DMA((ny + 2,))] + workspace(ny, 2, nx),
-        compiler_params=pltpu.CompilerParams(vmem_limit_bytes=20 * 2**20),
+        in_specs=[SMEM] + [VMEM] * 3,
+        out_shape=(jax.ShapeDtypeStruct((ny, 16, nx), f32),) + (message,) * 4,
+        scratch_shapes=workspace(ny, 2, nx),
+        compiler_params=pltpu.CompilerParams(vmem_limit_bytes=16 * 2**20),
         cost_estimate=estimate(4),
         name="energy_ends",
-    )(flags, disp, dens, stiff)
+    )(flags, disp, dens, mat)
 
 
 def middle_kernel(disp, dens, fy, mat, ends, src, *work):
@@ -456,7 +459,7 @@
 COARSE = POINTS // FINE
 
 
-def table(n, nz, nx, amp, low, high, now, fine_s, vol, tgt, start):
+def table(n, nz, nx, amp, low, high, now, fine_s, vol, tgt, start, unroll):
     spacing = 2.0 * bracket_end / POINTS
 
     pair = 2
@@ -487,7 +490,7 @@
             begin = tuple(jnp.zeros((8, nx), f32) for _ in places)
         else:
             begin = tuple((start[0] if ref is vol else start[1])[at : at + 8] for ref, at in places)
-        acc = lax.fori_loop(0, n, volume, begin, unroll=2)
+        acc = lax.fori_loop(0, n, volume, begin, unroll=unroll)
         for (ref, at), value in zip(places, acc):
             ref[at : at + 8] = value
 
@@ -507,7 +510,7 @@
         amp[j], low[j], high[j], now_s[j] = limits(p3, dens[y], passive[y] == 1, solid[y] == 1)
 
     filter_block(s_s, d_s, ny - 1, (flags[2], flags[3]), None, finish, 4)
-    table(ny - 5, nz, nx, amp, low, high, now_s, fine_s, vol, tgt, None)
+    table(ny - 5, nz, nx, amp, low, high, now_s, fine_s, vol, tgt, None, 2)
 
 
 def inner_call(flags, src, rim, dens, passive, solid):
@@ -578,7 +581,7 @@
 
         edges = (flags[0], 1) if b == 0 else (1, flags[1])
         filter_block(s_s.at[b], d_s.at[b], 6 + b, (flags[2], flags[3]), edges, finish, True)
-    table(5, nz, nx, amp, low, high, now_s, fine_s, vol, tgt, (vol_i, tgt_i))
+    table(5, nz, nx, amp, low, high, now_s, fine_s, vol, tgt, (vol_i, tgt_i), 2)
 
     def lanes(ref, count):
         total = ref[pl.ds(0, count, stride=8), :]
@@ -674,7 +677,8 @@
     stiff_hbm = pltpu.with_memory_space_constraint(stiffness, pltpu.HBM)
 
     fy = to_lower(face_call(disp_hbm), "gy")
-    disp, dens, mat, mat_y, ends, up, down, z_even, z_odd = ends_call(flags, disp_hbm, dens_hbm, stiff_hbm)
+    disp, dens, mat, mat_y = load_call(disp_hbm, dens_hbm, stiff_hbm)
+    ends, up, down, z_even, z_odd = ends_call(flags, disp, dens, mat)
 
     z_got_even = swap(z_even, "gz", 0)
     z_got_odd = swap(z_odd, "gz", 1)

time: 49.6 us -> 47.4 us (0.956)
  Pallas kernels: 24.6 us -> 22.5 us
  waiting for transfers between devices: 0.01 us -> 0.77 us
  starting transfers between devices: 6.31 us -> 5.81 us
    pallas_call x1 -> x2, Pallas kernels: 7.44 us -> 5.3 us  [the longest x1 3.58 us: ends_call(): pl.pallas_call(ends_kernel, in_specs=[SMEM] + [VMEM] * 3, out_shape=(jax....]
    ppermute x1, waiting for transfers between devices: 0.01 us -> 0.75 us  [to_lower(): return lax.ppermute(value, axis, [(i + 1, i) for i in range(count - 1)])]
    ppermute x4, starting transfers between devices: 5.02 us -> 4.52 us  [swap(): return lax.ppermute(value, axis, pairs)]
  transfers between devices with their start and end apart: 5 -> 5, of which waited for: 0 -> 1; matrix products, arithmetic and copies ran while one was open for 0% -> 0% of each run, Pallas kernels for 36% -> 33%
where the time goes in v11:
time: 47.4 us; the launch traced here: 47.2 us
  Pallas kernels  22.5 us (47%)
  blocking collectives  17.2 us (36%)
  starting transfers between devices  5.81 us (12%)
  between operations  0.79 us (2%)
  waiting for transfers between devices  0.77 us (2%)
    all_to_all x1, blocking collectives, on_device(): tables = lax.all_to_all(everyone, ('gz', 'gy'), 0, 0, tiled=True)  17.2 us
    pallas_call x1, Pallas kernels, inner_call(): pl.pallas_call(inner_kernel, in_specs=[SMEM] + [VMEM] * 5, out_shape=(fie...  7.3 us
    ppermute x4, starting transfers between devices, swap(): return lax.ppermute(value, axis, pairs)  4.52 us
    pallas_call x1, Pallas kernels, outer_call(): pl.pallas_call(outer_kernel, in_specs=[SMEM] + [VMEM] * 11, out_shape=(fi...  3.96 us
    pallas_call x1, Pallas kernels, ends_call(): pl.pallas_call(ends_kernel, in_specs=[SMEM] + [VMEM] * 3, out_shape=(jax....  3.58 us
    pallas_call x1, Pallas kernels, middle_call(): pl.pallas_call(middle_kernel, in_specs=[VMEM] * 5, out_shape=jax.ShapeDty...  3.06 us
    pallas_call x1, Pallas kernels, load_call(): pl.pallas_call(load_kernel, in_specs=[HBM, HBM, HBM], out_shape=(jax.Shap...  1.72 us
    ppermute x1, starting transfers between devices, to_lower(): return lax.ppermute(value, axis, [(i + 1, i) for i in range(count - 1)])  1.29 us
  transfers between devices with their start and end apart: 5, of which 1 were waited for; matrix products, arithmetic and copies ran while one was open for 0% of the time, Pallas kernels for 33%

profile of v11, /device:TPU:0, one launch (start us, length us, event | category | flops | bytes accessed | tf_op | source)
XLA Modules:
  0.0 47.2 jit_solution(9475723376411431237)
XLA Ops:
  0.6 0.9 %face.1 = f32[9,32,128]{2,1,0:T(8,128)S(1)} custom-call(f32[9,16,32,128]{3,2,1,0:T(8,128)} %disp.1), custom_call_target="tpu_custom_call" | custom-call | tf_op jit(solution)/shard_map/face/pallas_call | solution.py:194
  1.6 1.3 %collective-permute-start = (f32[9,32,128]{2,1,0:T(8,128)S(1)}, f32[9,32,128]{2,1,0:T(8,128)S(1)}, u32[]{:S(2)}, u32[]{:S(2)}) collective-permute-start(f32[9,32,128]{2,1,0:T(8,128)S(1)} %face.1), channel_id=1, source_target_pairs={{1,0},{2,1},{3,2},{4,3},{5,4},{6,5},{7,6},{9,8},{10,9},{11,10},{12... | collective-permute-start | bytes 442376 | tf_op jit(solution)/shard_map/ppermute | solution.py:659
  2.9 0.1 stack.27
  3.0 1.7 %load.1 = (f32[9,16,32,128]{3,2,1,0:T(8,128)S(1)}, f32[16,32,128]{2,1,0:T(8,128)S(1)}, bf16[192,224]{1,0:T(8,128)(2,1)S(1)}, bf16[192,224]{1,0:T(8,128)(2,1)S(1)}) custom-call(f32[9,16,32,128]{3,2,1,0:T(8,128)} %disp.1, f32[16,32,128]{2,1,0:T(8,128)} %dens_h.1, f32[24,24]{1,0:T(8,128)} %stiff.1), custom_call_target="tpu_custom_call" | custom-call | flops 2000000000 | bytes 1048576 | tf_op jit(solution)/shard_map/load/pallas_call | solution.py:225
  4.7 3.6 %energy_ends.1 = (f32[16,16,128]{2,1,0:T(8,128)S(1)}, f32[14,16,128]{2,1,0:T(8,128)S(1)}, f32[14,16,128]{2,1,0:T(8,128)S(1)}, f32[14,16,128]{2,1,0:T(8,128)S(1)}, f32[14,16,128]{2,1,0:T(8,128)S(1)}) custom-call(s32[6]{0:T(128)S(1)} %convert_element_type.3.flags, f32[9,16,32,128]{3,2,1,0:T(8,128)S(1)} %get-tuple-element.26.disp, ...), custom_call_target="tpu_custom_call" | custom-call | flops 4000000000 | bytes 1048576 | tf_op jit(solution)/shard_map/energy_ends/pallas_call | solution.py:280
  8.3 0.5 %collective-permute-start.1 = (f32[14,16,128]{2,1,0:T(8,128)S(1)}, f32[14,16,128]{2,1,0:T(8,128)S(1)}, u32[]{:S(2)}, u32[]{:S(2)}) collective-permute-start(f32[14,16,128]{2,1,0:T(8,128)S(1)} %get-tuple-element.30), channel_id=1, source_target_pairs={{0,8},{8,0},{16,24},{24,16},{1,9},{9,1},{17,25},{25,17},{2,10},{10... | collective-permute-start | bytes 344072 | tf_op jit(solution)/shard_map/ppermute | solution.py:666
  8.8 0.7 %collective-permute-start.2 = (f32[14,16,128]{2,1,0:T(8,128)S(1)}, f32[14,16,128]{2,1,0:T(8,128)S(1)}, u32[]{:S(2)}, u32[]{:S(2)}) collective-permute-start(f32[14,16,128]{2,1,0:T(8,128)S(1)} %get-tuple-element.31), channel_id=1, source_target_pairs={{8,16},{16,8},{9,17},{17,9},{10,18},{18,10},{11,19},{19,11},{12,20... | collective-permute-start | bytes 344072 | tf_op jit(solution)/shard_map/ppermute | solution.py:666
  9.5 0.8 %collective-permute-done.fy = f32[9,32,128]{2,1,0:T(8,128)S(1)} collective-permute-done((f32[9,32,128]{2,1,0:T(8,128)S(1)}, f32[9,32,128]{2,1,0:T(8,128)S(1)}, u32[]{:S(2)}, u32[]{:S(2)}) %collective-permute-start) | collective-permute-done | bytes 147488 | tf_op jit(solution)/shard_map/ppermute | solution.py:659
  10.2 3.1 %energy_middle.1.src = f32[16,48,128]{2,1,0:T(8,128)S(1)} custom-call(f32[9,16,32,128]{3,2,1,0:T(8,128)S(1)} %get-tuple-element.26.disp, f32[16,32,128]{2,1,0:T(8,128)S(1)} %get-tuple-element.27.dens, f32[9,32,128]{2,1,0:T(8,128)S(1)} %collective-permute-done.fy, bf16[192,224]{1,0:T(8,128)(2,1)S(1)} %get-tuple-element.28.mat, ...), custom_call_target="tpu_custom_call" | custom-call | flops 4000000000 | bytes 1048576 | tf_op jit(solution)/shard_map/energy_middle/pallas_call | solution.py:318
  13.3 0.0 collective-permute-done.1.got_even
  13.3 0.0 collective-permute-done.2.got_odd
  13.3 0.0 copy-start
  13.3 0.0 copy-start.1
  13.4 1.0 %energy_rim.1 = (f32[16,8,128]{2,1,0:T(8,128)S(1)}, f32[2,10,8,128]{3,2,1,0:T(8,128)S(1)}, f32[160,128]{1,0:T(8,128)S(1)}, f32[160,128]{1,0:T(8,128)S(1)}) custom-call(s32[6]{0:T(128)S(1)} %convert_element_type.3.flags, f32[14,16,128]{2,1,0:T(8,128)S(1)} %collective-permute-done.1.got_even, f32[14,16,128]{2,1,0:T(8,128)S(1)} %collective-permute-done.2.got_odd, ...), custom_call_target="tpu_custom_call" | custom-call | flops 2000000000 | bytes 1048576 | tf_op jit(solution)/shard_map/energy_rim/pallas_call | solution.py:400
  14.3 2.7 %collective-permute-start.3 = (f32[160,128]{1,0:T(8,128)S(1)}, f32[160,128]{1,0:T(8,128)S(1)}, u32[]{:S(2)}, u32[]{:S(2)}) collective-permute-start(f32[160,128]{1,0:T(8,128)S(1)} %get-tuple-element.37), channel_id=1, source_target_pairs={{0,1},{1,0},{2,3},{3,2},{4,5},{5,4},{6,7},{7,6},{8,9},{9,8},{10,11... | collective-permute-start | bytes 245768 | tf_op jit(solution)/shard_map/ppermute | solution.py:666
  17.0 0.7 %collective-permute-start.4 = (f32[160,128]{1,0:T(8,128)S(1)}, f32[160,128]{1,0:T(8,128)S(1)}, u32[]{:S(2)}, u32[]{:S(2)}) collective-permute-start(f32[160,128]{1,0:T(8,128)S(1)} %get-tuple-element.38), channel_id=1, source_target_pairs={{1,2},{2,1},{3,4},{4,3},{5,6},{6,5},{9,10},{10,9},{11,12},{12,11},... | collective-permute-start | bytes 245768 | tf_op jit(solution)/shard_map/ppermute | solution.py:666
  17.7 0.0 copy-done
  17.7 0.0 copy-done.1
  17.7 7.3 %filter_inner.1 = (f32[11,32,128]{2,1,0:T(8,128)S(1)}, f32[11,32,128]{2,1,0:T(8,128)S(1)}, f32[11,32,128]{2,1,0:T(8,128)S(1)}, f32[2048,128]{1,0:T(8,128)S(1)}, f32[128,128]{1,0:T(8,128)S(1)}) custom-call(s32[6]{0:T(128)S(1)} %convert_element_type.3.flags, f32[16,48,128]{2,1,0:T(8,128)S(1)} %energy_middle.1.src, f32[16,8,128]{2,1,0:T(8,128)S(1)} %get-tuple-element.35.rim, ...), custom_call_target="tpu_custom_call" | custom-call | flops 8999999488 | bytes 1048576 | tf_op jit(solution)/shard_map/filter_inner/pallas_call | solution.py:519
  25.0 0.0 collective-permute-done.3.got_even
  25.0 0.0 collective-permute-done.4.got_odd
  25.0 4.0 %filter_outer.1 = (f32[5,32,128]{2,1,0:T(8,128)S(1)}, f32[5,32,128]{2,1,0:T(8,128)S(1)}, f32[5,32,128]{2,1,0:T(8,128)S(1)}, f32[1,256]{1,0:T(1,128)S(1)}) custom-call(s32[6]{0:T(128)S(1)} %convert_element_type.3.flags, f32[16,48,128]{2,1,0:T(8,128)S(1)} %energy_middle.1.src, f32[16,8,128]{2,1,0:T(8,128)S(1)} %get-tuple-element.35.rim, ...), custom_call_target="tpu_custom_call" | custom-call | flops 3000000000 | bytes 1048576 | tf_op jit(solution)/shard_map/filter_outer/pallas_call | solution.py:601
  29.0 17.2 %all_to_all.8 = f32[32,1,256]{2,1,0:T(1,128)S(1)} all-to-all(f32[32,1,256]{2,1,0:T(1,128)S(1)} %broadcast_in_dim.2), channel_id=1, replica_groups=mesh['gz'=4,'gy'=8] {'gz','gy'}, dimensions={0} | all-to-all | bytes 65536 | tf_op jit(solution)/shard_map/all_to_all | solution.py:694
  46.3 0.9 %update.1 = (f32[16,32,128]{2,1,0:T(8,128)}, f32[1]{0:T(128)}) custom-call(f32[32,256]{1,0:T(8,128)S(1)} %bitcast.11, f32[11,32,128]{2,1,0:T(8,128)S(1)} %get-tuple-element.42.amp_i, f32[11,32,128]{2,1,0:T(8,128)S(1)} %get-tuple-element.43.low_i, f32[11,32,128]{2,1,0:T(8,128)S(1)} %get-tuple-element.44.high_i, f32[5,32,128]{2,1,0:T(8,128)S(1)} %get-tuple-element.45.amp_o, ...), custom_call_target="tpu_custom_call" | custom-call | flops 1000000000 | bytes 1048576 | tf_op jit(solution)/shard_map/update/pallas_call | solution.py:646
  (3 shorter events, 0.0 us)
Async XLA Ops:
  1.6 8.7 %collective-permute-start = (f32[9,32,128]{2,1,0:T(8,128)S(1)}, f32[9,32,128]{2,1,0:T(8,128)S(1)}, u32[]{:S(2)}, u32[]{:S(2)}) collective-permute-start(f32[9,32,128]{2,1,0:T(8,128)S(1)} %face.1), channel_id=1, source_target_pairs={{1,0},{2,1},{3,2},{4,3},{5,4},{6,5},{7,6},{9,8},{10,9},{11,10},{12... | collective-permute-start | bytes 442376 | tf_op jit(solution)/shard_map/ppermute | solution.py:659
  8.3 5.0 %collective-permute-start.1 = (f32[14,16,128]{2,1,0:T(8,128)S(1)}, f32[14,16,128]{2,1,0:T(8,128)S(1)}, u32[]{:S(2)}, u32[]{:S(2)}) collective-permute-start(f32[14,16,128]{2,1,0:T(8,128)S(1)} %get-tuple-element.30), channel_id=1, source_target_pairs={{0,8},{8,0},{16,24},{24,16},{1,9},{9,1},{17,25},{25,17},{2,10},{10... | collective-permute-start | bytes 344072 | tf_op jit(solution)/shard_map/ppermute | solution.py:666
  8.8 4.5 %collective-permute-start.2 = (f32[14,16,128]{2,1,0:T(8,128)S(1)}, f32[14,16,128]{2,1,0:T(8,128)S(1)}, u32[]{:S(2)}, u32[]{:S(2)}) collective-permute-start(f32[14,16,128]{2,1,0:T(8,128)S(1)} %get-tuple-element.31), channel_id=1, source_target_pairs={{8,16},{16,8},{9,17},{17,9},{10,18},{18,10},{11,19},{19,11},{12,20... | collective-permute-start | bytes 344072 | tf_op jit(solution)/shard_map/ppermute | solution.py:666
  13.3 4.4 %copy-start = (s32[16,32,128]{2,1,0:T(8,128)S(1)}, s32[16,32,128]{2,1,0:T(8,128)}, u32[]{:S(2)}) copy-start(s32[16,32,128]{2,1,0:T(8,128)} %passive.3) | copy-start | bytes 786436
  13.3 4.4 %copy-start.1 = (s32[16,32,128]{2,1,0:T(8,128)S(1)}, s32[16,32,128]{2,1,0:T(8,128)}, u32[]{:S(2)}) copy-start(s32[16,32,128]{2,1,0:T(8,128)} %solid.3) | copy-start | bytes 786436
  14.3 10.7 %collective-permute-start.3 = (f32[160,128]{1,0:T(8,128)S(1)}, f32[160,128]{1,0:T(8,128)S(1)}, u32[]{:S(2)}, u32[]{:S(2)}) collective-permute-start(f32[160,128]{1,0:T(8,128)S(1)} %get-tuple-element.37), channel_id=1, source_target_pairs={{0,1},{1,0},{2,3},{3,2},{4,5},{5,4},{6,7},{7,6},{8,9},{9,8},{10,11... | collective-permute-start | bytes 245768 | tf_op jit(solution)/shard_map/ppermute | solution.py:666
  17.0 8.0 %collective-permute-start.4 = (f32[160,128]{1,0:T(8,128)S(1)}, f32[160,128]{1,0:T(8,128)S(1)}, u32[]{:S(2)}, u32[]{:S(2)}) collective-permute-start(f32[160,128]{1,0:T(8,128)S(1)} %get-tuple-element.38), channel_id=1, source_target_pairs={{1,2},{2,1},{3,4},{4,3},{5,6},{6,5},{9,10},{10,9},{11,12},{12,11},... | collective-permute-start | bytes 245768 | tf_op jit(solution)/shard_map/ppermute | solution.py:666

commit v12 on v11

--- a/solution.py
+++ b/solution.py
@@ -244,23 +244,28 @@
     def segments(p):
         return lambda i: [(disp[i, p, 0:8], disp[i, p, 8:9]), (disp[i, p, nz - 8 : nz], None)]
 
-    def put(y):
-        d = jnp.concatenate([dens[y, 0:8], dens[y, nz - 8 : nz]], axis=0)
-        ends[y] = energy_rows(y, mat, work, d)
-
-    sweep(ny - 1, segments, put, work)
     for ref in (up, down):
         ref[9:] = jnp.zeros((ref.shape[0] - 9, ny, nx), f32)
-    for y in range(ny):
-        row = slice(y, y + 1)
+
+    def pack(y):
+        row = pl.ds(y, 1)
         for i in range(9):
             up[i, row] = disp[i, y, nz - 1 : nz]
             down[i, row] = disp[i, y, 0:1]
         up[9, row] = dens[y, nz - 1 : nz]
-        if y < ny - 1:
-            up[10, row] = ends[y, 14:15]
-            down[9, row] = ends[y, 0:1]
-            down[10, row] = ends[y, 1:2]
+
+    def put(y):
+        d = jnp.concatenate([dens[y, 0:8], dens[y, nz - 8 : nz]], axis=0)
+        s = energy_rows(y, mat, work, d)
+        ends[y] = s
+        row = pl.ds(y, 1)
+        up[10, row] = s[14:15]
+        down[9, row] = s[0:1]
+        down[10, row] = s[1:2]
+        pack(y)
+
+    sweep(ny - 1, segments, put, work)
+    pack(ny - 1)
     for n, y in enumerate((0, ny - 1)):
         for i in range(9):
             up[extra(up, 9 * n + i)] = disp[i, y, nz - 2 : nz - 1]
@@ -510,7 +515,7 @@
         amp[j], low[j], high[j], now_s[j] = limits(p3, dens[y], passive[y] == 1, solid[y] == 1)
 
     filter_block(s_s, d_s, ny - 1, (flags[2], flags[3]), None, finish, 4)
-    table(ny - 5, nz, nx, amp, low, high, now_s, fine_s, vol, tgt, None, 2)
+    table(ny - 5, nz, nx, amp, low, high, now_s, fine_s, vol, tgt, None, 4)
 
 
 def inner_call(flags, src, rim, dens, passive, solid):
@@ -581,7 +586,7 @@
 
         edges = (flags[0], 1) if b == 0 else (1, flags[1])
         filter_block(s_s.at[b], d_s.at[b], 6 + b, (flags[2], flags[3]), edges, finish, True)
-    table(5, nz, nx, amp, low, high, now_s, fine_s, vol, tgt, (vol_i, tgt_i), 2)
+    table(5, nz, nx, amp, low, high, now_s, fine_s, vol, tgt, (vol_i, tgt_i), True)
 
     def lanes(ref, count):
         total = ref[pl.ds(0, count, stride=8), :]

time: 47.4 us -> 48.5 us (1.023)
  Pallas kernels: 22.5 us -> 23.5 us
    pallas_call x1, Pallas kernels: 3.96 us -> 5.31 us  [outer_call(): pl.pallas_call(outer_kernel, in_specs=[SMEM] + [VMEM] * 11, out_shape=(fi...]
  transfers between devices with their start and end apart: 5 -> 5, of which waited for: 1 -> 1; matrix products, arithmetic and copies ran while one was open for 0% -> 0% of each run, Pallas kernels for 33% -> 32%
where the time goes in v12:
time: 48.5 us; the launch traced here: 48.2 us
  Pallas kernels  23.5 us (48%)
  blocking collectives  17.1 us (35%)
  starting transfers between devices  5.81 us (12%)
  waiting for transfers between devices  0.85 us (2%)
  between operations  0.79 us (2%)
    all_to_all x1, blocking collectives, on_device(): tables = lax.all_to_all(everyone, ('gz', 'gy'), 0, 0, tiled=True)  17.1 us
    pallas_call x1, Pallas kernels, inner_call(): pl.pallas_call(inner_kernel, in_specs=[SMEM] + [VMEM] * 5, out_shape=(fie...  7.04 us
    pallas_call x1, Pallas kernels, outer_call(): pl.pallas_call(outer_kernel, in_specs=[SMEM] + [VMEM] * 11, out_shape=(fi...  5.31 us
    ppermute x4, starting transfers between devices, swap(): return lax.ppermute(value, axis, pairs)  4.52 us
    pallas_call x1, Pallas kernels, ends_call(): pl.pallas_call(ends_kernel, in_specs=[SMEM] + [VMEM] * 3, out_shape=(jax....  3.49 us
    pallas_call x1, Pallas kernels, middle_call(): pl.pallas_call(middle_kernel, in_specs=[VMEM] * 5, out_shape=jax.ShapeDty...  3.06 us
    pallas_call x1, Pallas kernels, load_call(): pl.pallas_call(load_kernel, in_specs=[HBM, HBM, HBM], out_shape=(jax.Shap...  1.72 us
    ppermute x1, starting transfers between devices, to_lower(): return lax.ppermute(value, axis, [(i + 1, i) for i in range(count - 1)])  1.29 us
  transfers between devices with their start and end apart: 5, of which 1 were waited for; matrix products, arithmetic and copies ran while one was open for 0% of the time, Pallas kernels for 32%

profile of v12, /device:TPU:0, one launch (start us, length us, event | category | flops | bytes accessed | tf_op | source)
XLA Modules:
  0.0 48.2 jit_solution(2183177702517056754)
XLA Ops:
  0.6 0.9 %face.1 = f32[9,32,128]{2,1,0:T(8,128)S(1)} custom-call(f32[9,16,32,128]{3,2,1,0:T(8,128)} %disp.1), custom_call_target="tpu_custom_call" | custom-call | tf_op jit(solution)/shard_map/face/pallas_call | solution.py:194
  1.6 1.3 %collective-permute-start = (f32[9,32,128]{2,1,0:T(8,128)S(1)}, f32[9,32,128]{2,1,0:T(8,128)S(1)}, u32[]{:S(2)}, u32[]{:S(2)}) collective-permute-start(f32[9,32,128]{2,1,0:T(8,128)S(1)} %face.1), channel_id=1, source_target_pairs={{1,0},{2,1},{3,2},{4,3},{5,4},{6,5},{7,6},{9,8},{10,9},{11,10},{12... | collective-permute-start | bytes 442376 | tf_op jit(solution)/shard_map/ppermute | solution.py:664
  2.9 0.1 stack.27
  3.0 1.7 %load.1 = (f32[9,16,32,128]{3,2,1,0:T(8,128)S(1)}, f32[16,32,128]{2,1,0:T(8,128)S(1)}, bf16[192,224]{1,0:T(8,128)(2,1)S(1)}, bf16[192,224]{1,0:T(8,128)(2,1)S(1)}) custom-call(f32[9,16,32,128]{3,2,1,0:T(8,128)} %disp.1, f32[16,32,128]{2,1,0:T(8,128)} %dens_h.1, f32[24,24]{1,0:T(8,128)} %stiff.1), custom_call_target="tpu_custom_call" | custom-call | flops 2000000000 | bytes 1048576 | tf_op jit(solution)/shard_map/load/pallas_call | solution.py:225
  4.7 3.5 %energy_ends.1 = (f32[16,16,128]{2,1,0:T(8,128)S(1)}, f32[14,16,128]{2,1,0:T(8,128)S(1)}, f32[14,16,128]{2,1,0:T(8,128)S(1)}, f32[14,16,128]{2,1,0:T(8,128)S(1)}, f32[14,16,128]{2,1,0:T(8,128)S(1)}) custom-call(s32[6]{0:T(128)S(1)} %convert_element_type.3.flags, f32[9,16,32,128]{3,2,1,0:T(8,128)S(1)} %get-tuple-element.26.disp, ...), custom_call_target="tpu_custom_call" | custom-call | flops 4000000000 | bytes 1048576 | tf_op jit(solution)/shard_map/energy_ends/pallas_call | solution.py:285
  8.2 0.5 %collective-permute-start.1 = (f32[14,16,128]{2,1,0:T(8,128)S(1)}, f32[14,16,128]{2,1,0:T(8,128)S(1)}, u32[]{:S(2)}, u32[]{:S(2)}) collective-permute-start(f32[14,16,128]{2,1,0:T(8,128)S(1)} %get-tuple-element.30), channel_id=1, source_target_pairs={{0,8},{8,0},{16,24},{24,16},{1,9},{9,1},{17,25},{25,17},{2,10},{10... | collective-permute-start | bytes 344072 | tf_op jit(solution)/shard_map/ppermute | solution.py:671
  8.7 0.7 %collective-permute-start.2 = (f32[14,16,128]{2,1,0:T(8,128)S(1)}, f32[14,16,128]{2,1,0:T(8,128)S(1)}, u32[]{:S(2)}, u32[]{:S(2)}) collective-permute-start(f32[14,16,128]{2,1,0:T(8,128)S(1)} %get-tuple-element.31), channel_id=1, source_target_pairs={{8,16},{16,8},{9,17},{17,9},{10,18},{18,10},{11,19},{19,11},{12,20... | collective-permute-start | bytes 344072 | tf_op jit(solution)/shard_map/ppermute | solution.py:671
  9.4 0.8 %collective-permute-done.fy = f32[9,32,128]{2,1,0:T(8,128)S(1)} collective-permute-done((f32[9,32,128]{2,1,0:T(8,128)S(1)}, f32[9,32,128]{2,1,0:T(8,128)S(1)}, u32[]{:S(2)}, u32[]{:S(2)}) %collective-permute-start) | collective-permute-done | bytes 147488 | tf_op jit(solution)/shard_map/ppermute | solution.py:664
  10.2 3.1 %energy_middle.1.src = f32[16,48,128]{2,1,0:T(8,128)S(1)} custom-call(f32[9,16,32,128]{3,2,1,0:T(8,128)S(1)} %get-tuple-element.26.disp, f32[16,32,128]{2,1,0:T(8,128)S(1)} %get-tuple-element.27.dens, f32[9,32,128]{2,1,0:T(8,128)S(1)} %collective-permute-done.fy, bf16[192,224]{1,0:T(8,128)(2,1)S(1)} %get-tuple-element.28.mat, ...), custom_call_target="tpu_custom_call" | custom-call | flops 4000000000 | bytes 1048576 | tf_op jit(solution)/shard_map/energy_middle/pallas_call | solution.py:323
  13.3 0.0 collective-permute-done.1.got_even
  13.3 0.0 collective-permute-done.2.got_odd
  13.3 0.0 copy-start
  13.3 0.0 copy-start.1
  13.4 1.0 %energy_rim.1 = (f32[16,8,128]{2,1,0:T(8,128)S(1)}, f32[2,10,8,128]{3,2,1,0:T(8,128)S(1)}, f32[160,128]{1,0:T(8,128)S(1)}, f32[160,128]{1,0:T(8,128)S(1)}) custom-call(s32[6]{0:T(128)S(1)} %convert_element_type.3.flags, f32[14,16,128]{2,1,0:T(8,128)S(1)} %collective-permute-done.1.got_even, f32[14,16,128]{2,1,0:T(8,128)S(1)} %collective-permute-done.2.got_odd, ...), custom_call_target="tpu_custom_call" | custom-call | flops 2000000000 | bytes 1048576 | tf_op jit(solution)/shard_map/energy_rim/pallas_call | solution.py:405
  14.3 2.7 %collective-permute-start.3 = (f32[160,128]{1,0:T(8,128)S(1)}, f32[160,128]{1,0:T(8,128)S(1)}, u32[]{:S(2)}, u32[]{:S(2)}) collective-permute-start(f32[160,128]{1,0:T(8,128)S(1)} %get-tuple-element.37), channel_id=1, source_target_pairs={{0,1},{1,0},{2,3},{3,2},{4,5},{5,4},{6,7},{7,6},{8,9},{9,8},{10,11... | collective-permute-start | bytes 245768 | tf_op jit(solution)/shard_map/ppermute | solution.py:671
  17.0 0.7 %collective-permute-start.4 = (f32[160,128]{1,0:T(8,128)S(1)}, f32[160,128]{1,0:T(8,128)S(1)}, u32[]{:S(2)}, u32[]{:S(2)}) collective-permute-start(f32[160,128]{1,0:T(8,128)S(1)} %get-tuple-element.38), channel_id=1, source_target_pairs={{1,2},{2,1},{3,4},{4,3},{5,6},{6,5},{9,10},{10,9},{11,12},{12,11},... | collective-permute-start | bytes 245768 | tf_op jit(solution)/shard_map/ppermute | solution.py:671
  17.7 0.0 copy-done
  17.7 0.0 copy-done.1
  17.7 7.0 %filter_inner.1 = (f32[11,32,128]{2,1,0:T(8,128)S(1)}, f32[11,32,128]{2,1,0:T(8,128)S(1)}, f32[11,32,128]{2,1,0:T(8,128)S(1)}, f32[2048,128]{1,0:T(8,128)S(1)}, f32[128,128]{1,0:T(8,128)S(1)}) custom-call(s32[6]{0:T(128)S(1)} %convert_element_type.3.flags, f32[16,48,128]{2,1,0:T(8,128)S(1)} %energy_middle.1.src, f32[16,8,128]{2,1,0:T(8,128)S(1)} %get-tuple-element.35.rim, ...), custom_call_target="tpu_custom_call" | custom-call | flops 8999999488 | bytes 1048576 | tf_op jit(solution)/shard_map/filter_inner/pallas_call | solution.py:524
  24.8 0.0 collective-permute-done.3.got_even
  24.8 0.0 collective-permute-done.4.got_odd
  24.8 5.3 %filter_outer.1 = (f32[5,32,128]{2,1,0:T(8,128)S(1)}, f32[5,32,128]{2,1,0:T(8,128)S(1)}, f32[5,32,128]{2,1,0:T(8,128)S(1)}, f32[1,256]{1,0:T(1,128)S(1)}) custom-call(s32[6]{0:T(128)S(1)} %convert_element_type.3.flags, f32[16,48,128]{2,1,0:T(8,128)S(1)} %energy_middle.1.src, f32[16,8,128]{2,1,0:T(8,128)S(1)} %get-tuple-element.35.rim, ...), custom_call_target="tpu_custom_call" | custom-call | flops 3000000000 | bytes 1048576 | tf_op jit(solution)/shard_map/filter_outer/pallas_call | solution.py:606
  30.1 17.1 %all_to_all.8 = f32[32,1,256]{2,1,0:T(1,128)S(1)} all-to-all(f32[32,1,256]{2,1,0:T(1,128)S(1)} %broadcast_in_dim.2), channel_id=1, replica_groups=mesh['gz'=4,'gy'=8] {'gz','gy'}, dimensions={0} | all-to-all | bytes 65536 | tf_op jit(solution)/shard_map/all_to_all | solution.py:699
  47.3 0.9 %update.1 = (f32[16,32,128]{2,1,0:T(8,128)}, f32[1]{0:T(128)}) custom-call(f32[32,256]{1,0:T(8,128)S(1)} %bitcast.11, f32[11,32,128]{2,1,0:T(8,128)S(1)} %get-tuple-element.42.amp_i, f32[11,32,128]{2,1,0:T(8,128)S(1)} %get-tuple-element.43.low_i, f32[11,32,128]{2,1,0:T(8,128)S(1)} %get-tuple-element.44.high_i, f32[5,32,128]{2,1,0:T(8,128)S(1)} %get-tuple-element.45.amp_o, ...), custom_call_target="tpu_custom_call" | custom-call | flops 1000000000 | bytes 1048576 | tf_op jit(solution)/shard_map/update/pallas_call | solution.py:651
  (3 shorter events, 0.0 us)
Async XLA Ops:
  1.6 8.7 %collective-permute-start = (f32[9,32,128]{2,1,0:T(8,128)S(1)}, f32[9,32,128]{2,1,0:T(8,128)S(1)}, u32[]{:S(2)}, u32[]{:S(2)}) collective-permute-start(f32[9,32,128]{2,1,0:T(8,128)S(1)} %face.1), channel_id=1, source_target_pairs={{1,0},{2,1},{3,2},{4,3},{5,4},{6,5},{7,6},{9,8},{10,9},{11,10},{12... | collective-permute-start | bytes 442376 | tf_op jit(solution)/shard_map/ppermute | solution.py:664
  8.2 5.1 %collective-permute-start.1 = (f32[14,16,128]{2,1,0:T(8,128)S(1)}, f32[14,16,128]{2,1,0:T(8,128)S(1)}, u32[]{:S(2)}, u32[]{:S(2)}) collective-permute-start(f32[14,16,128]{2,1,0:T(8,128)S(1)} %get-tuple-element.30), channel_id=1, source_target_pairs={{0,8},{8,0},{16,24},{24,16},{1,9},{9,1},{17,25},{25,17},{2,10},{10... | collective-permute-start | bytes 344072 | tf_op jit(solution)/shard_map/ppermute | solution.py:671
  8.7 4.6 %collective-permute-start.2 = (f32[14,16,128]{2,1,0:T(8,128)S(1)}, f32[14,16,128]{2,1,0:T(8,128)S(1)}, u32[]{:S(2)}, u32[]{:S(2)}) collective-permute-start(f32[14,16,128]{2,1,0:T(8,128)S(1)} %get-tuple-element.31), channel_id=1, source_target_pairs={{8,16},{16,8},{9,17},{17,9},{10,18},{18,10},{11,19},{19,11},{12,20... | collective-permute-start | bytes 344072 | tf_op jit(solution)/shard_map/ppermute | solution.py:671
  13.3 4.4 %copy-start = (s32[16,32,128]{2,1,0:T(8,128)S(1)}, s32[16,32,128]{2,1,0:T(8,128)}, u32[]{:S(2)}) copy-start(s32[16,32,128]{2,1,0:T(8,128)} %passive.3) | copy-start | bytes 786436
  13.3 4.4 %copy-start.1 = (s32[16,32,128]{2,1,0:T(8,128)S(1)}, s32[16,32,128]{2,1,0:T(8,128)}, u32[]{:S(2)}) copy-start(s32[16,32,128]{2,1,0:T(8,128)} %solid.3) | copy-start | bytes 786436
  14.3 10.4 %collective-permute-start.3 = (f32[160,128]{1,0:T(8,128)S(1)}, f32[160,128]{1,0:T(8,128)S(1)}, u32[]{:S(2)}, u32[]{:S(2)}) collective-permute-start(f32[160,128]{1,0:T(8,128)S(1)} %get-tuple-element.37), channel_id=1, source_target_pairs={{0,1},{1,0},{2,3},{3,2},{4,5},{5,4},{6,7},{7,6},{8,9},{9,8},{10,11... | collective-permute-start | bytes 245768 | tf_op jit(solution)/shard_map/ppermute | solution.py:671
  17.0 7.7 %collective-permute-start.4 = (f32[160,128]{1,0:T(8,128)S(1)}, f32[160,128]{1,0:T(8,128)S(1)}, u32[]{:S(2)}, u32[]{:S(2)}) collective-permute-start(f32[160,128]{1,0:T(8,128)S(1)} %get-tuple-element.38), channel_id=1, source_target_pairs={{1,2},{2,1},{3,4},{4,3},{5,6},{6,5},{9,10},{10,9},{11,12},{12,11},... | collective-permute-start | bytes 245768 | tf_op jit(solution)/shard_map/ppermute | solution.py:671

commit v13 on v12

--- a/solution.py
+++ b/solution.py
@@ -109,9 +109,10 @@
         mat[:, 112:224] = lo[:, 0:112]
 
 
-def prepare(segments, p, work):
+def prepare(segments, p, work, short=False):
     main_s, ext_s, mul_s = work
-    for l in range(3):
+
+    def load_case(l):
         for c in range(3):
             w0 = 0
             for u, x in segments(3 * l + c):
@@ -138,14 +139,22 @@
                     mul_s[p, l, k, 0, at] = m
                     mul_s[p, l, k, 1, at] = jnp.where(last, mx, pltpu.roll(m, size - 1, 0))
                 w0 += n
-
-
-def energy_rows(p, mat, work, density):
+        return 0
+
+    if short:
+        lax.fori_loop(0, 3, lambda l, _: load_case(l), 0)
+    else:
+        for l in range(3):
+            load_case(l)
+
+
+def energy_rows(p, mat, work, density, short=False):
     main_s, ext_s, mul_s = work
     rows, nx = density.shape
     count = rows // 8
-    acc = [None] * count
-    for l in range(3):
+
+    def load_case(l, acc):
+        acc = list(acc)
         ext = jnp.concatenate([ext_s[p, l], ext_s[p + 1, l]], axis=0).astype(bf16)
         one = jnp.concatenate([main_s[p, l], main_s[p + 1, l], ext], axis=0)
         force = jnp.dot(mat[...], jnp.concatenate([one, one], axis=0), preferred_element_type=f32)
@@ -156,8 +165,16 @@
                     for w in range(count):
                         at = slice(8 * w, 8 * w + 8)
                         term = force[8 * i : 8 * i + 8, w * nx : (w + 1) * nx] * mul_s[p + q, l, k, b, at]
-                        acc[w] = term if acc[w] is None else acc[w] + term
+                        acc[w] = acc[w] + term
                     i += 1
+        return tuple(acc)
+
+    acc = tuple(jnp.zeros((8, nx), f32) for _ in range(count))
+    if short:
+        acc = lax.fori_loop(0, 3, load_case, acc)
+    else:
+        for l in range(3):
+            acc = load_case(l, acc)
     return density * (-3.0 * density * density * jnp.concatenate(acc, axis=0))
 
 
@@ -171,15 +188,15 @@
 
 def sweep(rows, segments, put, work):
     work[1][...] = jnp.zeros_like(work[1])
-    for p in range(2):
-        prepare(segments(p), p, work)
 
     def body(y, _):
         put(y)
         prepare(segments(y + 2), y + 2, work)
         return 0
 
-    lax.fori_loop(0, rows - 1, body, 0, unroll=2)
+    for p in range(2):
+        prepare(segments(p), p, work, True)
+    lax.fori_loop(0, rows - 1, body, 0)
     put(rows - 1)
 
 
@@ -203,7 +220,7 @@
 
 def extra(ref, row):
     ny = ref.shape[1]
-    return 11 + row // ny, slice(row % ny, row % ny + 1)
+    return 11 + row // ny, pl.ds(row % ny, 1)
 
 
 def load_kernel(disp_h, dens_h, stiff, disp, dens, mat, mat_y, stiff_s, sems):
@@ -244,8 +261,12 @@
     def segments(p):
         return lambda i: [(disp[i, p, 0:8], disp[i, p, 8:9]), (disp[i, p, nz - 8 : nz], None)]
 
-    for ref in (up, down):
-        ref[9:] = jnp.zeros((ref.shape[0] - 9, ny, nx), f32)
+    def clear(e, _):
+        up[e] = jnp.zeros((ny, nx), f32)
+        down[e] = jnp.zeros((ny, nx), f32)
+        return 0
+
+    lax.fori_loop(9, up.shape[0], clear, 0)
 
     def pack(y):
         row = pl.ds(y, 1)
@@ -266,17 +287,27 @@
 
     sweep(ny - 1, segments, put, work)
     pack(ny - 1)
-    for n, y in enumerate((0, ny - 1)):
-        for i in range(9):
+
+    def more(i, _):
+        for n, y in enumerate((0, ny - 1)):
             up[extra(up, 9 * n + i)] = disp[i, y, nz - 2 : nz - 1]
             down[extra(down, 9 * n + i)] = disp[i, y, 1:2]
             down[extra(down, 18 + 9 * n + i)] = disp[i, y, 2:3]
+        return 0
+
+    lax.fori_loop(0, 9, more, 0)
     up[extra(up, 36)] = dens[ny - 1, nz - 2 : nz - 1]
     down[extra(down, 36)] = dens[ny - 1, 0:1]
     down[extra(down, 37)] = dens[ny - 1, 1:2]
     odd = flags[5] == 1
-    msg_even[...] = jnp.where(odd, down[...], up[...])
-    msg_odd[...] = jnp.where(odd, up[...], down[...])
+
+    def choose(e, _):
+        a, b = up[e], down[e]
+        msg_even[e] = jnp.where(odd, b, a)
+        msg_odd[e] = jnp.where(odd, a, b)
+        return 0
+
+    lax.fori_loop(0, up.shape[0], choose, 0, unroll=2)
 
 
 def ends_call(flags, disp, dens, mat):
@@ -312,10 +343,10 @@
 
     sweep(ny - 1, segments, put, work)
     last[1][...] = jnp.zeros_like(last[1])
-    prepare(lambda i: [(disp[i, ny - 1], None)], 0, last)
-    prepare(lambda i: [(fy[i], None)], 1, last)
+    prepare(lambda i: [(disp[i, ny - 1], None)], 0, last, True)
+    prepare(lambda i: [(fy[i], None)], 1, last, True)
     frame(ny - 1)
-    src[ny - 1, OFF : OFF + nz] = energy_rows(0, mat, last, dens[ny - 1])
+    src[ny - 1, OFF : OFF + nz] = energy_rows(0, mat, last, dens[ny - 1], True)
 
 
 def middle_call(disp, dens, fy, mat, ends):
@@ -333,28 +364,43 @@
 
 def rim_kernel(
     flags, got_even, got_odd, up, down, disp, dens, mat_y, src,
-    rim, nodes, msg_even, msg_odd, low_s, high_s, t_s, *work,
+    rim, nodes, msg_even, msg_odd, low_s, high_s, s_s, t_s, *work,
 ):
     ny, rows, nx = src.shape
     nz = rows - 2 * OFF
     odd = flags[5] == 1
-    low_s[...] = jnp.where(odd, got_even[...], got_odd[...])
-    high_s[...] = jnp.where(odd, got_odd[...], got_even[...])
+
+    def choose(e, _):
+        a, b = got_even[e], got_odd[e]
+        low_s[e] = jnp.where(odd, a, b)
+        high_s[e] = jnp.where(odd, b, a)
+        return 0
+
+    lax.fori_loop(0, up.shape[0], choose, 0, unroll=2)
     work[1][...] = jnp.zeros_like(work[1])
-    prepare(lambda i: [(low_s[i], None), (up[i], None)], 0, work)
-    prepare(lambda i: [(down[i], None), (high_s[i], None)], 1, work)
-    s = energy_rows(0, mat_y, work, jnp.concatenate([low_s[9], up[9]], axis=0))
-    columns = ((0, low_s[10]), (1, s[0:ny]), (3, s[ny : 2 * ny]), (4, high_s[9]), (5, high_s[10]))
-    for y in range(ny):
-        rim[y] = jnp.zeros((8, nx), f32)
-        for r, column in columns:
-            rim[y, r : r + 1] = column[y : y + 1]
+    prepare(lambda i: [(low_s[i], None), (up[i], None)], 0, work, True)
+    prepare(lambda i: [(down[i], None), (high_s[i], None)], 1, work, True)
+    s = energy_rows(0, mat_y, work, jnp.concatenate([low_s[9], up[9]], axis=0), True)
+    s_s[0:ny] = s[0:ny]
+    s_s[ny : 2 * ny] = s[ny : 2 * ny]
+
+    def spread(y, _):
+        row = pl.ds(y, 1)
+        zero = jnp.zeros((1, nx), f32)
+        last = s_s[pl.ds(ny + y, 1)]
+        rim[y] = jnp.concatenate(
+            [low_s[10, row], s_s[row], zero, last, high_s[9, row], high_s[10, row], zero, zero], axis=0
+        )
+        return 0
+
+    lax.fori_loop(0, ny, spread, 0, unroll=2)
     half = 2 * (nz + 8)
     zero = jnp.zeros((1, nx), f32)
     for n, y in enumerate((0, ny - 1)):
         row = slice(y, y + 1)
-        for i in range(9):
-            window = jnp.concatenate(
+
+        def window(i, _):
+            value = jnp.concatenate(
                 [
                     low_s[extra(low_s, 9 * n + i)],
                     low_s[i, row],
@@ -367,8 +413,11 @@
                 ],
                 axis=0,
             )
-            nodes[n, i] = window
-            t_s[n, half + 8 * i : half + 8 * i + 8] = window
+            nodes[n, i] = value
+            t_s[n, pl.ds(pl.multiple_of(half + 8 * i, 8), 8)] = value
+            return 0
+
+        lax.fori_loop(0, 9, window, 0, unroll=3)
         nodes[n, 9] = jnp.concatenate(
             [
                 low_s[extra(low_s, 36)],
@@ -414,6 +463,7 @@
         scratch_shapes=[
             pltpu.VMEM(up.shape, f32),
             pltpu.VMEM(up.shape, f32),
+            pltpu.VMEM((2 * ny, nx), f32),
             pltpu.VMEM((2, size, nx), f32),
         ]
         + workspace(2, 2 * (ny // 8), nx),
@@ -423,8 +473,8 @@
     )(flags, got_even, got_odd, up, down, disp, dens, mat_y, src)
 
 
-def filter_block(s_s, d_s, n, z_edges, y_edges, finish, unroll):
-    rows, nx = s_s.shape[1:]
+def filter_blocks(s_s, d_s, z_edges, y_edges, finish, unroll):
+    blocks, n, rows, nx = s_s.shape
     nz = rows - 2 * OFF
     alpha, beta, gamma, delta, eps = filter_weights()
     row = lax.broadcasted_iota(jnp.int32, (rows, nx), 0)
@@ -433,23 +483,31 @@
     def beside(v):
         return pltpu.roll(v, 1, 0) + pltpu.roll(v, rows - 1, 0) + lane_up(v) + lane_down(v)
 
-    def second(j, _):
-        c = s_s[j + 1]
-        d2 = alpha * c + beta * (beside(c) + s_s[j] + s_s[j + 2])
+    def place(at, count):
+        if blocks == 1:
+            return 0, at
+        b = jnp.where(at >= count, 1, 0)
+        return b, at - count * b
+
+    def second(at, _):
+        b, j = place(at, n - 2)
+        c = s_s[b, j + 1]
+        d2 = alpha * c + beta * (beside(c) + s_s[b, j] + s_s[b, j + 2])
         ok = keep
         if y_edges is not None:
-            ok = keep & (jnp.where(j == 0, y_edges[0], jnp.where(j == n - 3, y_edges[1], 1)) == 1)
-        d_s[j] = jnp.where(ok, d2, 0.0)
-        return 0
-
-    def third(j, _):
-        d2 = d_s[j + 1]
-        p3 = gamma * s_s[j + 2] + delta * d2 + eps * (beside(d2) + d_s[j] + d_s[j + 2])
-        finish(j, p3[OFF : OFF + nz])
-        return 0
-
-    lax.fori_loop(0, n - 2, second, 0, unroll=unroll)
-    lax.fori_loop(0, n - 4, third, 0, unroll=unroll)
+            ok = keep & (jnp.where(at == 0, y_edges[0], jnp.where(at == 2 * n - 5, y_edges[1], 1)) == 1)
+        d_s[b, j] = jnp.where(ok, d2, 0.0)
+        return 0
+
+    def third(at, _):
+        b, j = place(at, n - 4)
+        d2 = d_s[b, j + 1]
+        p3 = gamma * s_s[b, j + 2] + delta * d2 + eps * (beside(d2) + d_s[b, j] + d_s[b, j + 2])
+        finish(at, b, j, p3[OFF : OFF + nz])
+        return 0
+
+    lax.fori_loop(0, blocks * (n - 2), second, 0, unroll=unroll)
+    lax.fori_loop(0, blocks * (n - 4), third, 0, unroll=unroll)
 
 
 def limits(p3, d, pas, sol):
@@ -468,8 +526,12 @@
     spacing = 2.0 * bracket_end / POINTS
 
     pair = 2
-    for first in range(0, COARSE, pair):
-        inverse = [math.exp(0.5 * (-bracket_end + spacing * FINE * i)) for i in range(first, first + pair)]
+
+    def run(first, make):
+        inverse = [
+            jnp.exp(0.5 * (-bracket_end + spacing * FINE * jnp.full((8, nx), first + i, jnp.int32).astype(f32)))
+            for i in range(pair)
+        ]
 
         def volume(j, acc):
             acc = list(acc)
@@ -480,7 +542,7 @@
                 for i, c in enumerate(inverse):
                     acc[pair * FINE + i] = acc[pair * FINE + i] + d * c
                 for f in range(FINE):
-                    if first == 0:
+                    if make:
                         t = amp[j, at] * math.exp(-0.5 * spacing * f)
                         fine_s[f, j, at] = t
                     else:
@@ -489,38 +551,47 @@
                         acc[i * FINE + f] = acc[i * FINE + f] + jnp.minimum(jnp.maximum(t, los[i]), his[i])
             return tuple(acc)
 
-        places = [(vol, 8 * (first * FINE + e)) for e in range(pair * FINE)]
-        places += [(tgt, 8 * (first + i)) for i in range(pair)]
+        places = [(0, 8 * (first * FINE + e)) for e in range(pair * FINE)] + [(1, 8 * (first + i)) for i in range(pair)]
+        places = [(a, pl.ds(at if isinstance(at, int) else pl.multiple_of(at, 8), 8)) for a, at in places]
         if start is None:
             begin = tuple(jnp.zeros((8, nx), f32) for _ in places)
         else:
-            begin = tuple((start[0] if ref is vol else start[1])[at : at + 8] for ref, at in places)
+            begin = tuple(start[a][at] for a, at in places)
         acc = lax.fori_loop(0, n, volume, begin, unroll=unroll)
-        for (ref, at), value in zip(places, acc):
-            ref[at : at + 8] = value
+        for (a, at), value in zip(places, acc):
+            (vol, tgt)[a][at] = value
+
+    run(0, True)
+
+    def later(q, _):
+        run(pair * q, False)
+        return 0
+
+    lax.fori_loop(1, COARSE // pair, later, 0)
 
 
 def inner_kernel(flags, src, rim, dens, passive, solid, amp, low, high, vol, tgt, s_s, d_s, now_s, fine_s):
     ny, nz, nx = dens.shape
-    s_s[...] = src[0 : ny - 1]
-
-    def fix(y, _):
-        put_rim(s_s, y, rim[y], nz)
-        return 0
-
-    lax.fori_loop(0, ny - 1, fix, 0, unroll=5)
-
-    def finish(j, p3):
-        y = j + 2
+
+    def place(j, _):
+        s_s[0, j] = src[j + 1]
+        put_rim(s_s.at[0], j, rim[j + 1], nz)
+        return 0
+
+    lax.fori_loop(0, ny - 2, place, 0, unroll=2)
+
+    def finish(at, b, j, p3):
+        y = j + 3
         amp[j], low[j], high[j], now_s[j] = limits(p3, dens[y], passive[y] == 1, solid[y] == 1)
 
-    filter_block(s_s, d_s, ny - 1, (flags[2], flags[3]), None, finish, 4)
-    table(ny - 5, nz, nx, amp, low, high, now_s, fine_s, vol, tgt, None, 4)
+    filter_blocks(s_s, d_s, (flags[2], flags[3]), None, finish, 2)
+    table(ny - 6, nz, nx, amp, low, high, now_s, fine_s, vol, tgt, None, 2)
 
 
 def inner_call(flags, src, rim, dens, passive, solid):
     ny, nz, nx = dens.shape
-    field = jax.ShapeDtypeStruct((ny - 5, nz, nx), f32)
+    rows = nz + 2 * OFF
+    field = jax.ShapeDtypeStruct((ny - 6, nz, nx), f32)
     return pl.pallas_call(
         inner_kernel,
         in_specs=[SMEM] + [VMEM] * 5,
@@ -532,10 +603,10 @@
             jax.ShapeDtypeStruct((8 * COARSE, nx), f32),
         ),
         scratch_shapes=[
-            pltpu.VMEM((ny - 1, nz + 2 * OFF, nx), f32),
-            pltpu.VMEM((ny - 3, nz + 2 * OFF, nx), f32),
-            pltpu.VMEM((ny - 5, nz, nx), f32),
-            pltpu.VMEM((FINE, ny - 5, nz, nx), f32),
+            pltpu.VMEM((1, ny - 2, rows, nx), f32),
+            pltpu.VMEM((1, ny - 4, rows, nx), f32),
+            pltpu.VMEM((ny - 6, nz, nx), f32),
+            pltpu.VMEM((FINE, ny - 6, nz, nx), f32),
         ],
         compiler_params=pltpu.CompilerParams(vmem_limit_bytes=24 * 2**20),
         cost_estimate=estimate(9),
@@ -545,48 +616,61 @@
 
 def outer_kernel(
     flags, src, rim, nodes, got_even, got_odd, mat, dens, passive, solid, vol_i, tgt_i,
-    amp, low, high, excess, s_s, d_s, now_s, fine_s, vol, tgt, below, above, *work,
+    amp, low, high, excess, s_s, d_s, now_s, fine_s, vol, tgt, got_s, *work,
 ):
     ny, nz, nx = dens.shape
     odd = flags[4] == 1
-    below[...] = jnp.where(odd, got_even[...], got_odd[...])
-    above[...] = jnp.where(odd, got_odd[...], got_even[...])
-    half = 2 * (nz + 8)
-
-    def window(ref, i):
-        return ref[half + 8 * i : half + 8 * i + 8]
+    size = got_even.shape[0]
+    step = nz + 8
+    half = 2 * step
+
+    def choose(r, _):
+        at = pl.ds(pl.multiple_of(8 * r, 8), 8)
+        a, b = got_even[at], got_odd[at]
+        got_s[0, at] = jnp.where(odd, a, b)
+        got_s[1, at] = jnp.where(odd, b, a)
+        return 0
+
+    lax.fori_loop(0, size // 8, choose, 0, unroll=4)
+
+    def window(b, i):
+        return got_s[b, pl.ds(pl.multiple_of(half + 8 * i, 8), 8)]
 
     work[1][...] = jnp.zeros_like(work[1])
-    prepare(lambda i: [(window(below, i), None), (nodes[1, i], None)], 0, work)
-    prepare(lambda i: [(nodes[0, i], None), (window(above, i), None)], 1, work)
-    corner = energy_rows(0, mat, work, jnp.concatenate([window(below, 9), nodes[1, 9]], axis=0))
-    for b, ref in enumerate((below, above)):
-        for j in range(2):
-            at = j if b == 0 else 5 + j
-            start = j * (nz + 8)
-            s_s[b, at, 0:OFF] = jnp.zeros((OFF, nx), f32)
-            s_s[b, at, OFF : OFF + nz] = ref[start : start + nz]
-            s_s[b, at, OFF + nz :] = jnp.zeros((OFF, nx), f32)
-            put_rim(s_s.at[b], at, ref[start + nz : start + nz + 8], nz)
-    for j in range(4):
-        s_s[0, 2 + j] = src[j]
-        put_rim(s_s.at[0], 2 + j, rim[j], nz)
-    for j in range(5):
-        s_s[1, j] = src[ny - 5 + j]
-        put_rim(s_s.at[1], j, rim[ny - 5 + j], nz)
+    prepare(lambda i: [(window(0, i), None), (nodes[1, i], None)], 0, work, True)
+    prepare(lambda i: [(nodes[0, i], None), (window(1, i), None)], 1, work, True)
+    corner = energy_rows(0, mat, work, jnp.concatenate([window(0, 9), nodes[1, 9]], axis=0), True)
+
+    def received(at, _):
+        b = jnp.where(at >= 2, 1, 0)
+        j = at - 2 * b
+        to = j + 5 * b
+        start = pl.multiple_of(j * step, 8)
+        s_s[b, to, 0:OFF] = jnp.zeros((OFF, nx), f32)
+        s_s[b, to, OFF : OFF + nz] = got_s[b, pl.ds(start, nz)]
+        s_s[b, to, OFF + nz :] = jnp.zeros((OFF, nx), f32)
+        put_rim(s_s.at[b], to, got_s[b, pl.ds(start + nz, 8)], nz)
+        return 0
+
+    def own(at, _):
+        b = jnp.where(at >= 5, 1, 0)
+        y = at + (ny - 10) * b
+        to = at + 2 - 7 * b
+        s_s[b, to] = src[y]
+        put_rim(s_s.at[b], to, rim[y], nz)
+        return 0
+
+    lax.fori_loop(0, 4, received, 0)
+    lax.fori_loop(0, 10, own, 0, unroll=2)
     put_rim(s_s.at[0], 1, corner[0:8], nz)
     put_rim(s_s.at[1], 4, corner[8:16], nz)
-    for b in range(2):
-        y0 = 0 if b == 0 else ny - 3
-
-        def finish(j, p3):
-            y = y0 + j
-            at = 2 * b + j
-            amp[at], low[at], high[at], now_s[at] = limits(p3, dens[y], passive[y] == 1, solid[y] == 1)
-
-        edges = (flags[0], 1) if b == 0 else (1, flags[1])
-        filter_block(s_s.at[b], d_s.at[b], 6 + b, (flags[2], flags[3]), edges, finish, True)
-    table(5, nz, nx, amp, low, high, now_s, fine_s, vol, tgt, (vol_i, tgt_i), True)
+
+    def finish(at, b, j, p3):
+        y = j + (ny - 3) * b
+        amp[at], low[at], high[at], now_s[at] = limits(p3, dens[y], passive[y] == 1, solid[y] == 1)
+
+    filter_blocks(s_s, d_s, (flags[2], flags[3]), (flags[0], flags[1]), finish, 2)
+    table(6, nz, nx, amp, low, high, now_s, fine_s, vol, tgt, (vol_i, tgt_i), 2)
 
     def lanes(ref, count):
         total = ref[pl.ds(0, count, stride=8), :]
@@ -602,7 +686,7 @@
 def outer_call(flags, src, rim, nodes, got_even, got_odd, mat, dens, passive, solid, vol_i, tgt_i):
     ny, nz, nx = dens.shape
     rows = nz + 2 * OFF
-    field = jax.ShapeDtypeStruct((5, nz, nx), f32)
+    field = jax.ShapeDtypeStruct((6, nz, nx), f32)
     return pl.pallas_call(
         outer_kernel,
         in_specs=[SMEM] + [VMEM] * 11,
@@ -610,12 +694,11 @@
         scratch_shapes=[
             pltpu.VMEM((2, 7, rows, nx), f32),
             pltpu.VMEM((2, 5, rows, nx), f32),
-            pltpu.VMEM((5, nz, nx), f32),
-            pltpu.VMEM((FINE, 5, nz, nx), f32),
+            pltpu.VMEM((6, nz, nx), f32),
+            pltpu.VMEM((FINE, 6, nz, nx), f32),
             pltpu.VMEM((8 * POINTS, nx), f32),
             pltpu.VMEM((8 * COARSE, nx), f32),
-            pltpu.VMEM(got_odd.shape, f32),
-            pltpu.VMEM(got_odd.shape, f32),
+            pltpu.VMEM((2,) + got_odd.shape, f32),
         ]
         + workspace(2, 2, nx),
         compiler_params=pltpu.CompilerParams(vmem_limit_bytes=20 * 2**20),
@@ -638,12 +721,12 @@
         return jnp.minimum(jnp.maximum(amp * scale, low), high)
 
     def body(j, _):
-        new[j + 2] = new_row(amp_i[j], low_i[j], high_i[j])
+        new[j + 3] = new_row(amp_i[j], low_i[j], high_i[j])
         return 0
 
     lax.fori_loop(0, inner, body, 0)
-    for j in range(5):
-        new[j if j < 2 else inner + j] = new_row(amp_o[j], low_o[j], high_o[j])
+    for j in range(6):
+        new[j if j < 3 else inner + j] = new_row(amp_o[j], low_o[j], high_o[j])
 
 
 def update_call(tables, inner, outer):
@@ -652,7 +735,7 @@
         update_kernel,
         in_specs=[VMEM] * 7,
         out_specs=(VMEM, SMEM),
-        out_shape=(jax.ShapeDtypeStruct((n + 5, nz, nx), f32), jax.ShapeDtypeStruct((1,), f32)),
+        out_shape=(jax.ShapeDtypeStruct((n + 6, nz, nx), f32), jax.ShapeDtypeStruct((1,), f32)),
         compiler_params=pltpu.CompilerParams(vmem_limit_bytes=8 * 2**20),
         cost_estimate=estimate(1),
         name="update",

time: 48.5 us -> 54 us (1.11)
  Pallas kernels: 23.5 us -> 29.4 us
  waiting for transfers between devices: 0.85 us -> 0.01 us
    pallas_call x1, Pallas kernels: 3.06 us -> 5.71 us  [middle_call(): pl.pallas_call(middle_kernel, in_specs=[VMEM] * 5, out_shape=jax.ShapeDty...]
    pallas_call x1, Pallas kernels: 3.49 us -> 5.42 us  [ends_call(): pl.pallas_call(ends_kernel, in_specs=[SMEM] + [VMEM] * 3, out_shape=(jax....]
    pallas_call x1, Pallas kernels: 0.98 us -> 2.11 us  [rim_call(): pl.pallas_call(rim_kernel, in_specs=[SMEM] + [VMEM] * 8, out_shape=(jax.S...]
    ppermute x1, waiting for transfers between devices: 0.84 us -> 0.01 us  [to_lower(): return lax.ppermute(value, axis, [(i + 1, i) for i in range(count - 1)])]
    pallas_call x1, Pallas kernels: 5.31 us -> 5.88 us  [outer_call(): pl.pallas_call(outer_kernel, in_specs=[SMEM] + [VMEM] * 11, out_shape=(fi...]
  transfers between devices with their start and end apart: 5 -> 5, of which waited for: 1 -> 0; matrix products, arithmetic and copies ran while one was open for 0% -> 0% of each run, Pallas kernels for 32% -> 37%
where the time goes in v13:
time: 54 us; the launch traced here: 53.7 us
  Pallas kernels  29.4 us (54%)
  blocking collectives  17 us (31%)
  starting transfers between devices  6.31 us (12%)
  between operations  0.81 us (2%)
    all_to_all x1, blocking collectives, on_device(): tables = lax.all_to_all(everyone, ('gz', 'gy'), 0, 0, tiled=True)  17 us
    pallas_call x1, Pallas kernels, inner_call(): pl.pallas_call(inner_kernel, in_specs=[SMEM] + [VMEM] * 5, out_shape=(fie...  6.75 us
    pallas_call x1, Pallas kernels, outer_call(): pl.pallas_call(outer_kernel, in_specs=[SMEM] + [VMEM] * 11, out_shape=(fi...  5.88 us
    pallas_call x1, Pallas kernels, middle_call(): pl.pallas_call(middle_kernel, in_specs=[VMEM] * 5, out_shape=jax.ShapeDty...  5.71 us
    pallas_call x1, Pallas kernels, ends_call(): pl.pallas_call(ends_kernel, in_specs=[SMEM] + [VMEM] * 3, out_shape=(jax....  5.42 us
    ppermute x4, starting transfers between devices, swap(): return lax.ppermute(value, axis, pairs)  5.02 us
    pallas_call x1, Pallas kernels, rim_call(): pl.pallas_call(rim_kernel, in_specs=[SMEM] + [VMEM] * 8, out_shape=(jax.S...  2.11 us
    pallas_call x1, Pallas kernels, load_call(): pl.pallas_call(load_kernel, in_specs=[HBM, HBM, HBM], out_shape=(jax.Shap...  1.72 us
  transfers between devices with their start and end apart: 5, of which 0 were waited for; matrix products, arithmetic and copies ran while one was open for 0% of the time, Pallas kernels for 37%

profile of v13, /device:TPU:0, one launch (start us, length us, event | category | flops | bytes accessed | tf_op | source)
XLA Modules:
  0.0 53.7 jit_solution(1300126403317632775)
XLA Ops:
  0.6 0.9 %face.1 = f32[9,32,128]{2,1,0:T(8,128)S(1)} custom-call(f32[9,16,32,128]{3,2,1,0:T(8,128)} %disp.1), custom_call_target="tpu_custom_call" | custom-call | tf_op jit(solution)/shard_map/face/pallas_call | solution.py:211
  1.6 1.3 %collective-permute-start = (f32[9,32,128]{2,1,0:T(8,128)S(1)}, f32[9,32,128]{2,1,0:T(8,128)S(1)}, u32[]{:S(2)}, u32[]{:S(2)}) collective-permute-start(f32[9,32,128]{2,1,0:T(8,128)S(1)} %face.1), channel_id=1, source_target_pairs={{1,0},{2,1},{3,2},{4,3},{5,4},{6,5},{7,6},{9,8},{10,9},{11,10},{12... | collective-permute-start | bytes 442376 | tf_op jit(solution)/shard_map/ppermute | solution.py:747
  2.9 0.1 stack.27
  3.0 1.7 %load.1 = (f32[9,16,32,128]{3,2,1,0:T(8,128)S(1)}, f32[16,32,128]{2,1,0:T(8,128)S(1)}, bf16[192,224]{1,0:T(8,128)(2,1)S(1)}, bf16[192,224]{1,0:T(8,128)(2,1)S(1)}) custom-call(f32[9,16,32,128]{3,2,1,0:T(8,128)} %disp.1, f32[16,32,128]{2,1,0:T(8,128)} %dens_h.1, f32[24,24]{1,0:T(8,128)} %stiff.1), custom_call_target="tpu_custom_call" | custom-call | flops 2000000000 | bytes 1048576 | tf_op jit(solution)/shard_map/load/pallas_call | solution.py:242
  4.7 5.4 %energy_ends.1 = (f32[16,16,128]{2,1,0:T(8,128)S(1)}, f32[14,16,128]{2,1,0:T(8,128)S(1)}, f32[14,16,128]{2,1,0:T(8,128)S(1)}, f32[14,16,128]{2,1,0:T(8,128)S(1)}, f32[14,16,128]{2,1,0:T(8,128)S(1)}) custom-call(s32[6]{0:T(128)S(1)} %convert_element_type.3.flags, f32[9,16,32,128]{3,2,1,0:T(8,128)S(1)} %get-tuple-element.26.disp, ...), custom_call_target="tpu_custom_call" | custom-call | flops 4000000000 | bytes 1048576 | tf_op jit(solution)/shard_map/energy_ends/pallas_call | solution.py:316
  10.2 0.5 collective-permute-start.1
  10.7 0.7 %collective-permute-start.2 = (f32[14,16,128]{2,1,0:T(8,128)S(1)}, f32[14,16,128]{2,1,0:T(8,128)S(1)}, u32[]{:S(2)}, u32[]{:S(2)}) collective-permute-start(f32[14,16,128]{2,1,0:T(8,128)S(1)} %get-tuple-element.31), channel_id=1, source_target_pairs={{8,16},{16,8},{9,17},{17,9},{10,18},{18,10},{11,19},{19,11},{12,20... | collective-permute-start | bytes 344072 | tf_op jit(solution)/shard_map/ppermute | solution.py:754
  11.3 0.0 collective-permute-done.fy
  11.3 5.7 %energy_middle.1.src = f32[16,48,128]{2,1,0:T(8,128)S(1)} custom-call(f32[9,16,32,128]{3,2,1,0:T(8,128)S(1)} %get-tuple-element.26.disp, f32[16,32,128]{2,1,0:T(8,128)S(1)} %get-tuple-element.27.dens, f32[9,32,128]{2,1,0:T(8,128)S(1)} %collective-permute-done.fy, bf16[192,224]{1,0:T(8,128)(2,1)S(1)} %get-tuple-element.28.mat, ...), custom_call_target="tpu_custom_call" | custom-call | flops 4000000000 | bytes 1048576 | tf_op jit(solution)/shard_map/energy_middle/pallas_call | solution.py:354
  17.1 0.0 collective-permute-done.1.got_even
  17.1 0.0 collective-permute-done.2.got_odd
  17.1 0.0 copy-start
  17.1 0.0 copy-start.1
  17.1 2.1 %energy_rim.1 = (f32[16,8,128]{2,1,0:T(8,128)S(1)}, f32[2,10,8,128]{3,2,1,0:T(8,128)S(1)}, f32[160,128]{1,0:T(8,128)S(1)}, f32[160,128]{1,0:T(8,128)S(1)}) custom-call(s32[6]{0:T(128)S(1)} %convert_element_type.3.flags, f32[14,16,128]{2,1,0:T(8,128)S(1)} %collective-permute-done.1.got_even, f32[14,16,128]{2,1,0:T(8,128)S(1)} %collective-permute-done.2.got_odd, ...), custom_call_target="tpu_custom_call" | custom-call | flops 2000000000 | bytes 1048576 | tf_op jit(solution)/shard_map/energy_rim/pallas_call | solution.py:454
  19.2 3.2 %collective-permute-start.3 = (f32[160,128]{1,0:T(8,128)S(1)}, f32[160,128]{1,0:T(8,128)S(1)}, u32[]{:S(2)}, u32[]{:S(2)}) collective-permute-start(f32[160,128]{1,0:T(8,128)S(1)} %get-tuple-element.37), channel_id=1, source_target_pairs={{0,1},{1,0},{2,3},{3,2},{4,5},{5,4},{6,7},{7,6},{8,9},{9,8},{10,11... | collective-permute-start | bytes 245768 | tf_op jit(solution)/shard_map/ppermute | solution.py:754
  22.4 0.7 %collective-permute-start.4 = (f32[160,128]{1,0:T(8,128)S(1)}, f32[160,128]{1,0:T(8,128)S(1)}, u32[]{:S(2)}, u32[]{:S(2)}) collective-permute-start(f32[160,128]{1,0:T(8,128)S(1)} %get-tuple-element.38), channel_id=1, source_target_pairs={{1,2},{2,1},{3,4},{4,3},{5,6},{6,5},{9,10},{10,9},{11,12},{12,11},... | collective-permute-start | bytes 245768 | tf_op jit(solution)/shard_map/ppermute | solution.py:754
  23.1 0.0 copy-done
  23.1 0.0 copy-done.1
  23.1 6.8 %filter_inner.1 = (f32[10,32,128]{2,1,0:T(8,128)S(1)}, f32[10,32,128]{2,1,0:T(8,128)S(1)}, f32[10,32,128]{2,1,0:T(8,128)S(1)}, f32[2048,128]{1,0:T(8,128)S(1)}, f32[128,128]{1,0:T(8,128)S(1)}) custom-call(s32[6]{0:T(128)S(1)} %convert_element_type.3.flags, f32[16,48,128]{2,1,0:T(8,128)S(1)} %energy_middle.1.src, f32[16,8,128]{2,1,0:T(8,128)S(1)} %get-tuple-element.35.rim, ...), custom_call_target="tpu_custom_call" | custom-call | flops 8999999488 | bytes 1048576 | tf_op jit(solution)/shard_map/filter_inner/pallas_call | solution.py:595
  29.9 0.0 collective-permute-done.3.got_even
  29.9 0.0 collective-permute-done.4.got_odd
  29.9 5.9 %filter_outer.1 = (f32[6,32,128]{2,1,0:T(8,128)S(1)}, f32[6,32,128]{2,1,0:T(8,128)S(1)}, f32[6,32,128]{2,1,0:T(8,128)S(1)}, f32[1,256]{1,0:T(1,128)S(1)}) custom-call(s32[6]{0:T(128)S(1)} %convert_element_type.3.flags, f32[16,48,128]{2,1,0:T(8,128)S(1)} %energy_middle.1.src, f32[16,8,128]{2,1,0:T(8,128)S(1)} %get-tuple-element.35.rim, ...), custom_call_target="tpu_custom_call" | custom-call | flops 3000000000 | bytes 1048576 | tf_op jit(solution)/shard_map/filter_outer/pallas_call | solution.py:690
  35.8 17.0 %all_to_all.8 = f32[32,1,256]{2,1,0:T(1,128)S(1)} all-to-all(f32[32,1,256]{2,1,0:T(1,128)S(1)} %broadcast_in_dim.2), channel_id=1, replica_groups=mesh['gz'=4,'gy'=8] {'gz','gy'}, dimensions={0} | all-to-all | bytes 65536 | tf_op jit(solution)/shard_map/all_to_all | solution.py:782
  52.8 0.9 %update.1 = (f32[16,32,128]{2,1,0:T(8,128)}, f32[1]{0:T(128)}) custom-call(f32[32,256]{1,0:T(8,128)S(1)} %bitcast.11, f32[10,32,128]{2,1,0:T(8,128)S(1)} %get-tuple-element.42.amp_i, f32[10,32,128]{2,1,0:T(8,128)S(1)} %get-tuple-element.43.low_i, f32[10,32,128]{2,1,0:T(8,128)S(1)} %get-tuple-element.44.high_i, f32[6,32,128]{2,1,0:T(8,128)S(1)} %get-tuple-element.45.amp_o, ...), custom_call_target="tpu_custom_call" | custom-call | flops 1000000000 | bytes 1048576 | tf_op jit(solution)/shard_map/update/pallas_call | solution.py:734
  (3 shorter events, 0.0 us)
Async XLA Ops:
  1.6 9.8 %collective-permute-start = (f32[9,32,128]{2,1,0:T(8,128)S(1)}, f32[9,32,128]{2,1,0:T(8,128)S(1)}, u32[]{:S(2)}, u32[]{:S(2)}) collective-permute-start(f32[9,32,128]{2,1,0:T(8,128)S(1)} %face.1), channel_id=1, source_target_pairs={{1,0},{2,1},{3,2},{4,3},{5,4},{6,5},{7,6},{9,8},{10,9},{11,10},{12... | collective-permute-start | bytes 442376 | tf_op jit(solution)/shard_map/ppermute | solution.py:747
  10.2 6.9 %collective-permute-start.1 = (f32[14,16,128]{2,1,0:T(8,128)S(1)}, f32[14,16,128]{2,1,0:T(8,128)S(1)}, u32[]{:S(2)}, u32[]{:S(2)}) collective-permute-start(f32[14,16,128]{2,1,0:T(8,128)S(1)} %get-tuple-element.30), channel_id=1, source_target_pairs={{0,8},{8,0},{16,24},{24,16},{1,9},{9,1},{17,25},{25,17},{2,10},{10... | collective-permute-start | bytes 344072 | tf_op jit(solution)/shard_map/ppermute | solution.py:754
  10.7 6.4 %collective-permute-start.2 = (f32[14,16,128]{2,1,0:T(8,128)S(1)}, f32[14,16,128]{2,1,0:T(8,128)S(1)}, u32[]{:S(2)}, u32[]{:S(2)}) collective-permute-start(f32[14,16,128]{2,1,0:T(8,128)S(1)} %get-tuple-element.31), channel_id=1, source_target_pairs={{8,16},{16,8},{9,17},{17,9},{10,18},{18,10},{11,19},{19,11},{12,20... | collective-permute-start | bytes 344072 | tf_op jit(solution)/shard_map/ppermute | solution.py:754
  17.1 6.0 %copy-start = (s32[16,32,128]{2,1,0:T(8,128)S(1)}, s32[16,32,128]{2,1,0:T(8,128)}, u32[]{:S(2)}) copy-start(s32[16,32,128]{2,1,0:T(8,128)} %passive.3) | copy-start | bytes 786436
  17.1 6.0 %copy-start.1 = (s32[16,32,128]{2,1,0:T(8,128)S(1)}, s32[16,32,128]{2,1,0:T(8,128)}, u32[]{:S(2)}) copy-start(s32[16,32,128]{2,1,0:T(8,128)} %solid.3) | copy-start | bytes 786436
  19.2 10.6 %collective-permute-start.3 = (f32[160,128]{1,0:T(8,128)S(1)}, f32[160,128]{1,0:T(8,128)S(1)}, u32[]{:S(2)}, u32[]{:S(2)}) collective-permute-start(f32[160,128]{1,0:T(8,128)S(1)} %get-tuple-element.37), channel_id=1, source_target_pairs={{0,1},{1,0},{2,3},{3,2},{4,5},{5,4},{6,7},{7,6},{8,9},{9,8},{10,11... | collective-permute-start | bytes 245768 | tf_op jit(solution)/shard_map/ppermute | solution.py:754
  22.4 7.5 %collective-permute-start.4 = (f32[160,128]{1,0:T(8,128)S(1)}, f32[160,128]{1,0:T(8,128)S(1)}, u32[]{:S(2)}, u32[]{:S(2)}) collective-permute-start(f32[160,128]{1,0:T(8,128)S(1)} %get-tuple-element.38), channel_id=1, source_target_pairs={{1,2},{2,1},{3,4},{4,3},{5,6},{6,5},{9,10},{10,9},{11,12},{12,11},... | collective-permute-start | bytes 245768 | tf_op jit(solution)/shard_map/ppermute | solution.py:754

commit v14 on v12

--- a/solution.py
+++ b/solution.py
@@ -179,7 +179,7 @@
         prepare(segments(y + 2), y + 2, work)
         return 0
 
-    lax.fori_loop(0, rows - 1, body, 0, unroll=2)
+    lax.fori_loop(0, rows - 1, body, 0, unroll=7)
     put(rows - 1)
 
 
@@ -586,7 +586,7 @@
 
         edges = (flags[0], 1) if b == 0 else (1, flags[1])
         filter_block(s_s.at[b], d_s.at[b], 6 + b, (flags[2], flags[3]), edges, finish, True)
-    table(5, nz, nx, amp, low, high, now_s, fine_s, vol, tgt, (vol_i, tgt_i), True)
+    table(5, nz, nx, amp, low, high, now_s, fine_s, vol, tgt, (vol_i, tgt_i), 2)
 
     def lanes(ref, count):
         total = ref[pl.ds(0, count, stride=8), :]

time: 48.5 us -> 46.4 us (0.957)
  Pallas kernels: 23.5 us -> 20.6 us
  waiting for transfers between devices: 0.85 us -> 1.6 us
    pallas_call x1, Pallas kernels: 5.31 us -> 3.96 us  [outer_call(): pl.pallas_call(outer_kernel, in_specs=[SMEM] + [VMEM] * 11, out_shape=(fi...]
    pallas_call x1, Pallas kernels: 3.06 us -> 2.27 us  [middle_call(): pl.pallas_call(middle_kernel, in_specs=[VMEM] * 5, out_shape=jax.ShapeDty...]
    pallas_call x1, Pallas kernels: 3.49 us -> 2.74 us  [ends_call(): pl.pallas_call(ends_kernel, in_specs=[SMEM] + [VMEM] * 3, out_shape=(jax....]
    ppermute x1, waiting for transfers between devices: 0.84 us -> 1.59 us  [to_lower(): return lax.ppermute(value, axis, [(i + 1, i) for i in range(count - 1)])]
  transfers between devices with their start and end apart: 5 -> 5, of which waited for: 1 -> 1; matrix products, arithmetic and copies ran while one was open for 0% -> 0% of each run, Pallas kernels for 32% -> 30%
where the time goes in v14:
time: 46.4 us; the launch traced here: 46.1 us
  Pallas kernels  20.6 us (44%)
  blocking collectives  17.2 us (37%)
  starting transfers between devices  5.82 us (13%)
  waiting for transfers between devices  1.6 us (3%)
  between operations  0.79 us (2%)
    all_to_all x1, blocking collectives, on_device(): tables = lax.all_to_all(everyone, ('gz', 'gy'), 0, 0, tiled=True)  17.2 us
    pallas_call x1, Pallas kernels, inner_call(): pl.pallas_call(inner_kernel, in_specs=[SMEM] + [VMEM] * 5, out_shape=(fie...  7.04 us
    ppermute x4, starting transfers between devices, swap(): return lax.ppermute(value, axis, pairs)  4.53 us
    pallas_call x1, Pallas kernels, outer_call(): pl.pallas_call(outer_kernel, in_specs=[SMEM] + [VMEM] * 11, out_shape=(fi...  3.96 us
    pallas_call x1, Pallas kernels, ends_call(): pl.pallas_call(ends_kernel, in_specs=[SMEM] + [VMEM] * 3, out_shape=(jax....  2.74 us
    pallas_call x1, Pallas kernels, middle_call(): pl.pallas_call(middle_kernel, in_specs=[VMEM] * 5, out_shape=jax.ShapeDty...  2.27 us
    pallas_call x1, Pallas kernels, load_call(): pl.pallas_call(load_kernel, in_specs=[HBM, HBM, HBM], out_shape=(jax.Shap...  1.72 us
    ppermute x1, waiting for transfers between devices, to_lower(): return lax.ppermute(value, axis, [(i + 1, i) for i in range(count - 1)])  1.59 us
  transfers between devices with their start and end apart: 5, of which 1 were waited for; matrix products, arithmetic and copies ran while one was open for 0% of the time, Pallas kernels for 30%

profile of v14, /device:TPU:0, one launch (start us, length us, event | category | flops | bytes accessed | tf_op | source)
XLA Modules:
  0.0 46.1 jit_solution(4648144329285737597)
XLA Ops:
  0.6 0.9 %face.1 = f32[9,32,128]{2,1,0:T(8,128)S(1)} custom-call(f32[9,16,32,128]{3,2,1,0:T(8,128)} %disp.1), custom_call_target="tpu_custom_call" | custom-call | tf_op jit(solution)/shard_map/face/pallas_call | solution.py:194
  1.6 1.3 %collective-permute-start = (f32[9,32,128]{2,1,0:T(8,128)S(1)}, f32[9,32,128]{2,1,0:T(8,128)S(1)}, u32[]{:S(2)}, u32[]{:S(2)}) collective-permute-start(f32[9,32,128]{2,1,0:T(8,128)S(1)} %face.1), channel_id=1, source_target_pairs={{1,0},{2,1},{3,2},{4,3},{5,4},{6,5},{7,6},{9,8},{10,9},{11,10},{12... | collective-permute-start | bytes 442376 | tf_op jit(solution)/shard_map/ppermute | solution.py:664
  2.9 0.1 stack.27
  3.0 1.7 %load.1 = (f32[9,16,32,128]{3,2,1,0:T(8,128)S(1)}, f32[16,32,128]{2,1,0:T(8,128)S(1)}, bf16[192,224]{1,0:T(8,128)(2,1)S(1)}, bf16[192,224]{1,0:T(8,128)(2,1)S(1)}) custom-call(f32[9,16,32,128]{3,2,1,0:T(8,128)} %disp.1, f32[16,32,128]{2,1,0:T(8,128)} %dens_h.1, f32[24,24]{1,0:T(8,128)} %stiff.1), custom_call_target="tpu_custom_call" | custom-call | flops 2000000000 | bytes 1048576 | tf_op jit(solution)/shard_map/load/pallas_call | solution.py:225
  4.7 2.7 %energy_ends.1 = (f32[16,16,128]{2,1,0:T(8,128)S(1)}, f32[14,16,128]{2,1,0:T(8,128)S(1)}, f32[14,16,128]{2,1,0:T(8,128)S(1)}, f32[14,16,128]{2,1,0:T(8,128)S(1)}, f32[14,16,128]{2,1,0:T(8,128)S(1)}) custom-call(s32[6]{0:T(128)S(1)} %convert_element_type.3.flags, f32[9,16,32,128]{3,2,1,0:T(8,128)S(1)} %get-tuple-element.26.disp, ...), custom_call_target="tpu_custom_call" | custom-call | flops 4000000000 | bytes 1048576 | tf_op jit(solution)/shard_map/energy_ends/pallas_call | solution.py:285
  7.5 0.5 %collective-permute-start.1 = (f32[14,16,128]{2,1,0:T(8,128)S(1)}, f32[14,16,128]{2,1,0:T(8,128)S(1)}, u32[]{:S(2)}, u32[]{:S(2)}) collective-permute-start(f32[14,16,128]{2,1,0:T(8,128)S(1)} %get-tuple-element.30), channel_id=1, source_target_pairs={{0,8},{8,0},{16,24},{24,16},{1,9},{9,1},{17,25},{25,17},{2,10},{10... | collective-permute-start | bytes 344072 | tf_op jit(solution)/shard_map/ppermute | solution.py:671
  8.0 0.7 %collective-permute-start.2 = (f32[14,16,128]{2,1,0:T(8,128)S(1)}, f32[14,16,128]{2,1,0:T(8,128)S(1)}, u32[]{:S(2)}, u32[]{:S(2)}) collective-permute-start(f32[14,16,128]{2,1,0:T(8,128)S(1)} %get-tuple-element.31), channel_id=1, source_target_pairs={{8,16},{16,8},{9,17},{17,9},{10,18},{18,10},{11,19},{19,11},{12,20... | collective-permute-start | bytes 344072 | tf_op jit(solution)/shard_map/ppermute | solution.py:671
  8.7 1.6 %collective-permute-done.fy = f32[9,32,128]{2,1,0:T(8,128)S(1)} collective-permute-done((f32[9,32,128]{2,1,0:T(8,128)S(1)}, f32[9,32,128]{2,1,0:T(8,128)S(1)}, u32[]{:S(2)}, u32[]{:S(2)}) %collective-permute-start) | collective-permute-done | bytes 147488 | tf_op jit(solution)/shard_map/ppermute | solution.py:664
  10.2 2.3 %energy_middle.1.src = f32[16,48,128]{2,1,0:T(8,128)S(1)} custom-call(f32[9,16,32,128]{3,2,1,0:T(8,128)S(1)} %get-tuple-element.26.disp, f32[16,32,128]{2,1,0:T(8,128)S(1)} %get-tuple-element.27.dens, f32[9,32,128]{2,1,0:T(8,128)S(1)} %collective-permute-done.fy, bf16[192,224]{1,0:T(8,128)(2,1)S(1)} %get-tuple-element.28.mat, ...), custom_call_target="tpu_custom_call" | custom-call | flops 4000000000 | bytes 1048576 | tf_op jit(solution)/shard_map/energy_middle/pallas_call | solution.py:323
  12.5 0.0 collective-permute-done.1.got_even
  12.5 0.0 collective-permute-done.2.got_odd
  12.5 0.0 copy-start
  12.6 0.0 copy-start.1
  12.6 1.0 %energy_rim.1 = (f32[16,8,128]{2,1,0:T(8,128)S(1)}, f32[2,10,8,128]{3,2,1,0:T(8,128)S(1)}, f32[160,128]{1,0:T(8,128)S(1)}, f32[160,128]{1,0:T(8,128)S(1)}) custom-call(s32[6]{0:T(128)S(1)} %convert_element_type.3.flags, f32[14,16,128]{2,1,0:T(8,128)S(1)} %collective-permute-done.1.got_even, f32[14,16,128]{2,1,0:T(8,128)S(1)} %collective-permute-done.2.got_odd, ...), custom_call_target="tpu_custom_call" | custom-call | flops 2000000000 | bytes 1048576 | tf_op jit(solution)/shard_map/energy_rim/pallas_call | solution.py:405
  13.5 2.7 %collective-permute-start.3 = (f32[160,128]{1,0:T(8,128)S(1)}, f32[160,128]{1,0:T(8,128)S(1)}, u32[]{:S(2)}, u32[]{:S(2)}) collective-permute-start(f32[160,128]{1,0:T(8,128)S(1)} %get-tuple-element.37), channel_id=1, source_target_pairs={{0,1},{1,0},{2,3},{3,2},{4,5},{5,4},{6,7},{7,6},{8,9},{9,8},{10,11... | collective-permute-start | bytes 245768 | tf_op jit(solution)/shard_map/ppermute | solution.py:671
  16.2 0.7 %collective-permute-start.4 = (f32[160,128]{1,0:T(8,128)S(1)}, f32[160,128]{1,0:T(8,128)S(1)}, u32[]{:S(2)}, u32[]{:S(2)}) collective-permute-start(f32[160,128]{1,0:T(8,128)S(1)} %get-tuple-element.38), channel_id=1, source_target_pairs={{1,2},{2,1},{3,4},{4,3},{5,6},{6,5},{9,10},{10,9},{11,12},{12,11},... | collective-permute-start | bytes 245768 | tf_op jit(solution)/shard_map/ppermute | solution.py:671
  16.9 0.0 copy-done
  16.9 0.0 copy-done.1
  16.9 7.0 %filter_inner.1 = (f32[11,32,128]{2,1,0:T(8,128)S(1)}, f32[11,32,128]{2,1,0:T(8,128)S(1)}, f32[11,32,128]{2,1,0:T(8,128)S(1)}, f32[2048,128]{1,0:T(8,128)S(1)}, f32[128,128]{1,0:T(8,128)S(1)}) custom-call(s32[6]{0:T(128)S(1)} %convert_element_type.3.flags, f32[16,48,128]{2,1,0:T(8,128)S(1)} %energy_middle.1.src, f32[16,8,128]{2,1,0:T(8,128)S(1)} %get-tuple-element.35.rim, ...), custom_call_target="tpu_custom_call" | custom-call | flops 8999999488 | bytes 1048576 | tf_op jit(solution)/shard_map/filter_inner/pallas_call | solution.py:524
  24.0 0.0 collective-permute-done.3.got_even
  24.0 0.0 collective-permute-done.4.got_odd
  24.0 4.0 %filter_outer.1 = (f32[5,32,128]{2,1,0:T(8,128)S(1)}, f32[5,32,128]{2,1,0:T(8,128)S(1)}, f32[5,32,128]{2,1,0:T(8,128)S(1)}, f32[1,256]{1,0:T(1,128)S(1)}) custom-call(s32[6]{0:T(128)S(1)} %convert_element_type.3.flags, f32[16,48,128]{2,1,0:T(8,128)S(1)} %energy_middle.1.src, f32[16,8,128]{2,1,0:T(8,128)S(1)} %get-tuple-element.35.rim, ...), custom_call_target="tpu_custom_call" | custom-call | flops 3000000000 | bytes 1048576 | tf_op jit(solution)/shard_map/filter_outer/pallas_call | solution.py:606
  28.0 17.2 %all_to_all.8 = f32[32,1,256]{2,1,0:T(1,128)S(1)} all-to-all(f32[32,1,256]{2,1,0:T(1,128)S(1)} %broadcast_in_dim.2), channel_id=1, replica_groups=mesh['gz'=4,'gy'=8] {'gz','gy'}, dimensions={0} | all-to-all | bytes 65536 | tf_op jit(solution)/shard_map/all_to_all | solution.py:699
  45.2 0.9 %update.1 = (f32[16,32,128]{2,1,0:T(8,128)}, f32[1]{0:T(128)}) custom-call(f32[32,256]{1,0:T(8,128)S(1)} %bitcast.11, f32[11,32,128]{2,1,0:T(8,128)S(1)} %get-tuple-element.42.amp_i, f32[11,32,128]{2,1,0:T(8,128)S(1)} %get-tuple-element.43.low_i, f32[11,32,128]{2,1,0:T(8,128)S(1)} %get-tuple-element.44.high_i, f32[5,32,128]{2,1,0:T(8,128)S(1)} %get-tuple-element.45.amp_o, ...), custom_call_target="tpu_custom_call" | custom-call | flops 1000000000 | bytes 1048576 | tf_op jit(solution)/shard_map/update/pallas_call | solution.py:651
  (3 shorter events, 0.0 us)
Async XLA Ops:
  1.6 8.7 %collective-permute-start = (f32[9,32,128]{2,1,0:T(8,128)S(1)}, f32[9,32,128]{2,1,0:T(8,128)S(1)}, u32[]{:S(2)}, u32[]{:S(2)}) collective-permute-start(f32[9,32,128]{2,1,0:T(8,128)S(1)} %face.1), channel_id=1, source_target_pairs={{1,0},{2,1},{3,2},{4,3},{5,4},{6,5},{7,6},{9,8},{10,9},{11,10},{12... | collective-permute-start | bytes 442376 | tf_op jit(solution)/shard_map/ppermute | solution.py:664
  7.5 5.0 %collective-permute-start.1 = (f32[14,16,128]{2,1,0:T(8,128)S(1)}, f32[14,16,128]{2,1,0:T(8,128)S(1)}, u32[]{:S(2)}, u32[]{:S(2)}) collective-permute-start(f32[14,16,128]{2,1,0:T(8,128)S(1)} %get-tuple-element.30), channel_id=1, source_target_pairs={{0,8},{8,0},{16,24},{24,16},{1,9},{9,1},{17,25},{25,17},{2,10},{10... | collective-permute-start | bytes 344072 | tf_op jit(solution)/shard_map/ppermute | solution.py:671
  8.0 4.5 %collective-permute-start.2 = (f32[14,16,128]{2,1,0:T(8,128)S(1)}, f32[14,16,128]{2,1,0:T(8,128)S(1)}, u32[]{:S(2)}, u32[]{:S(2)}) collective-permute-start(f32[14,16,128]{2,1,0:T(8,128)S(1)} %get-tuple-element.31), channel_id=1, source_target_pairs={{8,16},{16,8},{9,17},{17,9},{10,18},{18,10},{11,19},{19,11},{12,20... | collective-permute-start | bytes 344072 | tf_op jit(solution)/shard_map/ppermute | solution.py:671
  12.5 4.4 %copy-start = (s32[16,32,128]{2,1,0:T(8,128)S(1)}, s32[16,32,128]{2,1,0:T(8,128)}, u32[]{:S(2)}) copy-start(s32[16,32,128]{2,1,0:T(8,128)} %passive.3) | copy-start | bytes 786436
  12.6 4.4 %copy-start.1 = (s32[16,32,128]{2,1,0:T(8,128)S(1)}, s32[16,32,128]{2,1,0:T(8,128)}, u32[]{:S(2)}) copy-start(s32[16,32,128]{2,1,0:T(8,128)} %solid.3) | copy-start | bytes 786436
  13.5 10.4 %collective-permute-start.3 = (f32[160,128]{1,0:T(8,128)S(1)}, f32[160,128]{1,0:T(8,128)S(1)}, u32[]{:S(2)}, u32[]{:S(2)}) collective-permute-start(f32[160,128]{1,0:T(8,128)S(1)} %get-tuple-element.37), channel_id=1, source_target_pairs={{0,1},{1,0},{2,3},{3,2},{4,5},{5,4},{6,7},{7,6},{8,9},{9,8},{10,11... | collective-permute-start | bytes 245768 | tf_op jit(solution)/shard_map/ppermute | solution.py:671
  16.2 7.7 %collective-permute-start.4 = (f32[160,128]{1,0:T(8,128)S(1)}, f32[160,128]{1,0:T(8,128)S(1)}, u32[]{:S(2)}, u32[]{:S(2)}) collective-permute-start(f32[160,128]{1,0:T(8,128)S(1)} %get-tuple-element.38), channel_id=1, source_target_pairs={{1,2},{2,1},{3,4},{4,3},{5,6},{6,5},{9,10},{10,9},{11,12},{12,11},... | collective-permute-start | bytes 245768 | tf_op jit(solution)/shard_map/ppermute | solution.py:671

commit v15 on v14

--- a/solution.py
+++ b/solution.py
@@ -293,7 +293,7 @@
     )(flags, disp, dens, mat)
 
 
-def middle_kernel(disp, dens, fy, mat, ends, src, *work):
+def middle_kernel(disp, dens, fy, mat, ends, passive, solid, src, low, high, tgt, now_s, *work):
     _, ny, nz, nx = disp.shape
     work, last = work[:3], work[3:]
 
@@ -317,18 +317,33 @@
     frame(ny - 1)
     src[ny - 1, OFF : OFF + nz] = energy_rows(0, mat, last, dens[ny - 1])
 
-
-def middle_call(disp, dens, fy, mat, ends):
+    def bound(y, _):
+        low[y], high[y], now_s[y] = limits(dens[y], passive[y] == 1, solid[y] == 1)
+        return 0
+
+    lax.fori_loop(0, ny, bound, 0, unroll=4)
+    targets(((ny - 5, inner_row), (5, outer_row(ny))), nz, nx, now_s, tgt)
+
+
+def middle_call(disp, dens, fy, mat, ends, passive, solid):
     _, ny, nz, nx = disp.shape
+    field = jax.ShapeDtypeStruct((ny, nz, nx), f32)
     return pl.pallas_call(
         middle_kernel,
-        in_specs=[VMEM] * 5,
-        out_shape=jax.ShapeDtypeStruct((ny, nz + 2 * OFF, nx), f32),
-        scratch_shapes=workspace(ny, nz // 8 - 2, nx) + workspace(2, nz // 8, nx),
+        in_specs=[VMEM] * 7,
+        out_shape=(
+            jax.ShapeDtypeStruct((ny, nz + 2 * OFF, nx), f32),
+            field,
+            field,
+            jax.ShapeDtypeStruct((8 * COARSE, nx), f32),
+        ),
+        scratch_shapes=[pltpu.VMEM((ny, nz, nx), f32)]
+        + workspace(ny, nz // 8 - 2, nx)
+        + workspace(2, nz // 8, nx),
         compiler_params=pltpu.CompilerParams(vmem_limit_bytes=24 * 2**20),
         cost_estimate=estimate(4),
         name="energy_middle",
-    )(disp, dens, fy, mat, ends)
+    )(disp, dens, fy, mat, ends, passive, solid)
 
 
 def rim_kernel(
@@ -452,36 +467,55 @@
     lax.fori_loop(0, n - 4, third, 0, unroll=unroll)
 
 
-def limits(p3, d, pas, sol):
-    amp = jnp.sqrt(jnp.maximum(-p3 * d, 0.0))
+def limits(d, pas, sol):
     lower = jnp.maximum(d - move_limit, floor_density)
     upper = jnp.minimum(d + move_limit, 1.0)
-    low, high, now = (jnp.where(sol, 1.0, jnp.where(pas, floor_density, v)) for v in (lower, upper, d))
-    return amp, low, high, now
+    return tuple(jnp.where(sol, 1.0, jnp.where(pas, floor_density, v)) for v in (lower, upper, d))
 
 
 FINE = 16
 COARSE = POINTS // FINE
 
 
-def table(n, nz, nx, amp, low, high, now, fine_s, vol, tgt, start, unroll):
-    spacing = 2.0 * bracket_end / POINTS
-
+SPACING = 2.0 * bracket_end / POINTS
+
+
+def inverse_coarse(i):
+    return math.exp(0.5 * (-bracket_end + SPACING * FINE * i))
+
+
+def targets(rows, nz, nx, now, tgt):
+    acc = tuple(jnp.zeros((8, nx), f32) for _ in range(COARSE))
+    for n, row in rows:
+
+        def add(j, acc):
+            acc = list(acc)
+            for w in range(nz // 8):
+                d = now[row(j), 8 * w : 8 * w + 8]
+                for i in range(COARSE):
+                    acc[i] = acc[i] + d * inverse_coarse(i)
+            return tuple(acc)
+
+        acc = lax.fori_loop(0, n, add, acc, unroll=2)
+    for i in range(COARSE):
+        tgt[8 * i : 8 * i + 8] = acc[i]
+
+
+def table(n, nz, nx, amp, low, high, row, fine_s, vol, start, unroll):
     pair = 2
     for first in range(0, COARSE, pair):
-        inverse = [math.exp(0.5 * (-bracket_end + spacing * FINE * i)) for i in range(first, first + pair)]
+        inverse = [inverse_coarse(i) for i in range(first, first + pair)]
 
         def volume(j, acc):
             acc = list(acc)
+            y = row(j)
             for w in range(nz // 8):
                 at = slice(8 * w, 8 * w + 8)
-                lo, hi, d = low[j, at], high[j, at], now[j, at]
+                lo, hi = low[y, at], high[y, at]
                 los, his = [lo * c for c in inverse], [hi * c for c in inverse]
-                for i, c in enumerate(inverse):
-                    acc[pair * FINE + i] = acc[pair * FINE + i] + d * c
                 for f in range(FINE):
                     if first == 0:
-                        t = amp[j, at] * math.exp(-0.5 * spacing * f)
+                        t = amp[j, at] * math.exp(-0.5 * SPACING * f)
                         fine_s[f, j, at] = t
                     else:
                         t = fine_s[f, j, at]
@@ -489,18 +523,22 @@
                         acc[i * FINE + f] = acc[i * FINE + f] + jnp.minimum(jnp.maximum(t, los[i]), his[i])
             return tuple(acc)
 
-        places = [(vol, 8 * (first * FINE + e)) for e in range(pair * FINE)]
-        places += [(tgt, 8 * (first + i)) for i in range(pair)]
-        if start is None:
-            begin = tuple(jnp.zeros((8, nx), f32) for _ in places)
-        else:
-            begin = tuple((start[0] if ref is vol else start[1])[at : at + 8] for ref, at in places)
+        places = [slice(8 * (first * FINE + e), 8 * (first * FINE + e) + 8) for e in range(pair * FINE)]
+        begin = tuple(jnp.zeros((8, nx), f32) if start is None else start[at] for at in places)
         acc = lax.fori_loop(0, n, volume, begin, unroll=unroll)
-        for (ref, at), value in zip(places, acc):
-            ref[at : at + 8] = value
-
-
-def inner_kernel(flags, src, rim, dens, passive, solid, amp, low, high, vol, tgt, s_s, d_s, now_s, fine_s):
+        for at, value in zip(places, acc):
+            vol[at] = value
+
+
+def inner_row(j):
+    return j + 2
+
+
+def outer_row(ny):
+    return lambda j: jnp.where(j < 2, j, j + ny - 5)
+
+
+def inner_kernel(flags, src, rim, dens, low, high, amp, vol, s_s, d_s, fine_s):
     ny, nz, nx = dens.shape
     s_s[...] = src[0 : ny - 1]
 
@@ -511,41 +549,36 @@
     lax.fori_loop(0, ny - 1, fix, 0, unroll=5)
 
     def finish(j, p3):
-        y = j + 2
-        amp[j], low[j], high[j], now_s[j] = limits(p3, dens[y], passive[y] == 1, solid[y] == 1)
-
-    filter_block(s_s, d_s, ny - 1, (flags[2], flags[3]), None, finish, 4)
-    table(ny - 5, nz, nx, amp, low, high, now_s, fine_s, vol, tgt, None, 4)
-
-
-def inner_call(flags, src, rim, dens, passive, solid):
+        amp[j] = jnp.sqrt(jnp.maximum(-p3 * dens[inner_row(j)], 0.0))
+
+    filter_block(s_s, d_s, ny - 1, (flags[2], flags[3]), None, finish, True)
+    table(ny - 5, nz, nx, amp, low, high, inner_row, fine_s, vol, None, 4)
+
+
+def inner_call(flags, src, rim, dens, low, high):
     ny, nz, nx = dens.shape
-    field = jax.ShapeDtypeStruct((ny - 5, nz, nx), f32)
+    rows = nz + 2 * OFF
     return pl.pallas_call(
         inner_kernel,
         in_specs=[SMEM] + [VMEM] * 5,
         out_shape=(
-            field,
-            field,
-            field,
+            jax.ShapeDtypeStruct((ny - 5, nz, nx), f32),
             jax.ShapeDtypeStruct((8 * POINTS, nx), f32),
-            jax.ShapeDtypeStruct((8 * COARSE, nx), f32),
         ),
         scratch_shapes=[
-            pltpu.VMEM((ny - 1, nz + 2 * OFF, nx), f32),
-            pltpu.VMEM((ny - 3, nz + 2 * OFF, nx), f32),
-            pltpu.VMEM((ny - 5, nz, nx), f32),
+            pltpu.VMEM((ny - 1, rows, nx), f32),
+            pltpu.VMEM((ny - 3, rows, nx), f32),
             pltpu.VMEM((FINE, ny - 5, nz, nx), f32),
         ],
         compiler_params=pltpu.CompilerParams(vmem_limit_bytes=24 * 2**20),
         cost_estimate=estimate(9),
         name="filter_inner",
-    )(flags, src, rim, dens, passive, solid)
+    )(flags, src, rim, dens, low, high)
 
 
 def outer_kernel(
-    flags, src, rim, nodes, got_even, got_odd, mat, dens, passive, solid, vol_i, tgt_i,
-    amp, low, high, excess, s_s, d_s, now_s, fine_s, vol, tgt, below, above, *work,
+    flags, src, rim, nodes, got_even, got_odd, mat, dens, low, high, vol_i, tgt,
+    amp, excess, s_s, d_s, fine_s, vol, below, above, *work,
 ):
     ny, nz, nx = dens.shape
     odd = flags[4] == 1
@@ -580,13 +613,11 @@
         y0 = 0 if b == 0 else ny - 3
 
         def finish(j, p3):
-            y = y0 + j
-            at = 2 * b + j
-            amp[at], low[at], high[at], now_s[at] = limits(p3, dens[y], passive[y] == 1, solid[y] == 1)
+            amp[2 * b + j] = jnp.sqrt(jnp.maximum(-p3 * dens[y0 + j], 0.0))
 
         edges = (flags[0], 1) if b == 0 else (1, flags[1])
         filter_block(s_s.at[b], d_s.at[b], 6 + b, (flags[2], flags[3]), edges, finish, True)
-    table(5, nz, nx, amp, low, high, now_s, fine_s, vol, tgt, (vol_i, tgt_i), 2)
+    table(5, nz, nx, amp, low, high, outer_row(ny), fine_s, vol, vol_i, 2)
 
     def lanes(ref, count):
         total = ref[pl.ds(0, count, stride=8), :]
@@ -594,26 +625,23 @@
             total = total + ref[pl.ds(s, count, stride=8), :]
         return total
 
-    volumes, targets = lanes(vol, POINTS), lanes(tgt, COARSE)
-    over = [volumes[FINE * i : FINE * i + FINE] - targets[i : i + 1] for i in range(COARSE)]
+    volumes, present = lanes(vol, POINTS), lanes(tgt, COARSE)
+    over = [volumes[FINE * i : FINE * i + FINE] - present[i : i + 1] for i in range(COARSE)]
     excess[...] = jnp.sum(jnp.transpose(jnp.concatenate(over, axis=0)), axis=0, keepdims=True)
 
 
-def outer_call(flags, src, rim, nodes, got_even, got_odd, mat, dens, passive, solid, vol_i, tgt_i):
+def outer_call(flags, src, rim, nodes, got_even, got_odd, mat, dens, low, high, vol_i, tgt):
     ny, nz, nx = dens.shape
     rows = nz + 2 * OFF
-    field = jax.ShapeDtypeStruct((5, nz, nx), f32)
     return pl.pallas_call(
         outer_kernel,
         in_specs=[SMEM] + [VMEM] * 11,
-        out_shape=(field, field, field, jax.ShapeDtypeStruct((1, POINTS), f32)),
+        out_shape=(jax.ShapeDtypeStruct((5, nz, nx), f32), jax.ShapeDtypeStruct((1, POINTS), f32)),
         scratch_shapes=[
             pltpu.VMEM((2, 7, rows, nx), f32),
             pltpu.VMEM((2, 5, rows, nx), f32),
-            pltpu.VMEM((5, nz, nx), f32),
             pltpu.VMEM((FINE, 5, nz, nx), f32),
             pltpu.VMEM((8 * POINTS, nx), f32),
-            pltpu.VMEM((8 * COARSE, nx), f32),
             pltpu.VMEM(got_odd.shape, f32),
             pltpu.VMEM(got_odd.shape, f32),
         ]
@@ -621,10 +649,10 @@
         compiler_params=pltpu.CompilerParams(vmem_limit_bytes=20 * 2**20),
         cost_estimate=estimate(3),
         name="filter_outer",
-    )(flags, src, rim, nodes, got_even, got_odd, mat, dens, passive, solid, vol_i, tgt_i)
-
-
-def update_kernel(tables, amp_i, low_i, high_i, amp_o, low_o, high_o, new, logm):
+    )(flags, src, rim, nodes, got_even, got_odd, mat, dens, low, high, vol_i, tgt)
+
+
+def update_kernel(tables, amp_i, amp_o, low, high, new, logm):
     inner = amp_i.shape[0]
     nx = amp_i.shape[-1]
     total = jnp.sum(tables[...], axis=0, keepdims=True)
@@ -634,29 +662,28 @@
     logm[0] = middle
     scale = jnp.exp(jnp.full((1, nx), -0.5 * middle, f32))
 
-    def new_row(amp, low, high):
-        return jnp.minimum(jnp.maximum(amp * scale, low), high)
+    def new_row(y, amp):
+        new[y] = jnp.minimum(jnp.maximum(amp * scale, low[y]), high[y])
 
     def body(j, _):
-        new[j + 2] = new_row(amp_i[j], low_i[j], high_i[j])
+        new_row(inner_row(j), amp_i[j])
         return 0
 
-    lax.fori_loop(0, inner, body, 0)
+    lax.fori_loop(0, inner, body, 0, unroll=4)
     for j in range(5):
-        new[j if j < 2 else inner + j] = new_row(amp_o[j], low_o[j], high_o[j])
-
-
-def update_call(tables, inner, outer):
-    n, nz, nx = inner[0].shape
+        new_row(j if j < 2 else inner + j, amp_o[j])
+
+
+def update_call(tables, amp_i, amp_o, low, high):
     return pl.pallas_call(
         update_kernel,
-        in_specs=[VMEM] * 7,
+        in_specs=[VMEM] * 5,
         out_specs=(VMEM, SMEM),
-        out_shape=(jax.ShapeDtypeStruct((n + 5, nz, nx), f32), jax.ShapeDtypeStruct((1,), f32)),
+        out_shape=(jax.ShapeDtypeStruct(low.shape, f32), jax.ShapeDtypeStruct((1,), f32)),
         compiler_params=pltpu.CompilerParams(vmem_limit_bytes=8 * 2**20),
         cost_estimate=estimate(1),
         name="update",
-    )(tables, *inner, *outer)
+    )(tables, amp_i, amp_o, low, high)
 
 
 def to_lower(value, axis):
@@ -687,17 +714,17 @@
 
     z_got_even = swap(z_even, "gz", 0)
     z_got_odd = swap(z_odd, "gz", 1)
-    src = middle_call(disp, dens, fy, mat, ends)
+    src, low, high, tgt = middle_call(disp, dens, fy, mat, ends, passive, solid)
     rim, nodes, msg_even, msg_odd = rim_call(flags, z_got_even, z_got_odd, up, down, disp, dens, mat_y, src)
 
     got_even = swap(msg_even, "gy", 0)
     got_odd = swap(msg_odd, "gy", 1)
-    *inner, vol, tgt = inner_call(flags, src, rim, dens, passive, solid)
-    *outer, excess = outer_call(flags, src, rim, nodes, got_even, got_odd, mat, dens, passive, solid, vol, tgt)
+    amp_i, vol = inner_call(flags, src, rim, dens, low, high)
+    amp_o, excess = outer_call(flags, src, rim, nodes, got_even, got_odd, mat, dens, low, high, vol, tgt)
 
     everyone = jnp.broadcast_to(excess, (gz * gy, POINTS))
     tables = lax.all_to_all(everyone, ("gz", "gy"), 0, 0, tiled=True)
-    new, logm = update_call(tables, inner, outer)
+    new, logm = update_call(tables, amp_i, amp_o, low, high)
     return new, logm.reshape(())
 
 

time: 46.4 us -> 45.3 us (0.976)
  Pallas kernels: 20.6 us -> 19.8 us
    pallas_call x4, Pallas kernels: 14.2 us -> 13.6 us  [the longest x1 6.2 us: inner_call(): pl.pallas_call(inner_kernel, in_specs=[SMEM] + [VMEM] * 5, out_shape=(jax...]
  transfers between devices with their start and end apart: 5 -> 5, of which waited for: 1 -> 1; matrix products, arithmetic and copies ran while one was open for 0% -> 0% of each run, Pallas kernels for 30% -> 29%
where the time goes in v15:
time: 45.3 us; the launch traced here: 45 us
  Pallas kernels  19.8 us (44%)
  blocking collectives  16.8 us (37%)
  starting transfers between devices  5.82 us (13%)
  waiting for transfers between devices  1.7 us (4%)
  between operations  0.78 us (2%)
    all_to_all x1, blocking collectives, on_device(): tables = lax.all_to_all(everyone, ('gz', 'gy'), 0, 0, tiled=True)  16.8 us
    pallas_call x1, Pallas kernels, inner_call(): pl.pallas_call(inner_kernel, in_specs=[SMEM] + [VMEM] * 5, out_shape=(jax...  6.2 us
    ppermute x4, starting transfers between devices, swap(): return lax.ppermute(value, axis, pairs)  4.53 us
    pallas_call x1, Pallas kernels, outer_call(): pl.pallas_call(outer_kernel, in_specs=[SMEM] + [VMEM] * 11, out_shape=(ja...  3.85 us
    pallas_call x1, Pallas kernels, ends_call(): pl.pallas_call(ends_kernel, in_specs=[SMEM] + [VMEM] * 3, out_shape=(jax....  2.62 us
    pallas_call x1, Pallas kernels, middle_call(): pl.pallas_call(middle_kernel, in_specs=[VMEM] * 7, out_shape=(jax.ShapeDt...  2.6 us
    pallas_call x1, Pallas kernels, load_call(): pl.pallas_call(load_kernel, in_specs=[HBM, HBM, HBM], out_shape=(jax.Shap...  1.72 us
    ppermute x1, waiting for transfers between devices, to_lower(): return lax.ppermute(value, axis, [(i + 1, i) for i in range(count - 1)])  1.69 us
  transfers between devices with their start and end apart: 5, of which 1 were waited for; matrix products, arithmetic and copies ran while one was open for 0% of the time, Pallas kernels for 29%

profile of v15, /device:TPU:0, one launch (start us, length us, event | category | flops | bytes accessed | tf_op | source)
XLA Modules:
  0.0 45.0 jit_solution(4717551520249029890)
XLA Ops:
  0.6 0.9 %face.1 = f32[9,32,128]{2,1,0:T(8,128)S(1)} custom-call(f32[9,16,32,128]{3,2,1,0:T(8,128)} %disp.1), custom_call_target="tpu_custom_call" | custom-call | tf_op jit(solution)/shard_map/face/pallas_call | solution.py:194
  1.6 1.3 %collective-permute-start = (f32[9,32,128]{2,1,0:T(8,128)S(1)}, f32[9,32,128]{2,1,0:T(8,128)S(1)}, u32[]{:S(2)}, u32[]{:S(2)}) collective-permute-start(f32[9,32,128]{2,1,0:T(8,128)S(1)} %face.1), channel_id=1, source_target_pairs={{1,0},{2,1},{3,2},{4,3},{5,4},{6,5},{7,6},{9,8},{10,9},{11,10},{12... | collective-permute-start | bytes 442376 | tf_op jit(solution)/shard_map/ppermute | solution.py:691
  2.9 0.1 stack.27
  3.0 1.7 %load.1 = (f32[9,16,32,128]{3,2,1,0:T(8,128)S(1)}, f32[16,32,128]{2,1,0:T(8,128)S(1)}, bf16[192,224]{1,0:T(8,128)(2,1)S(1)}, bf16[192,224]{1,0:T(8,128)(2,1)S(1)}) custom-call(f32[9,16,32,128]{3,2,1,0:T(8,128)} %disp.1, f32[16,32,128]{2,1,0:T(8,128)} %dens_h.1, f32[24,24]{1,0:T(8,128)} %stiff.1), custom_call_target="tpu_custom_call" | custom-call | flops 2000000000 | bytes 1048576 | tf_op jit(solution)/shard_map/load/pallas_call | solution.py:225
  4.7 0.0 copy-start
  4.7 0.0 copy-start.1
  4.7 2.6 %energy_ends.1 = (f32[16,16,128]{2,1,0:T(8,128)S(1)}, f32[14,16,128]{2,1,0:T(8,128)S(1)}, f32[14,16,128]{2,1,0:T(8,128)S(1)}, f32[14,16,128]{2,1,0:T(8,128)S(1)}, f32[14,16,128]{2,1,0:T(8,128)S(1)}) custom-call(s32[6]{0:T(128)S(1)} %convert_element_type.3.flags, f32[9,16,32,128]{3,2,1,0:T(8,128)S(1)} %get-tuple-element.25.disp, ...), custom_call_target="tpu_custom_call" | custom-call | flops 4000000000 | bytes 1048576 | tf_op jit(solution)/shard_map/energy_ends/pallas_call | solution.py:285
  7.4 0.5 %collective-permute-start.1 = (f32[14,16,128]{2,1,0:T(8,128)S(1)}, f32[14,16,128]{2,1,0:T(8,128)S(1)}, u32[]{:S(2)}, u32[]{:S(2)}) collective-permute-start(f32[14,16,128]{2,1,0:T(8,128)S(1)} %get-tuple-element.30), channel_id=1, source_target_pairs={{0,8},{8,0},{16,24},{24,16},{1,9},{9,1},{17,25},{25,17},{2,10},{10... | collective-permute-start | bytes 344072 | tf_op jit(solution)/shard_map/ppermute | solution.py:698
  7.9 0.7 %collective-permute-start.2 = (f32[14,16,128]{2,1,0:T(8,128)S(1)}, f32[14,16,128]{2,1,0:T(8,128)S(1)}, u32[]{:S(2)}, u32[]{:S(2)}) collective-permute-start(f32[14,16,128]{2,1,0:T(8,128)S(1)} %get-tuple-element.31), channel_id=1, source_target_pairs={{8,16},{16,8},{9,17},{17,9},{10,18},{18,10},{11,19},{19,11},{12,20... | collective-permute-start | bytes 344072 | tf_op jit(solution)/shard_map/ppermute | solution.py:698
  8.6 1.7 %collective-permute-done.fy = f32[9,32,128]{2,1,0:T(8,128)S(1)} collective-permute-done((f32[9,32,128]{2,1,0:T(8,128)S(1)}, f32[9,32,128]{2,1,0:T(8,128)S(1)}, u32[]{:S(2)}, u32[]{:S(2)}) %collective-permute-start) | collective-permute-done | bytes 147488 | tf_op jit(solution)/shard_map/ppermute | solution.py:691
  10.2 0.0 copy-done
  10.2 0.0 copy-done.1
  10.2 2.6 %energy_middle.1 = (f32[16,48,128]{2,1,0:T(8,128)S(1)}, f32[16,32,128]{2,1,0:T(8,128)S(1)}, f32[16,32,128]{2,1,0:T(8,128)S(1)}, f32[128,128]{1,0:T(8,128)S(1)}) custom-call(f32[9,16,32,128]{3,2,1,0:T(8,128)S(1)} %get-tuple-element.25.disp, f32[16,32,128]{2,1,0:T(8,128)S(1)} %get-tuple-element.26.dens, f32[9,32,128]{2,1,0:T(8,128)S(1)} %collective-permute-done.fy, ...), custom_call_target="tpu_custom_call" | custom-call | flops 4000000000 | bytes 1048576 | tf_op jit(solution)/shard_map/energy_middle/pallas_call | solution.py:331
  12.9 0.0 collective-permute-done.1.got_even
  12.9 0.0 collective-permute-done.2.got_odd
  12.9 1.0 %energy_rim.1 = (f32[16,8,128]{2,1,0:T(8,128)S(1)}, f32[2,10,8,128]{3,2,1,0:T(8,128)S(1)}, f32[160,128]{1,0:T(8,128)S(1)}, f32[160,128]{1,0:T(8,128)S(1)}) custom-call(s32[6]{0:T(128)S(1)} %convert_element_type.3.flags, f32[14,16,128]{2,1,0:T(8,128)S(1)} %collective-permute-done.1.got_even, f32[14,16,128]{2,1,0:T(8,128)S(1)} %collective-permute-done.2.got_odd, ...), custom_call_target="tpu_custom_call" | custom-call | flops 2000000000 | bytes 1048576 | tf_op jit(solution)/shard_map/energy_rim/pallas_call | solution.py:420
  13.9 2.7 %collective-permute-start.3 = (f32[160,128]{1,0:T(8,128)S(1)}, f32[160,128]{1,0:T(8,128)S(1)}, u32[]{:S(2)}, u32[]{:S(2)}) collective-permute-start(f32[160,128]{1,0:T(8,128)S(1)} %get-tuple-element.37), channel_id=1, source_target_pairs={{0,1},{1,0},{2,3},{3,2},{4,5},{5,4},{6,7},{7,6},{8,9},{9,8},{10,11... | collective-permute-start | bytes 245768 | tf_op jit(solution)/shard_map/ppermute | solution.py:698
  16.6 0.7 %collective-permute-start.4 = (f32[160,128]{1,0:T(8,128)S(1)}, f32[160,128]{1,0:T(8,128)S(1)}, u32[]{:S(2)}, u32[]{:S(2)}) collective-permute-start(f32[160,128]{1,0:T(8,128)S(1)} %get-tuple-element.38), channel_id=1, source_target_pairs={{1,2},{2,1},{3,4},{4,3},{5,6},{6,5},{9,10},{10,9},{11,12},{12,11},... | collective-permute-start | bytes 245768 | tf_op jit(solution)/shard_map/ppermute | solution.py:698
  17.2 6.2 %filter_inner.1 = (f32[11,32,128]{2,1,0:T(8,128)S(1)}, f32[2048,128]{1,0:T(8,128)S(1)}) custom-call(s32[6]{0:T(128)S(1)} %convert_element_type.3.flags, f32[16,48,128]{2,1,0:T(8,128)S(1)} %get-tuple-element.29.src, f32[16,8,128]{2,1,0:T(8,128)S(1)} %get-tuple-element.35.rim, f32[16,32,128]{2,1,0:T(8,128)S(1)} %get-tuple-element.26.dens, ...), custom_call_target="tpu_custom_call" | custom-call | flops 8999999488 | bytes 1048576 | tf_op jit(solution)/shard_map/filter_inner/pallas_call | solution.py:561
  23.4 0.0 collective-permute-done.3.got_even
  23.4 0.0 collective-permute-done.4.got_odd
  23.4 3.9 %filter_outer.1 = (f32[5,32,128]{2,1,0:T(8,128)S(1)}, f32[1,256]{1,0:T(1,128)S(1)}) custom-call(s32[6]{0:T(128)S(1)} %convert_element_type.3.flags, f32[16,48,128]{2,1,0:T(8,128)S(1)} %get-tuple-element.29.src, f32[16,8,128]{2,1,0:T(8,128)S(1)} %get-tuple-element.35.rim, f32[2,10,8,128]{3,2,1,0:T(8,128)S(1)} %get-tuple-element.36.nodes, ...), custom_call_target="tpu_custom_call" | custom-call | flops 3000000000 | bytes 1048576 | tf_op jit(solution)/shard_map/filter_outer/pallas_call | solution.py:636
  27.3 16.8 %all_to_all.8 = f32[32,1,256]{2,1,0:T(1,128)S(1)} all-to-all(f32[32,1,256]{2,1,0:T(1,128)S(1)} %broadcast_in_dim.2), channel_id=1, replica_groups=mesh['gz'=4,'gy'=8] {'gz','gy'}, dimensions={0} | all-to-all | bytes 65536 | tf_op jit(solution)/shard_map/all_to_all | solution.py:726
  44.1 0.9 %update.1 = (f32[16,32,128]{2,1,0:T(8,128)}, f32[1]{0:T(128)}) custom-call(f32[32,256]{1,0:T(8,128)S(1)} %bitcast.11, f32[11,32,128]{2,1,0:T(8,128)S(1)} %get-tuple-element.44.amp_i, f32[5,32,128]{2,1,0:T(8,128)S(1)} %get-tuple-element.45.amp_o, f32[16,32,128]{2,1,0:T(8,128)S(1)} %get-tuple-element.39.low, f32[16,32,128]{2,1,0:T(8,128)S(1)} %get-tuple-element.40.high), custom_call_target="tpu_custom_call" | custom-call | flops 1000000000 | bytes 1048576 | tf_op jit(solution)/shard_map/update/pallas_call | solution.py:678
  (3 shorter events, 0.0 us)
Async XLA Ops:
  1.6 8.7 %collective-permute-start = (f32[9,32,128]{2,1,0:T(8,128)S(1)}, f32[9,32,128]{2,1,0:T(8,128)S(1)}, u32[]{:S(2)}, u32[]{:S(2)}) collective-permute-start(f32[9,32,128]{2,1,0:T(8,128)S(1)} %face.1), channel_id=1, source_target_pairs={{1,0},{2,1},{3,2},{4,3},{5,4},{6,5},{7,6},{9,8},{10,9},{11,10},{12... | collective-permute-start | bytes 442376 | tf_op jit(solution)/shard_map/ppermute | solution.py:691
  4.7 5.5 %copy-start = (s32[16,32,128]{2,1,0:T(8,128)S(1)}, s32[16,32,128]{2,1,0:T(8,128)}, u32[]{:S(2)}) copy-start(s32[16,32,128]{2,1,0:T(8,128)} %passive.1) | copy-start | bytes 786436
  4.7 5.5 %copy-start.1 = (s32[16,32,128]{2,1,0:T(8,128)S(1)}, s32[16,32,128]{2,1,0:T(8,128)}, u32[]{:S(2)}) copy-start(s32[16,32,128]{2,1,0:T(8,128)} %solid.1) | copy-start | bytes 786436
  7.4 5.5 %collective-permute-start.1 = (f32[14,16,128]{2,1,0:T(8,128)S(1)}, f32[14,16,128]{2,1,0:T(8,128)S(1)}, u32[]{:S(2)}, u32[]{:S(2)}) collective-permute-start(f32[14,16,128]{2,1,0:T(8,128)S(1)} %get-tuple-element.30), channel_id=1, source_target_pairs={{0,8},{8,0},{16,24},{24,16},{1,9},{9,1},{17,25},{25,17},{2,10},{10... | collective-permute-start | bytes 344072 | tf_op jit(solution)/shard_map/ppermute | solution.py:698
  7.9 5.0 %collective-permute-start.2 = (f32[14,16,128]{2,1,0:T(8,128)S(1)}, f32[14,16,128]{2,1,0:T(8,128)S(1)}, u32[]{:S(2)}, u32[]{:S(2)}) collective-permute-start(f32[14,16,128]{2,1,0:T(8,128)S(1)} %get-tuple-element.31), channel_id=1, source_target_pairs={{8,16},{16,8},{9,17},{17,9},{10,18},{18,10},{11,19},{19,11},{12,20... | collective-permute-start | bytes 344072 | tf_op jit(solution)/shard_map/ppermute | solution.py:698
  13.9 9.6 %collective-permute-start.3 = (f32[160,128]{1,0:T(8,128)S(1)}, f32[160,128]{1,0:T(8,128)S(1)}, u32[]{:S(2)}, u32[]{:S(2)}) collective-permute-start(f32[160,128]{1,0:T(8,128)S(1)} %get-tuple-element.37), channel_id=1, source_target_pairs={{0,1},{1,0},{2,3},{3,2},{4,5},{5,4},{6,7},{7,6},{8,9},{9,8},{10,11... | collective-permute-start | bytes 245768 | tf_op jit(solution)/shard_map/ppermute | solution.py:698
  16.6 6.9 %collective-permute-start.4 = (f32[160,128]{1,0:T(8,128)S(1)}, f32[160,128]{1,0:T(8,128)S(1)}, u32[]{:S(2)}, u32[]{:S(2)}) collective-permute-start(f32[160,128]{1,0:T(8,128)S(1)} %get-tuple-element.38), channel_id=1, source_target_pairs={{1,2},{2,1},{3,4},{4,3},{5,6},{6,5},{9,10},{10,9},{11,12},{12,11},... | collective-permute-start | bytes 245768 | tf_op jit(solution)/shard_map/ppermute | solution.py:698

commit v16 on v15

--- a/solution.py
+++ b/solution.py
@@ -183,59 +183,35 @@
     put(rows - 1)
 
 
-def face_kernel(disp, face, sem):
-    copy = pltpu.make_async_copy(disp.at[:, 0], face, sem)
-    copy.start()
-    copy.wait()
-
-
-def face_call(disp):
-    _, _, nz, nx = disp.shape
-    return pl.pallas_call(
-        face_kernel,
-        in_specs=[HBM],
-        out_shape=jax.ShapeDtypeStruct((9, nz, nx), f32),
-        scratch_shapes=[pltpu.SemaphoreType.DMA],
-        compiler_params=pltpu.CompilerParams(vmem_limit_bytes=2**20),
-        name="face",
-    )(disp)
-
-
-def extra(ref, row):
-    ny = ref.shape[1]
-    return 11 + row // ny, slice(row % ny, row % ny + 1)
-
-
-def load_kernel(disp_h, dens_h, stiff, disp, dens, mat, mat_y, stiff_s, sems):
-    copies = [pltpu.make_async_copy(stiff, stiff_s, sems.at[0])]
-    for l in range(3):
-        part = pl.ds(3 * l, 3)
-        copies.append(pltpu.make_async_copy(disp_h.at[part], disp.at[part], sems.at[1 + l]))
-    copies.append(pltpu.make_async_copy(dens_h, dens, sems.at[4]))
+def start_kernel(disp, stiff, face, mat, mat_y, stiff_s, sems):
+    copies = [
+        pltpu.make_async_copy(stiff, stiff_s, sems.at[0]),
+        pltpu.make_async_copy(disp.at[:, 0], face, sems.at[1]),
+    ]
     for copy in copies:
         copy.start()
     copies[0].wait()
     build_matrices(stiff_s[...], ((mat, 4, 2), (mat_y, 2, 4)))
-    for copy in copies[1:]:
-        copy.wait()
-
-
-def load_call(disp, dens, stiff):
+    copies[1].wait()
+
+
+def start_call(disp, stiff):
+    _, _, nz, nx = disp.shape
     matrix = jax.ShapeDtypeStruct((192, 224), bf16)
     return pl.pallas_call(
-        load_kernel,
-        in_specs=[HBM, HBM, HBM],
-        out_shape=(
-            jax.ShapeDtypeStruct(disp.shape, f32),
-            jax.ShapeDtypeStruct(dens.shape, f32),
-            matrix,
-            matrix,
-        ),
-        scratch_shapes=[pltpu.VMEM((24, 24), f32), pltpu.SemaphoreType.DMA((5,))],
-        compiler_params=pltpu.CompilerParams(vmem_limit_bytes=16 * 2**20),
-        cost_estimate=estimate(2),
-        name="load",
-    )(disp, dens, stiff)
+        start_kernel,
+        in_specs=[HBM, HBM],
+        out_shape=(jax.ShapeDtypeStruct((9, nz, nx), f32), matrix, matrix),
+        scratch_shapes=[pltpu.VMEM((24, 24), f32), pltpu.SemaphoreType.DMA((2,))],
+        compiler_params=pltpu.CompilerParams(vmem_limit_bytes=4 * 2**20),
+        cost_estimate=estimate(10),
+        name="start",
+    )(disp, stiff)
+
+
+def extra(ref, row):
+    ny = ref.shape[1]
+    return 11 + row // ny, slice(row % ny, row % ny + 1)
 
 
 def ends_kernel(flags, disp, dens, mat, ends, up, down, msg_even, msg_odd, *work):
@@ -705,22 +681,21 @@
     flags = jnp.stack([iy > 0, iy < gy - 1, iz > 0, iz < gz - 1, iy % 2 == 1, iz % 2 == 1]).astype(jnp.int32)
 
     disp_hbm = pltpu.with_memory_space_constraint(displacement, pltpu.HBM)
-    dens_hbm = pltpu.with_memory_space_constraint(density, pltpu.HBM)
     stiff_hbm = pltpu.with_memory_space_constraint(stiffness, pltpu.HBM)
 
-    fy = to_lower(face_call(disp_hbm), "gy")
-    disp, dens, mat, mat_y = load_call(disp_hbm, dens_hbm, stiff_hbm)
-    ends, up, down, z_even, z_odd = ends_call(flags, disp, dens, mat)
+    face, mat, mat_y = start_call(disp_hbm, stiff_hbm)
+    fy = to_lower(face, "gy")
+    ends, up, down, z_even, z_odd = ends_call(flags, displacement, density, mat)
 
     z_got_even = swap(z_even, "gz", 0)
     z_got_odd = swap(z_odd, "gz", 1)
-    src, low, high, tgt = middle_call(disp, dens, fy, mat, ends, passive, solid)
-    rim, nodes, msg_even, msg_odd = rim_call(flags, z_got_even, z_got_odd, up, down, disp, dens, mat_y, src)
+    src, low, high, tgt = middle_call(displacement, density, fy, mat, ends, passive, solid)
+    rim, nodes, msg_even, msg_odd = rim_call(flags, z_got_even, z_got_odd, up, down, displacement, density, mat_y, src)
 
     got_even = swap(msg_even, "gy", 0)
     got_odd = swap(msg_odd, "gy", 1)
-    amp_i, vol = inner_call(flags, src, rim, dens, low, high)
-    amp_o, excess = outer_call(flags, src, rim, nodes, got_even, got_odd, mat, dens, low, high, vol, tgt)
+    amp_i, vol = inner_call(flags, src, rim, density, low, high)
+    amp_o, excess = outer_call(flags, src, rim, nodes, got_even, got_odd, mat, density, low, high, vol, tgt)
 
     everyone = jnp.broadcast_to(excess, (gz * gy, POINTS))
     tables = lax.all_to_all(everyone, ("gz", "gy"), 0, 0, tiled=True)

time: 45.3 us -> 43.8 us (0.967)
  blocking collectives: 16.8 us -> 15 us
  waiting for transfers between devices: 1.7 us -> 3.42 us
  Pallas kernels: 19.8 us -> 18.4 us
    ppermute x1, waiting for transfers between devices: 1.69 us -> 3.41 us  [to_lower(): return lax.ppermute(value, axis, [(i + 1, i) for i in range(count - 1)])]
    all_to_all x1, blocking collectives: 16.8 us -> 15 us  [on_device(): tables = lax.all_to_all(everyone, ('gz', 'gy'), 0, 0, tiled=True)]
    pallas_call x2 -> x1, Pallas kernels: 2.64 us -> 1.19 us  [start_call(): pl.pallas_call(start_kernel, in_specs=[HBM, HBM], out_shape=(jax.ShapeDty...]
  transfers between devices with their start and end apart: 5 -> 5, of which waited for: 1 -> 1; matrix products, arithmetic and copies ran while one was open for 0% -> 0% of each run, Pallas kernels for 29% -> 26%
where the time goes in v16:
time: 43.8 us; the launch traced here: 43.6 us
  Pallas kernels  18.4 us (42%)
  blocking collectives  15 us (34%)
  starting transfers between devices  5.82 us (13%)
  waiting for transfers between devices  3.42 us (8%)
  between operations  0.79 us (2%)
    all_to_all x1, blocking collectives, on_device(): tables = lax.all_to_all(everyone, ('gz', 'gy'), 0, 0, tiled=True)  15 us
    pallas_call x1, Pallas kernels, inner_call(): pl.pallas_call(inner_kernel, in_specs=[SMEM] + [VMEM] * 5, out_shape=(jax...  6.2 us
    ppermute x4, starting transfers between devices, swap(): return lax.ppermute(value, axis, pairs)  4.53 us
    pallas_call x1, Pallas kernels, outer_call(): pl.pallas_call(outer_kernel, in_specs=[SMEM] + [VMEM] * 11, out_shape=(ja...  3.85 us
    ppermute x1, waiting for transfers between devices, to_lower(): return lax.ppermute(value, axis, [(i + 1, i) for i in range(count - 1)])  3.41 us
    pallas_call x1, Pallas kernels, ends_call(): pl.pallas_call(ends_kernel, in_specs=[SMEM] + [VMEM] * 3, out_shape=(jax....  2.63 us
    pallas_call x1, Pallas kernels, middle_call(): pl.pallas_call(middle_kernel, in_specs=[VMEM] * 7, out_shape=(jax.ShapeDt...  2.6 us
    ppermute x1, starting transfers between devices, to_lower(): return lax.ppermute(value, axis, [(i + 1, i) for i in range(count - 1)])  1.29 us
  transfers between devices with their start and end apart: 5, of which 1 were waited for; matrix products, arithmetic and copies ran while one was open for 0% of the time, Pallas kernels for 26%

profile of v16, /device:TPU:0, one launch (start us, length us, event | category | flops | bytes accessed | tf_op | source)
XLA Modules:
  0.0 43.6 jit_solution(12213116241695233505)
XLA Ops:
  0.6 0.0 copy-start
  0.6 0.0 copy-start.3
  0.6 1.2 %start.1 = (f32[9,32,128]{2,1,0:T(8,128)S(1)}, bf16[192,224]{1,0:T(8,128)(2,1)S(1)}, bf16[192,224]{1,0:T(8,128)(2,1)S(1)}) custom-call(f32[9,16,32,128]{3,2,1,0:T(8,128)} %disp.7, f32[24,24]{1,0:T(8,128)} %stiff.1), custom_call_target="tpu_custom_call" | custom-call | flops 10000000000 | bytes 1048576 | tf_op jit(solution)/shard_map/start/pallas_call | solution.py:201
  1.8 1.3 %collective-permute-start = (f32[9,32,128]{2,1,0:T(8,128)S(1)}, f32[9,32,128]{2,1,0:T(8,128)S(1)}, u32[]{:S(2)}, u32[]{:S(2)}) collective-permute-start(f32[9,32,128]{2,1,0:T(8,128)S(1)} %get-tuple-element.24), channel_id=1, source_target_pairs={{1,0},{2,1},{3,2},{4,3},{5,4},{6,5},{7,6},{9,8},{10,9},{11,10},{12... | collective-permute-start | bytes 442376 | tf_op jit(solution)/shard_map/ppermute | solution.py:667
  3.2 0.1 stack.27
  3.3 0.0 copy-done
  3.3 0.0 copy-start.1
  3.3 0.0 copy-start.2
  3.3 2.6 %energy_ends.1 = (f32[16,16,128]{2,1,0:T(8,128)S(1)}, f32[14,16,128]{2,1,0:T(8,128)S(1)}, f32[14,16,128]{2,1,0:T(8,128)S(1)}, f32[14,16,128]{2,1,0:T(8,128)S(1)}, f32[14,16,128]{2,1,0:T(8,128)S(1)}) custom-call(s32[6]{0:T(128)S(1)} %convert_element_type.3.flags, f32[9,16,32,128]{3,2,1,0:T(8,128)S(1)} %copy-done, f32[16,32,128]{2,1,0:T(8,128)S(1)} %copy-done.3, ...), custom_call_target="tpu_custom_call" | custom-call | flops 4000000000 | bytes 1048576 | tf_op jit(solution)/shard_map/energy_ends/pallas_call | solution.py:261
  5.9 0.5 %collective-permute-start.1 = (f32[14,16,128]{2,1,0:T(8,128)S(1)}, f32[14,16,128]{2,1,0:T(8,128)S(1)}, u32[]{:S(2)}, u32[]{:S(2)}) collective-permute-start(f32[14,16,128]{2,1,0:T(8,128)S(1)} %get-tuple-element.28), channel_id=1, source_target_pairs={{0,8},{8,0},{16,24},{24,16},{1,9},{9,1},{17,25},{25,17},{2,10},{10... | collective-permute-start | bytes 344072 | tf_op jit(solution)/shard_map/ppermute | solution.py:674
  6.5 0.7 %collective-permute-start.2 = (f32[14,16,128]{2,1,0:T(8,128)S(1)}, f32[14,16,128]{2,1,0:T(8,128)S(1)}, u32[]{:S(2)}, u32[]{:S(2)}) collective-permute-start(f32[14,16,128]{2,1,0:T(8,128)S(1)} %get-tuple-element.29), channel_id=1, source_target_pairs={{8,16},{16,8},{9,17},{17,9},{10,18},{18,10},{11,19},{19,11},{12,20... | collective-permute-start | bytes 344072 | tf_op jit(solution)/shard_map/ppermute | solution.py:674
  7.1 3.4 %collective-permute-done.fy = f32[9,32,128]{2,1,0:T(8,128)S(1)} collective-permute-done((f32[9,32,128]{2,1,0:T(8,128)S(1)}, f32[9,32,128]{2,1,0:T(8,128)S(1)}, u32[]{:S(2)}, u32[]{:S(2)}) %collective-permute-start) | collective-permute-done | bytes 147488 | tf_op jit(solution)/shard_map/ppermute | solution.py:667
  10.5 2.6 %energy_middle.1 = (f32[16,48,128]{2,1,0:T(8,128)S(1)}, f32[16,32,128]{2,1,0:T(8,128)S(1)}, f32[16,32,128]{2,1,0:T(8,128)S(1)}, f32[128,128]{1,0:T(8,128)S(1)}) custom-call(f32[9,16,32,128]{3,2,1,0:T(8,128)S(1)} %copy-done, f32[16,32,128]{2,1,0:T(8,128)S(1)} %copy-done.3, f32[9,32,128]{2,1,0:T(8,128)S(1)} %collective-permute-done.fy, ...), custom_call_target="tpu_custom_call" | custom-call | flops 4000000000 | bytes 1048576 | tf_op jit(solution)/shard_map/energy_middle/pallas_call | solution.py:307
  13.2 0.0 collective-permute-done.1.got_even
  13.2 0.0 collective-permute-done.2.got_odd
  13.2 1.0 %energy_rim.1 = (f32[16,8,128]{2,1,0:T(8,128)S(1)}, f32[2,10,8,128]{3,2,1,0:T(8,128)S(1)}, f32[160,128]{1,0:T(8,128)S(1)}, f32[160,128]{1,0:T(8,128)S(1)}) custom-call(s32[6]{0:T(128)S(1)} %convert_element_type.3.flags, f32[14,16,128]{2,1,0:T(8,128)S(1)} %collective-permute-done.1.got_even, f32[14,16,128]{2,1,0:T(8,128)S(1)} %collective-permute-done.2.got_odd, ...), custom_call_target="tpu_custom_call" | custom-call | flops 2000000000 | bytes 1048576 | tf_op jit(solution)/shard_map/energy_rim/pallas_call | solution.py:396
  14.2 2.7 %collective-permute-start.3 = (f32[160,128]{1,0:T(8,128)S(1)}, f32[160,128]{1,0:T(8,128)S(1)}, u32[]{:S(2)}, u32[]{:S(2)}) collective-permute-start(f32[160,128]{1,0:T(8,128)S(1)} %get-tuple-element.35), channel_id=1, source_target_pairs={{0,1},{1,0},{2,3},{3,2},{4,5},{5,4},{6,7},{7,6},{8,9},{9,8},{10,11... | collective-permute-start | bytes 245768 | tf_op jit(solution)/shard_map/ppermute | solution.py:674
  16.9 0.7 %collective-permute-start.4 = (f32[160,128]{1,0:T(8,128)S(1)}, f32[160,128]{1,0:T(8,128)S(1)}, u32[]{:S(2)}, u32[]{:S(2)}) collective-permute-start(f32[160,128]{1,0:T(8,128)S(1)} %get-tuple-element.36), channel_id=1, source_target_pairs={{1,2},{2,1},{3,4},{4,3},{5,6},{6,5},{9,10},{10,9},{11,12},{12,11},... | collective-permute-start | bytes 245768 | tf_op jit(solution)/shard_map/ppermute | solution.py:674
  17.5 6.2 %filter_inner.1 = (f32[11,32,128]{2,1,0:T(8,128)S(1)}, f32[2048,128]{1,0:T(8,128)S(1)}) custom-call(s32[6]{0:T(128)S(1)} %convert_element_type.3.flags, f32[16,48,128]{2,1,0:T(8,128)S(1)} %get-tuple-element.27.src, f32[16,8,128]{2,1,0:T(8,128)S(1)} %get-tuple-element.33.rim, f32[16,32,128]{2,1,0:T(8,128)S(1)} %copy-done.3, ...), custom_call_target="tpu_custom_call" | custom-call | flops 8999999488 | bytes 1048576 | tf_op jit(solution)/shard_map/filter_inner/pallas_call | solution.py:537
  23.7 0.0 collective-permute-done.3.got_even
  23.7 0.0 collective-permute-done.4.got_odd
  23.7 3.9 %filter_outer.1 = (f32[5,32,128]{2,1,0:T(8,128)S(1)}, f32[1,256]{1,0:T(1,128)S(1)}) custom-call(s32[6]{0:T(128)S(1)} %convert_element_type.3.flags, f32[16,48,128]{2,1,0:T(8,128)S(1)} %get-tuple-element.27.src, f32[16,8,128]{2,1,0:T(8,128)S(1)} %get-tuple-element.33.rim, f32[2,10,8,128]{3,2,1,0:T(8,128)S(1)} %get-tuple-element.34.nodes, ...), custom_call_target="tpu_custom_call" | custom-call | flops 3000000000 | bytes 1048576 | tf_op jit(solution)/shard_map/filter_outer/pallas_call | solution.py:612
  27.6 15.0 %all_to_all.8 = f32[32,1,256]{2,1,0:T(1,128)S(1)} all-to-all(f32[32,1,256]{2,1,0:T(1,128)S(1)} %broadcast_in_dim.2), channel_id=1, replica_groups=mesh['gz'=4,'gy'=8] {'gz','gy'}, dimensions={0} | all-to-all | bytes 65536 | tf_op jit(solution)/shard_map/all_to_all | solution.py:701
  42.7 0.9 %update.1 = (f32[16,32,128]{2,1,0:T(8,128)}, f32[1]{0:T(128)}) custom-call(f32[32,256]{1,0:T(8,128)S(1)} %bitcast.11, f32[11,32,128]{2,1,0:T(8,128)S(1)} %get-tuple-element.42.amp_i, f32[5,32,128]{2,1,0:T(8,128)S(1)} %get-tuple-element.43.amp_o, f32[16,32,128]{2,1,0:T(8,128)S(1)} %get-tuple-element.37.low, f32[16,32,128]{2,1,0:T(8,128)S(1)} %get-tuple-element.38.high), custom_call_target="tpu_custom_call" | custom-call | flops 1000000000 | bytes 1048576 | tf_op jit(solution)/shard_map/update/pallas_call | solution.py:654
  (6 shorter events, 0.0 us)
Async XLA Ops:
  0.6 2.7 %copy-start = (f32[9,16,32,128]{3,2,1,0:T(8,128)S(1)}, f32[9,16,32,128]{3,2,1,0:T(8,128)}, u32[]{:S(2)}) copy-start(f32[9,16,32,128]{3,2,1,0:T(8,128)} %disp.7) | copy-start | bytes 7077892
  0.6 2.7 %copy-start.3 = (f32[16,32,128]{2,1,0:T(8,128)S(1)}, f32[16,32,128]{2,1,0:T(8,128)}, u32[]{:S(2)}) copy-start(f32[16,32,128]{2,1,0:T(8,128)} %dens.9) | copy-start | bytes 786436
  1.8 8.7 %collective-permute-start = (f32[9,32,128]{2,1,0:T(8,128)S(1)}, f32[9,32,128]{2,1,0:T(8,128)S(1)}, u32[]{:S(2)}, u32[]{:S(2)}) collective-permute-start(f32[9,32,128]{2,1,0:T(8,128)S(1)} %get-tuple-element.24), channel_id=1, source_target_pairs={{1,0},{2,1},{3,2},{4,3},{5,4},{6,5},{7,6},{9,8},{10,9},{11,10},{12... | collective-permute-start | bytes 442376 | tf_op jit(solution)/shard_map/ppermute | solution.py:667
  3.3 7.2 %copy-start.1 = (s32[16,32,128]{2,1,0:T(8,128)S(1)}, s32[16,32,128]{2,1,0:T(8,128)}, u32[]{:S(2)}) copy-start(s32[16,32,128]{2,1,0:T(8,128)} %passive.1) | copy-start | bytes 786436
  3.3 7.2 %copy-start.2 = (s32[16,32,128]{2,1,0:T(8,128)S(1)}, s32[16,32,128]{2,1,0:T(8,128)}, u32[]{:S(2)}) copy-start(s32[16,32,128]{2,1,0:T(8,128)} %solid.1) | copy-start | bytes 786436
  5.9 7.2 %collective-permute-start.1 = (f32[14,16,128]{2,1,0:T(8,128)S(1)}, f32[14,16,128]{2,1,0:T(8,128)S(1)}, u32[]{:S(2)}, u32[]{:S(2)}) collective-permute-start(f32[14,16,128]{2,1,0:T(8,128)S(1)} %get-tuple-element.28), channel_id=1, source_target_pairs={{0,8},{8,0},{16,24},{24,16},{1,9},{9,1},{17,25},{25,17},{2,10},{10... | collective-permute-start | bytes 344072 | tf_op jit(solution)/shard_map/ppermute | solution.py:674
  6.5 6.7 %collective-permute-start.2 = (f32[14,16,128]{2,1,0:T(8,128)S(1)}, f32[14,16,128]{2,1,0:T(8,128)S(1)}, u32[]{:S(2)}, u32[]{:S(2)}) collective-permute-start(f32[14,16,128]{2,1,0:T(8,128)S(1)} %get-tuple-element.29), channel_id=1, source_target_pairs={{8,16},{16,8},{9,17},{17,9},{10,18},{18,10},{11,19},{19,11},{12,20... | collective-permute-start | bytes 344072 | tf_op jit(solution)/shard_map/ppermute | solution.py:674
  14.2 9.6 %collective-permute-start.3 = (f32[160,128]{1,0:T(8,128)S(1)}, f32[160,128]{1,0:T(8,128)S(1)}, u32[]{:S(2)}, u32[]{:S(2)}) collective-permute-start(f32[160,128]{1,0:T(8,128)S(1)} %get-tuple-element.35), channel_id=1, source_target_pairs={{0,1},{1,0},{2,3},{3,2},{4,5},{5,4},{6,7},{7,6},{8,9},{9,8},{10,11... | collective-permute-start | bytes 245768 | tf_op jit(solution)/shard_map/ppermute | solution.py:674
  16.9 6.9 %collective-permute-start.4 = (f32[160,128]{1,0:T(8,128)S(1)}, f32[160,128]{1,0:T(8,128)S(1)}, u32[]{:S(2)}, u32[]{:S(2)}) collective-permute-start(f32[160,128]{1,0:T(8,128)S(1)} %get-tuple-element.36), channel_id=1, source_target_pairs={{1,2},{2,1},{3,4},{4,3},{5,6},{6,5},{9,10},{10,9},{11,12},{12,11},... | collective-permute-start | bytes 245768 | tf_op jit(solution)/shard_map/ppermute | solution.py:674

commit v17 on v16

--- a/solution.py
+++ b/solution.py
@@ -183,7 +183,7 @@
     put(rows - 1)
 
 
-def start_kernel(disp, stiff, face, mat, mat_y, stiff_s, sems):
+def start_kernel(disp, stiff, face, mat, stiff_s, sems):
     copies = [
         pltpu.make_async_copy(stiff, stiff_s, sems.at[0]),
         pltpu.make_async_copy(disp.at[:, 0], face, sems.at[1]),
@@ -191,7 +191,7 @@
     for copy in copies:
         copy.start()
     copies[0].wait()
-    build_matrices(stiff_s[...], ((mat, 4, 2), (mat_y, 2, 4)))
+    build_matrices(stiff_s[...], ((mat, 4, 2),))
     copies[1].wait()
 
 
@@ -201,7 +201,7 @@
     return pl.pallas_call(
         start_kernel,
         in_specs=[HBM, HBM],
-        out_shape=(jax.ShapeDtypeStruct((9, nz, nx), f32), matrix, matrix),
+        out_shape=(jax.ShapeDtypeStruct((9, nz, nx), f32), matrix),
         scratch_shapes=[pltpu.VMEM((24, 24), f32), pltpu.SemaphoreType.DMA((2,))],
         compiler_params=pltpu.CompilerParams(vmem_limit_bytes=4 * 2**20),
         cost_estimate=estimate(10),
@@ -269,7 +269,7 @@
     )(flags, disp, dens, mat)
 
 
-def middle_kernel(disp, dens, fy, mat, ends, passive, solid, src, low, high, tgt, now_s, *work):
+def middle_kernel(disp, dens, fy, mat, ends, passive, solid, stiff, src, low, high, tgt, mat_y, now_s, *work):
     _, ny, nz, nx = disp.shape
     work, last = work[:3], work[3:]
 
@@ -298,20 +298,22 @@
         return 0
 
     lax.fori_loop(0, ny, bound, 0, unroll=4)
+    build_matrices(stiff[...], ((mat_y, 2, 4),))
     targets(((ny - 5, inner_row), (5, outer_row(ny))), nz, nx, now_s, tgt)
 
 
-def middle_call(disp, dens, fy, mat, ends, passive, solid):
+def middle_call(disp, dens, fy, mat, ends, passive, solid, stiff):
     _, ny, nz, nx = disp.shape
     field = jax.ShapeDtypeStruct((ny, nz, nx), f32)
     return pl.pallas_call(
         middle_kernel,
-        in_specs=[VMEM] * 7,
+        in_specs=[VMEM] * 8,
         out_shape=(
             jax.ShapeDtypeStruct((ny, nz + 2 * OFF, nx), f32),
             field,
             field,
             jax.ShapeDtypeStruct((8 * COARSE, nx), f32),
+            jax.ShapeDtypeStruct((192, 224), bf16),
         ),
         scratch_shapes=[pltpu.VMEM((ny, nz, nx), f32)]
         + workspace(ny, nz // 8 - 2, nx)
@@ -319,7 +321,7 @@
         compiler_params=pltpu.CompilerParams(vmem_limit_bytes=24 * 2**20),
         cost_estimate=estimate(4),
         name="energy_middle",
-    )(disp, dens, fy, mat, ends, passive, solid)
+    )(disp, dens, fy, mat, ends, passive, solid, stiff)
 
 
 def rim_kernel(
@@ -683,13 +685,13 @@
     disp_hbm = pltpu.with_memory_space_constraint(displacement, pltpu.HBM)
     stiff_hbm = pltpu.with_memory_space_constraint(stiffness, pltpu.HBM)
 
-    face, mat, mat_y = start_call(disp_hbm, stiff_hbm)
+    face, mat = start_call(disp_hbm, stiff_hbm)
     fy = to_lower(face, "gy")
     ends, up, down, z_even, z_odd = ends_call(flags, displacement, density, mat)
 
     z_got_even = swap(z_even, "gz", 0)
     z_got_odd = swap(z_odd, "gz", 1)
-    src, low, high, tgt = middle_call(displacement, density, fy, mat, ends, passive, solid)
+    src, low, high, tgt, mat_y = middle_call(displacement, density, fy, mat, ends, passive, solid, stiffness)
     rim, nodes, msg_even, msg_odd = rim_call(flags, z_got_even, z_got_odd, up, down, displacement, density, mat_y, src)
 
     got_even = swap(msg_even, "gy", 0)

time: 43.8 us -> 43.7 us (level)
  transfers between devices with their start and end apart: 5 -> 5, of which waited for: 1 -> 1; matrix products, arithmetic and copies ran while one was open for 0% -> 0% of each run, Pallas kernels for 26% -> 27%
where the time goes in v17:
time: 43.7 us; the launch traced here: 43.5 us
  Pallas kernels  18.6 us (43%)
  blocking collectives  14.8 us (34%)
  starting transfers between devices  5.83 us (13%)
  waiting for transfers between devices  3.4 us (8%)
  between operations  0.8 us (2%)
    all_to_all x1, blocking collectives, on_device(): tables = lax.all_to_all(everyone, ('gz', 'gy'), 0, 0, tiled=True)  14.8 us
    pallas_call x1, Pallas kernels, inner_call(): pl.pallas_call(inner_kernel, in_specs=[SMEM] + [VMEM] * 5, out_shape=(jax...  6.2 us
    ppermute x4, starting transfers between devices, swap(): return lax.ppermute(value, axis, pairs)  4.54 us
    pallas_call x1, Pallas kernels, outer_call(): pl.pallas_call(outer_kernel, in_specs=[SMEM] + [VMEM] * 11, out_shape=(ja...  3.85 us
    ppermute x1, waiting for transfers between devices, to_lower(): return lax.ppermute(value, axis, [(i + 1, i) for i in range(count - 1)])  3.39 us
    pallas_call x1, Pallas kernels, middle_call(): pl.pallas_call(middle_kernel, in_specs=[VMEM] * 8, out_shape=(jax.ShapeDt...  2.86 us
    pallas_call x1, Pallas kernels, ends_call(): pl.pallas_call(ends_kernel, in_specs=[SMEM] + [VMEM] * 3, out_shape=(jax....  2.63 us
    ppermute x1, starting transfers between devices, to_lower(): return lax.ppermute(value, axis, [(i + 1, i) for i in range(count - 1)])  1.29 us
  transfers between devices with their start and end apart: 5, of which 1 were waited for; matrix products, arithmetic and copies ran while one was open for 0% of the time, Pallas kernels for 27%

profile of v17, /device:TPU:0, one launch (start us, length us, event | category | flops | bytes accessed | tf_op | source)
XLA Modules:
  0.0 43.5 jit_solution(15587373831663232077)
XLA Ops:
  0.6 0.0 copy-start
  0.6 1.1 %start.1 = (f32[9,32,128]{2,1,0:T(8,128)S(1)}, bf16[192,224]{1,0:T(8,128)(2,1)S(1)}) custom-call(f32[9,16,32,128]{3,2,1,0:T(8,128)} %disp.7, f32[24,24]{1,0:T(8,128)} %stiff.3), custom_call_target="tpu_custom_call" | custom-call | flops 10000000000 | bytes 1048576 | tf_op jit(solution)/shard_map/start/pallas_call | solution.py:201
  1.8 1.3 %collective-permute-start = (f32[9,32,128]{2,1,0:T(8,128)S(1)}, f32[9,32,128]{2,1,0:T(8,128)S(1)}, u32[]{:S(2)}, u32[]{:S(2)}) collective-permute-start(f32[9,32,128]{2,1,0:T(8,128)S(1)} %get-tuple-element.24), channel_id=1, source_target_pairs={{1,0},{2,1},{3,2},{4,3},{5,4},{6,5},{7,6},{9,8},{10,9},{11,10},{12... | collective-permute-start | bytes 442376 | tf_op jit(solution)/shard_map/ppermute | solution.py:669
  3.1 0.1 stack.27
  3.2 0.0 copy-start.1
  3.3 0.0 copy-start.2
  3.3 0.0 copy-start.4
  3.3 2.6 %energy_ends.1 = (f32[16,16,128]{2,1,0:T(8,128)S(1)}, f32[14,16,128]{2,1,0:T(8,128)S(1)}, f32[14,16,128]{2,1,0:T(8,128)S(1)}, f32[14,16,128]{2,1,0:T(8,128)S(1)}, f32[14,16,128]{2,1,0:T(8,128)S(1)}) custom-call(s32[6]{0:T(128)S(1)} %convert_element_type.3.flags, f32[9,16,32,128]{3,2,1,0:T(8,128)S(1)} %copy-done, f32[16,32,128]{2,1,0:T(8,128)S(1)} %copy-done.3, ...), custom_call_target="tpu_custom_call" | custom-call | flops 4000000000 | bytes 1048576 | tf_op jit(solution)/shard_map/energy_ends/pallas_call | solution.py:261
  5.9 0.5 %collective-permute-start.1 = (f32[14,16,128]{2,1,0:T(8,128)S(1)}, f32[14,16,128]{2,1,0:T(8,128)S(1)}, u32[]{:S(2)}, u32[]{:S(2)}) collective-permute-start(f32[14,16,128]{2,1,0:T(8,128)S(1)} %get-tuple-element.28), channel_id=1, source_target_pairs={{0,8},{8,0},{16,24},{24,16},{1,9},{9,1},{17,25},{25,17},{2,10},{10... | collective-permute-start | bytes 344072 | tf_op jit(solution)/shard_map/ppermute | solution.py:676
  6.4 0.7 %collective-permute-start.2 = (f32[14,16,128]{2,1,0:T(8,128)S(1)}, f32[14,16,128]{2,1,0:T(8,128)S(1)}, u32[]{:S(2)}, u32[]{:S(2)}) collective-permute-start(f32[14,16,128]{2,1,0:T(8,128)S(1)} %get-tuple-element.29), channel_id=1, source_target_pairs={{8,16},{16,8},{9,17},{17,9},{10,18},{18,10},{11,19},{19,11},{12,20... | collective-permute-start | bytes 344072 | tf_op jit(solution)/shard_map/ppermute | solution.py:676
  7.1 3.4 %collective-permute-done.fy = f32[9,32,128]{2,1,0:T(8,128)S(1)} collective-permute-done((f32[9,32,128]{2,1,0:T(8,128)S(1)}, f32[9,32,128]{2,1,0:T(8,128)S(1)}, u32[]{:S(2)}, u32[]{:S(2)}) %collective-permute-start) | collective-permute-done | bytes 147488 | tf_op jit(solution)/shard_map/ppermute | solution.py:669
  10.5 0.0 copy-done.4
  10.5 2.9 %energy_middle.1 = (f32[16,48,128]{2,1,0:T(8,128)S(1)}, f32[16,32,128]{2,1,0:T(8,128)S(1)}, f32[16,32,128]{2,1,0:T(8,128)S(1)}, f32[128,128]{1,0:T(8,128)S(1)}, bf16[192,224]{1,0:T(8,128)(2,1)S(1)}) custom-call(f32[9,16,32,128]{3,2,1,0:T(8,128)S(1)} %copy-done, f32[16,32,128]{2,1,0:T(8,128)S(1)} %copy-done.3, f32[9,32,128]{2,1,0:T(8,128)S(1)} %collective-permute-done.fy, ...), custom_call_target="tpu_custom_call" | custom-call | flops 4000000000 | bytes 1048576 | tf_op jit(solution)/shard_map/energy_middle/pallas_call | solution.py:308
  13.4 0.0 collective-permute-done.1.got_even
  13.4 0.0 collective-permute-done.2.got_odd
  13.4 1.0 %energy_rim.1 = (f32[16,8,128]{2,1,0:T(8,128)S(1)}, f32[2,10,8,128]{3,2,1,0:T(8,128)S(1)}, f32[160,128]{1,0:T(8,128)S(1)}, f32[160,128]{1,0:T(8,128)S(1)}) custom-call(s32[6]{0:T(128)S(1)} %convert_element_type.3.flags, f32[14,16,128]{2,1,0:T(8,128)S(1)} %collective-permute-done.1.got_even, f32[14,16,128]{2,1,0:T(8,128)S(1)} %collective-permute-done.2.got_odd, ...), custom_call_target="tpu_custom_call" | custom-call | flops 2000000000 | bytes 1048576 | tf_op jit(solution)/shard_map/energy_rim/pallas_call | solution.py:398
  14.4 2.7 %collective-permute-start.3 = (f32[160,128]{1,0:T(8,128)S(1)}, f32[160,128]{1,0:T(8,128)S(1)}, u32[]{:S(2)}, u32[]{:S(2)}) collective-permute-start(f32[160,128]{1,0:T(8,128)S(1)} %get-tuple-element.35), channel_id=1, source_target_pairs={{0,1},{1,0},{2,3},{3,2},{4,5},{5,4},{6,7},{7,6},{8,9},{9,8},{10,11... | collective-permute-start | bytes 245768 | tf_op jit(solution)/shard_map/ppermute | solution.py:676
  17.1 0.7 %collective-permute-start.4 = (f32[160,128]{1,0:T(8,128)S(1)}, f32[160,128]{1,0:T(8,128)S(1)}, u32[]{:S(2)}, u32[]{:S(2)}) collective-permute-start(f32[160,128]{1,0:T(8,128)S(1)} %get-tuple-element.36), channel_id=1, source_target_pairs={{1,2},{2,1},{3,4},{4,3},{5,6},{6,5},{9,10},{10,9},{11,12},{12,11},... | collective-permute-start | bytes 245768 | tf_op jit(solution)/shard_map/ppermute | solution.py:676
  17.7 6.2 %filter_inner.1 = (f32[11,32,128]{2,1,0:T(8,128)S(1)}, f32[2048,128]{1,0:T(8,128)S(1)}) custom-call(s32[6]{0:T(128)S(1)} %convert_element_type.3.flags, f32[16,48,128]{2,1,0:T(8,128)S(1)} %get-tuple-element.27.src, f32[16,8,128]{2,1,0:T(8,128)S(1)} %get-tuple-element.33.rim, f32[16,32,128]{2,1,0:T(8,128)S(1)} %copy-done.3, ...), custom_call_target="tpu_custom_call" | custom-call | flops 8999999488 | bytes 1048576 | tf_op jit(solution)/shard_map/filter_inner/pallas_call | solution.py:539
  23.9 0.0 collective-permute-done.3.got_even
  24.0 0.0 collective-permute-done.4.got_odd
  24.0 3.9 %filter_outer.1 = (f32[5,32,128]{2,1,0:T(8,128)S(1)}, f32[1,256]{1,0:T(1,128)S(1)}) custom-call(s32[6]{0:T(128)S(1)} %convert_element_type.3.flags, f32[16,48,128]{2,1,0:T(8,128)S(1)} %get-tuple-element.27.src, f32[16,8,128]{2,1,0:T(8,128)S(1)} %get-tuple-element.33.rim, f32[2,10,8,128]{3,2,1,0:T(8,128)S(1)} %get-tuple-element.34.nodes, ...), custom_call_target="tpu_custom_call" | custom-call | flops 3000000000 | bytes 1048576 | tf_op jit(solution)/shard_map/filter_outer/pallas_call | solution.py:614
  27.8 14.8 %all_to_all.8 = f32[32,1,256]{2,1,0:T(1,128)S(1)} all-to-all(f32[32,1,256]{2,1,0:T(1,128)S(1)} %broadcast_in_dim.2), channel_id=1, replica_groups=mesh['gz'=4,'gy'=8] {'gz','gy'}, dimensions={0} | all-to-all | bytes 65536 | tf_op jit(solution)/shard_map/all_to_all | solution.py:703
  42.6 0.9 %update.1 = (f32[16,32,128]{2,1,0:T(8,128)}, f32[1]{0:T(128)}) custom-call(f32[32,256]{1,0:T(8,128)S(1)} %bitcast.11, f32[11,32,128]{2,1,0:T(8,128)S(1)} %get-tuple-element.42.amp_i, f32[5,32,128]{2,1,0:T(8,128)S(1)} %get-tuple-element.43.amp_o, f32[16,32,128]{2,1,0:T(8,128)S(1)} %get-tuple-element.37.low, f32[16,32,128]{2,1,0:T(8,128)S(1)} %get-tuple-element.38.high), custom_call_target="tpu_custom_call" | custom-call | flops 1000000000 | bytes 1048576 | tf_op jit(solution)/shard_map/update/pallas_call | solution.py:656
  (8 shorter events, 0.0 us)
Async XLA Ops:
  0.6 2.6 %copy-start = (f32[9,16,32,128]{3,2,1,0:T(8,128)S(1)}, f32[9,16,32,128]{3,2,1,0:T(8,128)}, u32[]{:S(2)}) copy-start(f32[9,16,32,128]{3,2,1,0:T(8,128)} %disp.7) | copy-start | bytes 7077892
  0.6 2.6 %copy-start.3 = (f32[16,32,128]{2,1,0:T(8,128)S(1)}, f32[16,32,128]{2,1,0:T(8,128)}, u32[]{:S(2)}) copy-start(f32[16,32,128]{2,1,0:T(8,128)} %dens.9) | copy-start | bytes 786436
  1.8 8.7 %collective-permute-start = (f32[9,32,128]{2,1,0:T(8,128)S(1)}, f32[9,32,128]{2,1,0:T(8,128)S(1)}, u32[]{:S(2)}, u32[]{:S(2)}) collective-permute-start(f32[9,32,128]{2,1,0:T(8,128)S(1)} %get-tuple-element.24), channel_id=1, source_target_pairs={{1,0},{2,1},{3,2},{4,3},{5,4},{6,5},{7,6},{9,8},{10,9},{11,10},{12... | collective-permute-start | bytes 442376 | tf_op jit(solution)/shard_map/ppermute | solution.py:669
  3.2 7.2 %copy-start.1 = (s32[16,32,128]{2,1,0:T(8,128)S(1)}, s32[16,32,128]{2,1,0:T(8,128)}, u32[]{:S(2)}) copy-start(s32[16,32,128]{2,1,0:T(8,128)} %passive.1) | copy-start | bytes 786436
  3.3 7.2 %copy-start.2 = (s32[16,32,128]{2,1,0:T(8,128)S(1)}, s32[16,32,128]{2,1,0:T(8,128)}, u32[]{:S(2)}) copy-start(s32[16,32,128]{2,1,0:T(8,128)} %solid.1) | copy-start | bytes 786436
  3.3 7.2 %copy-start.4 = (f32[24,24]{1,0:T(8,128)S(1)}, f32[24,24]{1,0:T(8,128)}, u32[]{:S(2)}) copy-start(f32[24,24]{1,0:T(8,128)} %stiff.3) | copy-start | bytes 6916
  5.9 7.5 %collective-permute-start.1 = (f32[14,16,128]{2,1,0:T(8,128)S(1)}, f32[14,16,128]{2,1,0:T(8,128)S(1)}, u32[]{:S(2)}, u32[]{:S(2)}) collective-permute-start(f32[14,16,128]{2,1,0:T(8,128)S(1)} %get-tuple-element.28), channel_id=1, source_target_pairs={{0,8},{8,0},{16,24},{24,16},{1,9},{9,1},{17,25},{25,17},{2,10},{10... | collective-permute-start | bytes 344072 | tf_op jit(solution)/shard_map/ppermute | solution.py:676
  6.4 6.9 %collective-permute-start.2 = (f32[14,16,128]{2,1,0:T(8,128)S(1)}, f32[14,16,128]{2,1,0:T(8,128)S(1)}, u32[]{:S(2)}, u32[]{:S(2)}) collective-permute-start(f32[14,16,128]{2,1,0:T(8,128)S(1)} %get-tuple-element.29), channel_id=1, source_target_pairs={{8,16},{16,8},{9,17},{17,9},{10,18},{18,10},{11,19},{19,11},{12,20... | collective-permute-start | bytes 344072 | tf_op jit(solution)/shard_map/ppermute | solution.py:676
  14.4 9.6 %collective-permute-start.3 = (f32[160,128]{1,0:T(8,128)S(1)}, f32[160,128]{1,0:T(8,128)S(1)}, u32[]{:S(2)}, u32[]{:S(2)}) collective-permute-start(f32[160,128]{1,0:T(8,128)S(1)} %get-tuple-element.35), channel_id=1, source_target_pairs={{0,1},{1,0},{2,3},{3,2},{4,5},{5,4},{6,7},{7,6},{8,9},{9,8},{10,11... | collective-permute-start | bytes 245768 | tf_op jit(solution)/shard_map/ppermute | solution.py:676
  17.1 6.9 %collective-permute-start.4 = (f32[160,128]{1,0:T(8,128)S(1)}, f32[160,128]{1,0:T(8,128)S(1)}, u32[]{:S(2)}, u32[]{:S(2)}) collective-permute-start(f32[160,128]{1,0:T(8,128)S(1)} %get-tuple-element.36), channel_id=1, source_target_pairs={{1,2},{2,1},{3,4},{4,3},{5,6},{6,5},{9,10},{10,9},{11,12},{12,11},... | collective-permute-start | bytes 245768 | tf_op jit(solution)/shard_map/ppermute | solution.py:676

commit v18 on v17

--- a/solution.py
+++ b/solution.py
@@ -481,29 +481,30 @@
 
 def table(n, nz, nx, amp, low, high, row, fine_s, vol, start, unroll):
     pair = 2
+    tiles = nz // 8
     for first in range(0, COARSE, pair):
         inverse = [inverse_coarse(i) for i in range(first, first + pair)]
 
-        def volume(j, acc):
+        def volume(step, acc):
             acc = list(acc)
+            j = step // tiles
+            at = pl.ds(pl.multiple_of(8 * (step % tiles), 8), 8)
             y = row(j)
-            for w in range(nz // 8):
-                at = slice(8 * w, 8 * w + 8)
-                lo, hi = low[y, at], high[y, at]
-                los, his = [lo * c for c in inverse], [hi * c for c in inverse]
-                for f in range(FINE):
-                    if first == 0:
-                        t = amp[j, at] * math.exp(-0.5 * SPACING * f)
-                        fine_s[f, j, at] = t
-                    else:
-                        t = fine_s[f, j, at]
-                    for i in range(pair):
-                        acc[i * FINE + f] = acc[i * FINE + f] + jnp.minimum(jnp.maximum(t, los[i]), his[i])
+            lo, hi = low[y, at], high[y, at]
+            los, his = [lo * c for c in inverse], [hi * c for c in inverse]
+            for f in range(FINE):
+                if first == 0:
+                    t = amp[j, at] * math.exp(-0.5 * SPACING * f)
+                    fine_s[f, j, at] = t
+                else:
+                    t = fine_s[f, j, at]
+                for i in range(pair):
+                    acc[i * FINE + f] = acc[i * FINE + f] + jnp.minimum(jnp.maximum(t, los[i]), his[i])
             return tuple(acc)
 
         places = [slice(8 * (first * FINE + e), 8 * (first * FINE + e) + 8) for e in range(pair * FINE)]
         begin = tuple(jnp.zeros((8, nx), f32) if start is None else start[at] for at in places)
-        acc = lax.fori_loop(0, n, volume, begin, unroll=unroll)
+        acc = lax.fori_loop(0, n * tiles, volume, begin, unroll=unroll)
         for at, value in zip(places, acc):
             vol[at] = value
 
@@ -530,7 +531,7 @@
         amp[j] = jnp.sqrt(jnp.maximum(-p3 * dens[inner_row(j)], 0.0))
 
     filter_block(s_s, d_s, ny - 1, (flags[2], flags[3]), None, finish, True)
-    table(ny - 5, nz, nx, amp, low, high, inner_row, fine_s, vol, None, 4)
+    table(ny - 5, nz, nx, amp, low, high, inner_row, fine_s, vol, None, 11)
 
 
 def inner_call(flags, src, rim, dens, low, high):
@@ -595,7 +596,7 @@
 
         edges = (flags[0], 1) if b == 0 else (1, flags[1])
         filter_block(s_s.at[b], d_s.at[b], 6 + b, (flags[2], flags[3]), edges, finish, True)
-    table(5, nz, nx, amp, low, high, outer_row(ny), fine_s, vol, vol_i, 2)
+    table(5, nz, nx, amp, low, high, outer_row(ny), fine_s, vol, vol_i, 10)
 
     def lanes(ref, count):
         total = ref[pl.ds(0, count, stride=8), :]

time: 43.7 us -> 44.6 us (1.021)
  Pallas kernels: 18.6 us -> 19.4 us
    pallas_call x1, Pallas kernels: 6.2 us -> 6.85 us  [inner_call(): pl.pallas_call(inner_kernel, in_specs=[SMEM] + [VMEM] * 5, out_shape=(jax...]
  transfers between devices with their start and end apart: 5 -> 5, of which waited for: 1 -> 1; matrix products, arithmetic and copies ran while one was open for 0% -> 0% of each run, Pallas kernels for 27% -> 28%
where the time goes in v18:
time: 44.6 us; the launch traced here: 44.4 us
  Pallas kernels  19.4 us (43%)
  blocking collectives  14.8 us (33%)
  starting transfers between devices  5.83 us (13%)
  waiting for transfers between devices  3.4 us (8%)
  between operations  0.8 us (2%)
    all_to_all x1, blocking collectives, on_device(): tables = lax.all_to_all(everyone, ('gz', 'gy'), 0, 0, tiled=True)  14.8 us
    pallas_call x1, Pallas kernels, inner_call(): pl.pallas_call(inner_kernel, in_specs=[SMEM] + [VMEM] * 5, out_shape=(jax...  6.85 us
    ppermute x4, starting transfers between devices, swap(): return lax.ppermute(value, axis, pairs)  4.54 us
    pallas_call x1, Pallas kernels, outer_call(): pl.pallas_call(outer_kernel, in_specs=[SMEM] + [VMEM] * 11, out_shape=(ja...  4.07 us
    ppermute x1, waiting for transfers between devices, to_lower(): return lax.ppermute(value, axis, [(i + 1, i) for i in range(count - 1)])  3.39 us
    pallas_call x1, Pallas kernels, middle_call(): pl.pallas_call(middle_kernel, in_specs=[VMEM] * 8, out_shape=(jax.ShapeDt...  2.86 us
    pallas_call x1, Pallas kernels, ends_call(): pl.pallas_call(ends_kernel, in_specs=[SMEM] + [VMEM] * 3, out_shape=(jax....  2.63 us
    ppermute x1, starting transfers between devices, to_lower(): return lax.ppermute(value, axis, [(i + 1, i) for i in range(count - 1)])  1.29 us
  transfers between devices with their start and end apart: 5, of which 1 were waited for; matrix products, arithmetic and copies ran while one was open for 0% of the time, Pallas kernels for 28%

profile of v18, /device:TPU:0, one launch (start us, length us, event | category | flops | bytes accessed | tf_op | source)
XLA Modules:
  0.0 44.4 jit_solution(3367867502346304260)
XLA Ops:
  0.6 0.0 copy-start
  0.6 1.1 %start.1 = (f32[9,32,128]{2,1,0:T(8,128)S(1)}, bf16[192,224]{1,0:T(8,128)(2,1)S(1)}) custom-call(f32[9,16,32,128]{3,2,1,0:T(8,128)} %disp.7, f32[24,24]{1,0:T(8,128)} %stiff.3), custom_call_target="tpu_custom_call" | custom-call | flops 10000000000 | bytes 1048576 | tf_op jit(solution)/shard_map/start/pallas_call | solution.py:201
  1.8 1.3 %collective-permute-start = (f32[9,32,128]{2,1,0:T(8,128)S(1)}, f32[9,32,128]{2,1,0:T(8,128)S(1)}, u32[]{:S(2)}, u32[]{:S(2)}) collective-permute-start(f32[9,32,128]{2,1,0:T(8,128)S(1)} %get-tuple-element.24), channel_id=1, source_target_pairs={{1,0},{2,1},{3,2},{4,3},{5,4},{6,5},{7,6},{9,8},{10,9},{11,10},{12... | collective-permute-start | bytes 442376 | tf_op jit(solution)/shard_map/ppermute | solution.py:670
  3.1 0.1 stack.27
  3.2 0.0 copy-start.1
  3.3 0.0 copy-start.2
  3.3 0.0 copy-start.4
  3.3 2.6 %energy_ends.1 = (f32[16,16,128]{2,1,0:T(8,128)S(1)}, f32[14,16,128]{2,1,0:T(8,128)S(1)}, f32[14,16,128]{2,1,0:T(8,128)S(1)}, f32[14,16,128]{2,1,0:T(8,128)S(1)}, f32[14,16,128]{2,1,0:T(8,128)S(1)}) custom-call(s32[6]{0:T(128)S(1)} %convert_element_type.3.flags, f32[9,16,32,128]{3,2,1,0:T(8,128)S(1)} %copy-done, f32[16,32,128]{2,1,0:T(8,128)S(1)} %copy-done.3, ...), custom_call_target="tpu_custom_call" | custom-call | flops 4000000000 | bytes 1048576 | tf_op jit(solution)/shard_map/energy_ends/pallas_call | solution.py:261
  5.9 0.5 %collective-permute-start.1 = (f32[14,16,128]{2,1,0:T(8,128)S(1)}, f32[14,16,128]{2,1,0:T(8,128)S(1)}, u32[]{:S(2)}, u32[]{:S(2)}) collective-permute-start(f32[14,16,128]{2,1,0:T(8,128)S(1)} %get-tuple-element.28), channel_id=1, source_target_pairs={{0,8},{8,0},{16,24},{24,16},{1,9},{9,1},{17,25},{25,17},{2,10},{10... | collective-permute-start | bytes 344072 | tf_op jit(solution)/shard_map/ppermute | solution.py:677
  6.4 0.7 %collective-permute-start.2 = (f32[14,16,128]{2,1,0:T(8,128)S(1)}, f32[14,16,128]{2,1,0:T(8,128)S(1)}, u32[]{:S(2)}, u32[]{:S(2)}) collective-permute-start(f32[14,16,128]{2,1,0:T(8,128)S(1)} %get-tuple-element.29), channel_id=1, source_target_pairs={{8,16},{16,8},{9,17},{17,9},{10,18},{18,10},{11,19},{19,11},{12,20... | collective-permute-start | bytes 344072 | tf_op jit(solution)/shard_map/ppermute | solution.py:677
  7.1 3.4 %collective-permute-done.fy = f32[9,32,128]{2,1,0:T(8,128)S(1)} collective-permute-done((f32[9,32,128]{2,1,0:T(8,128)S(1)}, f32[9,32,128]{2,1,0:T(8,128)S(1)}, u32[]{:S(2)}, u32[]{:S(2)}) %collective-permute-start) | collective-permute-done | bytes 147488 | tf_op jit(solution)/shard_map/ppermute | solution.py:670
  10.5 0.0 copy-done.4
  10.5 2.9 %energy_middle.1 = (f32[16,48,128]{2,1,0:T(8,128)S(1)}, f32[16,32,128]{2,1,0:T(8,128)S(1)}, f32[16,32,128]{2,1,0:T(8,128)S(1)}, f32[128,128]{1,0:T(8,128)S(1)}, bf16[192,224]{1,0:T(8,128)(2,1)S(1)}) custom-call(f32[9,16,32,128]{3,2,1,0:T(8,128)S(1)} %copy-done, f32[16,32,128]{2,1,0:T(8,128)S(1)} %copy-done.3, f32[9,32,128]{2,1,0:T(8,128)S(1)} %collective-permute-done.fy, ...), custom_call_target="tpu_custom_call" | custom-call | flops 4000000000 | bytes 1048576 | tf_op jit(solution)/shard_map/energy_middle/pallas_call | solution.py:308
  13.4 0.0 collective-permute-done.1.got_even
  13.4 0.0 collective-permute-done.2.got_odd
  13.4 1.0 %energy_rim.1 = (f32[16,8,128]{2,1,0:T(8,128)S(1)}, f32[2,10,8,128]{3,2,1,0:T(8,128)S(1)}, f32[160,128]{1,0:T(8,128)S(1)}, f32[160,128]{1,0:T(8,128)S(1)}) custom-call(s32[6]{0:T(128)S(1)} %convert_element_type.3.flags, f32[14,16,128]{2,1,0:T(8,128)S(1)} %collective-permute-done.1.got_even, f32[14,16,128]{2,1,0:T(8,128)S(1)} %collective-permute-done.2.got_odd, ...), custom_call_target="tpu_custom_call" | custom-call | flops 2000000000 | bytes 1048576 | tf_op jit(solution)/shard_map/energy_rim/pallas_call | solution.py:398
  14.4 2.7 %collective-permute-start.3 = (f32[160,128]{1,0:T(8,128)S(1)}, f32[160,128]{1,0:T(8,128)S(1)}, u32[]{:S(2)}, u32[]{:S(2)}) collective-permute-start(f32[160,128]{1,0:T(8,128)S(1)} %get-tuple-element.35), channel_id=1, source_target_pairs={{0,1},{1,0},{2,3},{3,2},{4,5},{5,4},{6,7},{7,6},{8,9},{9,8},{10,11... | collective-permute-start | bytes 245768 | tf_op jit(solution)/shard_map/ppermute | solution.py:677
  17.1 0.7 %collective-permute-start.4 = (f32[160,128]{1,0:T(8,128)S(1)}, f32[160,128]{1,0:T(8,128)S(1)}, u32[]{:S(2)}, u32[]{:S(2)}) collective-permute-start(f32[160,128]{1,0:T(8,128)S(1)} %get-tuple-element.36), channel_id=1, source_target_pairs={{1,2},{2,1},{3,4},{4,3},{5,6},{6,5},{9,10},{10,9},{11,12},{12,11},... | collective-permute-start | bytes 245768 | tf_op jit(solution)/shard_map/ppermute | solution.py:677
  17.7 6.9 %filter_inner.1 = (f32[11,32,128]{2,1,0:T(8,128)S(1)}, f32[2048,128]{1,0:T(8,128)S(1)}) custom-call(s32[6]{0:T(128)S(1)} %convert_element_type.3.flags, f32[16,48,128]{2,1,0:T(8,128)S(1)} %get-tuple-element.27.src, f32[16,8,128]{2,1,0:T(8,128)S(1)} %get-tuple-element.33.rim, f32[16,32,128]{2,1,0:T(8,128)S(1)} %copy-done.3, ...), custom_call_target="tpu_custom_call" | custom-call | flops 8999999488 | bytes 1048576 | tf_op jit(solution)/shard_map/filter_inner/pallas_call | solution.py:540
  24.6 0.0 collective-permute-done.3.got_even
  24.6 0.0 collective-permute-done.4.got_odd
  24.6 4.1 %filter_outer.1 = (f32[5,32,128]{2,1,0:T(8,128)S(1)}, f32[1,256]{1,0:T(1,128)S(1)}) custom-call(s32[6]{0:T(128)S(1)} %convert_element_type.3.flags, f32[16,48,128]{2,1,0:T(8,128)S(1)} %get-tuple-element.27.src, f32[16,8,128]{2,1,0:T(8,128)S(1)} %get-tuple-element.33.rim, f32[2,10,8,128]{3,2,1,0:T(8,128)S(1)} %get-tuple-element.34.nodes, ...), custom_call_target="tpu_custom_call" | custom-call | flops 3000000000 | bytes 1048576 | tf_op jit(solution)/shard_map/filter_outer/pallas_call | solution.py:615
  28.7 14.8 %all_to_all.8 = f32[32,1,256]{2,1,0:T(1,128)S(1)} all-to-all(f32[32,1,256]{2,1,0:T(1,128)S(1)} %broadcast_in_dim.2), channel_id=1, replica_groups=mesh['gz'=4,'gy'=8] {'gz','gy'}, dimensions={0} | all-to-all | bytes 65536 | tf_op jit(solution)/shard_map/all_to_all | solution.py:704
  43.5 0.9 %update.1 = (f32[16,32,128]{2,1,0:T(8,128)}, f32[1]{0:T(128)}) custom-call(f32[32,256]{1,0:T(8,128)S(1)} %bitcast.11, f32[11,32,128]{2,1,0:T(8,128)S(1)} %get-tuple-element.42.amp_i, f32[5,32,128]{2,1,0:T(8,128)S(1)} %get-tuple-element.43.amp_o, f32[16,32,128]{2,1,0:T(8,128)S(1)} %get-tuple-element.37.low, f32[16,32,128]{2,1,0:T(8,128)S(1)} %get-tuple-element.38.high), custom_call_target="tpu_custom_call" | custom-call | flops 1000000000 | bytes 1048576 | tf_op jit(solution)/shard_map/update/pallas_call | solution.py:657
  (8 shorter events, 0.0 us)
Async XLA Ops:
  0.6 2.6 %copy-start = (f32[9,16,32,128]{3,2,1,0:T(8,128)S(1)}, f32[9,16,32,128]{3,2,1,0:T(8,128)}, u32[]{:S(2)}) copy-start(f32[9,16,32,128]{3,2,1,0:T(8,128)} %disp.7) | copy-start | bytes 7077892
  0.6 2.6 %copy-start.3 = (f32[16,32,128]{2,1,0:T(8,128)S(1)}, f32[16,32,128]{2,1,0:T(8,128)}, u32[]{:S(2)}) copy-start(f32[16,32,128]{2,1,0:T(8,128)} %dens.9) | copy-start | bytes 786436
  1.8 8.7 %collective-permute-start = (f32[9,32,128]{2,1,0:T(8,128)S(1)}, f32[9,32,128]{2,1,0:T(8,128)S(1)}, u32[]{:S(2)}, u32[]{:S(2)}) collective-permute-start(f32[9,32,128]{2,1,0:T(8,128)S(1)} %get-tuple-element.24), channel_id=1, source_target_pairs={{1,0},{2,1},{3,2},{4,3},{5,4},{6,5},{7,6},{9,8},{10,9},{11,10},{12... | collective-permute-start | bytes 442376 | tf_op jit(solution)/shard_map/ppermute | solution.py:670
  3.2 7.2 %copy-start.1 = (s32[16,32,128]{2,1,0:T(8,128)S(1)}, s32[16,32,128]{2,1,0:T(8,128)}, u32[]{:S(2)}) copy-start(s32[16,32,128]{2,1,0:T(8,128)} %passive.1) | copy-start | bytes 786436
  3.3 7.2 %copy-start.2 = (s32[16,32,128]{2,1,0:T(8,128)S(1)}, s32[16,32,128]{2,1,0:T(8,128)}, u32[]{:S(2)}) copy-start(s32[16,32,128]{2,1,0:T(8,128)} %solid.1) | copy-start | bytes 786436
  3.3 7.2 %copy-start.4 = (f32[24,24]{1,0:T(8,128)S(1)}, f32[24,24]{1,0:T(8,128)}, u32[]{:S(2)}) copy-start(f32[24,24]{1,0:T(8,128)} %stiff.3) | copy-start | bytes 6916
  5.9 7.5 %collective-permute-start.1 = (f32[14,16,128]{2,1,0:T(8,128)S(1)}, f32[14,16,128]{2,1,0:T(8,128)S(1)}, u32[]{:S(2)}, u32[]{:S(2)}) collective-permute-start(f32[14,16,128]{2,1,0:T(8,128)S(1)} %get-tuple-element.28), channel_id=1, source_target_pairs={{0,8},{8,0},{16,24},{24,16},{1,9},{9,1},{17,25},{25,17},{2,10},{10... | collective-permute-start | bytes 344072 | tf_op jit(solution)/shard_map/ppermute | solution.py:677
  6.4 6.9 %collective-permute-start.2 = (f32[14,16,128]{2,1,0:T(8,128)S(1)}, f32[14,16,128]{2,1,0:T(8,128)S(1)}, u32[]{:S(2)}, u32[]{:S(2)}) collective-permute-start(f32[14,16,128]{2,1,0:T(8,128)S(1)} %get-tuple-element.29), channel_id=1, source_target_pairs={{8,16},{16,8},{9,17},{17,9},{10,18},{18,10},{11,19},{19,11},{12,20... | collective-permute-start | bytes 344072 | tf_op jit(solution)/shard_map/ppermute | solution.py:677
  14.4 10.2 %collective-permute-start.3 = (f32[160,128]{1,0:T(8,128)S(1)}, f32[160,128]{1,0:T(8,128)S(1)}, u32[]{:S(2)}, u32[]{:S(2)}) collective-permute-start(f32[160,128]{1,0:T(8,128)S(1)} %get-tuple-element.35), channel_id=1, source_target_pairs={{0,1},{1,0},{2,3},{3,2},{4,5},{5,4},{6,7},{7,6},{8,9},{9,8},{10,11... | collective-permute-start | bytes 245768 | tf_op jit(solution)/shard_map/ppermute | solution.py:677
  17.1 7.5 %collective-permute-start.4 = (f32[160,128]{1,0:T(8,128)S(1)}, f32[160,128]{1,0:T(8,128)S(1)}, u32[]{:S(2)}, u32[]{:S(2)}) collective-permute-start(f32[160,128]{1,0:T(8,128)S(1)} %get-tuple-element.36), channel_id=1, source_target_pairs={{1,2},{2,1},{3,4},{4,3},{5,6},{6,5},{9,10},{10,9},{11,12},{12,11},... | collective-permute-start | bytes 245768 | tf_op jit(solution)/shard_map/ppermute | solution.py:677

commit v19 on v17

--- a/solution.py
+++ b/solution.py
@@ -481,8 +481,16 @@
 
 def table(n, nz, nx, amp, low, high, row, fine_s, vol, start, unroll):
     pair = 2
-    for first in range(0, COARSE, pair):
-        inverse = [inverse_coarse(i) for i in range(first, first + pair)]
+
+    def run(first, make):
+        inverse = []
+        for i in range(pair):
+            c = inverse_coarse(i)
+            if not make:
+                c = jnp.float32(inverse_coarse(pair + i))
+                for other in range(2 * pair, COARSE, pair):
+                    c = jnp.where(first == other, jnp.float32(inverse_coarse(other + i)), c)
+            inverse.append(c)
 
         def volume(j, acc):
             acc = list(acc)
@@ -492,7 +500,7 @@
                 lo, hi = low[y, at], high[y, at]
                 los, his = [lo * c for c in inverse], [hi * c for c in inverse]
                 for f in range(FINE):
-                    if first == 0:
+                    if make:
                         t = amp[j, at] * math.exp(-0.5 * SPACING * f)
                         fine_s[f, j, at] = t
                     else:
@@ -501,11 +509,19 @@
                         acc[i * FINE + f] = acc[i * FINE + f] + jnp.minimum(jnp.maximum(t, los[i]), his[i])
             return tuple(acc)
 
-        places = [slice(8 * (first * FINE + e), 8 * (first * FINE + e) + 8) for e in range(pair * FINE)]
+        places = [pl.ds(pl.multiple_of(8 * FINE * first + 8 * e, 8), 8) for e in range(pair * FINE)]
         begin = tuple(jnp.zeros((8, nx), f32) if start is None else start[at] for at in places)
         acc = lax.fori_loop(0, n, volume, begin, unroll=unroll)
         for at, value in zip(places, acc):
             vol[at] = value
+
+    run(0, True)
+
+    def later(q, _):
+        run(pair * q, False)
+        return 0
+
+    lax.fori_loop(1, COARSE // pair, later, 0)
 
 
 def inner_row(j):

time: 43.7 us -> 43.6 us (level)
  no operation moved by 1% of the time
where the time goes in v19:
time: 43.6 us; the launch traced here: 43.4 us
  Pallas kernels  18.4 us (42%)
  blocking collectives  14.8 us (34%)
  starting transfers between devices  5.83 us (13%)
  waiting for transfers between devices  3.4 us (8%)
  between operations  0.8 us (2%)
    all_to_all x1, blocking collectives, on_device(): tables = lax.all_to_all(everyone, ('gz', 'gy'), 0, 0, tiled=True)  14.8 us
    pallas_call x1, Pallas kernels, inner_call(): pl.pallas_call(inner_kernel, in_specs=[SMEM] + [VMEM] * 5, out_shape=(jax...  6.11 us
    ppermute x4, starting transfers between devices, swap(): return lax.ppermute(value, axis, pairs)  4.54 us
    pallas_call x1, Pallas kernels, outer_call(): pl.pallas_call(outer_kernel, in_specs=[SMEM] + [VMEM] * 11, out_shape=(ja...  3.78 us
    ppermute x1, waiting for transfers between devices, to_lower(): return lax.ppermute(value, axis, [(i + 1, i) for i in range(count - 1)])  3.39 us
    pallas_call x1, Pallas kernels, middle_call(): pl.pallas_call(middle_kernel, in_specs=[VMEM] * 8, out_shape=(jax.ShapeDt...  2.86 us
    pallas_call x1, Pallas kernels, ends_call(): pl.pallas_call(ends_kernel, in_specs=[SMEM] + [VMEM] * 3, out_shape=(jax....  2.63 us
    ppermute x1, starting transfers between devices, to_lower(): return lax.ppermute(value, axis, [(i + 1, i) for i in range(count - 1)])  1.29 us
  transfers between devices with their start and end apart: 5, of which 1 were waited for; matrix products, arithmetic and copies ran while one was open for 0% of the time, Pallas kernels for 27%

profile of v19, /device:TPU:0, one launch (start us, length us, event | category | flops | bytes accessed | tf_op | source)
XLA Modules:
  0.0 43.4 jit_solution(2345687195897808123)
XLA Ops:
  0.6 0.0 copy-start
  0.6 1.1 %start.1 = (f32[9,32,128]{2,1,0:T(8,128)S(1)}, bf16[192,224]{1,0:T(8,128)(2,1)S(1)}) custom-call(f32[9,16,32,128]{3,2,1,0:T(8,128)} %disp.7, f32[24,24]{1,0:T(8,128)} %stiff.3), custom_call_target="tpu_custom_call" | custom-call | flops 10000000000 | bytes 1048576 | tf_op jit(solution)/shard_map/start/pallas_call | solution.py:201
  1.8 1.3 %collective-permute-start = (f32[9,32,128]{2,1,0:T(8,128)S(1)}, f32[9,32,128]{2,1,0:T(8,128)S(1)}, u32[]{:S(2)}, u32[]{:S(2)}) collective-permute-start(f32[9,32,128]{2,1,0:T(8,128)S(1)} %get-tuple-element.24), channel_id=1, source_target_pairs={{1,0},{2,1},{3,2},{4,3},{5,4},{6,5},{7,6},{9,8},{10,9},{11,10},{12... | collective-permute-start | bytes 442376 | tf_op jit(solution)/shard_map/ppermute | solution.py:685
  3.1 0.1 stack.27
  3.2 0.0 copy-start.1
  3.3 0.0 copy-start.2
  3.3 0.0 copy-start.4
  3.3 2.6 %energy_ends.1 = (f32[16,16,128]{2,1,0:T(8,128)S(1)}, f32[14,16,128]{2,1,0:T(8,128)S(1)}, f32[14,16,128]{2,1,0:T(8,128)S(1)}, f32[14,16,128]{2,1,0:T(8,128)S(1)}, f32[14,16,128]{2,1,0:T(8,128)S(1)}) custom-call(s32[6]{0:T(128)S(1)} %convert_element_type.3.flags, f32[9,16,32,128]{3,2,1,0:T(8,128)S(1)} %copy-done, f32[16,32,128]{2,1,0:T(8,128)S(1)} %copy-done.3, ...), custom_call_target="tpu_custom_call" | custom-call | flops 4000000000 | bytes 1048576 | tf_op jit(solution)/shard_map/energy_ends/pallas_call | solution.py:261
  5.9 0.5 %collective-permute-start.1 = (f32[14,16,128]{2,1,0:T(8,128)S(1)}, f32[14,16,128]{2,1,0:T(8,128)S(1)}, u32[]{:S(2)}, u32[]{:S(2)}) collective-permute-start(f32[14,16,128]{2,1,0:T(8,128)S(1)} %get-tuple-element.28), channel_id=1, source_target_pairs={{0,8},{8,0},{16,24},{24,16},{1,9},{9,1},{17,25},{25,17},{2,10},{10... | collective-permute-start | bytes 344072 | tf_op jit(solution)/shard_map/ppermute | solution.py:692
  6.4 0.7 %collective-permute-start.2 = (f32[14,16,128]{2,1,0:T(8,128)S(1)}, f32[14,16,128]{2,1,0:T(8,128)S(1)}, u32[]{:S(2)}, u32[]{:S(2)}) collective-permute-start(f32[14,16,128]{2,1,0:T(8,128)S(1)} %get-tuple-element.29), channel_id=1, source_target_pairs={{8,16},{16,8},{9,17},{17,9},{10,18},{18,10},{11,19},{19,11},{12,20... | collective-permute-start | bytes 344072 | tf_op jit(solution)/shard_map/ppermute | solution.py:692
  7.1 3.4 %collective-permute-done.fy = f32[9,32,128]{2,1,0:T(8,128)S(1)} collective-permute-done((f32[9,32,128]{2,1,0:T(8,128)S(1)}, f32[9,32,128]{2,1,0:T(8,128)S(1)}, u32[]{:S(2)}, u32[]{:S(2)}) %collective-permute-start) | collective-permute-done | bytes 147488 | tf_op jit(solution)/shard_map/ppermute | solution.py:685
  10.5 0.0 copy-done.4
  10.5 2.9 %energy_middle.1 = (f32[16,48,128]{2,1,0:T(8,128)S(1)}, f32[16,32,128]{2,1,0:T(8,128)S(1)}, f32[16,32,128]{2,1,0:T(8,128)S(1)}, f32[128,128]{1,0:T(8,128)S(1)}, bf16[192,224]{1,0:T(8,128)(2,1)S(1)}) custom-call(f32[9,16,32,128]{3,2,1,0:T(8,128)S(1)} %copy-done, f32[16,32,128]{2,1,0:T(8,128)S(1)} %copy-done.3, f32[9,32,128]{2,1,0:T(8,128)S(1)} %collective-permute-done.fy, ...), custom_call_target="tpu_custom_call" | custom-call | flops 4000000000 | bytes 1048576 | tf_op jit(solution)/shard_map/energy_middle/pallas_call | solution.py:308
  13.4 0.0 collective-permute-done.1.got_even
  13.4 0.0 collective-permute-done.2.got_odd
  13.4 1.0 %energy_rim.1 = (f32[16,8,128]{2,1,0:T(8,128)S(1)}, f32[2,10,8,128]{3,2,1,0:T(8,128)S(1)}, f32[160,128]{1,0:T(8,128)S(1)}, f32[160,128]{1,0:T(8,128)S(1)}) custom-call(s32[6]{0:T(128)S(1)} %convert_element_type.3.flags, f32[14,16,128]{2,1,0:T(8,128)S(1)} %collective-permute-done.1.got_even, f32[14,16,128]{2,1,0:T(8,128)S(1)} %collective-permute-done.2.got_odd, ...), custom_call_target="tpu_custom_call" | custom-call | flops 2000000000 | bytes 1048576 | tf_op jit(solution)/shard_map/energy_rim/pallas_call | solution.py:398
  14.4 2.7 %collective-permute-start.3 = (f32[160,128]{1,0:T(8,128)S(1)}, f32[160,128]{1,0:T(8,128)S(1)}, u32[]{:S(2)}, u32[]{:S(2)}) collective-permute-start(f32[160,128]{1,0:T(8,128)S(1)} %get-tuple-element.35), channel_id=1, source_target_pairs={{0,1},{1,0},{2,3},{3,2},{4,5},{5,4},{6,7},{7,6},{8,9},{9,8},{10,11... | collective-permute-start | bytes 245768 | tf_op jit(solution)/shard_map/ppermute | solution.py:692
  17.1 0.7 %collective-permute-start.4 = (f32[160,128]{1,0:T(8,128)S(1)}, f32[160,128]{1,0:T(8,128)S(1)}, u32[]{:S(2)}, u32[]{:S(2)}) collective-permute-start(f32[160,128]{1,0:T(8,128)S(1)} %get-tuple-element.36), channel_id=1, source_target_pairs={{1,2},{2,1},{3,4},{4,3},{5,6},{6,5},{9,10},{10,9},{11,12},{12,11},... | collective-permute-start | bytes 245768 | tf_op jit(solution)/shard_map/ppermute | solution.py:692
  17.7 6.1 %filter_inner.1 = (f32[11,32,128]{2,1,0:T(8,128)S(1)}, f32[2048,128]{1,0:T(8,128)S(1)}) custom-call(s32[6]{0:T(128)S(1)} %convert_element_type.3.flags, f32[16,48,128]{2,1,0:T(8,128)S(1)} %get-tuple-element.27.src, f32[16,8,128]{2,1,0:T(8,128)S(1)} %get-tuple-element.33.rim, f32[16,32,128]{2,1,0:T(8,128)S(1)} %copy-done.3, ...), custom_call_target="tpu_custom_call" | custom-call | flops 8999999488 | bytes 1048576 | tf_op jit(solution)/shard_map/filter_inner/pallas_call | solution.py:555
  23.9 0.0 collective-permute-done.3.got_even
  23.9 0.0 collective-permute-done.4.got_odd
  23.9 3.8 %filter_outer.1 = (f32[5,32,128]{2,1,0:T(8,128)S(1)}, f32[1,256]{1,0:T(1,128)S(1)}) custom-call(s32[6]{0:T(128)S(1)} %convert_element_type.3.flags, f32[16,48,128]{2,1,0:T(8,128)S(1)} %get-tuple-element.27.src, f32[16,8,128]{2,1,0:T(8,128)S(1)} %get-tuple-element.33.rim, f32[2,10,8,128]{3,2,1,0:T(8,128)S(1)} %get-tuple-element.34.nodes, ...), custom_call_target="tpu_custom_call" | custom-call | flops 3000000000 | bytes 1048576 | tf_op jit(solution)/shard_map/filter_outer/pallas_call | solution.py:630
  27.7 14.8 %all_to_all.8 = f32[32,1,256]{2,1,0:T(1,128)S(1)} all-to-all(f32[32,1,256]{2,1,0:T(1,128)S(1)} %broadcast_in_dim.2), channel_id=1, replica_groups=mesh['gz'=4,'gy'=8] {'gz','gy'}, dimensions={0} | all-to-all | bytes 65536 | tf_op jit(solution)/shard_map/all_to_all | solution.py:719
  42.5 0.9 %update.1 = (f32[16,32,128]{2,1,0:T(8,128)}, f32[1]{0:T(128)}) custom-call(f32[32,256]{1,0:T(8,128)S(1)} %bitcast.11, f32[11,32,128]{2,1,0:T(8,128)S(1)} %get-tuple-element.42.amp_i, f32[5,32,128]{2,1,0:T(8,128)S(1)} %get-tuple-element.43.amp_o, f32[16,32,128]{2,1,0:T(8,128)S(1)} %get-tuple-element.37.low, f32[16,32,128]{2,1,0:T(8,128)S(1)} %get-tuple-element.38.high), custom_call_target="tpu_custom_call" | custom-call | flops 1000000000 | bytes 1048576 | tf_op jit(solution)/shard_map/update/pallas_call | solution.py:672
  (8 shorter events, 0.0 us)
Async XLA Ops:
  0.6 2.6 %copy-start = (f32[9,16,32,128]{3,2,1,0:T(8,128)S(1)}, f32[9,16,32,128]{3,2,1,0:T(8,128)}, u32[]{:S(2)}) copy-start(f32[9,16,32,128]{3,2,1,0:T(8,128)} %disp.7) | copy-start | bytes 7077892
  0.6 2.6 %copy-start.3 = (f32[16,32,128]{2,1,0:T(8,128)S(1)}, f32[16,32,128]{2,1,0:T(8,128)}, u32[]{:S(2)}) copy-start(f32[16,32,128]{2,1,0:T(8,128)} %dens.9) | copy-start | bytes 786436
  1.8 8.7 %collective-permute-start = (f32[9,32,128]{2,1,0:T(8,128)S(1)}, f32[9,32,128]{2,1,0:T(8,128)S(1)}, u32[]{:S(2)}, u32[]{:S(2)}) collective-permute-start(f32[9,32,128]{2,1,0:T(8,128)S(1)} %get-tuple-element.24), channel_id=1, source_target_pairs={{1,0},{2,1},{3,2},{4,3},{5,4},{6,5},{7,6},{9,8},{10,9},{11,10},{12... | collective-permute-start | bytes 442376 | tf_op jit(solution)/shard_map/ppermute | solution.py:685
  3.2 7.2 %copy-start.1 = (s32[16,32,128]{2,1,0:T(8,128)S(1)}, s32[16,32,128]{2,1,0:T(8,128)}, u32[]{:S(2)}) copy-start(s32[16,32,128]{2,1,0:T(8,128)} %passive.1) | copy-start | bytes 786436
  3.3 7.2 %copy-start.2 = (s32[16,32,128]{2,1,0:T(8,128)S(1)}, s32[16,32,128]{2,1,0:T(8,128)}, u32[]{:S(2)}) copy-start(s32[16,32,128]{2,1,0:T(8,128)} %solid.1) | copy-start | bytes 786436
  3.3 7.2 %copy-start.4 = (f32[24,24]{1,0:T(8,128)S(1)}, f32[24,24]{1,0:T(8,128)}, u32[]{:S(2)}) copy-start(f32[24,24]{1,0:T(8,128)} %stiff.3) | copy-start | bytes 6916
  5.9 7.5 %collective-permute-start.1 = (f32[14,16,128]{2,1,0:T(8,128)S(1)}, f32[14,16,128]{2,1,0:T(8,128)S(1)}, u32[]{:S(2)}, u32[]{:S(2)}) collective-permute-start(f32[14,16,128]{2,1,0:T(8,128)S(1)} %get-tuple-element.28), channel_id=1, source_target_pairs={{0,8},{8,0},{16,24},{24,16},{1,9},{9,1},{17,25},{25,17},{2,10},{10... | collective-permute-start | bytes 344072 | tf_op jit(solution)/shard_map/ppermute | solution.py:692
  6.4 6.9 %collective-permute-start.2 = (f32[14,16,128]{2,1,0:T(8,128)S(1)}, f32[14,16,128]{2,1,0:T(8,128)S(1)}, u32[]{:S(2)}, u32[]{:S(2)}) collective-permute-start(f32[14,16,128]{2,1,0:T(8,128)S(1)} %get-tuple-element.29), channel_id=1, source_target_pairs={{8,16},{16,8},{9,17},{17,9},{10,18},{18,10},{11,19},{19,11},{12,20... | collective-permute-start | bytes 344072 | tf_op jit(solution)/shard_map/ppermute | solution.py:692
  14.4 9.5 %collective-permute-start.3 = (f32[160,128]{1,0:T(8,128)S(1)}, f32[160,128]{1,0:T(8,128)S(1)}, u32[]{:S(2)}, u32[]{:S(2)}) collective-permute-start(f32[160,128]{1,0:T(8,128)S(1)} %get-tuple-element.35), channel_id=1, source_target_pairs={{0,1},{1,0},{2,3},{3,2},{4,5},{5,4},{6,7},{7,6},{8,9},{9,8},{10,11... | collective-permute-start | bytes 245768 | tf_op jit(solution)/shard_map/ppermute | solution.py:692
  17.1 6.8 %collective-permute-start.4 = (f32[160,128]{1,0:T(8,128)S(1)}, f32[160,128]{1,0:T(8,128)S(1)}, u32[]{:S(2)}, u32[]{:S(2)}) collective-permute-start(f32[160,128]{1,0:T(8,128)S(1)} %get-tuple-element.36), channel_id=1, source_target_pairs={{1,2},{2,1},{3,4},{4,3},{5,6},{6,5},{9,10},{10,9},{11,12},{12,11},... | collective-permute-start | bytes 245768 | tf_op jit(solution)/shard_map/ppermute | solution.py:692

commit v20 on v19

--- a/solution.py
+++ b/solution.py
@@ -611,7 +611,7 @@
 
         edges = (flags[0], 1) if b == 0 else (1, flags[1])
         filter_block(s_s.at[b], d_s.at[b], 6 + b, (flags[2], flags[3]), edges, finish, True)
-    table(5, nz, nx, amp, low, high, outer_row(ny), fine_s, vol, vol_i, 2)
+    table(5, nz, nx, amp, low, high, outer_row(ny), fine_s, vol, vol_i, True)
 
     def lanes(ref, count):
         total = ref[pl.ds(0, count, stride=8), :]

time: 43.6 us -> 43.6 us (level)
  no operation moved by 1% of the time
where the time goes in v20:
time: 43.6 us; the launch traced here: 43.4 us
  Pallas kernels  18.4 us (42%)
  blocking collectives  14.8 us (34%)
  starting transfers between devices  5.83 us (13%)
  waiting for transfers between devices  3.4 us (8%)
  between operations  0.8 us (2%)
    all_to_all x1, blocking collectives, on_device(): tables = lax.all_to_all(everyone, ('gz', 'gy'), 0, 0, tiled=True)  14.8 us
    pallas_call x1, Pallas kernels, inner_call(): pl.pallas_call(inner_kernel, in_specs=[SMEM] + [VMEM] * 5, out_shape=(jax...  6.11 us
    ppermute x4, starting transfers between devices, swap(): return lax.ppermute(value, axis, pairs)  4.54 us
    pallas_call x1, Pallas kernels, outer_call(): pl.pallas_call(outer_kernel, in_specs=[SMEM] + [VMEM] * 11, out_shape=(ja...  3.81 us
    ppermute x1, waiting for transfers between devices, to_lower(): return lax.ppermute(value, axis, [(i + 1, i) for i in range(count - 1)])  3.39 us
    pallas_call x1, Pallas kernels, middle_call(): pl.pallas_call(middle_kernel, in_specs=[VMEM] * 8, out_shape=(jax.ShapeDt...  2.86 us
    pallas_call x1, Pallas kernels, ends_call(): pl.pallas_call(ends_kernel, in_specs=[SMEM] + [VMEM] * 3, out_shape=(jax....  2.63 us
    ppermute x1, starting transfers between devices, to_lower(): return lax.ppermute(value, axis, [(i + 1, i) for i in range(count - 1)])  1.29 us
  transfers between devices with their start and end apart: 5, of which 1 were waited for; matrix products, arithmetic and copies ran while one was open for 0% of the time, Pallas kernels for 27%

profile of v20, /device:TPU:0, one launch (start us, length us, event | category | flops | bytes accessed | tf_op | source)
XLA Modules:
  0.0 43.4 jit_solution(9215201522988079616)
XLA Ops:
  0.6 0.0 copy-start
  0.6 1.1 %start.1 = (f32[9,32,128]{2,1,0:T(8,128)S(1)}, bf16[192,224]{1,0:T(8,128)(2,1)S(1)}) custom-call(f32[9,16,32,128]{3,2,1,0:T(8,128)} %disp.7, f32[24,24]{1,0:T(8,128)} %stiff.3), custom_call_target="tpu_custom_call" | custom-call | flops 10000000000 | bytes 1048576 | tf_op jit(solution)/shard_map/start/pallas_call | solution.py:201
  1.8 1.3 %collective-permute-start = (f32[9,32,128]{2,1,0:T(8,128)S(1)}, f32[9,32,128]{2,1,0:T(8,128)S(1)}, u32[]{:S(2)}, u32[]{:S(2)}) collective-permute-start(f32[9,32,128]{2,1,0:T(8,128)S(1)} %get-tuple-element.24), channel_id=1, source_target_pairs={{1,0},{2,1},{3,2},{4,3},{5,4},{6,5},{7,6},{9,8},{10,9},{11,10},{12... | collective-permute-start | bytes 442376 | tf_op jit(solution)/shard_map/ppermute | solution.py:685
  3.1 0.1 stack.27
  3.2 0.0 copy-start.1
  3.3 0.0 copy-start.2
  3.3 0.0 copy-start.4
  3.3 2.6 %energy_ends.1 = (f32[16,16,128]{2,1,0:T(8,128)S(1)}, f32[14,16,128]{2,1,0:T(8,128)S(1)}, f32[14,16,128]{2,1,0:T(8,128)S(1)}, f32[14,16,128]{2,1,0:T(8,128)S(1)}, f32[14,16,128]{2,1,0:T(8,128)S(1)}) custom-call(s32[6]{0:T(128)S(1)} %convert_element_type.3.flags, f32[9,16,32,128]{3,2,1,0:T(8,128)S(1)} %copy-done, f32[16,32,128]{2,1,0:T(8,128)S(1)} %copy-done.3, ...), custom_call_target="tpu_custom_call" | custom-call | flops 4000000000 | bytes 1048576 | tf_op jit(solution)/shard_map/energy_ends/pallas_call | solution.py:261
  5.9 0.5 %collective-permute-start.1 = (f32[14,16,128]{2,1,0:T(8,128)S(1)}, f32[14,16,128]{2,1,0:T(8,128)S(1)}, u32[]{:S(2)}, u32[]{:S(2)}) collective-permute-start(f32[14,16,128]{2,1,0:T(8,128)S(1)} %get-tuple-element.28), channel_id=1, source_target_pairs={{0,8},{8,0},{16,24},{24,16},{1,9},{9,1},{17,25},{25,17},{2,10},{10... | collective-permute-start | bytes 344072 | tf_op jit(solution)/shard_map/ppermute | solution.py:692
  6.4 0.7 %collective-permute-start.2 = (f32[14,16,128]{2,1,0:T(8,128)S(1)}, f32[14,16,128]{2,1,0:T(8,128)S(1)}, u32[]{:S(2)}, u32[]{:S(2)}) collective-permute-start(f32[14,16,128]{2,1,0:T(8,128)S(1)} %get-tuple-element.29), channel_id=1, source_target_pairs={{8,16},{16,8},{9,17},{17,9},{10,18},{18,10},{11,19},{19,11},{12,20... | collective-permute-start | bytes 344072 | tf_op jit(solution)/shard_map/ppermute | solution.py:692
  7.1 3.4 %collective-permute-done.fy = f32[9,32,128]{2,1,0:T(8,128)S(1)} collective-permute-done((f32[9,32,128]{2,1,0:T(8,128)S(1)}, f32[9,32,128]{2,1,0:T(8,128)S(1)}, u32[]{:S(2)}, u32[]{:S(2)}) %collective-permute-start) | collective-permute-done | bytes 147488 | tf_op jit(solution)/shard_map/ppermute | solution.py:685
  10.5 0.0 copy-done.4
  10.5 2.9 %energy_middle.1 = (f32[16,48,128]{2,1,0:T(8,128)S(1)}, f32[16,32,128]{2,1,0:T(8,128)S(1)}, f32[16,32,128]{2,1,0:T(8,128)S(1)}, f32[128,128]{1,0:T(8,128)S(1)}, bf16[192,224]{1,0:T(8,128)(2,1)S(1)}) custom-call(f32[9,16,32,128]{3,2,1,0:T(8,128)S(1)} %copy-done, f32[16,32,128]{2,1,0:T(8,128)S(1)} %copy-done.3, f32[9,32,128]{2,1,0:T(8,128)S(1)} %collective-permute-done.fy, ...), custom_call_target="tpu_custom_call" | custom-call | flops 4000000000 | bytes 1048576 | tf_op jit(solution)/shard_map/energy_middle/pallas_call | solution.py:308
  13.4 0.0 collective-permute-done.1.got_even
  13.4 0.0 collective-permute-done.2.got_odd
  13.4 1.0 %energy_rim.1 = (f32[16,8,128]{2,1,0:T(8,128)S(1)}, f32[2,10,8,128]{3,2,1,0:T(8,128)S(1)}, f32[160,128]{1,0:T(8,128)S(1)}, f32[160,128]{1,0:T(8,128)S(1)}) custom-call(s32[6]{0:T(128)S(1)} %convert_element_type.3.flags, f32[14,16,128]{2,1,0:T(8,128)S(1)} %collective-permute-done.1.got_even, f32[14,16,128]{2,1,0:T(8,128)S(1)} %collective-permute-done.2.got_odd, ...), custom_call_target="tpu_custom_call" | custom-call | flops 2000000000 | bytes 1048576 | tf_op jit(solution)/shard_map/energy_rim/pallas_call | solution.py:398
  14.4 2.7 %collective-permute-start.3 = (f32[160,128]{1,0:T(8,128)S(1)}, f32[160,128]{1,0:T(8,128)S(1)}, u32[]{:S(2)}, u32[]{:S(2)}) collective-permute-start(f32[160,128]{1,0:T(8,128)S(1)} %get-tuple-element.35), channel_id=1, source_target_pairs={{0,1},{1,0},{2,3},{3,2},{4,5},{5,4},{6,7},{7,6},{8,9},{9,8},{10,11... | collective-permute-start | bytes 245768 | tf_op jit(solution)/shard_map/ppermute | solution.py:692
  17.1 0.7 %collective-permute-start.4 = (f32[160,128]{1,0:T(8,128)S(1)}, f32[160,128]{1,0:T(8,128)S(1)}, u32[]{:S(2)}, u32[]{:S(2)}) collective-permute-start(f32[160,128]{1,0:T(8,128)S(1)} %get-tuple-element.36), channel_id=1, source_target_pairs={{1,2},{2,1},{3,4},{4,3},{5,6},{6,5},{9,10},{10,9},{11,12},{12,11},... | collective-permute-start | bytes 245768 | tf_op jit(solution)/shard_map/ppermute | solution.py:692
  17.7 6.1 %filter_inner.1 = (f32[11,32,128]{2,1,0:T(8,128)S(1)}, f32[2048,128]{1,0:T(8,128)S(1)}) custom-call(s32[6]{0:T(128)S(1)} %convert_element_type.3.flags, f32[16,48,128]{2,1,0:T(8,128)S(1)} %get-tuple-element.27.src, f32[16,8,128]{2,1,0:T(8,128)S(1)} %get-tuple-element.33.rim, f32[16,32,128]{2,1,0:T(8,128)S(1)} %copy-done.3, ...), custom_call_target="tpu_custom_call" | custom-call | flops 8999999488 | bytes 1048576 | tf_op jit(solution)/shard_map/filter_inner/pallas_call | solution.py:555
  23.9 0.0 collective-permute-done.3.got_even
  23.9 0.0 collective-permute-done.4.got_odd
  23.9 3.8 %filter_outer.1 = (f32[5,32,128]{2,1,0:T(8,128)S(1)}, f32[1,256]{1,0:T(1,128)S(1)}) custom-call(s32[6]{0:T(128)S(1)} %convert_element_type.3.flags, f32[16,48,128]{2,1,0:T(8,128)S(1)} %get-tuple-element.27.src, f32[16,8,128]{2,1,0:T(8,128)S(1)} %get-tuple-element.33.rim, f32[2,10,8,128]{3,2,1,0:T(8,128)S(1)} %get-tuple-element.34.nodes, ...), custom_call_target="tpu_custom_call" | custom-call | flops 3000000000 | bytes 1048576 | tf_op jit(solution)/shard_map/filter_outer/pallas_call | solution.py:630
  27.7 14.8 %all_to_all.8 = f32[32,1,256]{2,1,0:T(1,128)S(1)} all-to-all(f32[32,1,256]{2,1,0:T(1,128)S(1)} %broadcast_in_dim.2), channel_id=1, replica_groups=mesh['gz'=4,'gy'=8] {'gz','gy'}, dimensions={0} | all-to-all | bytes 65536 | tf_op jit(solution)/shard_map/all_to_all | solution.py:719
  42.5 0.9 %update.1 = (f32[16,32,128]{2,1,0:T(8,128)}, f32[1]{0:T(128)}) custom-call(f32[32,256]{1,0:T(8,128)S(1)} %bitcast.11, f32[11,32,128]{2,1,0:T(8,128)S(1)} %get-tuple-element.42.amp_i, f32[5,32,128]{2,1,0:T(8,128)S(1)} %get-tuple-element.43.amp_o, f32[16,32,128]{2,1,0:T(8,128)S(1)} %get-tuple-element.37.low, f32[16,32,128]{2,1,0:T(8,128)S(1)} %get-tuple-element.38.high), custom_call_target="tpu_custom_call" | custom-call | flops 1000000000 | bytes 1048576 | tf_op jit(solution)/shard_map/update/pallas_call | solution.py:672
  (8 shorter events, 0.0 us)
Async XLA Ops:
  0.6 2.6 %copy-start = (f32[9,16,32,128]{3,2,1,0:T(8,128)S(1)}, f32[9,16,32,128]{3,2,1,0:T(8,128)}, u32[]{:S(2)}) copy-start(f32[9,16,32,128]{3,2,1,0:T(8,128)} %disp.7) | copy-start | bytes 7077892
  0.6 2.6 %copy-start.3 = (f32[16,32,128]{2,1,0:T(8,128)S(1)}, f32[16,32,128]{2,1,0:T(8,128)}, u32[]{:S(2)}) copy-start(f32[16,32,128]{2,1,0:T(8,128)} %dens.9) | copy-start | bytes 786436
  1.8 8.7 %collective-permute-start = (f32[9,32,128]{2,1,0:T(8,128)S(1)}, f32[9,32,128]{2,1,0:T(8,128)S(1)}, u32[]{:S(2)}, u32[]{:S(2)}) collective-permute-start(f32[9,32,128]{2,1,0:T(8,128)S(1)} %get-tuple-element.24), channel_id=1, source_target_pairs={{1,0},{2,1},{3,2},{4,3},{5,4},{6,5},{7,6},{9,8},{10,9},{11,10},{12... | collective-permute-start | bytes 442376 | tf_op jit(solution)/shard_map/ppermute | solution.py:685
  3.2 7.2 %copy-start.1 = (s32[16,32,128]{2,1,0:T(8,128)S(1)}, s32[16,32,128]{2,1,0:T(8,128)}, u32[]{:S(2)}) copy-start(s32[16,32,128]{2,1,0:T(8,128)} %passive.1) | copy-start | bytes 786436
  3.3 7.2 %copy-start.2 = (s32[16,32,128]{2,1,0:T(8,128)S(1)}, s32[16,32,128]{2,1,0:T(8,128)}, u32[]{:S(2)}) copy-start(s32[16,32,128]{2,1,0:T(8,128)} %solid.1) | copy-start | bytes 786436
  3.3 7.2 %copy-start.4 = (f32[24,24]{1,0:T(8,128)S(1)}, f32[24,24]{1,0:T(8,128)}, u32[]{:S(2)}) copy-start(f32[24,24]{1,0:T(8,128)} %stiff.3) | copy-start | bytes 6916
  5.9 7.5 %collective-permute-start.1 = (f32[14,16,128]{2,1,0:T(8,128)S(1)}, f32[14,16,128]{2,1,0:T(8,128)S(1)}, u32[]{:S(2)}, u32[]{:S(2)}) collective-permute-start(f32[14,16,128]{2,1,0:T(8,128)S(1)} %get-tuple-element.28), channel_id=1, source_target_pairs={{0,8},{8,0},{16,24},{24,16},{1,9},{9,1},{17,25},{25,17},{2,10},{10... | collective-permute-start | bytes 344072 | tf_op jit(solution)/shard_map/ppermute | solution.py:692
  6.4 6.9 %collective-permute-start.2 = (f32[14,16,128]{2,1,0:T(8,128)S(1)}, f32[14,16,128]{2,1,0:T(8,128)S(1)}, u32[]{:S(2)}, u32[]{:S(2)}) collective-permute-start(f32[14,16,128]{2,1,0:T(8,128)S(1)} %get-tuple-element.29), channel_id=1, source_target_pairs={{8,16},{16,8},{9,17},{17,9},{10,18},{18,10},{11,19},{19,11},{12,20... | collective-permute-start | bytes 344072 | tf_op jit(solution)/shard_map/ppermute | solution.py:692
  14.4 9.5 %collective-permute-start.3 = (f32[160,128]{1,0:T(8,128)S(1)}, f32[160,128]{1,0:T(8,128)S(1)}, u32[]{:S(2)}, u32[]{:S(2)}) collective-permute-start(f32[160,128]{1,0:T(8,128)S(1)} %get-tuple-element.35), channel_id=1, source_target_pairs={{0,1},{1,0},{2,3},{3,2},{4,5},{5,4},{6,7},{7,6},{8,9},{9,8},{10,11... | collective-permute-start | bytes 245768 | tf_op jit(solution)/shard_map/ppermute | solution.py:692
  17.1 6.8 %collective-permute-start.4 = (f32[160,128]{1,0:T(8,128)S(1)}, f32[160,128]{1,0:T(8,128)S(1)}, u32[]{:S(2)}, u32[]{:S(2)}) collective-permute-start(f32[160,128]{1,0:T(8,128)S(1)} %get-tuple-element.36), channel_id=1, source_target_pairs={{1,2},{2,1},{3,4},{4,3},{5,6},{6,5},{9,10},{10,9},{11,12},{12,11},... | collective-permute-start | bytes 245768 | tf_op jit(solution)/shard_map/ppermute | solution.py:692
